TPU v7x, 32 devices: a whole 2x2x4 slice. The times are simulated.
32 devices in a mesh: dp: 8 (over y, x, core), chan: 4 (over z).
Axes of the slice: x: 2, y: 2, z: 4, core: 2. Of those that a mesh axis runs over, the one named last changes fastest.
Arguments:
- spectra: bfloat16 [16, 256, 3072], P('dp', 'chan'), may hold values from -6 to 6
- lengths: int32 [16], P('dp'), may hold values from 25 to 384, as said below
- weight_in: bfloat16 [9, 512, 256], P(None, 'chan'), may hold values from -0.125 to 0.125
- gamma_in: float32 [512], P('chan'), may hold values from 0.5 to 2
- beta_in: float32 [512], P('chan'), may hold values from -2 to 2
- weight_mid: bfloat16 [9, 512, 512], P(None, 'chan'), may hold values from -0.09375 to 0.09375
- gamma_mid: float32 [512], P('chan'), may hold values from 0.5 to 2
- beta_mid: float32 [512], P('chan'), may hold values from -2 to 2
- cotangent: bfloat16 [16, 512, 768], P('dp', 'chan'), may hold values from -6 to 6
Outputs:
- block_out: bfloat16 [16, 512, 768], P('dp', 'chan')
- spectra_grad: float32 [16, 256, 3072], P('dp', 'chan')
- weight_in_grad: float32 [9, 512, 256], P(None, 'chan')
- gamma_in_grad: float32 [512], P('chan')
- beta_in_grad: float32 [512], P('chan')
- weight_mid_grad: float32 [9, 512, 512], P(None, 'chan')
- gamma_mid_grad: float32 [512], P('chan')
- beta_mid_grad: float32 [512], P('chan')
- root_squares: float32 [4], replicated
Inputs may be any that keep to these rules, and one draw needn't show every extreme that they name: `lengths`: some clip has exactly 384 valid frames.
All inputs are finite; a program needn't handle non-finite values.
Results may differ from a plain program's by a relative error of at most 0.014.
Values may be sent and summed in bfloat16 or wider, within the bound.
No kernel may reach another device: no remote copies, remote signals or barrier semaphores. Data moves between devices by JAX's collectives and lax.ppermute only.
A program may use at most 256 MiB of HBM per device.

v0:
```python
import functools

import jax
import jax.numpy as jnp
from jax import lax
from jax.experimental import pallas as pl
from jax.experimental.pallas import tpu as pltpu
from jax.sharding import PartitionSpec as P

MEL = 8
HALO = 16
BF = jnp.bfloat16
F32 = jnp.float32
MIB = 1024 * 1024

VMEM = pl.BlockSpec(memory_space=pltpu.VMEM)
SMEM = pl.BlockSpec(memory_space=pltpu.SMEM)
ANY = pl.BlockSpec(memory_space=pl.ANY)
HBM = pl.BlockSpec(memory_space=pltpu.HBM)


def bits_of(n):
    return n.bit_length() - 1


class Geometry:
    def __init__(self, ndp, nch, clips, frames, c_in, c_mid):
        self.ndp, self.nch, self.ndev = ndp, nch, ndp * nch
        self.clips, self.frames = clips, frames
        self.ci_all, self.cm = c_in, c_mid
        self.ci, self.co = c_in // nch, c_mid // nch
        self.segs = nch // clips
        self.seg = frames // self.segs
        self.win = self.seg + HALO * min(self.segs - 1, 2)
        starts = [min(max(s * self.seg - HALO, 0), frames - self.win) for s in range(self.segs)]
        self.cwin = min(frames, (self.win + 48 + 63) // 64 * 64)
        assert all(min(s // 64 * 64, frames - self.cwin) + self.cwin >= s + self.win for s in starts)
        self.rows = max(16, self.co // ndp)
        self.pieces = self.co // self.rows
        self.planes = self.pieces // 2
        self.turns = bits_of(self.planes)
        self.zturns = bits_of(nch)

    def mask(self, core, turn):
        low, high = 1 << turn, 1 << (self.turns - 1 - turn)
        return low + core * (high - low)

    def plane_of(self, core, e):
        rel = 0
        for t in range(self.turns):
            if (e >> (self.turns - 1 - t)) & 1:
                rel = rel ^ self.mask(core, t)
        return rel

    def row_of(self, core, plane):
        return core * (self.co // 2) + plane * self.rows

    def zed_of(self, e):
        return sum(1 << t for t in range(self.zturns) if (e >> (self.zturns - 1 - t)) & 1)


class Here:
    def __init__(self, g, lens):
        self.z = lax.axis_index("chan")
        self.d = lax.axis_index("dp")
        self.core = lax.rem(self.d, 2)
        self.plane = lax.rem(self.d, g.pieces) // 2
        clip, seg = self.z // g.segs, lax.rem(self.z, g.segs)
        self.length = lens[clip]
        self.start, self.cstart = g_starts(g, seg)
        self.off = seg * g.seg - self.start
        self.qoff = self.start - self.cstart


def g_starts(g, seg):
    start = jnp.clip(seg * g.seg - HALO, 0, g.frames - g.win)
    return start, jnp.minimum(start // 64 * 64, g.frames - g.cwin)


def aligned(x, n=16):
    return pl.multiple_of(x, n)


def dot(a, b, contract):
    return lax.dot_general(a, b, ((contract[0], contract[1]), ((), ())), preferred_element_type=F32)


def call(body, out, ins, args, scratch, limit, flops, nbytes, name, aliases=None):
    return pl.pallas_call(
        body,
        out_shape=[pltpu.VMEM(o.shape, o.dtype) if isinstance(o, jax.ShapeDtypeStruct) else o for o in out],
        in_specs=ins,
        out_specs=[VMEM if isinstance(o, jax.ShapeDtypeStruct) else ANY for o in out],
        scratch_shapes=scratch,
        input_output_aliases=aliases or {},
        compiler_params=pltpu.CompilerParams(vmem_limit_bytes=limit * MIB),
        cost_estimate=pl.CostEstimate(
            flops=int(flops), bytes_accessed=int(nbytes), transcendentals=0
        ),
        name=name,
    )(*args)


def arr(shape, dtype):
    return jax.ShapeDtypeStruct(shape, dtype)


def keep_near(*xs):
    return [pltpu.with_memory_space_constraint(x, pltpu.VMEM) for x in xs]


class Copies:
    def __init__(self, sems):
        self.sems, self.n, self.open = sems, 0, []

    def start(self, src, dst):
        c = pltpu.make_async_copy(src, dst, self.sems.at[self.n])
        self.n += 1
        c.start()
        self.open.append(c)
        return c

    def wait(self, c):
        self.open = [o for o in self.open if o is not c]
        c.wait()

    def wait_all(self, some=None):
        for c in list(self.open if some is None else some):
            self.wait(c)


def sems(n):
    return pltpu.SemaphoreType.DMA((n,))


def row_masks(g, here, width):
    r = lax.broadcasted_iota(jnp.int32, (g.win, 128), 0)
    valid = (r + here.start) < here.length
    own = valid & (r >= here.off) & (r < here.off + g.seg)
    return widen(valid.astype(F32), width), widen(own.astype(F32), width)


def widen(x, width):
    return jnp.concatenate([x] * (width // 128), axis=1)


def shifted(x):
    n = x.shape[0]
    r = lax.broadcasted_iota(jnp.int32, (8, 1), 0)
    before, after = pltpu.roll(x, 1, 0), pltpu.roll(x, n - 1, 0)
    before = jnp.concatenate([jnp.where(r == 0, 0.0, before[:8]), before[8:]], axis=0)
    after = jnp.concatenate([after[:-8], jnp.where(r == 7, 0.0, after[-8:])], axis=0)
    return before, after


def grid_order(rows=16):
    n = MEL * rows
    r = lax.broadcasted_iota(jnp.int32, (n, n), 0)
    c = lax.broadcasted_iota(jnp.int32, (n, n), 1)
    return (c == (r % rows) * MEL + r // rows).astype(BF)


def lanes(vector):
    n = vector.shape[1] // 128
    return jnp.concatenate([vector[:, 128 * i : 128 * (i + 1)] for i in range(n)], axis=0)


def unlanes(rows):
    return jnp.concatenate([rows[i : i + 1] for i in range(rows.shape[0])], axis=1)


def misc_row(*scalars):
    lane = lax.broadcasted_iota(jnp.int32, (1, 128), 1)
    row = jnp.zeros((1, 128), F32)
    for i, s in enumerate(scalars):
        row = jnp.where(lane == i, s, row)
    return row


def pick(row, i):
    lane = lax.broadcasted_iota(jnp.int32, (1, 128), 1)
    return jnp.sum(jnp.where(lane == i, row, 0.0), axis=1, keepdims=True)


def sum_rows(x):
    return jnp.sum(x, axis=0, keepdims=True)


def payload(rows, *parts):
    have = sum(r.shape[0] for r in parts)
    if have < rows:
        parts = (*parts, jnp.zeros((rows - have, 128), F32))
    return jnp.concatenate(parts, axis=0)


def fan_kernel(pay, *rest):
    out = rest[-1]
    out[...] = jnp.broadcast_to(pay[...][None], out.shape)


def fan(g, pay, *after):
    out = [arr((g.ndev, *pay.shape), F32)]
    ins = [VMEM] + [ANY] * len(after)
    return call(fan_kernel, out, ins, [pay, *after], [], 4, 0, 1e5, "fan")[0]


def total_of(g, ref):
    n = g.cm // 128
    block = jnp.sum(ref[:, : 2 * n, :], axis=0)
    return unlanes(block[:n]), unlanes(block[n:])


def misc_of(g, ref):
    return jnp.sum(ref[:, 2 * (g.cm // 128), :], axis=0, keepdims=True)


def side_by_side(x3, m, low, c, first, last):
    x3[m, :, 0:c] = first.astype(BF)
    x3[m, :, c : 2 * c] = low
    x3[m, :, 2 * c : 3 * c] = last.astype(BF)


def cut_weights_kernel(g, w_in, w_mid, out, sem):
    d = lax.axis_index("dp")
    core, plane = lax.rem(d, 2), lax.rem(d, g.pieces) // 2
    rows = pl.ds(aligned(g.row_of(core, plane)), g.rows)
    copies = Copies(sem)
    copies.start(w_in.at[:, rows, :], out.at[:, :, : g.ci_all])
    copies.start(w_mid.at[:, rows, :], out.at[:, :, g.ci_all :])
    copies.wait_all()


def cut_weights(g, w_in, w_mid):
    out = [arr((9, g.rows, g.ci_all + g.cm), BF)]
    args = [in_hbm(w_in), in_hbm(w_mid)]
    body = functools.partial(cut_weights_kernel, g)
    return call(body, out, [ANY] * 2, args, [sems(2)], 4, 0, 4e5, "cut_weights")[0]


def stack_kernel(*refs):
    for k, r in enumerate(refs[:-1]):
        refs[-1][k] = r[...]


def stack(parts, name):
    out = [arr((len(parts), *parts[0].shape), parts[0].dtype)]
    return call(stack_kernel, out, [VMEM] * len(parts), parts, [], 4, 0, 1e6, name)[0]


def cut_maps_kernel(g, spec, after, *rest):
    n = g.nch
    xs, sem = rest[:n], rest[n]
    z = lax.axis_index("chan")
    copies = Copies(sem)
    for k in range(n):
        to = z ^ k
        clip, seg = to // g.segs, lax.rem(to, g.segs)
        start, _ = g_starts(g, seg)
        copies.start(spec.at[clip, :, pl.ds(aligned(start * MEL, 128), g.win * MEL)], xs[k])
    copies.wait_all()


def cut_maps(g, spec, after):
    n = g.nch
    out = [arr((g.ci, g.win * MEL), BF)] * n
    body = functools.partial(cut_maps_kernel, g)
    return call(body, out, [ANY] * 2, [in_hbm(spec), after], [sems(n)], 4, 0, 2e6, "cut_maps")


def cut_cot_kernel(g, cot, after, *rest):
    n = g.nch
    cs, sem = rest[:n], rest[n]
    z = lax.axis_index("chan")
    copies = Copies(sem)
    for k in range(n):
        to = z ^ k
        clip, seg = to // g.segs, lax.rem(to, g.segs)
        _, cstart = g_starts(g, seg)
        copies.start(cot.at[clip, :, pl.ds(aligned(cstart * 2, 128), g.cwin * 2)], cs[k])
    copies.wait_all()


def cut_cot(g, cot, after):
    n = g.nch
    out = [arr((g.co, g.cwin * 2), BF)] * n
    body = functools.partial(cut_cot_kernel, g)
    return call(body, out, [ANY] * 2, [in_hbm(cot), after], [sems(n)], 4, 0, 1e6, "cut_cotangent")


def in_hbm(x):
    return pltpu.with_memory_space_constraint(x, pltpu.HBM)


def join_kernel(g, own_in, own_mid, *rest):
    parts, w_in, w_mid = rest[:-2], rest[-2], rest[-1]
    z, d = lax.axis_index("chan"), lax.axis_index("dp")
    mine, plane = lax.rem(d, 2), lax.rem(d, g.pieces) // 2
    w_in[:, pl.ds(aligned(z * g.co), g.co), :] = own_in[...]
    w_mid[:, pl.ds(aligned(z * g.co), g.co), :] = own_mid[...]
    for side in range(2):
        core = mine if side == 0 else 1 - mine
        for e in range(g.planes):
            row = g.row_of(core, plane ^ g.plane_of(core, e))
            for k in range(1, g.nch):
                at = pl.ds(aligned((z ^ k) * g.co + row), g.rows)
                part = parts[side * g.planes + e]
                w_in[:, at, :] = part[k - 1, :, :, : g.ci_all]
                w_mid[:, at, :] = part[k - 1, :, :, g.ci_all :]


def join(g, own_in, own_mid, parts):
    body = functools.partial(join_kernel, g)
    args = [own_in, own_mid, *parts]
    ins = [VMEM] * len(args)
    out = [arr((9, g.cm, g.ci_all), BF), arr((9, g.cm, g.cm), BF)]
    return call(body, out, ins, args, [], 8, 0, 4 * MIB, "join")


def convolve(g, v3, w, part, back, finish, carry):
    def taps(t):
        b = 2 - t if back else t
        return jnp.concatenate([w[b], w[3 + b], w[6 + b]], axis=0 if back else 1)

    contract = ((1,), (0,)) if back else ((1,), (1,))
    depth = v3.shape[2]

    def times(first, n, t):
        return dot(v3[pl.ds(first, n)].reshape(n * g.win, depth), taps(t), contract)

    def step(i, carry):
        part[pl.ds(3 * i + 1, 3)] = times(5 * i, 3, 2 * i).reshape(3, g.win, part.shape[2])
        part[7 * i] = jnp.zeros(part.shape[1:], F32)
        total = times(4 * i, 4, 1) + times(1 + 2 * i, 4, 2 - 2 * i)
        for k in range(4):
            m = 4 * i + k
            carry = finish(m, part[m] + total[k * g.win : (k + 1) * g.win], carry)
        return carry

    return lax.fori_loop(0, 2, step, carry)


def convolve_sums(g, here, x3, w, pre):
    _, own = row_masks(g, here, g.cm)

    def finish(m, total, sums):
        pre[m] = total
        kept = total * own
        return sums[0] + sum_rows(kept), sums[1] + sum_rows(kept * total)

    zero = jnp.zeros((1, g.cm), F32)
    return convolve(g, x3, w, pre, False, finish, (zero, zero))


def first_kernel(g, lens, gains, w, *rest):
    xs, (pre, x3, pay, maps) = rest[: g.nch], rest[g.nch :]
    here = Here(g, lens)
    c = g.ci_all
    for k in range(g.nch):
        maps[pl.ds(aligned((here.z ^ k) * g.ci), g.ci), :] = xs[k][...]
    order = grid_order()
    row = lax.broadcasted_iota(jnp.int32, (MEL * 16, 128), 0) % 16

    def place_cells(j, square):
        cells = maps[:, 128 * j : 128 * (j + 1)]
        frame = row + 16 * j
        valid = (frame + here.start) < here.length
        own = (frame >= here.off) & (frame < here.off + g.seg)
        block = dot(order, cells, ((1,), (1,))) * widen(valid.astype(F32), c)
        x3[:, 16 * j : 16 * (j + 1), c : 2 * c] = block.astype(BF).reshape(MEL, 16, c)
        return square + sum_rows(block * block * widen(own.astype(F32), c))

    square = jnp.zeros((1, c), F32)
    for j in range(g.win // 16):
        square = place_cells(j, square)
    for m in range(MEL):
        before, after_ = shifted(x3[m, :, c : 2 * c].astype(F32))
        x3[m, :, 0:c] = before.astype(BF)
        x3[m, :, 2 * c : 3 * c] = after_.astype(BF)

    one, two = convolve_sums(g, here, x3, w, pre)
    frame_total = 0
    pair_total = 0
    for i in range(g.clips):
        frame_total = frame_total + lens[i]
        pair_total = pair_total + (lens[i] + 1) // 2
    row = misc_row(
        frame_total.astype(F32), pair_total.astype(F32), jnp.sum(square, axis=1, keepdims=True)
    )
    pay[...] = payload(16, lanes(one), lanes(two), row, gains[...])


def first(g, lens, gains, maps, w):
    body = functools.partial(first_kernel, g)
    out = [
        arr((MEL, g.win, g.cm), F32),
        arr((MEL, g.win, 3 * g.ci_all), BF),
        arr((16, 128), F32),
    ]
    args = [lens, gains, *keep_near(w, *maps)]
    ins = [SMEM] + [VMEM] * (2 + g.nch)
    flops = 2 * 9 * MEL * g.win * g.ci_all * g.cm
    scratch = [pltpu.VMEM((g.ci_all, g.win * MEL), BF)]
    return call(body, out, ins, args, scratch, 10, flops, 10 * MIB, "first_conv")


MEAN1, INV1, GAMMA1, BETA1, GAMMA2, BETA2, COUNT, PAIRS, SQ0, MEAN2, INV2 = range(11)
TABLE = 16


def half_affine(mean, inverse, gamma, beta):
    scale = 0.5 * gamma * inverse
    return scale, 0.5 * beta - mean * scale


def second_kernel(g, lens, got, pre1, w, pre, x3, table, pay, misc_out):
    here = Here(g, lens)
    c = g.cm
    valid, own = row_masks(g, here, c)
    one, two = total_of(g, got)
    misc = misc_of(g, got)
    count = MEL * pick(misc, 0) / g.nch
    pairs = (MEL // 2) * pick(misc, 1) / g.nch
    at = 2 * (c // 128) + 1
    vectors = [
        jnp.concatenate([got[zz, at + i : at + i + 1, : g.co] for zz in range(g.nch)], axis=1)
        for i in range(4)
    ]
    mean = one / count
    inverse = lax.rsqrt(two / count - mean * mean + 1e-05)
    wide = jnp.zeros((1, c), F32)
    table[...] = jnp.concatenate(
        [mean, inverse, *vectors, wide + count, wide + pairs, wide + pick(misc, 2)]
        + [wide] * (TABLE - 9),
        axis=0,
    )
    scale, shift = half_affine(mean, inverse, vectors[0], vectors[1])


    def activate(m, square):
        half = pre1[m] * scale + shift
        act = half * (1.0 + jnp.tanh(half)) * valid
        low = act.astype(BF)
        before, after = shifted(low.astype(F32))
        side_by_side(x3, m, low, c, before, after)
        return square + sum_rows(act * act * own)

    square = lax.fori_loop(0, MEL, activate, jnp.zeros((1, c), F32))
    one, two = convolve_sums(g, here, x3, w, pre)
    pay[...] = payload(8, lanes(one), lanes(two))
    misc_out[...] = payload(8, misc_row(jnp.sum(square, axis=1, keepdims=True)))


def second(g, lens, got, pre1, w):
    body = functools.partial(second_kernel, g)
    out = [
        arr((MEL, g.win, g.cm), F32),
        arr((MEL, g.win, 3 * g.cm), BF),
        arr((TABLE, g.cm), F32),
        arr((8, 128), F32),
        arr((8, 128), F32),
    ]
    args = [lens, *keep_near(got, pre1, w)]
    flops = 2 * 9 * MEL * g.win * g.cm * g.cm
    ins = [SMEM, VMEM, VMEM, VMEM]
    return call(body, out, ins, args, [], 10, flops, 17 * MIB, "second_conv")


def pool_kernel(g, lens, got, old_ref, pre2, *rest):
    n, c = g.nch, g.cm
    cs, outs = rest[:n], rest[n : 2 * n]
    local_ref, table, pay, misc_out, held, grads, pooled_ref, flat = rest[2 * n :]
    here = Here(g, lens)
    for k in range(n):
        held[pl.ds(aligned((here.z ^ k) * g.co), g.co), :] = cs[k][...]
    r = lax.broadcasted_iota(jnp.int32, (256, 128), 0)
    l = lax.broadcasted_iota(jnp.int32, (256, 128), 1)
    spread = (l == (r % 64) // 2 * 4 + r // 64).astype(BF)

    @pl.loop(0, g.cwin // 64)
    def _(j):
        cells = held[:, pl.ds(aligned(128 * j, 128), 128)]
        block = dot(spread, cells, ((1,), (1,)))
        grads[:, pl.ds(aligned(64 * j), 64), :] = block.reshape(MEL // 2, 64, c)

    one, two = total_of(g, got)
    old = old_ref[...]
    count = old[COUNT : COUNT + 1]
    mean = one / count
    inverse = lax.rsqrt(two / count - mean * mean + 1e-05)
    wide = jnp.zeros((1, c), F32)
    table[...] = jnp.concatenate([old[:MEAN2], mean, inverse] + [wide] * (TABLE - 11), axis=0)
    half_gamma, half_beta = 0.5 * old[GAMMA2 : GAMMA2 + 1], 0.5 * old[BETA2 : BETA2 + 1]
    less = -mean * inverse
    valid, own = row_masks(g, here, c)
    r = lax.broadcasted_iota(jnp.int32, (g.win, 128), 0) + here.start
    share = widen(jnp.where(here.length - r // 2 * 2 >= 2, 0.25, 0.5), c)
    half_share = 0.5 * share * valid
    window = pl.ds(aligned(here.qoff), g.win)
    segment = pl.ds(aligned(here.off), g.seg)

    def step(k, sums):
        beta_sum, gamma_sum, square = sums
        given = grads[k, window, :] * half_share
        pair = None
        for i in range(2):
            m = 2 * k + i
            scaled = pre2[m] * inverse + less
            half = scaled * half_gamma + half_beta
            bend = jnp.tanh(half)
            twice = 1.0 + bend
            act = half * twice * own
            square = square + sum_rows(act * act)
            local = given * (twice * (1.0 + half * (1.0 - bend)))
            local_ref[m] = local
            kept = local * own
            beta_sum = beta_sum + sum_rows(kept)
            gamma_sum = gamma_sum + sum_rows(kept * scaled)
            pair = act if pair is None else pair + act
        pooled_ref[k] = pair * share
        return beta_sum, gamma_sum, square

    zero = jnp.zeros((1, c), F32)
    beta_sum, gamma_sum, square = lax.fori_loop(0, MEL // 2, step, (zero, zero, zero))
    wide_rows = (MEL // 2) * g.seg
    values = jnp.concatenate([pooled_ref[k, segment, :] for k in range(MEL // 2)], axis=0)
    high = values.astype(BF)
    low = (values - high.astype(F32)).astype(BF)
    r = lax.broadcasted_iota(jnp.int32, (wide_rows, 2 * g.seg), 0)
    l = lax.broadcasted_iota(jnp.int32, (wide_rows, 2 * g.seg), 1)
    gather = (l == (r % g.seg) // 2 * 4 + r // g.seg).astype(BF)
    pooled = dot(high, gather, ((0,), (0,))) + dot(low, gather, ((0,), (0,)))
    flat[...] = pooled.astype(BF)
    for k in range(n):
        outs[k][...] = flat[pl.ds(aligned((here.z ^ k) * g.co), g.co), :]
    pooled_square = sum_rows(jnp.sum(pooled * pooled, axis=1, keepdims=True))
    block = payload(8, lanes(beta_sum), lanes(gamma_sum))
    pay[...] = jnp.broadcast_to(block[None], pay.shape)
    misc_out[...] = payload(8, misc_row(jnp.sum(square, axis=1, keepdims=True), pooled_square))


def pool(g, lens, got, table, pre2, cs):
    n = g.nch
    body = functools.partial(pool_kernel, g)
    out = [arr((g.co, 2 * g.seg), BF)] * n + [
        arr((MEL, g.win, g.cm), F32),
        arr((TABLE, g.cm), F32),
        arr((g.ndev, 8, 128), F32),
        arr((8, 128), F32),
    ]
    scratch = [
        pltpu.VMEM((g.cm, g.cwin * 2), BF),
        pltpu.VMEM((MEL // 2, g.cwin, g.cm), F32),
        pltpu.VMEM((MEL // 2, g.win, g.cm), F32),
        pltpu.VMEM((g.cm, 2 * g.seg), BF),
    ]
    args = [lens, *keep_near(got, table, pre2, *cs)]
    ins = [SMEM] + [VMEM] * (len(args) - 1)
    out = call(body, out, ins, args, scratch, 12, 4e9, 8 * MIB, "pool")
    return out[:n], *out[n:]


def terms_kernel(g, depth, norm, lens, got, table, pre, local, x3, after, *rest):
    grad, sums, roots, terms, give, own_grad = rest
    here = Here(g, lens)
    c = g.cm
    valid, own = row_masks(g, here, c)
    beta_sum, gamma_sum = total_of(g, got)
    t = table[...]
    mean, inverse, gamma = (t[i : i + 1] for i in norm)
    count = t[COUNT : COUNT + 1]
    sums[...] = jnp.concatenate([beta_sum, gamma_sum] + [jnp.zeros((1, c), F32)] * 6, axis=0)
    if got.shape[1] > 8:
        at = 2 * (c // 128)
        square1 = pick(jnp.sum(got[:, at, :], axis=0, keepdims=True), 0)
        later = jnp.sum(got[:, at + 1, :], axis=0, keepdims=True)
        tops = misc_row(pick(t[SQ0 : SQ0 + 1, :128], 0), square1, pick(later, 0), pick(later, 1))
        lane = lax.broadcasted_iota(jnp.int32, (1, 128), 1)
        cells, pairs = count[:, :128], t[PAIRS : PAIRS + 1, :128]
        under = jnp.where(lane == 0, cells * g.ci_all, jnp.where(lane == 3, pairs * c, cells * c))
        roots[...] = jnp.broadcast_to(jnp.sqrt(tops / under), (8, 128))
    factor = gamma * inverse
    slope = factor * inverse * gamma_sum / count
    level = factor * beta_sum / count - mean * slope

    @pl.loop(0, MEL)
    def _(m):
        value = valid * (local[m] * factor - pre[m] * slope - level)
        grad[m] = value.astype(BF)
        own_grad[m] = (value * own).astype(BF)

    @pl.loop(0, 3)
    def _(a):
        lanes_of = pl.ds(aligned(a * depth, 128), depth)
        for b in (1, 0, 2):
            low = max(0, 1 - b)
            high = min(MEL, MEL + 1 - b)
            rows = (high - low) * g.win
            left = own_grad[low:high].reshape(rows, c)
            right = x3[low + b - 1 : high + b - 1, :, lanes_of].reshape(rows, depth)
            term = dot(left, right, ((0,), (0,))).astype(BF)
            for z in range(g.nch):
                for s in range(2):
                    for p in range(g.planes):
                        at = z * g.co + g.row_of(s, p)
                        terms[s, z, p, 3 * a + b] = term[at : at + g.rows]

    give[...] = terms[1 - here.core]


def terms_of(g, lens, got, table, pre, local, x3, after, depth, norm, name):
    body = functools.partial(terms_kernel, g, depth, norm)
    shape = (g.nch, g.planes, 9, g.rows, depth)
    out = [
        arr((MEL, g.win, g.cm), BF),
        arr((8, g.cm), F32),
        arr((8, 128), F32),
        arr((2, *shape), BF),
        arr(shape, BF),
    ]
    scratch = [pltpu.VMEM((MEL, g.win, g.cm), BF)]
    args = [lens, *keep_near(got, table, pre, local, x3), after]
    ins = [SMEM] + [VMEM] * 5 + [ANY]
    flops = 2 * 9 * MEL * g.win * g.cm * depth
    return call(body, out, ins, args, scratch, 10, flops, 15 * MIB, name)


def back_kernel(g, lens, table, grad, pre1, w, misc2, misc3, local1, pay, g3):
    here = Here(g, lens)
    c = g.cm
    valid, own = row_masks(g, here, c)
    t = table[...]

    def row(i):
        return t[i : i + 1]


    @pl.loop(0, MEL)
    def _(m):
        low = grad[m]
        before, after = shifted(low.astype(F32))
        side_by_side(g3, m, low, c, after, before)

    inverse, less = row(INV1), -row(MEAN1) * row(INV1)
    half_gamma, half_beta = 0.5 * row(GAMMA1), 0.5 * row(BETA1)
    half_valid = 0.5 * valid

    def finish(m, given, sums):
        scaled = pre1[m] * inverse + less
        half = scaled * half_gamma + half_beta
        bend = jnp.tanh(half)
        local = given * half_valid * ((1.0 + bend) * (1.0 + half * (1.0 - bend)))
        local1[m] = local
        kept = local * own
        return sums[0] + sum_rows(kept), sums[1] + sum_rows(kept * scaled)

    zero = jnp.zeros((1, c), F32)
    beta_sum, gamma_sum = convolve(g, g3, w, local1, True, finish, (zero, zero))
    squares = jnp.concatenate([misc2[0:1], misc3[0:1]], axis=0)
    pay[...] = payload(16, lanes(beta_sum), lanes(gamma_sum), squares)


def back(g, lens, table, grad, pre1, w, misc2, misc3):
    body = functools.partial(back_kernel, g)
    out = [arr((MEL, g.win, g.cm), F32), arr((16, 128), F32)]
    scratch = [pltpu.VMEM((MEL, g.win, 3 * g.cm), BF)]
    args = [lens, *keep_near(table, grad, pre1, w, misc2, misc3)]
    flops = 2 * 9 * MEL * g.win * g.cm * g.cm
    ins = [SMEM] + [VMEM] * 6
    return call(body, out, ins, args, scratch, 14, flops, 20 * MIB, "second_back")


def release_kernel(*refs):
    pass


def release(gates, arrays):
    out = [arr(x.shape, x.dtype) for x in arrays]
    n = len(gates)
    ins = [ANY] * n + [VMEM] * len(arrays)
    aliases = {i + n: i for i in range(len(arrays))}
    args = [*gates, *keep_near(*arrays)]
    return call(release_kernel, out, ins, args, [], 2, 0, 1, "release", aliases)


def spectra_kernel(g, lens, grad, after, w, *rest):
    n, c = g.nch, g.cm
    outs, (g3, rows, flat, part) = rest[:n], rest[n:]
    here = Here(g, lens)

    @pl.loop(0, MEL)
    def _(m):
        low = grad[m]
        before, after_ = shifted(low.astype(F32))
        side_by_side(g3, m, low, c, after_, before)

    _, own = row_masks(g, here, g.ci_all)

    def finish(m, total, carry):
        rows[m] = (total * own).astype(BF)
        return carry

    convolve(g, g3, w, part, True, finish, 0)
    order = grid_order()

    for j in range(g.seg // 16):
        block = rows[:, pl.ds(aligned(here.off + 16 * j), 16), :].reshape(MEL * 16, g.ci_all)
        flat[:, 128 * j : 128 * (j + 1)] = dot(block, order, ((0,), (0,))).astype(BF)

    for k in range(n):
        outs[k][...] = flat[pl.ds(aligned((here.z ^ k) * g.ci), g.ci), :]


def spectra_back(g, lens, grad, after, w):
    n = g.nch
    body = functools.partial(spectra_kernel, g)
    out = [arr((g.ci, g.seg * MEL), BF)] * n
    scratch = [
        pltpu.VMEM((MEL, g.win, 3 * g.cm), BF),
        pltpu.VMEM((MEL, g.win, g.ci_all), BF),
        pltpu.VMEM((g.ci_all, g.seg * MEL), BF),
        pltpu.VMEM((MEL, g.win, g.ci_all), F32),
    ]
    grad, w = keep_near(grad, w)
    args = [lens, grad, after, w]
    flops = 2 * 9 * MEL * g.win * g.cm * g.ci_all
    ins = [SMEM, VMEM, ANY, VMEM]
    return call(body, out, ins, args, scratch, 14, flops, 5 * MIB, "spectra_back")


def place_kernel(g, width, *rest):
    n = g.nch
    parts, out = rest[:n], rest[n]
    z = lax.axis_index("chan")
    for k in range(n):
        source = z ^ k
        for zz in range(n):

            @pl.when(source == zz)
            def _():
                at = zz % g.segs * width
                out[zz // g.segs, :, at : at + width] = parts[k][...].astype(out.dtype)


def place(g, parts, dtype, name):
    channels, width = parts[0].shape
    return pl.pallas_call(
        functools.partial(place_kernel, g, width),
        out_shape=jax.ShapeDtypeStruct((g.clips, channels, g.segs * width), dtype),
        in_specs=[VMEM] * g.nch,
        out_specs=VMEM,
        compiler_params=pltpu.CompilerParams(vmem_limit_bytes=8 * MIB),
        name=name,
    )(*parts)


def core_sum_kernel(g, terms, got, after, stay, go):
    d, z = lax.axis_index("dp"), lax.axis_index("chan")
    core, plane = lax.rem(d, 2), lax.rem(d, g.pieces) // 2
    half = g.planes // 2
    for e in range(g.planes):
        at = plane ^ g.plane_of(core, e)
        for k in range(g.nch):
            source = z ^ g.zed_of(k)
            value = terms[core, source, at].astype(F32) + got[source, at].astype(F32)
            to = stay if e < half else go
            to[(e % half) * g.nch + k] = value.astype(BF)


def core_sum(g, terms, got, after, name):
    shape = (g.planes // 2 * g.nch, *got.shape[2:])
    return pl.pallas_call(
        functools.partial(core_sum_kernel, g),
        out_shape=[pltpu.VMEM(shape, BF)] * 2,
        in_specs=[VMEM, VMEM, ANY],
        out_specs=[VMEM] * 2,
        compiler_params=pltpu.CompilerParams(vmem_limit_bytes=16 * MIB),
        name=name,
    )(keep_near(terms)[0], got, after)


def halve_kernel(stay, got, *rest):
    n = stay.shape[0]
    outs = rest[-2:] if n > 1 else rest[-1:]
    for i in range(n):
        value = stay[i].astype(F32) + got[i].astype(F32)
        if n == 1:
            outs[0][...] = value.astype(BF)
        else:
            outs[i // (n // 2)][i % (n // 2)] = value.astype(BF)


def halve(stay, got, gates, name):
    n = stay.shape[0]
    if n == 1:
        out = [jax.ShapeDtypeStruct(stay.shape[1:], BF)]
    else:
        out = [jax.ShapeDtypeStruct((n // 2, *stay.shape[1:]), BF)] * 2
    return pl.pallas_call(
        halve_kernel,
        out_shape=out,
        in_specs=[VMEM, VMEM] + [ANY] * len(gates),
        out_specs=[VMEM] * len(out),
        compiler_params=pltpu.CompilerParams(vmem_limit_bytes=8 * MIB),
        name=name,
    )(stay, got, *gates)


def spread_kernel(g, *rest):
    parts, out = rest[:-1], rest[-1]
    d = lax.axis_index("dp")
    core, plane = lax.rem(d, 2), lax.rem(d, g.pieces) // 2
    for side in range(2):
        c = core if side == 0 else 1 - core
        for e in range(g.planes):
            at = aligned(g.row_of(c, plane ^ g.plane_of(c, e)))
            out[:, pl.ds(at, g.rows), :] = parts[side * g.planes + e][...].astype(F32)


def spread_out(g, parts, depth, name):
    return pl.pallas_call(
        functools.partial(spread_kernel, g),
        out_shape=jax.ShapeDtypeStruct((9, g.co, depth), F32),
        in_specs=[VMEM] * g.pieces,
        out_specs=VMEM,
        compiler_params=pltpu.CompilerParams(vmem_limit_bytes=12 * MIB),
        name=name,
    )(*parts)


class Links:
    def __init__(self, g):
        self.g = g

    def core(self, x):
        return lax.ppermute(x, "dp", [(i, i ^ 1) for i in range(self.g.ndp)])

    def dp(self, x, bit):
        return lax.ppermute(x, "dp", [(i, i ^ bit) for i in range(self.g.ndp)])

    def plane(self, x, turn):
        g = self.g
        return lax.ppermute(x, "dp", [(i, i ^ (2 * g.mask(i & 1, turn))) for i in range(g.ndp)])

    def chan(self, x, k):
        return lax.ppermute(x, "chan", [(i, i ^ k) for i in range(self.g.nch)])

    def exchange(self, parts):
        return [parts[0]] + [self.chan(parts[k], k) for k in range(1, self.g.nch)]

    def gather_plane(self, x, gates=()):
        have = [x]
        for turn in reversed(range(self.g.turns)):
            last = have[-1]
            if gates and turn == 0 and len(have) > 1:
                (last,) = release(gates, [last])
            have = have + [self.plane(h, turn) for h in (*have[:-1], last)]
        return have + [self.core(h) for h in have]


def everyone(x):
    return lax.all_to_all(x, ("dp", "chan"), 0, 0)


def make_body(ndp, nch):
    def body(
        spectra, lengths, weight_in, gamma_in, beta_in, weight_mid, gamma_mid, beta_mid, cotangent
    ):
        g = Geometry(
            ndp,
            nch,
            spectra.shape[0],
            spectra.shape[2] // MEL,
            weight_in.shape[2],
            weight_mid.shape[2],
        )
        links = Links(g)
        gains = jnp.stack([gamma_in, beta_in, gamma_mid, beta_mid])
        gains = jnp.pad(gains, ((0, 0), (0, 128 - g.co)))

        piece = cut_weights(g, weight_in, weight_mid)
        pieces = stack([links.chan(piece, k) for k in range(1, nch)], "stack_pieces")
        maps = links.exchange(cut_maps(g, spectra, piece))
        cots = cut_cot(g, cotangent, pieces)
        w_in, w_mid = join(g, weight_in, weight_mid, links.gather_plane(pieces, maps[1:]))

        pre1, x3_in, pay = first(g, lengths, gains, maps, w_in)
        got = everyone(fan(g, pay, cots[0]))
        cs = links.exchange(release([got], cots))
        pre2, x3_mid, table, pay, misc2 = second(g, lengths, got, pre1, w_mid)
        got = everyone(fan(g, pay, *cs[1:]))
        pooled, local2, table, pay, misc3 = pool(g, lengths, got, table, pre2, cs)
        got = everyone(pay)
        pooled = links.exchange(release([got], pooled))
        grad2, sums2, _, terms_mid, give_mid = terms_of(
            g, lengths, got, table, pre2, local2, x3_mid, got, g.cm, (MEAN2, INV2, GAMMA2), "weight_mid_terms"
        )
        got_mid = links.core(give_mid)
        local1, pay = back(g, lengths, table, grad2, pre1, w_mid, misc2, misc3)
        stay_mid, go_mid = core_sum(g, terms_mid, got_mid, pay, "mid_core_sum")
        block_out = place(g, pooled, BF, "place_pooled")
        got = everyone(fan(g, pay, stay_mid, block_out))
        (go_mid,) = release([got], [go_mid])
        grad1, sums1, roots, terms_in, give_in = terms_of(
            g, lengths, got, table, pre1, local1, x3_in, got, g.ci_all, (MEAN1, INV1, GAMMA1), "weight_in_terms"
        )
        got_in = links.core(give_in)

        class Chain:
            def __init__(self, stay, go, depth, name):
                self.stay, self.go, self.depth, self.name = stay, go, depth, name
                self.turns = [functools.partial(links.plane, turn=t) for t in range(g.turns)]
                self.turns += [functools.partial(links.chan, k=1 << t) for t in range(g.zturns)]

            def turn(self, i, *gates):
                got = self.turns[i](self.go)
                done = halve(self.stay, got, gates, f"{self.name}_sum_{i}")
                self.stay, self.go = done if len(done) == 2 else (done[0], None)
                return self.stay

            def out(self):
                bit = g.pieces
                while bit < ndp:
                    got = links.dp(self.stay, bit)
                    self.stay = halve(self.stay[None], got[None], [], self.name + "_rest")[0]
                    bit *= 2
                return spread_out(g, links.gather_plane(self.stay), self.depth, self.name + "_out")

        turns = g.turns + g.zturns
        mid = Chain(stay_mid, go_mid, g.cm, "mid")
        parts = spectra_back(g, lengths, grad1, grad1, w_in)
        at = mid.turn(0, parts[0])
        stay_in, go_in = core_sum(g, terms_in, got_in, parts[0], "in_core_sum")
        inner = Chain(stay_in, go_in, g.ci_all, "in")
        parts = links.exchange(parts)
        spectra_grad = place(g, parts, F32, "place_spectra")
        arrivals = [parts[1 : nch - 1], parts[nch - 1 :]]
        for i in range(turns):
            if i + 1 < turns:
                at = mid.turn(i + 1, at, *(arrivals.pop(0) if arrivals else []))
            at = inner.turn(i, at)
        weight_mid_grad = mid.out()
        weight_in_grad = inner.out()
        z = lax.axis_index("chan")

        def share(sums, i):
            return lax.dynamic_slice_in_dim(sums[i], z * g.co, g.co)

        return (
            block_out,
            spectra_grad,
            weight_in_grad,
            share(sums1, 1),
            share(sums1, 0),
            weight_mid_grad,
            share(sums2, 1),
            share(sums2, 0),
            roots[0, :4],
        )

    return body


def solution(mesh):
    placed = (
        P("dp", "chan", None),
        P("dp"),
        P(None, "chan", None),
        P("chan"),
        P("chan"),
        P(None, "chan", None),
        P("chan"),
        P("chan"),
        P("dp", "chan", None),
    )
    return jax.shard_map(
        make_body(mesh.shape["dp"], mesh.shape["chan"]),
        mesh=mesh,
        in_specs=placed,
        out_specs=(
            P("dp", "chan", None),
            P("dp", "chan", None),
            P(None, "chan", None),
            P("chan"),
            P("chan"),
            P(None, "chan", None),
            P("chan"),
            P("chan"),
            P(),
        ),
        check_vma=False,
    )
```

profile of v0, /device:TPU:0, one launch (start us, length us, event | category | flops | bytes accessed | tf_op | source)
XLA Modules:
  0.0 236.5 jit_solution(6736076706420990466)
XLA Ops:
  0.6 1.0 cut_weights.1.after
  1.6 3.1 %collective-permute-start = (bf16[9,16,768]{2,1,0:T(8,128)(2,1)S(1)}, bf16[9,16,768]{2,1,0:T(8,128)(2,1)S(1)}, u32[]{:S(2)}, u32[]{:S(2)}) collective-permute-start(bf16[9,16,768]{2,1,0:T(8,128)(2,1)S(1)} %cut_weights.1.after), channel_id=1, source_target_pairs={{0,1},{1,0},{2,3},{3,2},{4,5},{5,4},{6,7},{7,6},{8,9},{9,8},{10,11... | collective-permute-start | bytes 663560 | tf_op jit(solution)/shard_map/ppermute | solution.py:845
  4.7 2.6 %collective-permute-start.1 = (bf16[9,16,768]{2,1,0:T(8,128)(2,1)S(1)}, bf16[9,16,768]{2,1,0:T(8,128)(2,1)S(1)}, u32[]{:S(2)}, u32[]{:S(2)}) collective-permute-start(bf16[9,16,768]{2,1,0:T(8,128)(2,1)S(1)} %cut_weights.1.after), channel_id=1, source_target_pairs={{0,2},{1,3},{2,0},{3,1},{4,6},{5,7},{6,4},{7,5},{8,10},{9,11},{10,... | collective-permute-start | bytes 663560 | tf_op jit(solution)/shard_map/ppermute | solution.py:845
  7.3 6.8 %collective-permute-done.refs_0_ = bf16[9,16,768]{2,1,0:T(8,128)(2,1)S(1)} collective-permute-done((bf16[9,16,768]{2,1,0:T(8,128)(2,1)S(1)}, bf16[9,16,768]{2,1,0:T(8,128)(2,1)S(1)}, u32[]{:S(2)}, u32[]{:S(2)}) %collective-permute-start) | collective-permute-done | bytes 221216 | tf_op jit(solution)/shard_map/ppermute | solution.py:845
  14.1 9.3 %collective-permute-done.1.refs_1_ = bf16[9,16,768]{2,1,0:T(8,128)(2,1)S(1)} collective-permute-done((bf16[9,16,768]{2,1,0:T(8,128)(2,1)S(1)}, bf16[9,16,768]{2,1,0:T(8,128)(2,1)S(1)}, u32[]{:S(2)}, u32[]{:S(2)}) %collective-permute-start.1) | collective-permute-done | bytes 221216 | tf_op jit(solution)/shard_map/ppermute | solution.py:845
  23.6 1.6 collective-permute-start.3
  25.1 1.3 cut_maps.1
  26.5 3.9 %collective-permute-start.5 = (bf16[64,1664]{1,0:T(8,128)(2,1)S(1)}, bf16[64,1664]{1,0:T(8,128)(2,1)S(1)}, u32[]{:S(2)}, u32[]{:S(2)}) collective-permute-start(bf16[64,1664]{1,0:T(8,128)(2,1)S(1)} %get-tuple-element.74), channel_id=1, source_target_pairs={{0,1},{1,0},{2,3},{3,2},{4,5},{5,4},{6,7},{7,6},{8,9},{9,8},{10,11... | collective-permute-start | bytes 638984 | tf_op jit(solution)/shard_map/ppermute | solution.py:845
  30.4 1.1 collective-permute-start.6
  31.5 1.4 collective-permute-start.7
  32.9 1.5 collective-permute-start.4
  34.4 0.9 collective-permute-done.3.rest_1_
  35.3 1.7 collective-permute-done.5.refs_0_.rest_1_
  37.0 11.0 %collective-permute-done.6.refs_1_.rest_2_ = bf16[64,1664]{1,0:T(8,128)(2,1)S(1)} collective-permute-done((bf16[64,1664]{1,0:T(8,128)(2,1)S(1)}, bf16[64,1664]{1,0:T(8,128)(2,1)S(1)}, u32[]{:S(2)}, u32[]{:S(2)}) %collective-permute-start.6) | collective-permute-done | bytes 213024 | tf_op jit(solution)/shard_map/ppermute | solution.py:845
  49.0 9.7 %collective-permute-done.8.rest_3_ = bf16[3,9,16,768]{3,2,1,0:T(8,128)(2,1)S(1)} collective-permute-done((bf16[3,9,16,768]{3,2,1,0:T(8,128)(2,1)S(1)}, bf16[3,9,16,768]{3,2,1,0:T(8,128)(2,1)S(1)}, u32[]{:S(2)}, u32[]{:S(2)}) %collective-permute-start.8) | collective-permute-done | bytes 663584 | tf_op jit(solution)/shard_map/ppermute | solution.py:842
  58.7 1.2 cut_cotangent.1
  60.0 0.8 collective-permute-done.12.rest_7_
  61.3 6.0 %first_conv.1 = (f32[8,208,512]{2,1,0:T(8,128)S(1)}, bf16[8,208,768]{2,1,0:T(8,128)(2,1)S(1)}, f32[16,128]{1,0:T(8,128)S(1)}) custom-call(s32[2]{0:T(128)S(1)} %copy-done.3, f32[4,128]{1,0:T(4,128)S(1)} %pad_maximum_fusion.gains, bf16[9,512,256]{2,1,0:T(8,128)(2,1)S(1)} %get-tuple-element.77.w, bf16[64,1664]{1,0:T(8,128)(2,1)S(1)} %get-tuple-element.78.rest_0_, ...), custom_call_target="tpu_custom_call" | custom-call | flops 3925868544 | bytes 10485760 | tf_op jit(solution)/shard_map/first_conv/pallas_call | solution.py:89
  67.3 15.2 %all_to_all.20.got.refs_0_ = f32[32,16,128]{2,1,0:T(8,128)S(1)} all-to-all(f32[32,16,128]{2,1,0:T(8,128)S(1)} %fan.3), channel_id=1, replica_groups=mesh['dp'=8,'chan'=4] {'dp','chan'}, dimensions={0} | all-to-all | bytes 524288 | tf_op jit(solution)/shard_map/all_to_all | solution.py:861
  82.5 1.1 collective-permute-start.13
  83.6 1.2 collective-permute-start.14
  84.8 2.1 collective-permute-start.15
  86.9 10.4 %second_conv.1 = (f32[8,208,512]{2,1,0:T(8,128)S(1)}, bf16[8,208,1536]{2,1,0:T(8,128)(2,1)S(1)}, f32[16,512]{1,0:T(8,128)S(1)}, f32[8,128]{1,0:T(8,128)S(1)}, f32[8,128]{1,0:T(8,128)S(1)}) custom-call(s32[2]{0:T(128)S(1)} %copy-done.3, f32[32,16,128]{2,1,0:T(8,128)S(1)} %all_to_all.20.got.refs_0_, f32[8,208,512]{2,1,0:T(8,128)S(1)} %get-tuple-element.81.pre1.pre, ...), custom_call_target="tpu_custom_call" | custom-call | flops 7851737088 | bytes 17825792 | tf_op jit(solution)/shard_map/second_conv/pallas_call | solution.py:89
  97.3 10.9 %all_to_all.21.got = f32[32,8,128]{2,1,0:T(8,128)S(1)} all-to-all(f32[32,8,128]{2,1,0:T(8,128)S(1)} %fan.4), channel_id=1, replica_groups=mesh['dp'=8,'chan'=4] {'dp','chan'}, dimensions={0} | all-to-all | bytes 262144 | tf_op jit(solution)/shard_map/all_to_all | solution.py:861
  108.2 5.9 %pool.1 = (bf16[128,384]{1,0:T(8,128)(2,1)S(1)}, bf16[128,384]{1,0:T(8,128)(2,1)S(1)}, bf16[128,384]{1,0:T(8,128)(2,1)S(1)}, bf16[128,384]{1,0:T(8,128)(2,1)S(1)...) custom-call(s32[2]{0:T(128)S(1)} %copy-done.3, ...), custom_call_target="tpu_custom_call" | custom-call | flops 4000000000 | bytes 8388608 | tf_op jit(solution)/shard_map/pool/pallas_call | solution.py:89
  114.2 10.1 %all_to_all.22.refs_0_.got.after = f32[32,8,128]{2,1,0:T(8,128)S(1)} all-to-all(f32[32,8,128]{2,1,0:T(8,128)S(1)} %get-tuple-element.93), channel_id=1, replica_groups=mesh['dp'=8,'chan'=4] {'dp','chan'}, dimensions={0} | all-to-all | bytes 262144 | tf_op jit(solution)/shard_map/all_to_all | solution.py:861
  124.3 10.0 %weight_mid_terms.1 = (bf16[8,208,512]{2,1,0:T(8,128)(2,1)S(1)}, f32[8,512]{1,0:T(8,128)S(1)}, f32[8,128]{1,0:T(8,128)}, bf16[2,4,4,9,16,512]{5,4,3,2,1,0:T(8,128)(2,1)S(1)}, bf16[4,4,9,16,512]{4,3,2,1,0:T(8,128)(2,1)S(1)}) custom-call(s32[2]{0:T(128)S(1)} %copy-done.3, f32[32,8,128]{2,1,0:T(8,128)S(1)} %all_to_all.22.refs_0_.got.after, ...), custom_call_target="tpu_custom_call" | custom-call | flops 7851737088 | bytes 15728640 | tf_op jit(solution)/shard_map/weight_mid_terms/pallas_call | solution.py:89
  134.6 1.5 collective-permute-start.17
  136.1 2.7 %collective-permute-start.18 = (bf16[128,384]{1,0:T(8,128)(2,1)S(1)}, bf16[128,384]{1,0:T(8,128)(2,1)S(1)}, u32[]{:S(2)}, u32[]{:S(2)}) collective-permute-start(bf16[128,384]{1,0:T(8,128)(2,1)S(1)} %get-tuple-element.101), channel_id=1, source_target_pairs={{0,3},{1,2},{2,1},{3,0},{4,7},{5,6},{6,5},{7,4},{8,11},{9,10},{10,... | collective-permute-start | bytes 294920 | tf_op jit(solution)/shard_map/ppermute | solution.py:845
  138.8 10.6 %second_back.1 = (f32[8,208,512]{2,1,0:T(8,128)S(1)}, f32[16,128]{1,0:T(8,128)S(1)}) custom-call(s32[2]{0:T(128)S(1)} %copy-done.3, f32[16,512]{1,0:T(8,128)S(1)} %get-tuple-element.102.table, bf16[8,208,512]{2,1,0:T(8,128)(2,1)S(1)} %get-tuple-element.105.grad, f32[8,208,512]{2,1,0:T(8,128)S(1)} %get-tuple-element.81.pre1.pre, ...), custom_call_target="tpu_custom_call" | custom-call | flops 7851737088 | bytes 20971520 | tf_op jit(solution)/shard_map/second_back/pallas_call | solution.py:89
  149.5 0.9 place_pooled.1.rest_1_
  150.3 0.5 mid_core_sum.1
  151.3 11.9 %all_to_all.23.got.after.refs_0_ = f32[32,16,128]{2,1,0:T(8,128)S(1)} all-to-all(f32[32,16,128]{2,1,0:T(8,128)S(1)} %fan.5), channel_id=1, replica_groups=mesh['dp'=8,'chan'=4] {'dp','chan'}, dimensions={0} | all-to-all | bytes 524288 | tf_op jit(solution)/shard_map/all_to_all | solution.py:861
  163.2 1.0 collective-permute-start.25
  164.3 6.2 %weight_in_terms.1 = (bf16[8,208,512]{2,1,0:T(8,128)(2,1)S(1)}, f32[8,512]{1,0:T(8,128)S(1)}, f32[8,128]{1,0:T(8,128)S(1)}, bf16[2,4,4,9,16,256]{5,4,3,2,1,0:T(8,128)(2,1)S(1)}, bf16[4,4,9,16,256]{4,3,2,1,0:T(8,128)(2,1)S(1)}) custom-call(s32[2]{0:T(128)S(1)} %copy-done.3, f32[32,16,128]{2,1,0:T(8,128)S(1)} %all_to_all.23.got.after.refs_0_, ...), custom_call_target="tpu_custom_call" | custom-call | flops 3925868544 | bytes 15728640 | tf_op jit(solution)/shard_map/weight_in_terms/pallas_call | solution.py:89
  170.5 5.9 %spectra_back.1 = (bf16[64,1536]{1,0:T(8,128)(2,1)S(1)}, bf16[64,1536]{1,0:T(8,128)(2,1)S(1)}, bf16[64,1536]{1,0:T(8,128)(2,1)S(1)}, bf16[64,1536]{1,0:T(8,128)(2,1)S(1)}) custom-call(s32[2]{0:T(128)S(1)} %copy-done.3, bf16[8,208,512]{2,1,0:T(8,128)(2,1)S(1)} %get-tuple-element.114.grad.after, bf16[8,208,512]{2,1,0:T(8,128)(2,1)S(1)} %get-tuple-element.114.grad.after, ...), custom_call_target="tpu_custom_call" | custom-call | flops 3925868544 | bytes 5242880 | tf_op jit(solution)/shard_map/spectra_back/pallas_call | solution.py:89
  176.5 3.0 %collective-permute-done.25.got = bf16[8,9,16,512]{3,2,1,0:T(8,128)(2,1)S(1)} collective-permute-done((bf16[8,9,16,512]{3,2,1,0:T(8,128)(2,1)S(1)}, bf16[8,9,16,512]{3,2,1,0:T(8,128)(2,1)S(1)}, u32[]{:S(2)}, u32[]{:S(2)}) %collective-permute-start.25) | collective-permute-done | bytes 1179680 | tf_op jit(solution)/shard_map/ppermute | solution.py:842
  179.7 1.1 collective-permute-start.26
  181.1 0.6 collective-permute-start.24
  181.7 1.0 collective-permute-start.20
  182.6 1.3 collective-permute-start.21
  183.9 6.2 %collective-permute-done.20.rest_1_ = bf16[64,1536]{1,0:T(8,128)(2,1)S(1)} collective-permute-done((bf16[64,1536]{1,0:T(8,128)(2,1)S(1)}, bf16[64,1536]{1,0:T(8,128)(2,1)S(1)}, u32[]{:S(2)}, u32[]{:S(2)}) %collective-permute-start.20) | collective-permute-done | bytes 196640 | tf_op jit(solution)/shard_map/ppermute | solution.py:845
  190.1 2.8 %collective-permute-done.21.rest_2_ = bf16[64,1536]{1,0:T(8,128)(2,1)S(1)} collective-permute-done((bf16[64,1536]{1,0:T(8,128)(2,1)S(1)}, bf16[64,1536]{1,0:T(8,128)(2,1)S(1)}, u32[]{:S(2)}, u32[]{:S(2)}) %collective-permute-start.21) | collective-permute-done | bytes 196640 | tf_op jit(solution)/shard_map/ppermute | solution.py:845
  193.0 2.5 %collective-permute-done.26.got = bf16[4,9,16,512]{3,2,1,0:T(8,128)(2,1)S(1)} collective-permute-done((bf16[4,9,16,512]{3,2,1,0:T(8,128)(2,1)S(1)}, bf16[4,9,16,512]{3,2,1,0:T(8,128)(2,1)S(1)}, u32[]{:S(2)}, u32[]{:S(2)}) %collective-permute-start.26) | collective-permute-done | bytes 589856 | tf_op jit(solution)/shard_map/ppermute | solution.py:842
  195.9 1.4 collective-permute-start.27
  197.3 1.2 collective-permute-start.22
  198.5 9.1 %collective-permute-done.22.rest_3_.rest_1_ = bf16[64,1536]{1,0:T(8,128)(2,1)S(1)} collective-permute-done((bf16[64,1536]{1,0:T(8,128)(2,1)S(1)}, bf16[64,1536]{1,0:T(8,128)(2,1)S(1)}, u32[]{:S(2)}, u32[]{:S(2)}) %collective-permute-start.22) | collective-permute-done | bytes 196640 | tf_op jit(solution)/shard_map/ppermute | solution.py:845
  207.7 1.1 collective-permute-start.30
  208.9 1.3 collective-permute-start.29
  210.1 3.8 %collective-permute-done.30.got = bf16[1,9,16,512]{3,2,1,0:T(8,128)(2,1)S(1)} collective-permute-done((bf16[1,9,16,512]{3,2,1,0:T(8,128)(2,1)S(1)}, bf16[1,9,16,512]{3,2,1,0:T(8,128)(2,1)S(1)}, u32[]{:S(2)}, u32[]{:S(2)}) %collective-permute-start.30) | collective-permute-done | bytes 147488 | tf_op jit(solution)/shard_map/ppermute | solution.py:845
  214.0 1.7 collective-permute-start.40
  215.7 2.7 %collective-permute-start.31 = (bf16[1,9,16,256]{3,2,1,0:T(8,128)(2,1)S(1)}, bf16[1,9,16,256]{3,2,1,0:T(8,128)(2,1)S(1)}, u32[]{:S(2)}, u32[]{:S(2)}) collective-permute-start(bf16[1,9,16,256]{3,2,1,0:T(8,128)(2,1)S(1)} %get-tuple-element.135), channel_id=1, source_target_pairs={{0,2},{1,3},{2,0},{3,1},{4,6},{5,7},{6,4},{7,5},{8,10},{9,11},{10,... | collective-permute-start | bytes 221192 | tf_op jit(solution)/shard_map/ppermute | solution.py:845
  218.5 2.6 %collective-permute-done.31.got = bf16[1,9,16,256]{3,2,1,0:T(8,128)(2,1)S(1)} collective-permute-done((bf16[1,9,16,256]{3,2,1,0:T(8,128)(2,1)S(1)}, bf16[1,9,16,256]{3,2,1,0:T(8,128)(2,1)S(1)}, u32[]{:S(2)}, u32[]{:S(2)}) %collective-permute-start.31) | collective-permute-done | bytes 73760 | tf_op jit(solution)/shard_map/ppermute | solution.py:845
  221.1 1.9 collective-permute-start.32
  223.0 0.5 fusion.2
  223.5 0.6 collective-permute-start.33
  224.0 1.5 collective-permute-start.41
  225.5 1.1 collective-permute-start.34
  226.7 1.2 collective-permute-done.33.rest_2_
  228.4 1.9 collective-permute-done.34.rest_3_
  232.0 0.5 fusion
  232.5 1.3 place_spectra.1
  233.8 1.1 in_out.1
  235.0 1.6 mid_out.1
  (88 shorter events, 6.1 us)
Async XLA Ops:
  1.6 12.5 %collective-permute-start = (bf16[9,16,768]{2,1,0:T(8,128)(2,1)S(1)}, bf16[9,16,768]{2,1,0:T(8,128)(2,1)S(1)}, u32[]{:S(2)}, u32[]{:S(2)}) collective-permute-start(bf16[9,16,768]{2,1,0:T(8,128)(2,1)S(1)} %cut_weights.1.after), channel_id=1, source_target_pairs={{0,1},{1,0},{2,3},{3,2},{4,5},{5,4},{6,7},{7,6},{8,9},{9,8},{10,11... | collective-permute-start | bytes 663560 | tf_op jit(solution)/shard_map/ppermute | solution.py:845
  4.7 18.7 %collective-permute-start.1 = (bf16[9,16,768]{2,1,0:T(8,128)(2,1)S(1)}, bf16[9,16,768]{2,1,0:T(8,128)(2,1)S(1)}, u32[]{:S(2)}, u32[]{:S(2)}) collective-permute-start(bf16[9,16,768]{2,1,0:T(8,128)(2,1)S(1)} %cut_weights.1.after), channel_id=1, source_target_pairs={{0,2},{1,3},{2,0},{3,1},{4,6},{5,7},{6,4},{7,5},{8,10},{9,11},{10,... | collective-permute-start | bytes 663560 | tf_op jit(solution)/shard_map/ppermute | solution.py:845
  7.3 16.1 %collective-permute-start.2 = (bf16[9,16,768]{2,1,0:T(8,128)(2,1)S(1)}, bf16[9,16,768]{2,1,0:T(8,128)(2,1)S(1)}, u32[]{:S(2)}, u32[]{:S(2)}) collective-permute-start(bf16[9,16,768]{2,1,0:T(8,128)(2,1)S(1)} %cut_weights.1.after), channel_id=1, source_target_pairs={{0,3},{1,2},{2,1},{3,0},{4,7},{5,6},{6,5},{7,4},{8,11},{9,10},{10,... | collective-permute-start | bytes 663560 | tf_op jit(solution)/shard_map/ppermute | solution.py:845
  23.5 35.2 %copy-start.4 = (f32[128]{0:T(128)S(1)}, f32[128]{0:T(128)}, u32[]{:S(2)}) copy-start(f32[128]{0:T(128)} %param.16) | copy-start | bytes 1540
  23.5 35.2 %copy-start.5 = (f32[128]{0:T(128)S(1)}, f32[128]{0:T(128)}, u32[]{:S(2)}) copy-start(f32[128]{0:T(128)} %param.15) | copy-start | bytes 1540
  23.5 35.2 %copy-start.6 = (f32[128]{0:T(128)S(1)}, f32[128]{0:T(128)}, u32[]{:S(2)}) copy-start(f32[128]{0:T(128)} %param.13) | copy-start | bytes 1540
  23.5 35.2 %copy-start.7 = (f32[128]{0:T(128)S(1)}, f32[128]{0:T(128)}, u32[]{:S(2)}) copy-start(f32[128]{0:T(128)} %param.12) | copy-start | bytes 1540
  23.6 11.7 %collective-permute-start.3 = (bf16[3,9,16,768]{3,2,1,0:T(8,128)(2,1)S(1)}, bf16[3,9,16,768]{3,2,1,0:T(8,128)(2,1)S(1)}, u32[]{:S(2)}, u32[]{:S(2)}) collective-permute-start(bf16[3,9,16,768]{3,2,1,0:T(8,128)(2,1)S(1)} %stack_pieces.1.rest_0_.after), channel_id=1, source_target_pairs={{0,16},{4,12},{8,24},{12,4},{16,0},{20,28},{24,8},{28,20},{1,17},{... | collective-permute-start | bytes 1990664 | tf_op jit(solution)/shard_map/ppermute | solution.py:842
  26.4 34.4 %copy-start = (bf16[9,128,512]{2,1,0:T(8,128)(2,1)S(1)}, bf16[9,128,512]{2,1,0:T(8,128)(2,1)}, u32[]{:S(2)}) copy-start(bf16[9,128,512]{2,1,0:T(8,128)(2,1)} %own_mid.1) | copy-start | bytes 3538948
  26.4 34.4 %copy-start.1 = (bf16[9,128,256]{2,1,0:T(8,128)(2,1)S(1)}, bf16[9,128,256]{2,1,0:T(8,128)(2,1)}, u32[]{:S(2)}) copy-start(bf16[9,128,256]{2,1,0:T(8,128)(2,1)} %own_in.1) | copy-start | bytes 1769476
  26.5 10.6 %collective-permute-start.5 = (bf16[64,1664]{1,0:T(8,128)(2,1)S(1)}, bf16[64,1664]{1,0:T(8,128)(2,1)S(1)}, u32[]{:S(2)}, u32[]{:S(2)}) collective-permute-start(bf16[64,1664]{1,0:T(8,128)(2,1)S(1)} %get-tuple-element.74), channel_id=1, source_target_pairs={{0,1},{1,0},{2,3},{3,2},{4,5},{5,4},{6,7},{7,6},{8,9},{9,8},{10,11... | collective-permute-start | bytes 638984 | tf_op jit(solution)/shard_map/ppermute | solution.py:845
  30.4 17.6 %collective-permute-start.6 = (bf16[64,1664]{1,0:T(8,128)(2,1)S(1)}, bf16[64,1664]{1,0:T(8,128)(2,1)S(1)}, u32[]{:S(2)}, u32[]{:S(2)}) collective-permute-start(bf16[64,1664]{1,0:T(8,128)(2,1)S(1)} %get-tuple-element.75), channel_id=1, source_target_pairs={{0,2},{1,3},{2,0},{3,1},{4,6},{5,7},{6,4},{7,5},{8,10},{9,11},{10,... | collective-permute-start | bytes 638984 | tf_op jit(solution)/shard_map/ppermute | solution.py:845
  31.5 16.5 %collective-permute-start.7 = (bf16[64,1664]{1,0:T(8,128)(2,1)S(1)}, bf16[64,1664]{1,0:T(8,128)(2,1)S(1)}, u32[]{:S(2)}, u32[]{:S(2)}) collective-permute-start(bf16[64,1664]{1,0:T(8,128)(2,1)S(1)} %get-tuple-element.76), channel_id=1, source_target_pairs={{0,3},{1,2},{2,1},{3,0},{4,7},{5,6},{6,5},{7,4},{8,11},{9,10},{10,... | collective-permute-start | bytes 638984 | tf_op jit(solution)/shard_map/ppermute | solution.py:845
  32.9 16.1 %collective-permute-start.4 = (bf16[3,9,16,768]{3,2,1,0:T(8,128)(2,1)S(1)}, bf16[3,9,16,768]{3,2,1,0:T(8,128)(2,1)S(1)}, u32[]{:S(2)}, u32[]{:S(2)}) collective-permute-start(bf16[3,9,16,768]{3,2,1,0:T(8,128)(2,1)S(1)} %stack_pieces.1.rest_0_.after), channel_id=1, source_target_pairs={{0,8},{4,20},{8,0},{12,28},{16,24},{20,4},{24,16},{28,12},{1,9},{5... | collective-permute-start | bytes 1990664 | tf_op jit(solution)/shard_map/ppermute | solution.py:842
  48.0 10.7 %collective-permute-start.8 = (bf16[3,9,16,768]{3,2,1,0:T(8,128)(2,1)S(1)}, bf16[3,9,16,768]{3,2,1,0:T(8,128)(2,1)S(1)}, u32[]{:S(2)}, u32[]{:S(2)}) collective-permute-start(bf16[3,9,16,768]{3,2,1,0:T(8,128)(2,1)S(1)} %release.4), channel_id=1, source_target_pairs={{0,8},{4,20},{8,0},{12,28},{16,24},{20,4},{24,16},{28,12},{1,9},{5... | collective-permute-start | bytes 1990664 | tf_op jit(solution)/shard_map/ppermute | solution.py:842
  48.5 11.4 %collective-permute-start.9 = (bf16[3,9,16,768]{3,2,1,0:T(8,128)(2,1)S(1)}, bf16[3,9,16,768]{3,2,1,0:T(8,128)(2,1)S(1)}, u32[]{:S(2)}, u32[]{:S(2)}) collective-permute-start(bf16[3,9,16,768]{3,2,1,0:T(8,128)(2,1)S(1)} %stack_pieces.1.rest_0_.after), channel_id=1, source_target_pairs={{0,4},{4,0},{8,12},{12,8},{16,20},{20,16},{24,28},{28,24},{1,5},{5... | collective-permute-start | bytes 1990664 | tf_op jit(solution)/shard_map/ppermute | solution.py:835
  48.5 11.4 %collective-permute-start.10 = (bf16[3,9,16,768]{3,2,1,0:T(8,128)(2,1)S(1)}, bf16[3,9,16,768]{3,2,1,0:T(8,128)(2,1)S(1)}, u32[]{:S(2)}, u32[]{:S(2)}) collective-permute-start(bf16[3,9,16,768]{3,2,1,0:T(8,128)(2,1)S(1)} %collective-permute-done.3.rest_1_), channel_id=1, source_target_pairs={{0,4},{4,0},{8,12},{12,8},{16,20},{20,16},{24,28},{28,24},{1,5},{5... | collective-permute-start | bytes 1990664 | tf_op jit(solution)/shard_map/ppermute | solution.py:835
  49.0 10.9 %collective-permute-start.11 = (bf16[3,9,16,768]{3,2,1,0:T(8,128)(2,1)S(1)}, bf16[3,9,16,768]{3,2,1,0:T(8,128)(2,1)S(1)}, u32[]{:S(2)}, u32[]{:S(2)}) collective-permute-start(bf16[3,9,16,768]{3,2,1,0:T(8,128)(2,1)S(1)} %collective-permute-done.4.rest_2_), channel_id=1, source_target_pairs={{0,4},{4,0},{8,12},{12,8},{16,20},{20,16},{24,28},{28,24},{1,5},{5... | collective-permute-start | bytes 1990664 | tf_op jit(solution)/shard_map/ppermute | solution.py:835
  58.7 2.1 collective-permute-start.12
  59.9 1.4 copy-start.3
  82.5 14.8 %collective-permute-start.13 = (bf16[128,512]{1,0:T(8,128)(2,1)S(1)}, bf16[128,512]{1,0:T(8,128)(2,1)S(1)}, u32[]{:S(2)}, u32[]{:S(2)}) collective-permute-start(bf16[128,512]{1,0:T(8,128)(2,1)S(1)} %get-tuple-element.87), channel_id=1, source_target_pairs={{0,1},{1,0},{2,3},{3,2},{4,5},{5,4},{6,7},{7,6},{8,9},{9,8},{10,11... | collective-permute-start | bytes 393224 | tf_op jit(solution)/shard_map/ppermute | solution.py:845
  83.6 13.7 %collective-permute-start.14 = (bf16[128,512]{1,0:T(8,128)(2,1)S(1)}, bf16[128,512]{1,0:T(8,128)(2,1)S(1)}, u32[]{:S(2)}, u32[]{:S(2)}) collective-permute-start(bf16[128,512]{1,0:T(8,128)(2,1)S(1)} %get-tuple-element.88), channel_id=1, source_target_pairs={{0,2},{1,3},{2,0},{3,1},{4,6},{5,7},{6,4},{7,5},{8,10},{9,11},{10,... | collective-permute-start | bytes 393224 | tf_op jit(solution)/shard_map/ppermute | solution.py:845
  84.8 12.4 %collective-permute-start.15 = (bf16[128,512]{1,0:T(8,128)(2,1)S(1)}, bf16[128,512]{1,0:T(8,128)(2,1)S(1)}, u32[]{:S(2)}, u32[]{:S(2)}) collective-permute-start(bf16[128,512]{1,0:T(8,128)(2,1)S(1)} %get-tuple-element.89), channel_id=1, source_target_pairs={{0,3},{1,2},{2,1},{3,0},{4,7},{5,6},{6,5},{7,4},{8,11},{9,10},{10,... | collective-permute-start | bytes 393224 | tf_op jit(solution)/shard_map/ppermute | solution.py:845
  134.2 16.1 %collective-permute-start.19 = (bf16[4,4,9,16,512]{4,3,2,1,0:T(8,128)(2,1)S(1)}, bf16[4,4,9,16,512]{4,3,2,1,0:T(8,128)(2,1)S(1)}, u32[]{:S(2)}, u32[]{:S(2)}) collective-permute-start(bf16[4,4,9,16,512]{4,3,2,1,0:T(8,128)(2,1)S(1)} %get-tuple-element.110), channel_id=1, source_target_pairs={{0,4},{4,0},{8,12},{12,8},{16,20},{20,16},{24,28},{28,24},{1,5},{5... | collective-permute-start | bytes 7077896 | tf_op jit(solution)/shard_map/ppermute | solution.py:835
  134.3 15.1 %collective-permute-start.16 = (bf16[128,384]{1,0:T(8,128)(2,1)S(1)}, bf16[128,384]{1,0:T(8,128)(2,1)S(1)}, u32[]{:S(2)}, u32[]{:S(2)}) collective-permute-start(bf16[128,384]{1,0:T(8,128)(2,1)S(1)} %get-tuple-element.99), channel_id=1, source_target_pairs={{0,1},{1,0},{2,3},{3,2},{4,5},{5,4},{6,7},{7,6},{8,9},{9,8},{10,11... | collective-permute-start | bytes 294920 | tf_op jit(solution)/shard_map/ppermute | solution.py:845
  134.6 14.8 %collective-permute-start.17 = (bf16[128,384]{1,0:T(8,128)(2,1)S(1)}, bf16[128,384]{1,0:T(8,128)(2,1)S(1)}, u32[]{:S(2)}, u32[]{:S(2)}) collective-permute-start(bf16[128,384]{1,0:T(8,128)(2,1)S(1)} %get-tuple-element.100), channel_id=1, source_target_pairs={{0,2},{1,3},{2,0},{3,1},{4,6},{5,7},{6,4},{7,5},{8,10},{9,11},{10,... | collective-permute-start | bytes 294920 | tf_op jit(solution)/shard_map/ppermute | solution.py:845
  136.1 13.3 %collective-permute-start.18 = (bf16[128,384]{1,0:T(8,128)(2,1)S(1)}, bf16[128,384]{1,0:T(8,128)(2,1)S(1)}, u32[]{:S(2)}, u32[]{:S(2)}) collective-permute-start(bf16[128,384]{1,0:T(8,128)(2,1)S(1)} %get-tuple-element.101), channel_id=1, source_target_pairs={{0,3},{1,2},{2,1},{3,0},{4,7},{5,6},{6,5},{7,4},{8,11},{9,10},{10,... | collective-permute-start | bytes 294920 | tf_op jit(solution)/shard_map/ppermute | solution.py:845
  150.3 1.0 copy-start.2
  163.2 16.2 %collective-permute-start.25 = (bf16[8,9,16,512]{3,2,1,0:T(8,128)(2,1)S(1)}, bf16[8,9,16,512]{3,2,1,0:T(8,128)(2,1)S(1)}, u32[]{:S(2)}, u32[]{:S(2)}) collective-permute-start(bf16[8,9,16,512]{3,2,1,0:T(8,128)(2,1)S(1)} %release.7), channel_id=1, source_target_pairs={{0,8},{4,20},{8,0},{12,28},{16,24},{20,4},{24,16},{28,12},{1,9},{5... | collective-permute-start | bytes 3538952 | tf_op jit(solution)/shard_map/ppermute | solution.py:842
  170.5 10.4 %collective-permute-start.23 = (bf16[4,4,9,16,256]{4,3,2,1,0:T(8,128)(2,1)S(1)}, bf16[4,4,9,16,256]{4,3,2,1,0:T(8,128)(2,1)S(1)}, u32[]{:S(2)}, u32[]{:S(2)}) collective-permute-start(bf16[4,4,9,16,256]{4,3,2,1,0:T(8,128)(2,1)S(1)} %get-tuple-element.120), channel_id=1, source_target_pairs={{0,4},{4,0},{8,12},{12,8},{16,20},{20,16},{24,28},{28,24},{1,5},{5... | collective-permute-start | bytes 3538952 | tf_op jit(solution)/shard_map/ppermute | solution.py:835
  179.7 15.8 %collective-permute-start.26 = (bf16[4,9,16,512]{3,2,1,0:T(8,128)(2,1)S(1)}, bf16[4,9,16,512]{3,2,1,0:T(8,128)(2,1)S(1)}, u32[]{:S(2)}, u32[]{:S(2)}) collective-permute-start(bf16[4,9,16,512]{3,2,1,0:T(8,128)(2,1)S(1)} %get-tuple-element.125), channel_id=1, source_target_pairs={{0,16},{4,12},{8,24},{12,4},{16,0},{20,28},{24,8},{28,20},{1,17},{... | collective-permute-start | bytes 1769480 | tf_op jit(solution)/shard_map/ppermute | solution.py:842
  181.1 14.7 %collective-permute-start.24 = (bf16[8,9,16,256]{3,2,1,0:T(8,128)(2,1)S(1)}, bf16[8,9,16,256]{3,2,1,0:T(8,128)(2,1)S(1)}, u32[]{:S(2)}, u32[]{:S(2)}) collective-permute-start(bf16[8,9,16,256]{3,2,1,0:T(8,128)(2,1)S(1)} %get-tuple-element.122), channel_id=1, source_target_pairs={{0,8},{4,20},{8,0},{12,28},{16,24},{20,4},{24,16},{28,12},{1,9},{5... | collective-permute-start | bytes 1769480 | tf_op jit(solution)/shard_map/ppermute | solution.py:842
  181.7 8.5 %collective-permute-start.20 = (bf16[64,1536]{1,0:T(8,128)(2,1)S(1)}, bf16[64,1536]{1,0:T(8,128)(2,1)S(1)}, u32[]{:S(2)}, u32[]{:S(2)}) collective-permute-start(bf16[64,1536]{1,0:T(8,128)(2,1)S(1)} %get-tuple-element.116), channel_id=1, source_target_pairs={{0,1},{1,0},{2,3},{3,2},{4,5},{5,4},{6,7},{7,6},{8,9},{9,8},{10,11... | collective-permute-start | bytes 589832 | tf_op jit(solution)/shard_map/ppermute | solution.py:845
  182.6 10.3 %collective-permute-start.21 = (bf16[64,1536]{1,0:T(8,128)(2,1)S(1)}, bf16[64,1536]{1,0:T(8,128)(2,1)S(1)}, u32[]{:S(2)}, u32[]{:S(2)}) collective-permute-start(bf16[64,1536]{1,0:T(8,128)(2,1)S(1)} %get-tuple-element.117), channel_id=1, source_target_pairs={{0,2},{1,3},{2,0},{3,1},{4,6},{5,7},{6,4},{7,5},{8,10},{9,11},{10,... | collective-permute-start | bytes 589832 | tf_op jit(solution)/shard_map/ppermute | solution.py:845
  195.6 12.0 %collective-permute-start.28 = (bf16[2,9,16,512]{3,2,1,0:T(8,128)(2,1)S(1)}, bf16[2,9,16,512]{3,2,1,0:T(8,128)(2,1)S(1)}, u32[]{:S(2)}, u32[]{:S(2)}) collective-permute-start(bf16[2,9,16,512]{3,2,1,0:T(8,128)(2,1)S(1)} %get-tuple-element.129), channel_id=1, source_target_pairs={{0,1},{1,0},{2,3},{3,2},{4,5},{5,4},{6,7},{7,6},{8,9},{9,8},{10,11... | collective-permute-start | bytes 884744 | tf_op jit(solution)/shard_map/ppermute | solution.py:845
  195.9 12.9 %collective-permute-start.27 = (bf16[4,9,16,256]{3,2,1,0:T(8,128)(2,1)S(1)}, bf16[4,9,16,256]{3,2,1,0:T(8,128)(2,1)S(1)}, u32[]{:S(2)}, u32[]{:S(2)}) collective-permute-start(bf16[4,9,16,256]{3,2,1,0:T(8,128)(2,1)S(1)} %get-tuple-element.128), channel_id=1, source_target_pairs={{0,16},{4,12},{8,24},{12,4},{16,0},{20,28},{24,8},{28,20},{1,17},{... | collective-permute-start | bytes 884744 | tf_op jit(solution)/shard_map/ppermute | solution.py:842
  197.3 10.4 %collective-permute-start.22 = (bf16[64,1536]{1,0:T(8,128)(2,1)S(1)}, bf16[64,1536]{1,0:T(8,128)(2,1)S(1)}, u32[]{:S(2)}, u32[]{:S(2)}) collective-permute-start(bf16[64,1536]{1,0:T(8,128)(2,1)S(1)} %get-tuple-element.118), channel_id=1, source_target_pairs={{0,3},{1,2},{2,1},{3,0},{4,7},{5,6},{6,5},{7,4},{8,11},{9,10},{10,... | collective-permute-start | bytes 589832 | tf_op jit(solution)/shard_map/ppermute | solution.py:845
  207.7 6.2 %collective-permute-start.30 = (bf16[1,9,16,512]{3,2,1,0:T(8,128)(2,1)S(1)}, bf16[1,9,16,512]{3,2,1,0:T(8,128)(2,1)S(1)}, u32[]{:S(2)}, u32[]{:S(2)}) collective-permute-start(bf16[1,9,16,512]{3,2,1,0:T(8,128)(2,1)S(1)} %get-tuple-element.133), channel_id=1, source_target_pairs={{0,2},{1,3},{2,0},{3,1},{4,6},{5,7},{6,4},{7,5},{8,10},{9,11},{10,... | collective-permute-start | bytes 442376 | tf_op jit(solution)/shard_map/ppermute | solution.py:845
  208.9 6.8 %collective-permute-start.29 = (bf16[2,9,16,256]{3,2,1,0:T(8,128)(2,1)S(1)}, bf16[2,9,16,256]{3,2,1,0:T(8,128)(2,1)S(1)}, u32[]{:S(2)}, u32[]{:S(2)}) collective-permute-start(bf16[2,9,16,256]{3,2,1,0:T(8,128)(2,1)S(1)} %get-tuple-element.132), channel_id=1, source_target_pairs={{0,1},{1,0},{2,3},{3,2},{4,5},{5,4},{6,7},{7,6},{8,9},{9,8},{10,11... | collective-permute-start | bytes 442376 | tf_op jit(solution)/shard_map/ppermute | solution.py:845
  214.0 10.1 %collective-permute-start.39 = (bf16[9,16,512]{2,1,0:T(8,128)(2,1)S(1)}, bf16[9,16,512]{2,1,0:T(8,128)(2,1)S(1)}, u32[]{:S(2)}, u32[]{:S(2)}) collective-permute-start(bf16[9,16,512]{2,1,0:T(8,128)(2,1)S(1)} %mid_sum_3.1.rest_0_), channel_id=1, source_target_pairs={{0,16},{4,12},{8,24},{12,4},{16,0},{20,28},{24,8},{28,20},{1,17},{... | collective-permute-start | bytes 442376 | tf_op jit(solution)/shard_map/ppermute | solution.py:842
  214.0 12.6 %collective-permute-start.40 = (bf16[9,16,512]{2,1,0:T(8,128)(2,1)S(1)}, bf16[9,16,512]{2,1,0:T(8,128)(2,1)S(1)}, u32[]{:S(2)}, u32[]{:S(2)}) collective-permute-start(bf16[9,16,512]{2,1,0:T(8,128)(2,1)S(1)} %mid_sum_3.1.rest_0_), channel_id=1, source_target_pairs={{0,8},{4,20},{8,0},{12,28},{16,24},{20,4},{24,16},{28,12},{1,9},{5... | collective-permute-start | bytes 442376 | tf_op jit(solution)/shard_map/ppermute | solution.py:842
  215.7 5.3 %collective-permute-start.31 = (bf16[1,9,16,256]{3,2,1,0:T(8,128)(2,1)S(1)}, bf16[1,9,16,256]{3,2,1,0:T(8,128)(2,1)S(1)}, u32[]{:S(2)}, u32[]{:S(2)}) collective-permute-start(bf16[1,9,16,256]{3,2,1,0:T(8,128)(2,1)S(1)} %get-tuple-element.135), channel_id=1, source_target_pairs={{0,2},{1,3},{2,0},{3,1},{4,6},{5,7},{6,4},{7,5},{8,10},{9,11},{10,... | collective-permute-start | bytes 221192 | tf_op jit(solution)/shard_map/ppermute | solution.py:845
  221.1 4.4 %collective-permute-start.32 = (bf16[9,16,256]{2,1,0:T(8,128)(2,1)S(1)}, bf16[9,16,256]{2,1,0:T(8,128)(2,1)S(1)}, u32[]{:S(2)}, u32[]{:S(2)}) collective-permute-start(bf16[9,16,256]{2,1,0:T(8,128)(2,1)S(1)} %in_sum_3.1.rest_0_), channel_id=1, source_target_pairs={{0,16},{4,12},{8,24},{12,4},{16,0},{20,28},{24,8},{28,20},{1,17},{... | collective-permute-start | bytes 221192 | tf_op jit(solution)/shard_map/ppermute | solution.py:842
  223.5 4.4 %collective-permute-start.33 = (bf16[9,16,256]{2,1,0:T(8,128)(2,1)S(1)}, bf16[9,16,256]{2,1,0:T(8,128)(2,1)S(1)}, u32[]{:S(2)}, u32[]{:S(2)}) collective-permute-start(bf16[9,16,256]{2,1,0:T(8,128)(2,1)S(1)} %in_sum_3.1.rest_0_), channel_id=1, source_target_pairs={{0,8},{4,20},{8,0},{12,28},{16,24},{20,4},{24,16},{28,12},{1,9},{5... | collective-permute-start | bytes 221192 | tf_op jit(solution)/shard_map/ppermute | solution.py:842
  224.0 3.8 %collective-permute-start.35 = (bf16[9,16,256]{2,1,0:T(8,128)(2,1)S(1)}, bf16[9,16,256]{2,1,0:T(8,128)(2,1)S(1)}, u32[]{:S(2)}, u32[]{:S(2)}) collective-permute-start(bf16[9,16,256]{2,1,0:T(8,128)(2,1)S(1)} %in_sum_3.1.rest_0_), channel_id=1, source_target_pairs={{0,4},{4,0},{8,12},{12,8},{16,20},{20,16},{24,28},{28,24},{1,5},{5... | collective-permute-start | bytes 221192 | tf_op jit(solution)/shard_map/ppermute | solution.py:835
  224.0 6.7 %collective-permute-start.41 = (bf16[9,16,512]{2,1,0:T(8,128)(2,1)S(1)}, bf16[9,16,512]{2,1,0:T(8,128)(2,1)S(1)}, u32[]{:S(2)}, u32[]{:S(2)}) collective-permute-start(bf16[9,16,512]{2,1,0:T(8,128)(2,1)S(1)} %collective-permute-done.39.rest_1_), channel_id=1, source_target_pairs={{0,8},{4,20},{8,0},{12,28},{16,24},{20,4},{24,16},{28,12},{1,9},{5... | collective-permute-start | bytes 442376 | tf_op jit(solution)/shard_map/ppermute | solution.py:842
  225.5 4.7 %collective-permute-start.34 = (bf16[9,16,256]{2,1,0:T(8,128)(2,1)S(1)}, bf16[9,16,256]{2,1,0:T(8,128)(2,1)S(1)}, u32[]{:S(2)}, u32[]{:S(2)}) collective-permute-start(bf16[9,16,256]{2,1,0:T(8,128)(2,1)S(1)} %collective-permute-done.32.rest_1_), channel_id=1, source_target_pairs={{0,8},{4,20},{8,0},{12,28},{16,24},{20,4},{24,16},{28,12},{1,9},{5... | collective-permute-start | bytes 221192 | tf_op jit(solution)/shard_map/ppermute | solution.py:842
  226.7 3.5 %collective-permute-start.36 = (bf16[9,16,256]{2,1,0:T(8,128)(2,1)S(1)}, bf16[9,16,256]{2,1,0:T(8,128)(2,1)S(1)}, u32[]{:S(2)}, u32[]{:S(2)}) collective-permute-start(bf16[9,16,256]{2,1,0:T(8,128)(2,1)S(1)} %collective-permute-done.32.rest_1_), channel_id=1, source_target_pairs={{0,4},{4,0},{8,12},{12,8},{16,20},{20,16},{24,28},{28,24},{1,5},{5... | collective-permute-start | bytes 221192 | tf_op jit(solution)/shard_map/ppermute | solution.py:835
  227.8 7.1 %collective-permute-start.42 = (bf16[9,16,512]{2,1,0:T(8,128)(2,1)S(1)}, bf16[9,16,512]{2,1,0:T(8,128)(2,1)S(1)}, u32[]{:S(2)}, u32[]{:S(2)}) collective-permute-start(bf16[9,16,512]{2,1,0:T(8,128)(2,1)S(1)} %mid_sum_3.1.rest_0_), channel_id=1, source_target_pairs={{0,4},{4,0},{8,12},{12,8},{16,20},{20,16},{24,28},{28,24},{1,5},{5... | collective-permute-start | bytes 442376 | tf_op jit(solution)/shard_map/ppermute | solution.py:835
  227.8 7.1 %collective-permute-start.43 = (bf16[9,16,512]{2,1,0:T(8,128)(2,1)S(1)}, bf16[9,16,512]{2,1,0:T(8,128)(2,1)S(1)}, u32[]{:S(2)}, u32[]{:S(2)}) collective-permute-start(bf16[9,16,512]{2,1,0:T(8,128)(2,1)S(1)} %collective-permute-done.39.rest_1_), channel_id=1, source_target_pairs={{0,4},{4,0},{8,12},{12,8},{16,20},{20,16},{24,28},{28,24},{1,5},{5... | collective-permute-start | bytes 442376 | tf_op jit(solution)/shard_map/ppermute | solution.py:835
  230.2 4.7 %collective-permute-start.44 = (bf16[9,16,512]{2,1,0:T(8,128)(2,1)S(1)}, bf16[9,16,512]{2,1,0:T(8,128)(2,1)S(1)}, u32[]{:S(2)}, u32[]{:S(2)}) collective-permute-start(bf16[9,16,512]{2,1,0:T(8,128)(2,1)S(1)} %collective-permute-done.40.rest_2_), channel_id=1, source_target_pairs={{0,4},{4,0},{8,12},{12,8},{16,20},{20,16},{24,28},{28,24},{1,5},{5... | collective-permute-start | bytes 442376 | tf_op jit(solution)/shard_map/ppermute | solution.py:835
  230.2 1.5 collective-permute-start.37
  230.7 4.2 %collective-permute-start.45 = (bf16[9,16,512]{2,1,0:T(8,128)(2,1)S(1)}, bf16[9,16,512]{2,1,0:T(8,128)(2,1)S(1)}, u32[]{:S(2)}, u32[]{:S(2)}) collective-permute-start(bf16[9,16,512]{2,1,0:T(8,128)(2,1)S(1)} %collective-permute-done.41.rest_3_), channel_id=1, source_target_pairs={{0,4},{4,0},{8,12},{12,8},{16,20},{20,16},{24,28},{28,24},{1,5},{5... | collective-permute-start | bytes 442376 | tf_op jit(solution)/shard_map/ppermute | solution.py:835
  231.7 2.1 collective-permute-start.38
where the time goes:
time: 238 us; the launch traced here: 237 us
  waiting for transfers between devices  73.8 us (31%)
  Pallas kernels  65.4 us (27%)
  blocking collectives  48.1 us (20%)
  starting transfers between devices  46.1 us (19%)
    pallas_call x19, Pallas kernels, call(): pl.pallas_call(body, out_shape=[pltpu.VMEM(o.shape, o.dtype) if isinstanc...  59 us
    ppermute x19, waiting for transfers between devices, chan(): return lax.ppermute(x, 'chan', [(i, i ^ k) for i in range(self.g.nch)])  53.5 us
    all_to_all x4, blocking collectives, everyone(): return lax.all_to_all(x, ('dp', 'chan'), 0, 0)  48.1 us
    ppermute x19, starting transfers between devices, chan(): return lax.ppermute(x, 'chan', [(i, i ^ k) for i in range(self.g.nch)])  29.6 us
    ppermute x13, waiting for transfers between devices, plane(): lax.ppermute(x, 'dp', [(i, i ^ 2 * g.mask(i & 1, turn)) for i in range(g....  19.1 us
    ppermute x13, starting transfers between devices, plane(): lax.ppermute(x, 'dp', [(i, i ^ 2 * g.mask(i & 1, turn)) for i in range(g....  14.5 us
  transfers between devices with their start and end apart: 46, of which 17 were waited for; matrix products, arithmetic and copies ran while one was open for 1% of the time, Pallas kernels for 17%

commit v1 on v0

--- a/solution.py
+++ b/solution.py
@@ -12,6 +12,7 @@
 BF = jnp.bfloat16
 F32 = jnp.float32
 MIB = 1024 * 1024
+TINY = pl.CostEstimate(flops=1, bytes_accessed=1, transcendentals=0)
 
 VMEM = pl.BlockSpec(memory_space=pltpu.VMEM)
 SMEM = pl.BlockSpec(memory_space=pltpu.SMEM)
@@ -237,34 +238,44 @@
     return call(body, out, [ANY] * 2, args, [sems(2)], 4, 0, 4e5, "cut_weights")[0]
 
 
-def stack_kernel(*refs):
-    for k, r in enumerate(refs[:-1]):
-        refs[-1][k] = r[...]
-
-
-def stack(parts, name):
-    out = [arr((len(parts), *parts[0].shape), parts[0].dtype)]
-    return call(stack_kernel, out, [VMEM] * len(parts), parts, [], 4, 0, 1e6, name)[0]
-
-
-def cut_maps_kernel(g, spec, after, *rest):
-    n = g.nch
-    xs, sem = rest[:n], rest[n]
-    z = lax.axis_index("chan")
+def sort_kernel(g, *rest):
+    n = g.nch - 1
+    parts, first, second = rest[:n], rest[-2], rest[-1]
+    for k in range(n):
+        first[k] = parts[k][:, :, : g.ci_all]
+        second[k] = parts[k][:, :, g.ci_all :]
+
+
+def sort_pieces(g, parts, gates):
+    n = g.nch - 1
+    out = [arr((n, 9, g.rows, g.ci_all), BF), arr((n, 9, g.rows, g.cm), BF)]
+    body = functools.partial(sort_kernel, g)
+    ins = [VMEM] * n + [ANY] * len(gates)
+    return call(body, out, ins, [*parts, *gates], [], 4, 0, 1e6, "sort_pieces")
+
+
+def cut_maps_kernel(g, spec, after, out, held, sem):
     copies = Copies(sem)
-    for k in range(n):
-        to = z ^ k
-        clip, seg = to // g.segs, lax.rem(to, g.segs)
-        start, _ = g_starts(g, seg)
-        copies.start(spec.at[clip, :, pl.ds(aligned(start * MEL, 128), g.win * MEL)], xs[k])
+    first = []
+    for z in range(g.nch):
+        start = static_start(g, z % g.segs) * MEL
+        first.append(copies.start(spec.at[z // g.segs, :, start : start + g.win * MEL], held.at[z]))
+    for z in range(g.nch):
+        copies.wait(first[z])
+        copies.start(held.at[z], out.at[z])
     copies.wait_all()
 
 
 def cut_maps(g, spec, after):
-    n = g.nch
-    out = [arr((g.ci, g.win * MEL), BF)] * n
+    shape = (g.nch, g.ci, g.win * MEL)
     body = functools.partial(cut_maps_kernel, g)
-    return call(body, out, [ANY] * 2, [in_hbm(spec), after], [sems(n)], 4, 0, 2e6, "cut_maps")
+    args = [in_hbm(spec), after]
+    scratch = [pltpu.VMEM(shape, BF), sems(2 * g.nch)]
+    return call(body, [pltpu.HBM(shape, BF)], [ANY] * 2, args, scratch, 4, 0, 2e6, "cut_maps")[0]
+
+
+def static_start(g, seg):
+    return min(max(seg * g.seg - HALO, 0), g.frames - g.win)
 
 
 def cut_cot_kernel(g, cot, after, *rest):
@@ -291,32 +302,28 @@
     return pltpu.with_memory_space_constraint(x, pltpu.HBM)
 
 
-def join_kernel(g, own_in, own_mid, *rest):
-    parts, w_in, w_mid = rest[:-2], rest[-2], rest[-1]
+def join_kernel(g, own, *rest):
+    parts, w = rest[:-1], rest[-1]
     z, d = lax.axis_index("chan"), lax.axis_index("dp")
     mine, plane = lax.rem(d, 2), lax.rem(d, g.pieces) // 2
-    w_in[:, pl.ds(aligned(z * g.co), g.co), :] = own_in[...]
-    w_mid[:, pl.ds(aligned(z * g.co), g.co), :] = own_mid[...]
+    w[:, pl.ds(aligned(z * g.co), g.co), :] = own[...]
     for side in range(2):
         core = mine if side == 0 else 1 - mine
         for e in range(g.planes):
             row = g.row_of(core, plane ^ g.plane_of(core, e))
             for k in range(1, g.nch):
-                at = pl.ds(aligned((z ^ k) * g.co + row), g.rows)
-                part = parts[side * g.planes + e]
-                w_in[:, at, :] = part[k - 1, :, :, : g.ci_all]
-                w_mid[:, at, :] = part[k - 1, :, :, g.ci_all :]
-
-
-def join(g, own_in, own_mid, parts):
+                at = aligned((z ^ k) * g.co + row)
+                w[:, pl.ds(at, g.rows), :] = parts[side * g.planes + e][k - 1]
+
+
+def join(g, own, parts, depth, name):
     body = functools.partial(join_kernel, g)
-    args = [own_in, own_mid, *parts]
+    args = [*keep_near(own), *parts]
     ins = [VMEM] * len(args)
-    out = [arr((9, g.cm, g.ci_all), BF), arr((9, g.cm, g.cm), BF)]
-    return call(body, out, ins, args, [], 8, 0, 4 * MIB, "join")
-
-
-def convolve(g, v3, w, part, back, finish, carry):
+    return call(body, [arr((9, g.cm, depth), BF)], ins, args, [], 8, 0, 4 * MIB, name)[0]
+
+
+def convolve(v3, w, part, back, finish, carry, unrolled=False, window=None):
     def taps(t):
         b = 2 - t if back else t
         return jnp.concatenate([w[b], w[3 + b], w[6 + b]], axis=0 if back else 1)
@@ -324,22 +331,40 @@
     contract = ((1,), (0,)) if back else ((1,), (1,))
     depth = v3.shape[2]
 
+    size = part.shape[1]
+    window = pl.ds(0, size) if window is None else window
+
     def times(first, n, t):
-        return dot(v3[pl.ds(first, n)].reshape(n * g.win, depth), taps(t), contract)
+        return dot(v3[pl.ds(first, n), window, :].reshape(n * size, depth), taps(t), contract)
+
+    def rows_of(term, n):
+        return [term[k * size : (k + 1) * size] for k in range(n)]
+
+    if unrolled:
+        for i in range(2):
+            total = rows_of(times(4 * i, 4, 1), 4)
+            side = rows_of(times(1 + 2 * i, 4, 2 - 2 * i), 4)
+            edge = rows_of(times(5 * i, 3, 2 * i), 3)
+            for k in range(4):
+                value = total[k] + side[k]
+                if 0 <= k + i - 1 < 3:
+                    value = value + edge[k + i - 1]
+                carry = finish(4 * i + k, value, carry)
+        return carry
 
     def step(i, carry):
-        part[pl.ds(3 * i + 1, 3)] = times(5 * i, 3, 2 * i).reshape(3, g.win, part.shape[2])
+        part[pl.ds(3 * i + 1, 3)] = times(5 * i, 3, 2 * i).reshape(3, size, part.shape[2])
         part[7 * i] = jnp.zeros(part.shape[1:], F32)
         total = times(4 * i, 4, 1) + times(1 + 2 * i, 4, 2 - 2 * i)
         for k in range(4):
             m = 4 * i + k
-            carry = finish(m, part[m] + total[k * g.win : (k + 1) * g.win], carry)
+            carry = finish(m, part[m] + total[k * size : (k + 1) * size], carry)
         return carry
 
     return lax.fori_loop(0, 2, step, carry)
 
 
-def convolve_sums(g, here, x3, w, pre):
+def convolve_sums(g, here, x3, w, pre, unrolled):
     _, own = row_masks(g, here, g.cm)
 
     def finish(m, total, sums):
@@ -348,20 +373,17 @@
         return sums[0] + sum_rows(kept), sums[1] + sum_rows(kept * total)
 
     zero = jnp.zeros((1, g.cm), F32)
-    return convolve(g, x3, w, pre, False, finish, (zero, zero))
-
-
-def first_kernel(g, lens, gains, w, *rest):
-    xs, (pre, x3, pay, maps) = rest[: g.nch], rest[g.nch :]
+    return convolve(x3, w, pre, False, finish, (zero, zero), unrolled)
+
+
+def first_kernel(g, lens, gains, w, maps, pre, x3, pay):
     here = Here(g, lens)
     c = g.ci_all
-    for k in range(g.nch):
-        maps[pl.ds(aligned((here.z ^ k) * g.ci), g.ci), :] = xs[k][...]
     order = grid_order()
     row = lax.broadcasted_iota(jnp.int32, (MEL * 16, 128), 0) % 16
 
     def place_cells(j, square):
-        cells = maps[:, 128 * j : 128 * (j + 1)]
+        cells = maps[:, :, 128 * j : 128 * (j + 1)].reshape(c, 128)
         frame = row + 16 * j
         valid = (frame + here.start) < here.length
         own = (frame >= here.off) & (frame < here.off + g.seg)
@@ -377,7 +399,7 @@
         x3[m, :, 0:c] = before.astype(BF)
         x3[m, :, 2 * c : 3 * c] = after_.astype(BF)
 
-    one, two = convolve_sums(g, here, x3, w, pre)
+    one, two = convolve_sums(g, here, x3, w, pre, True)
     frame_total = 0
     pair_total = 0
     for i in range(g.clips):
@@ -396,11 +418,10 @@
         arr((MEL, g.win, 3 * g.ci_all), BF),
         arr((16, 128), F32),
     ]
-    args = [lens, gains, *keep_near(w, *maps)]
-    ins = [SMEM] + [VMEM] * (2 + g.nch)
+    args = [lens, gains, *keep_near(w, maps)]
+    ins = [SMEM] + [VMEM] * 3
     flops = 2 * 9 * MEL * g.win * g.ci_all * g.cm
-    scratch = [pltpu.VMEM((g.ci_all, g.win * MEL), BF)]
-    return call(body, out, ins, args, scratch, 10, flops, 10 * MIB, "first_conv")
+    return call(body, out, ins, args, [], 10, flops, 10 * MIB, "first_conv")
 
 
 MEAN1, INV1, GAMMA1, BETA1, GAMMA2, BETA2, COUNT, PAIRS, SQ0, MEAN2, INV2 = range(11)
@@ -444,8 +465,10 @@
         side_by_side(x3, m, low, c, before, after)
         return square + sum_rows(act * act * own)
 
-    square = lax.fori_loop(0, MEL, activate, jnp.zeros((1, c), F32))
-    one, two = convolve_sums(g, here, x3, w, pre)
+    square = jnp.zeros((1, c), F32)
+    for m in range(MEL):
+        square = activate(m, square)
+    one, two = convolve_sums(g, here, x3, w, pre, True)
     pay[...] = payload(8, lanes(one), lanes(two))
     misc_out[...] = payload(8, misc_row(jnp.sum(square, axis=1, keepdims=True)))
 
@@ -468,7 +491,7 @@
 def pool_kernel(g, lens, got, old_ref, pre2, *rest):
     n, c = g.nch, g.cm
     cs, outs = rest[:n], rest[n : 2 * n]
-    local_ref, table, pay, misc_out, held, grads, pooled_ref, flat = rest[2 * n :]
+    local_ref, table, pay, misc_out, held, grads, total, flat = rest[2 * n :]
     here = Here(g, lens)
     for k in range(n):
         held[pl.ds(aligned((here.z ^ k) * g.co), g.co), :] = cs[k][...]
@@ -496,7 +519,10 @@
     share = widen(jnp.where(here.length - r // 2 * 2 >= 2, 0.25, 0.5), c)
     half_share = 0.5 * share * valid
     window = pl.ds(aligned(here.qoff), g.win)
-    segment = pl.ds(aligned(here.off), g.seg)
+    out_row = lax.broadcasted_iota(jnp.int32, (g.win, 2 * g.seg), 0) - here.off
+    out_cell = lax.broadcasted_iota(jnp.int32, (g.win, 2 * g.seg), 1)
+    first_cell = jnp.where(out_row >= 0, out_row // 2 * 4, -MEL)
+    total[...] = jnp.zeros(total.shape, F32)
 
     def step(k, sums):
         beta_sum, gamma_sum, square = sums
@@ -508,27 +534,25 @@
             half = scaled * half_gamma + half_beta
             bend = jnp.tanh(half)
             twice = 1.0 + bend
-            act = half * twice * own
+            whole = half * twice
+            act = whole * own
             square = square + sum_rows(act * act)
-            local = given * (twice * (1.0 + half * (1.0 - bend)))
+            local = given * (twice + whole * (1.0 - bend))
             local_ref[m] = local
             kept = local * own
             beta_sum = beta_sum + sum_rows(kept)
             gamma_sum = gamma_sum + sum_rows(kept * scaled)
             pair = act if pair is None else pair + act
-        pooled_ref[k] = pair * share
+        pair = pair * share
+        high = pair.astype(BF)
+        low = (pair - high.astype(F32)).astype(BF)
+        gather = (out_cell == first_cell + k).astype(BF)
+        total[...] += dot(high, gather, ((0,), (0,))) + dot(low, gather, ((0,), (0,)))
         return beta_sum, gamma_sum, square
 
     zero = jnp.zeros((1, c), F32)
     beta_sum, gamma_sum, square = lax.fori_loop(0, MEL // 2, step, (zero, zero, zero))
-    wide_rows = (MEL // 2) * g.seg
-    values = jnp.concatenate([pooled_ref[k, segment, :] for k in range(MEL // 2)], axis=0)
-    high = values.astype(BF)
-    low = (values - high.astype(F32)).astype(BF)
-    r = lax.broadcasted_iota(jnp.int32, (wide_rows, 2 * g.seg), 0)
-    l = lax.broadcasted_iota(jnp.int32, (wide_rows, 2 * g.seg), 1)
-    gather = (l == (r % g.seg) // 2 * 4 + r // g.seg).astype(BF)
-    pooled = dot(high, gather, ((0,), (0,))) + dot(low, gather, ((0,), (0,)))
+    pooled = total[...]
     flat[...] = pooled.astype(BF)
     for k in range(n):
         outs[k][...] = flat[pl.ds(aligned((here.z ^ k) * g.co), g.co), :]
@@ -550,7 +574,7 @@
     scratch = [
         pltpu.VMEM((g.cm, g.cwin * 2), BF),
         pltpu.VMEM((MEL // 2, g.cwin, g.cm), F32),
-        pltpu.VMEM((MEL // 2, g.win, g.cm), F32),
+        pltpu.VMEM((g.cm, 2 * g.seg), F32),
         pltpu.VMEM((g.cm, 2 * g.seg), BF),
     ]
     args = [lens, *keep_near(got, table, pre2, *cs)]
@@ -560,10 +584,10 @@
 
 
 def terms_kernel(g, depth, norm, lens, got, table, pre, local, x3, after, *rest):
-    grad, sums, roots, terms, give, own_grad = rest
+    grad, sums, roots, terms, give = rest
     here = Here(g, lens)
     c = g.cm
-    valid, own = row_masks(g, here, c)
+    valid, _ = row_masks(g, here, c)
     beta_sum, gamma_sum = total_of(g, got)
     t = table[...]
     mean, inverse, gamma = (t[i : i + 1] for i in norm)
@@ -586,7 +610,8 @@
     def _(m):
         value = valid * (local[m] * factor - pre[m] * slope - level)
         grad[m] = value.astype(BF)
-        own_grad[m] = (value * own).astype(BF)
+
+    segment = pl.ds(aligned(here.off), g.seg)
 
     @pl.loop(0, 3)
     def _(a):
@@ -594,9 +619,9 @@
         for b in (1, 0, 2):
             low = max(0, 1 - b)
             high = min(MEL, MEL + 1 - b)
-            rows = (high - low) * g.win
-            left = own_grad[low:high].reshape(rows, c)
-            right = x3[low + b - 1 : high + b - 1, :, lanes_of].reshape(rows, depth)
+            rows = (high - low) * g.seg
+            left = grad[low:high, segment, :].reshape(rows, c)
+            right = x3[low + b - 1 : high + b - 1, segment, lanes_of].reshape(rows, depth)
             term = dot(left, right, ((0,), (0,))).astype(BF)
             for z in range(g.nch):
                 for s in range(2):
@@ -617,14 +642,13 @@
         arr((2, *shape), BF),
         arr(shape, BF),
     ]
-    scratch = [pltpu.VMEM((MEL, g.win, g.cm), BF)]
     args = [lens, *keep_near(got, table, pre, local, x3), after]
     ins = [SMEM] + [VMEM] * 5 + [ANY]
     flops = 2 * 9 * MEL * g.win * g.cm * depth
-    return call(body, out, ins, args, scratch, 10, flops, 15 * MIB, name)
-
-
-def back_kernel(g, lens, table, grad, pre1, w, misc2, misc3, local1, pay, g3):
+    return call(body, out, ins, args, [], 10, flops, 15 * MIB, name)
+
+
+def back_kernel(g, lens, table, grad, pre1, w, misc2, misc3, after, local1, pay, g3):
     here = Here(g, lens)
     c = g.cm
     valid, own = row_masks(g, here, c)
@@ -634,8 +658,7 @@
         return t[i : i + 1]
 
 
-    @pl.loop(0, MEL)
-    def _(m):
+    for m in range(MEL):
         low = grad[m]
         before, after = shifted(low.astype(F32))
         side_by_side(g3, m, low, c, after, before)
@@ -648,29 +671,43 @@
         scaled = pre1[m] * inverse + less
         half = scaled * half_gamma + half_beta
         bend = jnp.tanh(half)
-        local = given * half_valid * ((1.0 + bend) * (1.0 + half * (1.0 - bend)))
+        twice = 1.0 + bend
+        local = given * half_valid * (twice + half * twice * (1.0 - bend))
         local1[m] = local
         kept = local * own
         return sums[0] + sum_rows(kept), sums[1] + sum_rows(kept * scaled)
 
     zero = jnp.zeros((1, c), F32)
-    beta_sum, gamma_sum = convolve(g, g3, w, local1, True, finish, (zero, zero))
+    beta_sum, gamma_sum = convolve(g3, w, local1, True, finish, (zero, zero), True)
     squares = jnp.concatenate([misc2[0:1], misc3[0:1]], axis=0)
     pay[...] = payload(16, lanes(beta_sum), lanes(gamma_sum), squares)
 
 
-def back(g, lens, table, grad, pre1, w, misc2, misc3):
+def back(g, lens, table, grad, pre1, w, misc2, misc3, after):
     body = functools.partial(back_kernel, g)
     out = [arr((MEL, g.win, g.cm), F32), arr((16, 128), F32)]
     scratch = [pltpu.VMEM((MEL, g.win, 3 * g.cm), BF)]
-    args = [lens, *keep_near(table, grad, pre1, w, misc2, misc3)]
+    args = [lens, *keep_near(table, grad, pre1, w, misc2, misc3), after]
     flops = 2 * 9 * MEL * g.win * g.cm * g.cm
-    ins = [SMEM] + [VMEM] * 6
+    ins = [SMEM] + [VMEM] * 6 + [ANY]
     return call(body, out, ins, args, scratch, 14, flops, 20 * MIB, "second_back")
 
 
 def release_kernel(*refs):
     pass
+
+
+def release_far(gates, x):
+    n = len(gates)
+    return pl.pallas_call(
+        release_kernel,
+        out_shape=pltpu.HBM(x.shape, x.dtype),
+        in_specs=[ANY] * (n + 1),
+        out_specs=ANY,
+        input_output_aliases={n: 0},
+        compiler_params=pltpu.CompilerParams(vmem_limit_bytes=2 * MIB),
+        name="release_far",
+    )(*gates, in_hbm(x))
 
 
 def release(gates, arrays):
@@ -693,17 +730,18 @@
         before, after_ = shifted(low.astype(F32))
         side_by_side(g3, m, low, c, after_, before)
 
-    _, own = row_masks(g, here, g.ci_all)
+    r = lax.broadcasted_iota(jnp.int32, (g.seg, 128), 0) + here.off + here.start
+    valid = widen((r < here.length).astype(F32), g.ci_all)
 
     def finish(m, total, carry):
-        rows[m] = (total * own).astype(BF)
+        rows[m] = (total * valid).astype(BF)
         return carry
 
-    convolve(g, g3, w, part, True, finish, 0)
+    convolve(g3, w, part, True, finish, 0, False, pl.ds(aligned(here.off), g.seg))
     order = grid_order()
 
     for j in range(g.seg // 16):
-        block = rows[:, pl.ds(aligned(here.off + 16 * j), 16), :].reshape(MEL * 16, g.ci_all)
+        block = rows[:, 16 * j : 16 * (j + 1), :].reshape(MEL * 16, g.ci_all)
         flat[:, 128 * j : 128 * (j + 1)] = dot(block, order, ((0,), (0,))).astype(BF)
 
     for k in range(n):
@@ -716,9 +754,9 @@
     out = [arr((g.ci, g.seg * MEL), BF)] * n
     scratch = [
         pltpu.VMEM((MEL, g.win, 3 * g.cm), BF),
-        pltpu.VMEM((MEL, g.win, g.ci_all), BF),
+        pltpu.VMEM((MEL, g.seg, g.ci_all), BF),
         pltpu.VMEM((g.ci_all, g.seg * MEL), BF),
-        pltpu.VMEM((MEL, g.win, g.ci_all), F32),
+        pltpu.VMEM((MEL, g.seg, g.ci_all), F32),
     ]
     grad, w = keep_near(grad, w)
     args = [lens, grad, after, w]
@@ -729,8 +767,9 @@
 
 def place_kernel(g, width, *rest):
     n = g.nch
-    parts, out = rest[:n], rest[n]
+    parts, out, done = rest[:n], rest[n], rest[n + 1]
     z = lax.axis_index("chan")
+    done[...] = jnp.zeros(done.shape, F32)
     for k in range(n):
         source = z ^ k
         for zz in range(n):
@@ -745,10 +784,14 @@
     channels, width = parts[0].shape
     return pl.pallas_call(
         functools.partial(place_kernel, g, width),
-        out_shape=jax.ShapeDtypeStruct((g.clips, channels, g.segs * width), dtype),
+        out_shape=[
+            jax.ShapeDtypeStruct((g.clips, channels, g.segs * width), dtype),
+            jax.ShapeDtypeStruct((8, 128), F32),
+        ],
         in_specs=[VMEM] * g.nch,
-        out_specs=VMEM,
+        out_specs=[VMEM] * 2,
         compiler_params=pltpu.CompilerParams(vmem_limit_bytes=8 * MIB),
+        cost_estimate=TINY,
         name=name,
     )(*parts)
 
@@ -776,6 +819,53 @@
         compiler_params=pltpu.CompilerParams(vmem_limit_bytes=16 * MIB),
         name=name,
     )(keep_near(terms)[0], got, after)
+
+
+def quarter_kernel(g, terms, got, *outs):
+    d, z = lax.axis_index("dp"), lax.axis_index("chan")
+    core, plane = lax.rem(d, 2), lax.rem(d, g.pieces) // 2
+    for e in range(g.planes):
+        at = plane ^ g.plane_of(core, e)
+        for k in range(g.nch):
+            source = z ^ g.zed_of(k)
+            value = terms[core, source, at].astype(F32) + got[source, at].astype(F32)
+            outs[e][k] = value.astype(BF)
+
+
+def quarters(g, terms, got, name):
+    shape = (g.nch, *got.shape[2:])
+    return pl.pallas_call(
+        functools.partial(quarter_kernel, g),
+        out_shape=[pltpu.VMEM(shape, BF)] * g.planes,
+        in_specs=[VMEM, VMEM],
+        out_specs=[VMEM] * g.planes,
+        compiler_params=pltpu.CompilerParams(vmem_limit_bytes=16 * MIB),
+        name=name,
+    )(keep_near(terms)[0], got)
+
+
+def add_kernel(n, halves, *rest):
+    first = rest[0]
+    outs = rest[len(rest) - halves :]
+    count = first.shape[0] // halves
+    for i in range(first.shape[0]):
+        total = first[i].astype(F32)
+        for r in rest[1:n]:
+            total = total + r[i].astype(F32)
+        outs[i // count][i % count] = total.astype(BF)
+
+
+def add_up(parts, halves, gates, name):
+    n = len(parts)
+    shape = (parts[0].shape[0] // halves, *parts[0].shape[1:])
+    return pl.pallas_call(
+        functools.partial(add_kernel, n, halves),
+        out_shape=[pltpu.VMEM(shape, BF)] * halves,
+        in_specs=[VMEM] * n + [ANY] * len(gates),
+        out_specs=[VMEM] * halves,
+        compiler_params=pltpu.CompilerParams(vmem_limit_bytes=8 * MIB),
+        name=name,
+    )(*parts, *gates)
 
 
 def halve_kernel(stay, got, *rest):
@@ -805,26 +895,38 @@
     )(stay, got, *gates)
 
 
-def spread_kernel(g, *rest):
-    parts, out = rest[:-1], rest[-1]
+def spread_kernel(g, mine, other, out):
     d = lax.axis_index("dp")
     core, plane = lax.rem(d, 2), lax.rem(d, g.pieces) // 2
-    for side in range(2):
+    for side, part in enumerate((mine, other)):
         c = core if side == 0 else 1 - core
         for e in range(g.planes):
             at = aligned(g.row_of(c, plane ^ g.plane_of(c, e)))
-            out[:, pl.ds(at, g.rows), :] = parts[side * g.planes + e][...].astype(F32)
-
-
-def spread_out(g, parts, depth, name):
+            out[:, pl.ds(at, g.rows), :] = part[e].astype(F32)
+
+
+def spread_out(g, mine, other, depth, name):
     return pl.pallas_call(
         functools.partial(spread_kernel, g),
         out_shape=jax.ShapeDtypeStruct((9, g.co, depth), F32),
-        in_specs=[VMEM] * g.pieces,
+        in_specs=[VMEM] * 2,
         out_specs=VMEM,
         compiler_params=pltpu.CompilerParams(vmem_limit_bytes=12 * MIB),
         name=name,
-    )(*parts)
+    )(mine, other)
+
+
+def stack_kernel(n, *refs):
+    for k, r in enumerate(refs[:n]):
+        refs[-1][k] = r[...]
+
+
+def stack(parts, gates, name):
+    n = len(parts)
+    out = [arr((n, *parts[0].shape), parts[0].dtype)]
+    ins = [VMEM] * n + [ANY] * len(gates)
+    body = functools.partial(stack_kernel, n)
+    return call(body, out, ins, [*parts, *gates], [], 6, 0, 1e6, name)[0]
 
 
 class Links:
@@ -847,14 +949,23 @@
     def exchange(self, parts):
         return [parts[0]] + [self.chan(parts[k], k) for k in range(1, self.g.nch)]
 
-    def gather_plane(self, x, gates=()):
+    def gather_planes(self, x, gates=()):
         have = [x]
         for turn in reversed(range(self.g.turns)):
-            last = have[-1]
-            if gates and turn == 0 and len(have) > 1:
-                (last,) = release(gates, [last])
-            have = have + [self.plane(h, turn) for h in (*have[:-1], last)]
-        return have + [self.core(h) for h in have]
+            more = [self.plane(h, turn) for h in have[:1]]
+            rest = have[1:]
+            if gates and turn == 0 and rest:
+                rest = release([*gates, *more], rest)
+            have = have + more + [self.plane(h, turn) for h in rest]
+        return have
+
+    def gather_cores(self, have):
+        return [*have, *[self.core(h) for h in have]]
+
+    def gather_direct(self, x):
+        g = self.g
+        pairs = [[(i, i ^ (2 * g.plane_of(i & 1, e))) for i in range(g.ndp)] for e in range(g.planes)]
+        return [x] + [lax.ppermute(x, "dp", p) for p in pairs[1:]]
 
 
 def everyone(x):
@@ -878,13 +989,20 @@
         gains = jnp.pad(gains, ((0, 0), (0, 128 - g.co)))
 
         piece = cut_weights(g, weight_in, weight_mid)
-        pieces = stack([links.chan(piece, k) for k in range(1, nch)], "stack_pieces")
-        maps = links.exchange(cut_maps(g, spectra, piece))
-        cots = cut_cot(g, cotangent, pieces)
-        w_in, w_mid = join(g, weight_in, weight_mid, links.gather_plane(pieces, maps[1:]))
+        cells = cut_maps(g, spectra, piece)
+        cots = cut_cot(g, cotangent, cells)
+        pieces_in, pieces_mid = sort_pieces(
+            g, [links.chan(piece, k) for k in range(1, nch)], [cots[0]]
+        )
+        maps = lax.all_to_all(release_far([pieces_in], cells), "chan", 0, 0)
+        planes_in = links.gather_planes(pieces_in)
+        w_in = join(g, weight_in, links.gather_cores(planes_in), g.ci_all, "join_in")
+        planes_mid = links.gather_planes(pieces_mid, [maps])
 
         pre1, x3_in, pay = first(g, lengths, gains, maps, w_in)
-        got = everyone(fan(g, pay, cots[0]))
+        got = everyone(fan(g, pay, cots[0], *planes_mid[1:]))
+        planes_mid = release([got], planes_mid)
+        w_mid = join(g, weight_mid, links.gather_cores(planes_mid), g.cm, "join_mid")
         cs = links.exchange(release([got], cots))
         pre2, x3_mid, table, pay, misc2 = second(g, lengths, got, pre1, w_mid)
         got = everyone(fan(g, pay, *cs[1:]))
@@ -895,11 +1013,22 @@
             g, lengths, got, table, pre2, local2, x3_mid, got, g.cm, (MEAN2, INV2, GAMMA2), "weight_mid_terms"
         )
         got_mid = links.core(give_mid)
-        local1, pay = back(g, lengths, table, grad2, pre1, w_mid, misc2, misc3)
-        stay_mid, go_mid = core_sum(g, terms_mid, got_mid, pay, "mid_core_sum")
-        block_out = place(g, pooled, BF, "place_pooled")
-        got = everyone(fan(g, pay, stay_mid, block_out))
-        (go_mid,) = release([got], [go_mid])
+        split = g.turns == 2
+        if split:
+            stay_a, stay_b, go_a, go_b = quarters(g, terms_mid, got_mid, "mid_core_sum")
+            got_b = links.plane(go_b, 0)
+        else:
+            stay_mid, go_b = core_sum(g, terms_mid, got_mid, got_mid, "mid_core_sum")
+            got_b = go_b
+        local1, pay = back(g, lengths, table, grad2, pre1, w_mid, misc2, misc3, go_b)
+        got = everyone(fan(g, pay, got_b, *pooled[1:]))
+        block_out, pooled_done = place(g, pooled, BF, "place_pooled")
+        if split:
+            (go_1,) = add_up([stay_b, got_b], 1, [got], "mid_sum_b")
+            got_1 = links.plane(go_1, 1)
+            got_a = links.plane(release([got], [go_a])[0], 0)
+        else:
+            (go_mid,) = release([got], [go_b])
         grad1, sums1, roots, terms_in, give_in = terms_of(
             g, lengths, got, table, pre1, local1, x3_in, got, g.ci_all, (MEAN1, INV1, GAMMA1), "weight_in_terms"
         )
@@ -917,29 +1046,45 @@
                 self.stay, self.go = done if len(done) == 2 else (done[0], None)
                 return self.stay
 
-            def out(self):
+            def rest(self):
                 bit = g.pieces
                 while bit < ndp:
                     got = links.dp(self.stay, bit)
                     self.stay = halve(self.stay[None], got[None], [], self.name + "_rest")[0]
                     bit *= 2
-                return spread_out(g, links.gather_plane(self.stay), self.depth, self.name + "_out")
+
+            def out(self, planes, *gates):
+                mine = stack(planes, gates, self.name + "_stack")
+                return spread_out(g, mine, links.core(mine), self.depth, self.name + "_out")
 
         turns = g.turns + g.zturns
-        mid = Chain(stay_mid, go_mid, g.cm, "mid")
         parts = spectra_back(g, lengths, grad1, grad1, w_in)
-        at = mid.turn(0, parts[0])
         stay_in, go_in = core_sum(g, terms_in, got_in, parts[0], "in_core_sum")
         inner = Chain(stay_in, go_in, g.ci_all, "in")
         parts = links.exchange(parts)
-        spectra_grad = place(g, parts, F32, "place_spectra")
-        arrivals = [parts[1 : nch - 1], parts[nch - 1 :]]
-        for i in range(turns):
+        spectra_grad, spectra_done = place(g, parts, F32, "place_spectra")
+        if split:
+            halves = add_up([stay_a, got_a, got_1], 2, [stay_in], "mid_sum_1")
+            mid = Chain(*halves, g.cm, "mid")
+        else:
+            mid = Chain(stay_mid, go_mid, g.cm, "mid")
+            for i in range(g.turns):
+                mid.turn(i, stay_in)
+        gates = [parts[1 : nch - 1], [*parts[nch - 1 :], pooled_done]]
+        at = mid.stay
+        for i in range(g.turns):
+            at = inner.turn(i, at, *(gates[i] if i < 2 else []))
+            if i == 0:
+                at = mid.turn(g.turns, at)
+        for i in range(g.turns, turns):
+            at = inner.turn(i, at, *([spectra_done] if i == g.turns else []))
             if i + 1 < turns:
-                at = mid.turn(i + 1, at, *(arrivals.pop(0) if arrivals else []))
-            at = inner.turn(i, at)
-        weight_mid_grad = mid.out()
-        weight_in_grad = inner.out()
+                at = mid.turn(i + 1, at)
+        inner.rest()
+        mid.rest()
+        planes_in = links.gather_planes(inner.stay)
+        weight_mid_grad = mid.out(links.gather_planes(mid.stay), *planes_in[1:3])
+        weight_in_grad = inner.out(planes_in)
         z = lax.axis_index("chan")
 
         def share(sums, i):

time: 238 us -> 229 us (0.962)
  waiting for transfers between devices: 73.8 us -> 60.1 us
  starting transfers between devices: 46.1 us -> 51.1 us
    ppermute x19 -> x16, waiting for transfers between devices: 53.5 us -> 31.8 us  [chan(): return lax.ppermute(x, 'chan', [(i, i ^ k) for i in range(self.g.nch)])]
    ppermute x13 -> x17, waiting for transfers between devices: 19.1 us -> 26.6 us  [plane(): lax.ppermute(x, 'dp', [(i, i ^ 2 * g.mask(i & 1, turn)) for i in range(g....]
    ppermute x19 -> x16, starting transfers between devices: 29.6 us -> 23 us  [chan(): return lax.ppermute(x, 'chan', [(i, i ^ k) for i in range(self.g.nch)])]
    all_to_all x0 -> x1, starting transfers between devices: none -> 6.3 us  [body(): maps = lax.all_to_all(release_far([pieces_in], cells), 'chan', 0, 0)]
    ppermute x13 -> x17, starting transfers between devices: 14.5 us -> 18.9 us  [plane(): lax.ppermute(x, 'dp', [(i, i ^ 2 * g.mask(i & 1, turn)) for i in range(g....]
    pallas_call x19 -> x23, Pallas kernels: 59 us -> 57.9 us  [call(): pl.pallas_call(body, out_shape=[pltpu.VMEM(o.shape, o.dtype) if isinstanc...]
  transfers between devices with their start and end apart: 46 -> 46, of which waited for: 17 -> 21; matrix products, arithmetic and copies ran while one was open for 1% -> 1% of each run, Pallas kernels for 17% -> 17%
where the time goes in v1:
time: 229 us
  Pallas kernels  64.3 us (28%)
  waiting for transfers between devices  60.1 us (26%)
  starting transfers between devices  51.1 us (22%)
  blocking collectives  48.5 us (21%)
  local copies, waits for them, and re-layouts  3.45 us (2%)
    pallas_call x23, Pallas kernels, call(): pl.pallas_call(body, out_shape=[pltpu.VMEM(o.shape, o.dtype) if isinstanc...  57.9 us
    all_to_all x4, blocking collectives, everyone(): return lax.all_to_all(x, ('dp', 'chan'), 0, 0)  48.5 us
    ppermute x16, waiting for transfers between devices, chan(): return lax.ppermute(x, 'chan', [(i, i ^ k) for i in range(self.g.nch)])  31.8 us
    ppermute x17, waiting for transfers between devices, plane(): lax.ppermute(x, 'dp', [(i, i ^ 2 * g.mask(i & 1, turn)) for i in range(g....  26.6 us
    ppermute x16, starting transfers between devices, chan(): return lax.ppermute(x, 'chan', [(i, i ^ k) for i in range(self.g.nch)])  23 us
    ppermute x17, starting transfers between devices, plane(): lax.ppermute(x, 'dp', [(i, i ^ 2 * g.mask(i & 1, turn)) for i in range(g....  18.9 us
    all_to_all x1, starting transfers between devices, body(): maps = lax.all_to_all(release_far([pieces_in], cells), 'chan', 0, 0)  6.3 us
  transfers between devices with their start and end apart: 46, of which 21 were waited for; matrix products, arithmetic and copies ran while one was open for 1% of the time, Pallas kernels for 17%

profile of v1, /device:TPU:0, one launch (start us, length us, event | category | flops | bytes accessed | tf_op | source)
XLA Modules:
  0.0 228.6 jit_solution(16055278550056462458)
XLA Ops:
  0.6 1.0 cut_weights.1.after
  1.6 3.1 %collective-permute-start = (bf16[9,16,768]{2,1,0:T(8,128)(2,1)S(1)}, bf16[9,16,768]{2,1,0:T(8,128)(2,1)S(1)}, u32[]{:S(2)}, u32[]{:S(2)}) collective-permute-start(bf16[9,16,768]{2,1,0:T(8,128)(2,1)S(1)} %cut_weights.1.after), channel_id=1, source_target_pairs={{0,1},{1,0},{2,3},{3,2},{4,5},{5,4},{6,7},{7,6},{8,9},{9,8},{10,11... | collective-permute-start | bytes 663560 | tf_op jit(solution)/shard_map/ppermute | solution.py:947
  4.7 2.6 %collective-permute-start.1 = (bf16[9,16,768]{2,1,0:T(8,128)(2,1)S(1)}, bf16[9,16,768]{2,1,0:T(8,128)(2,1)S(1)}, u32[]{:S(2)}, u32[]{:S(2)}) collective-permute-start(bf16[9,16,768]{2,1,0:T(8,128)(2,1)S(1)} %cut_weights.1.after), channel_id=1, source_target_pairs={{0,2},{1,3},{2,0},{3,1},{4,6},{5,7},{6,4},{7,5},{8,10},{9,11},{10,... | collective-permute-start | bytes 663560 | tf_op jit(solution)/shard_map/ppermute | solution.py:947
  7.3 2.0 cut_maps.1.after.refs_1_
  9.3 1.1 copy-done
  10.5 1.1 cut_cotangent.1
  12.3 1.8 collective-permute-done.rest_0_
  14.1 9.3 %collective-permute-done.1.rest_1_ = bf16[9,16,768]{2,1,0:T(8,128)(2,1)S(1)} collective-permute-done((bf16[9,16,768]{2,1,0:T(8,128)(2,1)S(1)}, bf16[9,16,768]{2,1,0:T(8,128)(2,1)S(1)}, u32[]{:S(2)}, u32[]{:S(2)}) %collective-permute-start.1) | collective-permute-done | bytes 221216 | tf_op jit(solution)/shard_map/ppermute | solution.py:947
  23.5 0.7 sort_pieces.1
  24.2 6.3 %all-to-all-start = ((bf16[4,64,1664]{2,1,0:T(8,128)(2,1)}), bf16[4,64,1664]{2,1,0:T(8,128)(2,1)S(1)}, u32[]{:S(2)}, u32[]{:S(2)}) async-start(bf16[4,64,1664]{2,1,0:T(8,128)(2,1)} %release_far.1), calls=%async_computation | async-start | bytes 1703936 | tf_op jit(solution)/shard_map/all_to_all | solution.py:997
  30.5 1.5 collective-permute-start.3
  32.6 1.5 collective-permute-start.11
  34.6 4.6 %collective-permute-done.3.rest_1_ = bf16[3,9,16,256]{3,2,1,0:T(8,128)(2,1)} collective-permute-done((bf16[3,9,16,256]{3,2,1,0:T(8,128)(2,1)}, bf16[3,9,16,256]{3,2,1,0:T(8,128)(2,1)}, u32[]{:S(2)}, u32[]{:S(2)}) %collective-permute-start.3) | collective-permute-done | bytes 221216 | tf_op jit(solution)/shard_map/ppermute | solution.py:944
  39.2 1.5 collective-permute-start.5
  40.7 5.4 %collective-permute-done.4.rest_2_ = bf16[3,9,16,256]{3,2,1,0:T(8,128)(2,1)} collective-permute-done((bf16[3,9,16,256]{3,2,1,0:T(8,128)(2,1)}, bf16[3,9,16,256]{3,2,1,0:T(8,128)(2,1)}, u32[]{:S(2)}, u32[]{:S(2)}) %collective-permute-start.4) | collective-permute-done | bytes 221216 | tf_op jit(solution)/shard_map/ppermute | solution.py:944
  46.1 2.3 %collective-permute-done.5.rest_3_ = bf16[3,9,16,256]{3,2,1,0:T(8,128)(2,1)} collective-permute-done((bf16[3,9,16,256]{3,2,1,0:T(8,128)(2,1)}, bf16[3,9,16,256]{3,2,1,0:T(8,128)(2,1)}, u32[]{:S(2)}, u32[]{:S(2)}) %collective-permute-start.5) | collective-permute-done | bytes 221216 | tf_op jit(solution)/shard_map/ppermute | solution.py:944
  48.4 1.3 collective-permute-start.8
  49.8 1.1 all-to-all-done.maps.refs_0_
  50.9 1.5 collective-permute-start.12
  52.5 1.7 join_in.1.w
  54.2 5.1 %first_conv.1 = (f32[8,208,512]{2,1,0:T(8,128)S(1)}, bf16[8,208,768]{2,1,0:T(8,128)(2,1)S(1)}, f32[16,128]{1,0:T(8,128)S(1)}) custom-call(s32[2]{0:T(128)S(1)} %copy-done.7, f32[4,128]{1,0:T(4,128)S(1)} %pad_maximum_fusion.gains, bf16[9,512,256]{2,1,0:T(8,128)(2,1)S(1)} %join_in.1.w, bf16[4,64,1664]{2,1,0:T(8,128)(2,1)S(1)} %all-to-all-done.maps.refs_0_), custom_call_target="tpu_custom_call" | custom-call | flops 3925868544 | bytes 10485760 | tf_op jit(solution)/shard_map/first_conv/pallas_call | solution.py:90
  59.4 14.7 %all_to_all.25.refs_0_.got = f32[32,16,128]{2,1,0:T(8,128)S(1)} all-to-all(f32[32,16,128]{2,1,0:T(8,128)S(1)} %fan.3), channel_id=1, replica_groups=mesh['dp'=8,'chan'=4] {'dp','chan'}, dimensions={0} | all-to-all | bytes 524288 | tf_op jit(solution)/shard_map/all_to_all | solution.py:972
  75.1 1.1 collective-permute-start.17
  76.2 1.2 collective-permute-start.18
  77.4 2.1 collective-permute-start.19
  79.8 9.5 %second_conv.1 = (f32[8,208,512]{2,1,0:T(8,128)S(1)}, bf16[8,208,1536]{2,1,0:T(8,128)(2,1)S(1)}, f32[16,512]{1,0:T(8,128)S(1)}, f32[8,128]{1,0:T(8,128)S(1)}, f32[8,128]{1,0:T(8,128)S(1)}) custom-call(s32[2]{0:T(128)S(1)} %copy-done.7, f32[32,16,128]{2,1,0:T(8,128)S(1)} %all_to_all.25.refs_0_.got, f32[8,208,512]{2,1,0:T(8,128)S(1)} %get-tuple-element.82.pre1.pre, ...), custom_call_target="tpu_custom_call" | custom-call | flops 7851737088 | bytes 17825792 | tf_op jit(solution)/shard_map/second_conv/pallas_call | solution.py:90
  89.4 11.4 %all_to_all.26.got = f32[32,8,128]{2,1,0:T(8,128)S(1)} all-to-all(f32[32,8,128]{2,1,0:T(8,128)S(1)} %fan.4), channel_id=1, replica_groups=mesh['dp'=8,'chan'=4] {'dp','chan'}, dimensions={0} | all-to-all | bytes 262144 | tf_op jit(solution)/shard_map/all_to_all | solution.py:972
  100.8 6.2 %pool.1 = (bf16[128,384]{1,0:T(8,128)(2,1)S(1)}, bf16[128,384]{1,0:T(8,128)(2,1)S(1)}, bf16[128,384]{1,0:T(8,128)(2,1)S(1)}, bf16[128,384]{1,0:T(8,128)(2,1)S(1)...) custom-call(s32[2]{0:T(128)S(1)} %copy-done.7, ...), custom_call_target="tpu_custom_call" | custom-call | flops 4000000000 | bytes 8388608 | tf_op jit(solution)/shard_map/pool/pallas_call | solution.py:90
  107.0 10.1 %all_to_all.27.refs_0_.got.after = f32[32,8,128]{2,1,0:T(8,128)S(1)} all-to-all(f32[32,8,128]{2,1,0:T(8,128)S(1)} %get-tuple-element.97), channel_id=1, replica_groups=mesh['dp'=8,'chan'=4] {'dp','chan'}, dimensions={0} | all-to-all | bytes 262144 | tf_op jit(solution)/shard_map/all_to_all | solution.py:972
  117.1 9.4 %weight_mid_terms.1 = (bf16[8,208,512]{2,1,0:T(8,128)(2,1)S(1)}, f32[8,512]{1,0:T(8,128)S(1)}, f32[8,128]{1,0:T(8,128)}, bf16[2,4,4,9,16,512]{5,4,3,2,1,0:T(8,128)(2,1)S(1)}, bf16[4,4,9,16,512]{4,3,2,1,0:T(8,128)(2,1)S(1)}) custom-call(s32[2]{0:T(128)S(1)} %copy-done.7, f32[32,8,128]{2,1,0:T(8,128)S(1)} %all_to_all.27.refs_0_.got.after, ...), custom_call_target="tpu_custom_call" | custom-call | flops 7851737088 | bytes 15728640 | tf_op jit(solution)/shard_map/weight_mid_terms/pallas_call | solution.py:90
  126.9 1.5 collective-permute-start.21
  128.4 2.7 %collective-permute-start.22 = (bf16[128,384]{1,0:T(8,128)(2,1)S(1)}, bf16[128,384]{1,0:T(8,128)(2,1)S(1)}, u32[]{:S(2)}, u32[]{:S(2)}) collective-permute-start(bf16[128,384]{1,0:T(8,128)(2,1)S(1)} %get-tuple-element.105), channel_id=1, source_target_pairs={{0,3},{1,2},{2,1},{3,0},{4,7},{5,6},{6,5},{7,4},{8,11},{9,10},{10,... | collective-permute-start | bytes 294920 | tf_op jit(solution)/shard_map/ppermute | solution.py:947
  131.7 0.8 collective-permute-start.24
  132.5 9.3 %second_back.1 = (f32[8,208,512]{2,1,0:T(8,128)S(1)}, f32[16,128]{1,0:T(8,128)S(1)}) custom-call(s32[2]{0:T(128)S(1)} %copy-done.7, f32[16,512]{1,0:T(8,128)S(1)} %get-tuple-element.107.table, bf16[8,208,512]{2,1,0:T(8,128)(2,1)S(1)} %get-tuple-element.110.grad, f32[8,208,512]{2,1,0:T(8,128)S(1)} %get-tuple-element.82.pre1.pre, ...), custom_call_target="tpu_custom_call" | custom-call | flops 7851737088 | bytes 20971520 | tf_op jit(solution)/shard_map/second_back/pallas_call | solution.py:90
  141.9 12.4 %all_to_all.28.got.after.refs_0_.rest_2_ = f32[32,16,128]{2,1,0:T(8,128)S(1)} all-to-all(f32[32,16,128]{2,1,0:T(8,128)S(1)} %fan.5), channel_id=1, replica_groups=mesh['dp'=8,'chan'=4] {'dp','chan'}, dimensions={0} | all-to-all | bytes 524288 | tf_op jit(solution)/shard_map/all_to_all | solution.py:972
  154.3 5.7 %weight_in_terms.1 = (bf16[8,208,512]{2,1,0:T(8,128)(2,1)S(1)}, f32[8,512]{1,0:T(8,128)S(1)}, f32[8,128]{1,0:T(8,128)S(1)}, bf16[2,4,4,9,16,256]{5,4,3,2,1,0:T(8,128)(2,1)S(1)}, bf16[4,4,9,16,256]{4,3,2,1,0:T(8,128)(2,1)S(1)}) custom-call(s32[2]{0:T(128)S(1)} %copy-done.7, f32[32,16,128]{2,1,0:T(8,128)S(1)} %all_to_all.28.got.after.refs_0_.rest_2_, ...), custom_call_target="tpu_custom_call" | custom-call | flops 3925868544 | bytes 15728640 | tf_op jit(solution)/shard_map/weight_in_terms/pallas_call | solution.py:90
  160.6 1.0 collective-permute-start.31
  162.1 5.6 %spectra_back.1 = (bf16[64,1536]{1,0:T(8,128)(2,1)S(1)}, bf16[64,1536]{1,0:T(8,128)(2,1)S(1)}, bf16[64,1536]{1,0:T(8,128)(2,1)S(1)}, bf16[64,1536]{1,0:T(8,128)(2,1)S(1)}) custom-call(s32[2]{0:T(128)S(1)} %copy-done.7, bf16[8,208,512]{2,1,0:T(8,128)(2,1)S(1)} %get-tuple-element.119.grad.after, bf16[8,208,512]{2,1,0:T(8,128)(2,1)S(1)} %get-tuple-element.119.grad.after, ...), custom_call_target="tpu_custom_call" | custom-call | flops 3925868544 | bytes 5242880 | tf_op jit(solution)/shard_map/spectra_back/pallas_call | solution.py:90
  168.0 1.6 collective-permute-start.29
  170.1 1.7 collective-permute-start.26
  171.8 5.1 %collective-permute-done.31.rest_2_ = bf16[4,9,16,512]{3,2,1,0:T(8,128)(2,1)S(1)} collective-permute-done((bf16[4,9,16,512]{3,2,1,0:T(8,128)(2,1)S(1)}, bf16[4,9,16,512]{3,2,1,0:T(8,128)(2,1)S(1)}, u32[]{:S(2)}, u32[]{:S(2)}) %collective-permute-start.31) | collective-permute-done | bytes 589856 | tf_op jit(solution)/shard_map/ppermute | solution.py:944
  177.1 0.8 collective-permute-start.33
  177.9 1.1 collective-permute-done.25.rest_1_
  179.0 2.5 %collective-permute-done.26.rest_2_ = bf16[64,1536]{1,0:T(8,128)(2,1)S(1)} collective-permute-done((bf16[64,1536]{1,0:T(8,128)(2,1)S(1)}, bf16[64,1536]{1,0:T(8,128)(2,1)S(1)}, u32[]{:S(2)}, u32[]{:S(2)}) %collective-permute-start.26) | collective-permute-done | bytes 196640 | tf_op jit(solution)/shard_map/ppermute | solution.py:947
  181.5 0.8 collective-permute-done.29.got
  182.5 1.1 collective-permute-start.32
  183.6 1.9 collective-permute-start.27
  185.5 0.8 place_pooled.1
  186.3 0.7 collective-permute-done.33.got
  187.1 5.8 %collective-permute-done.27.rest_3_.rest_1_ = bf16[64,1536]{1,0:T(8,128)(2,1)S(1)} collective-permute-done((bf16[64,1536]{1,0:T(8,128)(2,1)S(1)}, bf16[64,1536]{1,0:T(8,128)(2,1)S(1)}, u32[]{:S(2)}, u32[]{:S(2)}) %collective-permute-start.27) | collective-permute-done | bytes 196640 | tf_op jit(solution)/shard_map/ppermute | solution.py:947
  192.9 2.9 %collective-permute-start.34 = (bf16[2,9,16,256]{3,2,1,0:T(8,128)(2,1)S(1)}, bf16[2,9,16,256]{3,2,1,0:T(8,128)(2,1)S(1)}, u32[]{:S(2)}, u32[]{:S(2)}) collective-permute-start(bf16[2,9,16,256]{3,2,1,0:T(8,128)(2,1)S(1)} %get-tuple-element.139), channel_id=1, source_target_pairs={{0,1},{1,0},{2,3},{3,2},{4,5},{5,4},{6,7},{7,6},{8,9},{9,8},{10,11... | collective-permute-start | bytes 442376 | tf_op jit(solution)/shard_map/ppermute | solution.py:947
  196.1 1.3 place_spectra.1
  197.4 3.6 %collective-permute-done.34.got = bf16[2,9,16,256]{3,2,1,0:T(8,128)(2,1)S(1)} collective-permute-done((bf16[2,9,16,256]{3,2,1,0:T(8,128)(2,1)S(1)}, bf16[2,9,16,256]{3,2,1,0:T(8,128)(2,1)S(1)}, u32[]{:S(2)}, u32[]{:S(2)}) %collective-permute-start.34) | collective-permute-done | bytes 147488 | tf_op jit(solution)/shard_map/ppermute | solution.py:947
  201.0 3.8 %collective-permute-done.36.got = bf16[1,9,16,512]{3,2,1,0:T(8,128)(2,1)S(1)} collective-permute-done((bf16[1,9,16,512]{3,2,1,0:T(8,128)(2,1)S(1)}, bf16[1,9,16,512]{3,2,1,0:T(8,128)(2,1)S(1)}, u32[]{:S(2)}, u32[]{:S(2)}) %collective-permute-start.36) | collective-permute-done | bytes 147488 | tf_op jit(solution)/shard_map/ppermute | solution.py:947
  205.6 1.8 collective-permute-start.42
  207.4 3.1 %collective-permute-done.35.got = bf16[1,9,16,256]{3,2,1,0:T(8,128)(2,1)S(1)} collective-permute-done((bf16[1,9,16,256]{3,2,1,0:T(8,128)(2,1)S(1)}, bf16[1,9,16,256]{3,2,1,0:T(8,128)(2,1)S(1)}, u32[]{:S(2)}, u32[]{:S(2)}) %collective-permute-start.35) | collective-permute-done | bytes 73760 | tf_op jit(solution)/shard_map/ppermute | solution.py:947
  210.5 1.9 collective-permute-start.37
  212.4 1.7 collective-permute-start.38
  214.9 1.8 collective-permute-done.38.refs_2_.refs_5_
  216.8 2.5 %collective-permute-done.43.refs_3_ = bf16[9,16,512]{2,1,0:T(8,128)(2,1)S(1)} collective-permute-done((bf16[9,16,512]{2,1,0:T(8,128)(2,1)S(1)}, bf16[9,16,512]{2,1,0:T(8,128)(2,1)S(1)}, u32[]{:S(2)}, u32[]{:S(2)}) %collective-permute-start.43) | collective-permute-done | bytes 147488 | tf_op jit(solution)/shard_map/ppermute | solution.py:944
  219.9 0.8 collective-permute-start.39
  220.7 3.6 %collective-permute-done.39.refs_3_ = bf16[9,16,256]{2,1,0:T(8,128)(2,1)S(1)} collective-permute-done((bf16[9,16,256]{2,1,0:T(8,128)(2,1)S(1)}, bf16[9,16,256]{2,1,0:T(8,128)(2,1)S(1)}, u32[]{:S(2)}, u32[]{:S(2)}) %collective-permute-start.39) | collective-permute-done | bytes 73760 | tf_op jit(solution)/shard_map/ppermute | solution.py:944
  225.9 1.1 in_out.1
  227.0 1.6 mid_out.1
  (101 shorter events, 10.9 us)
Async XLA Ops:
  1.6 12.5 %collective-permute-start = (bf16[9,16,768]{2,1,0:T(8,128)(2,1)S(1)}, bf16[9,16,768]{2,1,0:T(8,128)(2,1)S(1)}, u32[]{:S(2)}, u32[]{:S(2)}) collective-permute-start(bf16[9,16,768]{2,1,0:T(8,128)(2,1)S(1)} %cut_weights.1.after), channel_id=1, source_target_pairs={{0,1},{1,0},{2,3},{3,2},{4,5},{5,4},{6,7},{7,6},{8,9},{9,8},{10,11... | collective-permute-start | bytes 663560 | tf_op jit(solution)/shard_map/ppermute | solution.py:947
  4.7 18.7 %collective-permute-start.1 = (bf16[9,16,768]{2,1,0:T(8,128)(2,1)S(1)}, bf16[9,16,768]{2,1,0:T(8,128)(2,1)S(1)}, u32[]{:S(2)}, u32[]{:S(2)}) collective-permute-start(bf16[9,16,768]{2,1,0:T(8,128)(2,1)S(1)} %cut_weights.1.after), channel_id=1, source_target_pairs={{0,2},{1,3},{2,0},{3,1},{4,6},{5,7},{6,4},{7,5},{8,10},{9,11},{10,... | collective-permute-start | bytes 663560 | tf_op jit(solution)/shard_map/ppermute | solution.py:947
  7.3 16.1 %collective-permute-start.2 = (bf16[9,16,768]{2,1,0:T(8,128)(2,1)S(1)}, bf16[9,16,768]{2,1,0:T(8,128)(2,1)S(1)}, u32[]{:S(2)}, u32[]{:S(2)}) collective-permute-start(bf16[9,16,768]{2,1,0:T(8,128)(2,1)S(1)} %cut_weights.1.after), channel_id=1, source_target_pairs={{0,3},{1,2},{2,1},{3,0},{4,7},{5,6},{6,5},{7,4},{8,11},{9,10},{10,... | collective-permute-start | bytes 663560 | tf_op jit(solution)/shard_map/ppermute | solution.py:947
  9.3 1.2 copy-start
  11.6 0.7 copy-start.5
  12.3 11.9 %copy-start.3 = (bf16[128,512]{1,0:T(8,128)(2,1)}, bf16[128,512]{1,0:T(8,128)(2,1)S(1)}, u32[]{:S(2)}) copy-start(bf16[128,512]{1,0:T(8,128)(2,1)S(1)} %get-tuple-element.89.refs_3_) | copy-start | bytes 393220
  24.2 28.2 %copy-start.8 = (f32[128]{0:T(128)S(1)}, f32[128]{0:T(128)}, u32[]{:S(2)}) copy-start(f32[128]{0:T(128)} %param.16) | copy-start | bytes 1540
  24.2 28.2 %copy-start.9 = (f32[128]{0:T(128)S(1)}, f32[128]{0:T(128)}, u32[]{:S(2)}) copy-start(f32[128]{0:T(128)} %param.15) | copy-start | bytes 1540
  24.2 28.2 %copy-start.10 = (f32[128]{0:T(128)S(1)}, f32[128]{0:T(128)}, u32[]{:S(2)}) copy-start(f32[128]{0:T(128)} %param.13) | copy-start | bytes 1540
  24.2 28.2 %copy-start.11 = (f32[128]{0:T(128)S(1)}, f32[128]{0:T(128)}, u32[]{:S(2)}) copy-start(f32[128]{0:T(128)} %param.12) | copy-start | bytes 1540
  24.2 28.3 %copy-start.2 = (bf16[9,128,256]{2,1,0:T(8,128)(2,1)S(1)}, bf16[9,128,256]{2,1,0:T(8,128)(2,1)}, u32[]{:S(2)}) copy-start(bf16[9,128,256]{2,1,0:T(8,128)(2,1)} %own.2) | copy-start | bytes 1769476
  24.2 26.7 %all-to-all-start = ((bf16[4,64,1664]{2,1,0:T(8,128)(2,1)}), bf16[4,64,1664]{2,1,0:T(8,128)(2,1)S(1)}, u32[]{:S(2)}, u32[]{:S(2)}) async-start(bf16[4,64,1664]{2,1,0:T(8,128)(2,1)} %release_far.1), calls=%async_computation | async-start | bytes 1703936 | tf_op jit(solution)/shard_map/all_to_all | solution.py:997
  30.5 8.7 %collective-permute-start.3 = (bf16[3,9,16,256]{3,2,1,0:T(8,128)(2,1)}, bf16[3,9,16,256]{3,2,1,0:T(8,128)(2,1)}, u32[]{:S(2)}, u32[]{:S(2)}) collective-permute-start(bf16[3,9,16,256]{3,2,1,0:T(8,128)(2,1)} %get-tuple-element.79.rest_0_.refs_0_), channel_id=1, source_target_pairs={{0,16},{4,12},{8,24},{12,4},{16,0},{20,28},{24,8},{28,20},{1,17},{... | collective-permute-start | bytes 663560 | tf_op jit(solution)/shard_map/ppermute | solution.py:944
  32.1 17.7 %collective-permute-start.10 = (bf16[3,9,16,512]{3,2,1,0:T(8,128)(2,1)S(1)}, bf16[3,9,16,512]{3,2,1,0:T(8,128)(2,1)S(1)}, u32[]{:S(2)}, u32[]{:S(2)}) collective-permute-start(bf16[3,9,16,512]{3,2,1,0:T(8,128)(2,1)S(1)} %get-tuple-element.81.refs_1_), channel_id=1, source_target_pairs={{0,16},{4,12},{8,24},{12,4},{16,0},{20,28},{24,8},{28,20},{1,17},{... | collective-permute-start | bytes 1327112 | tf_op jit(solution)/shard_map/ppermute | solution.py:944
  32.6 17.2 %collective-permute-start.11 = (bf16[3,9,16,512]{3,2,1,0:T(8,128)(2,1)S(1)}, bf16[3,9,16,512]{3,2,1,0:T(8,128)(2,1)S(1)}, u32[]{:S(2)}, u32[]{:S(2)}) collective-permute-start(bf16[3,9,16,512]{3,2,1,0:T(8,128)(2,1)S(1)} %get-tuple-element.81.refs_1_), channel_id=1, source_target_pairs={{0,8},{4,20},{8,0},{12,28},{16,24},{20,4},{24,16},{28,12},{1,9},{5... | collective-permute-start | bytes 1327112 | tf_op jit(solution)/shard_map/ppermute | solution.py:944
  34.1 12.0 %collective-permute-start.4 = (bf16[3,9,16,256]{3,2,1,0:T(8,128)(2,1)}, bf16[3,9,16,256]{3,2,1,0:T(8,128)(2,1)}, u32[]{:S(2)}, u32[]{:S(2)}) collective-permute-start(bf16[3,9,16,256]{3,2,1,0:T(8,128)(2,1)} %get-tuple-element.79.rest_0_.refs_0_), channel_id=1, source_target_pairs={{0,8},{4,20},{8,0},{12,28},{16,24},{20,4},{24,16},{28,12},{1,9},{5... | collective-permute-start | bytes 663560 | tf_op jit(solution)/shard_map/ppermute | solution.py:944
  39.2 9.3 %collective-permute-start.5 = (bf16[3,9,16,256]{3,2,1,0:T(8,128)(2,1)}, bf16[3,9,16,256]{3,2,1,0:T(8,128)(2,1)}, u32[]{:S(2)}, u32[]{:S(2)}) collective-permute-start(bf16[3,9,16,256]{3,2,1,0:T(8,128)(2,1)} %collective-permute-done.3.rest_1_), channel_id=1, source_target_pairs={{0,8},{4,20},{8,0},{12,28},{16,24},{20,4},{24,16},{28,12},{1,9},{5... | collective-permute-start | bytes 663560 | tf_op jit(solution)/shard_map/ppermute | solution.py:944
  40.7 11.8 %collective-permute-start.6 = (bf16[3,9,16,256]{3,2,1,0:T(8,128)(2,1)}, bf16[3,9,16,256]{3,2,1,0:T(8,128)(2,1)}, u32[]{:S(2)}, u32[]{:S(2)}) collective-permute-start(bf16[3,9,16,256]{3,2,1,0:T(8,128)(2,1)} %get-tuple-element.79.rest_0_.refs_0_), channel_id=1, source_target_pairs={{0,4},{4,0},{8,12},{12,8},{16,20},{20,16},{24,28},{28,24},{1,5},{5... | collective-permute-start | bytes 663560 | tf_op jit(solution)/shard_map/ppermute | solution.py:937
  46.1 6.4 %collective-permute-start.7 = (bf16[3,9,16,256]{3,2,1,0:T(8,128)(2,1)}, bf16[3,9,16,256]{3,2,1,0:T(8,128)(2,1)}, u32[]{:S(2)}, u32[]{:S(2)}) collective-permute-start(bf16[3,9,16,256]{3,2,1,0:T(8,128)(2,1)} %collective-permute-done.3.rest_1_), channel_id=1, source_target_pairs={{0,4},{4,0},{8,12},{12,8},{16,20},{20,16},{24,28},{28,24},{1,5},{5... | collective-permute-start | bytes 663560 | tf_op jit(solution)/shard_map/ppermute | solution.py:937
  48.4 4.0 %collective-permute-start.8 = (bf16[3,9,16,256]{3,2,1,0:T(8,128)(2,1)}, bf16[3,9,16,256]{3,2,1,0:T(8,128)(2,1)}, u32[]{:S(2)}, u32[]{:S(2)}) collective-permute-start(bf16[3,9,16,256]{3,2,1,0:T(8,128)(2,1)} %collective-permute-done.4.rest_2_), channel_id=1, source_target_pairs={{0,4},{4,0},{8,12},{12,8},{16,20},{20,16},{24,28},{28,24},{1,5},{5... | collective-permute-start | bytes 663560 | tf_op jit(solution)/shard_map/ppermute | solution.py:937
  49.7 2.8 %collective-permute-start.9 = (bf16[3,9,16,256]{3,2,1,0:T(8,128)(2,1)}, bf16[3,9,16,256]{3,2,1,0:T(8,128)(2,1)}, u32[]{:S(2)}, u32[]{:S(2)}) collective-permute-start(bf16[3,9,16,256]{3,2,1,0:T(8,128)(2,1)} %collective-permute-done.5.rest_3_), channel_id=1, source_target_pairs={{0,4},{4,0},{8,12},{12,8},{16,20},{20,16},{24,28},{28,24},{1,5},{5... | collective-permute-start | bytes 663560 | tf_op jit(solution)/shard_map/ppermute | solution.py:937
  50.9 8.5 %collective-permute-start.12 = (bf16[3,9,16,512]{3,2,1,0:T(8,128)(2,1)S(1)}, bf16[3,9,16,512]{3,2,1,0:T(8,128)(2,1)S(1)}, u32[]{:S(2)}, u32[]{:S(2)}) collective-permute-start(bf16[3,9,16,512]{3,2,1,0:T(8,128)(2,1)S(1)} %release.5), channel_id=1, source_target_pairs={{0,8},{4,20},{8,0},{12,28},{16,24},{20,4},{24,16},{28,12},{1,9},{5... | collective-permute-start | bytes 1327112 | tf_op jit(solution)/shard_map/ppermute | solution.py:944
  52.4 1.8 copy-start.7
  59.3 15.8 %copy-start.4 = (bf16[128,512]{1,0:T(8,128)(2,1)S(1)}, bf16[128,512]{1,0:T(8,128)(2,1)}, u32[]{:S(2)}) copy-start(bf16[128,512]{1,0:T(8,128)(2,1)} %copy-done.3) | copy-start | bytes 393220
  59.4 15.7 %copy-start.6 = (bf16[128,512]{1,0:T(8,128)(2,1)S(1)}, bf16[128,512]{1,0:T(8,128)(2,1)}, u32[]{:S(2)}) copy-start(bf16[128,512]{1,0:T(8,128)(2,1)} %copy-done.5) | copy-start | bytes 393220
  59.4 20.1 %copy-start.1 = (bf16[9,128,512]{2,1,0:T(8,128)(2,1)S(1)}, bf16[9,128,512]{2,1,0:T(8,128)(2,1)}, u32[]{:S(2)}) copy-start(bf16[9,128,512]{2,1,0:T(8,128)(2,1)} %own.3) | copy-start | bytes 3538948
  74.1 2.1 collective-permute-start.13
  74.5 3.0 %collective-permute-start.14 = (bf16[3,9,16,512]{3,2,1,0:T(8,128)(2,1)S(1)}, bf16[3,9,16,512]{3,2,1,0:T(8,128)(2,1)S(1)}, u32[]{:S(2)}, u32[]{:S(2)}) collective-permute-start(bf16[3,9,16,512]{3,2,1,0:T(8,128)(2,1)S(1)} %get-tuple-element.84.rest_1_), channel_id=1, source_target_pairs={{0,4},{4,0},{8,12},{12,8},{16,20},{20,16},{24,28},{28,24},{1,5},{5... | collective-permute-start | bytes 1327112 | tf_op jit(solution)/shard_map/ppermute | solution.py:937
  74.6 4.9 %collective-permute-start.15 = (bf16[3,9,16,512]{3,2,1,0:T(8,128)(2,1)S(1)}, bf16[3,9,16,512]{3,2,1,0:T(8,128)(2,1)S(1)}, u32[]{:S(2)}, u32[]{:S(2)}) collective-permute-start(bf16[3,9,16,512]{3,2,1,0:T(8,128)(2,1)S(1)} %get-tuple-element.85.rest_2_), channel_id=1, source_target_pairs={{0,4},{4,0},{8,12},{12,8},{16,20},{20,16},{24,28},{28,24},{1,5},{5... | collective-permute-start | bytes 1327112 | tf_op jit(solution)/shard_map/ppermute | solution.py:937
  75.0 4.5 %collective-permute-start.16 = (bf16[3,9,16,512]{3,2,1,0:T(8,128)(2,1)S(1)}, bf16[3,9,16,512]{3,2,1,0:T(8,128)(2,1)S(1)}, u32[]{:S(2)}, u32[]{:S(2)}) collective-permute-start(bf16[3,9,16,512]{3,2,1,0:T(8,128)(2,1)S(1)} %get-tuple-element.86.rest_3_), channel_id=1, source_target_pairs={{0,4},{4,0},{8,12},{12,8},{16,20},{20,16},{24,28},{28,24},{1,5},{5... | collective-permute-start | bytes 1327112 | tf_op jit(solution)/shard_map/ppermute | solution.py:937
  75.1 14.3 %collective-permute-start.17 = (bf16[128,512]{1,0:T(8,128)(2,1)S(1)}, bf16[128,512]{1,0:T(8,128)(2,1)S(1)}, u32[]{:S(2)}, u32[]{:S(2)}) collective-permute-start(bf16[128,512]{1,0:T(8,128)(2,1)S(1)} %get-tuple-element.91), channel_id=1, source_target_pairs={{0,1},{1,0},{2,3},{3,2},{4,5},{5,4},{6,7},{7,6},{8,9},{9,8},{10,11... | collective-permute-start | bytes 393224 | tf_op jit(solution)/shard_map/ppermute | solution.py:947
  76.2 13.2 %collective-permute-start.18 = (bf16[128,512]{1,0:T(8,128)(2,1)S(1)}, bf16[128,512]{1,0:T(8,128)(2,1)S(1)}, u32[]{:S(2)}, u32[]{:S(2)}) collective-permute-start(bf16[128,512]{1,0:T(8,128)(2,1)S(1)} %get-tuple-element.92), channel_id=1, source_target_pairs={{0,2},{1,3},{2,0},{3,1},{4,6},{5,7},{6,4},{7,5},{8,10},{9,11},{10,... | collective-permute-start | bytes 393224 | tf_op jit(solution)/shard_map/ppermute | solution.py:947
  77.4 11.9 %collective-permute-start.19 = (bf16[128,512]{1,0:T(8,128)(2,1)S(1)}, bf16[128,512]{1,0:T(8,128)(2,1)S(1)}, u32[]{:S(2)}, u32[]{:S(2)}) collective-permute-start(bf16[128,512]{1,0:T(8,128)(2,1)S(1)} %get-tuple-element.93), channel_id=1, source_target_pairs={{0,3},{1,2},{2,1},{3,0},{4,7},{5,6},{6,5},{7,4},{8,11},{9,10},{10,... | collective-permute-start | bytes 393224 | tf_op jit(solution)/shard_map/ppermute | solution.py:947
  126.5 4.6 %collective-permute-start.23 = (bf16[4,4,9,16,512]{4,3,2,1,0:T(8,128)(2,1)S(1)}, bf16[4,4,9,16,512]{4,3,2,1,0:T(8,128)(2,1)S(1)}, u32[]{:S(2)}, u32[]{:S(2)}) collective-permute-start(bf16[4,4,9,16,512]{4,3,2,1,0:T(8,128)(2,1)S(1)} %get-tuple-element.114), channel_id=1, source_target_pairs={{0,4},{4,0},{8,12},{12,8},{16,20},{20,16},{24,28},{28,24},{1,5},{5... | collective-permute-start | bytes 7077896 | tf_op jit(solution)/shard_map/ppermute | solution.py:937
  126.6 15.2 %collective-permute-start.20 = (bf16[128,384]{1,0:T(8,128)(2,1)S(1)}, bf16[128,384]{1,0:T(8,128)(2,1)S(1)}, u32[]{:S(2)}, u32[]{:S(2)}) collective-permute-start(bf16[128,384]{1,0:T(8,128)(2,1)S(1)} %get-tuple-element.103), channel_id=1, source_target_pairs={{0,1},{1,0},{2,3},{3,2},{4,5},{5,4},{6,7},{7,6},{8,9},{9,8},{10,11... | collective-permute-start | bytes 294920 | tf_op jit(solution)/shard_map/ppermute | solution.py:947
  126.9 14.9 %collective-permute-start.21 = (bf16[128,384]{1,0:T(8,128)(2,1)S(1)}, bf16[128,384]{1,0:T(8,128)(2,1)S(1)}, u32[]{:S(2)}, u32[]{:S(2)}) collective-permute-start(bf16[128,384]{1,0:T(8,128)(2,1)S(1)} %get-tuple-element.104), channel_id=1, source_target_pairs={{0,2},{1,3},{2,0},{3,1},{4,6},{5,7},{6,4},{7,5},{8,10},{9,11},{10,... | collective-permute-start | bytes 294920 | tf_op jit(solution)/shard_map/ppermute | solution.py:947
  128.4 13.4 %collective-permute-start.22 = (bf16[128,384]{1,0:T(8,128)(2,1)S(1)}, bf16[128,384]{1,0:T(8,128)(2,1)S(1)}, u32[]{:S(2)}, u32[]{:S(2)}) collective-permute-start(bf16[128,384]{1,0:T(8,128)(2,1)S(1)} %get-tuple-element.105), channel_id=1, source_target_pairs={{0,3},{1,2},{2,1},{3,0},{4,7},{5,6},{6,5},{7,4},{8,11},{9,10},{10,... | collective-permute-start | bytes 294920 | tf_op jit(solution)/shard_map/ppermute | solution.py:947
  131.7 10.2 %collective-permute-start.24 = (bf16[4,9,16,512]{3,2,1,0:T(8,128)(2,1)S(1)}, bf16[4,9,16,512]{3,2,1,0:T(8,128)(2,1)S(1)}, u32[]{:S(2)}, u32[]{:S(2)}) collective-permute-start(bf16[4,9,16,512]{3,2,1,0:T(8,128)(2,1)S(1)} %get-tuple-element.115.after), channel_id=1, source_target_pairs={{0,8},{4,20},{8,0},{12,28},{16,24},{20,4},{24,16},{28,12},{1,9},{5... | collective-permute-start | bytes 1769480 | tf_op jit(solution)/shard_map/ppermute | solution.py:944
  160.0 7.7 %collective-permute-start.28 = (bf16[4,4,9,16,256]{4,3,2,1,0:T(8,128)(2,1)S(1)}, bf16[4,4,9,16,256]{4,3,2,1,0:T(8,128)(2,1)S(1)}, u32[]{:S(2)}, u32[]{:S(2)}) collective-permute-start(bf16[4,4,9,16,256]{4,3,2,1,0:T(8,128)(2,1)S(1)} %get-tuple-element.126), channel_id=1, source_target_pairs={{0,4},{4,0},{8,12},{12,8},{16,20},{20,16},{24,28},{28,24},{1,5},{5... | collective-permute-start | bytes 3538952 | tf_op jit(solution)/shard_map/ppermute | solution.py:937
  160.6 16.3 %collective-permute-start.31 = (bf16[4,9,16,512]{3,2,1,0:T(8,128)(2,1)S(1)}, bf16[4,9,16,512]{3,2,1,0:T(8,128)(2,1)S(1)}, u32[]{:S(2)}, u32[]{:S(2)}) collective-permute-start(bf16[4,9,16,512]{3,2,1,0:T(8,128)(2,1)S(1)} %mid_sum_b.1), channel_id=1, source_target_pairs={{0,16},{4,12},{8,24},{12,4},{16,0},{20,28},{24,8},{28,20},{1,17},{... | collective-permute-start | bytes 1769480 | tf_op jit(solution)/shard_map/ppermute | solution.py:944
  161.6 15.3 %collective-permute-start.30 = (bf16[4,9,16,512]{3,2,1,0:T(8,128)(2,1)S(1)}, bf16[4,9,16,512]{3,2,1,0:T(8,128)(2,1)S(1)}, u32[]{:S(2)}, u32[]{:S(2)}) collective-permute-start(bf16[4,9,16,512]{3,2,1,0:T(8,128)(2,1)S(1)} %release.9), channel_id=1, source_target_pairs={{0,8},{4,20},{8,0},{12,28},{16,24},{20,4},{24,16},{28,12},{1,9},{5... | collective-permute-start | bytes 1769480 | tf_op jit(solution)/shard_map/ppermute | solution.py:944
  168.0 14.3 %collective-permute-start.29 = (bf16[8,9,16,256]{3,2,1,0:T(8,128)(2,1)S(1)}, bf16[8,9,16,256]{3,2,1,0:T(8,128)(2,1)S(1)}, u32[]{:S(2)}, u32[]{:S(2)}) collective-permute-start(bf16[8,9,16,256]{3,2,1,0:T(8,128)(2,1)S(1)} %get-tuple-element.128), channel_id=1, source_target_pairs={{0,8},{4,20},{8,0},{12,28},{16,24},{20,4},{24,16},{28,12},{1,9},{5... | collective-permute-start | bytes 1769480 | tf_op jit(solution)/shard_map/ppermute | solution.py:944
  169.6 9.4 %collective-permute-start.25 = (bf16[64,1536]{1,0:T(8,128)(2,1)S(1)}, bf16[64,1536]{1,0:T(8,128)(2,1)S(1)}, u32[]{:S(2)}, u32[]{:S(2)}) collective-permute-start(bf16[64,1536]{1,0:T(8,128)(2,1)S(1)} %get-tuple-element.121), channel_id=1, source_target_pairs={{0,1},{1,0},{2,3},{3,2},{4,5},{5,4},{6,7},{7,6},{8,9},{9,8},{10,11... | collective-permute-start | bytes 589832 | tf_op jit(solution)/shard_map/ppermute | solution.py:947
  170.1 11.4 %collective-permute-start.26 = (bf16[64,1536]{1,0:T(8,128)(2,1)S(1)}, bf16[64,1536]{1,0:T(8,128)(2,1)S(1)}, u32[]{:S(2)}, u32[]{:S(2)}) collective-permute-start(bf16[64,1536]{1,0:T(8,128)(2,1)S(1)} %get-tuple-element.122), channel_id=1, source_target_pairs={{0,2},{1,3},{2,0},{3,1},{4,6},{5,7},{6,4},{7,5},{8,10},{9,11},{10,... | collective-permute-start | bytes 589832 | tf_op jit(solution)/shard_map/ppermute | solution.py:947
  177.1 9.9 %collective-permute-start.33 = (bf16[2,9,16,512]{3,2,1,0:T(8,128)(2,1)S(1)}, bf16[2,9,16,512]{3,2,1,0:T(8,128)(2,1)S(1)}, u32[]{:S(2)}, u32[]{:S(2)}) collective-permute-start(bf16[2,9,16,512]{3,2,1,0:T(8,128)(2,1)S(1)} %get-tuple-element.135), channel_id=1, source_target_pairs={{0,1},{1,0},{2,3},{3,2},{4,5},{5,4},{6,7},{7,6},{8,9},{9,8},{10,11... | collective-permute-start | bytes 884744 | tf_op jit(solution)/shard_map/ppermute | solution.py:947
  182.5 10.4 %collective-permute-start.32 = (bf16[4,9,16,256]{3,2,1,0:T(8,128)(2,1)S(1)}, bf16[4,9,16,256]{3,2,1,0:T(8,128)(2,1)S(1)}, u32[]{:S(2)}, u32[]{:S(2)}) collective-permute-start(bf16[4,9,16,256]{3,2,1,0:T(8,128)(2,1)S(1)} %get-tuple-element.134), channel_id=1, source_target_pairs={{0,16},{4,12},{8,24},{12,4},{16,0},{20,28},{24,8},{28,20},{1,17},{... | collective-permute-start | bytes 884744 | tf_op jit(solution)/shard_map/ppermute | solution.py:944
  183.6 9.2 %collective-permute-start.27 = (bf16[64,1536]{1,0:T(8,128)(2,1)S(1)}, bf16[64,1536]{1,0:T(8,128)(2,1)S(1)}, u32[]{:S(2)}, u32[]{:S(2)}) collective-permute-start(bf16[64,1536]{1,0:T(8,128)(2,1)S(1)} %get-tuple-element.123), channel_id=1, source_target_pairs={{0,3},{1,2},{2,1},{3,0},{4,7},{5,6},{6,5},{7,4},{8,11},{9,10},{10,... | collective-permute-start | bytes 589832 | tf_op jit(solution)/shard_map/ppermute | solution.py:947
  192.9 8.1 %collective-permute-start.34 = (bf16[2,9,16,256]{3,2,1,0:T(8,128)(2,1)S(1)}, bf16[2,9,16,256]{3,2,1,0:T(8,128)(2,1)S(1)}, u32[]{:S(2)}, u32[]{:S(2)}) collective-permute-start(bf16[2,9,16,256]{3,2,1,0:T(8,128)(2,1)S(1)} %get-tuple-element.139), channel_id=1, source_target_pairs={{0,1},{1,0},{2,3},{3,2},{4,5},{5,4},{6,7},{7,6},{8,9},{9,8},{10,11... | collective-permute-start | bytes 442376 | tf_op jit(solution)/shard_map/ppermute | solution.py:947
  195.8 9.1 %collective-permute-start.36 = (bf16[1,9,16,512]{3,2,1,0:T(8,128)(2,1)S(1)}, bf16[1,9,16,512]{3,2,1,0:T(8,128)(2,1)S(1)}, u32[]{:S(2)}, u32[]{:S(2)}) collective-permute-start(bf16[1,9,16,512]{3,2,1,0:T(8,128)(2,1)S(1)} %get-tuple-element.143), channel_id=1, source_target_pairs={{0,2},{1,3},{2,0},{3,1},{4,6},{5,7},{6,4},{7,5},{8,10},{9,11},{10,... | collective-permute-start | bytes 442376 | tf_op jit(solution)/shard_map/ppermute | solution.py:947
  204.9 9.2 %collective-permute-start.41 = (bf16[9,16,512]{2,1,0:T(8,128)(2,1)S(1)}, bf16[9,16,512]{2,1,0:T(8,128)(2,1)S(1)}, u32[]{:S(2)}, u32[]{:S(2)}) collective-permute-start(bf16[9,16,512]{2,1,0:T(8,128)(2,1)S(1)} %mid_sum_3.1.rest_0_.refs_0_), channel_id=1, source_target_pairs={{0,16},{4,12},{8,24},{12,4},{16,0},{20,28},{24,8},{28,20},{1,17},{... | collective-permute-start | bytes 442376 | tf_op jit(solution)/shard_map/ppermute | solution.py:944
  205.2 5.3 %collective-permute-start.35 = (bf16[1,9,16,256]{3,2,1,0:T(8,128)(2,1)S(1)}, bf16[1,9,16,256]{3,2,1,0:T(8,128)(2,1)S(1)}, u32[]{:S(2)}, u32[]{:S(2)}) collective-permute-start(bf16[1,9,16,256]{3,2,1,0:T(8,128)(2,1)S(1)} %get-tuple-element.142), channel_id=1, source_target_pairs={{0,2},{1,3},{2,0},{3,1},{4,6},{5,7},{6,4},{7,5},{8,10},{9,11},{10,... | collective-permute-start | bytes 221192 | tf_op jit(solution)/shard_map/ppermute | solution.py:947
  205.6 8.8 %collective-permute-start.42 = (bf16[9,16,512]{2,1,0:T(8,128)(2,1)S(1)}, bf16[9,16,512]{2,1,0:T(8,128)(2,1)S(1)}, u32[]{:S(2)}, u32[]{:S(2)}) collective-permute-start(bf16[9,16,512]{2,1,0:T(8,128)(2,1)S(1)} %mid_sum_3.1.rest_0_.refs_0_), channel_id=1, source_target_pairs={{0,8},{4,20},{8,0},{12,28},{16,24},{20,4},{24,16},{28,12},{1,9},{5... | collective-permute-start | bytes 442376 | tf_op jit(solution)/shard_map/ppermute | solution.py:944
  210.5 4.4 %collective-permute-start.37 = (bf16[9,16,256]{2,1,0:T(8,128)(2,1)S(1)}, bf16[9,16,256]{2,1,0:T(8,128)(2,1)S(1)}, u32[]{:S(2)}, u32[]{:S(2)}) collective-permute-start(bf16[9,16,256]{2,1,0:T(8,128)(2,1)S(1)} %in_sum_3.1.refs_0_), channel_id=1, source_target_pairs={{0,16},{4,12},{8,24},{12,4},{16,0},{20,28},{24,8},{28,20},{1,17},{... | collective-permute-start | bytes 221192 | tf_op jit(solution)/shard_map/ppermute | solution.py:944
  212.4 4.4 %collective-permute-start.38 = (bf16[9,16,256]{2,1,0:T(8,128)(2,1)S(1)}, bf16[9,16,256]{2,1,0:T(8,128)(2,1)S(1)}, u32[]{:S(2)}, u32[]{:S(2)}) collective-permute-start(bf16[9,16,256]{2,1,0:T(8,128)(2,1)S(1)} %in_sum_3.1.refs_0_), channel_id=1, source_target_pairs={{0,8},{4,20},{8,0},{12,28},{16,24},{20,4},{24,16},{28,12},{1,9},{5... | collective-permute-start | bytes 221192 | tf_op jit(solution)/shard_map/ppermute | solution.py:944
  214.1 5.1 %collective-permute-start.43 = (bf16[9,16,512]{2,1,0:T(8,128)(2,1)S(1)}, bf16[9,16,512]{2,1,0:T(8,128)(2,1)S(1)}, u32[]{:S(2)}, u32[]{:S(2)}) collective-permute-start(bf16[9,16,512]{2,1,0:T(8,128)(2,1)S(1)} %collective-permute-done.41.refs_1_), channel_id=1, source_target_pairs={{0,8},{4,20},{8,0},{12,28},{16,24},{20,4},{24,16},{28,12},{1,9},{5... | collective-permute-start | bytes 442376 | tf_op jit(solution)/shard_map/ppermute | solution.py:944
  219.3 7.7 %collective-permute-start.44 = (bf16[4,9,16,512]{3,2,1,0:T(8,128)(2,1)S(1)}, bf16[4,9,16,512]{3,2,1,0:T(8,128)(2,1)S(1)}, u32[]{:S(2)}, u32[]{:S(2)}) collective-permute-start(bf16[4,9,16,512]{3,2,1,0:T(8,128)(2,1)S(1)} %mid_stack.1.mine), channel_id=1, source_target_pairs={{0,4},{4,0},{8,12},{12,8},{16,20},{20,16},{24,28},{28,24},{1,5},{5... | collective-permute-start | bytes 1769480 | tf_op jit(solution)/shard_map/ppermute | solution.py:937
  219.9 4.4 %collective-permute-start.39 = (bf16[9,16,256]{2,1,0:T(8,128)(2,1)S(1)}, bf16[9,16,256]{2,1,0:T(8,128)(2,1)S(1)}, u32[]{:S(2)}, u32[]{:S(2)}) collective-permute-start(bf16[9,16,256]{2,1,0:T(8,128)(2,1)S(1)} %collective-permute-done.37.refs_1_.refs_4_), channel_id=1, source_target_pairs={{0,8},{4,20},{8,0},{12,28},{16,24},{20,4},{24,16},{28,12},{1,9},{5... | collective-permute-start | bytes 221192 | tf_op jit(solution)/shard_map/ppermute | solution.py:944
  224.2 1.6 collective-permute-start.40

commit v2 on v1

--- a/solution.py
+++ b/solution.py
@@ -161,15 +161,6 @@
     return (c == (r % rows) * MEL + r // rows).astype(BF)
 
 
-def lanes(vector):
-    n = vector.shape[1] // 128
-    return jnp.concatenate([vector[:, 128 * i : 128 * (i + 1)] for i in range(n)], axis=0)
-
-
-def unlanes(rows):
-    return jnp.concatenate([rows[i : i + 1] for i in range(rows.shape[0])], axis=1)
-
-
 def misc_row(*scalars):
     lane = lax.broadcasted_iota(jnp.int32, (1, 128), 1)
     row = jnp.zeros((1, 128), F32)
@@ -187,11 +178,8 @@
     return jnp.sum(x, axis=0, keepdims=True)
 
 
-def payload(rows, *parts):
-    have = sum(r.shape[0] for r in parts)
-    if have < rows:
-        parts = (*parts, jnp.zeros((rows - have, 128), F32))
-    return jnp.concatenate(parts, axis=0)
+def payload(*parts):
+    return jnp.concatenate(parts, axis=1)
 
 
 def fan_kernel(pay, *rest):
@@ -206,13 +194,8 @@
 
 
 def total_of(g, ref):
-    n = g.cm // 128
-    block = jnp.sum(ref[:, : 2 * n, :], axis=0)
-    return unlanes(block[:n]), unlanes(block[n:])
-
-
-def misc_of(g, ref):
-    return jnp.sum(ref[:, 2 * (g.cm // 128), :], axis=0, keepdims=True)
+    row = jnp.sum(ref[...], axis=0)
+    return row[:, : g.cm], row[:, g.cm : 2 * g.cm], row[:, 2 * g.cm :]
 
 
 def side_by_side(x3, m, low, c, first, last):
@@ -408,7 +391,7 @@
     row = misc_row(
         frame_total.astype(F32), pair_total.astype(F32), jnp.sum(square, axis=1, keepdims=True)
     )
-    pay[...] = payload(16, lanes(one), lanes(two), row, gains[...])
+    pay[...] = payload(one, two, row, *[gains[i : i + 1] for i in range(4)])
 
 
 def first(g, lens, gains, maps, w):
@@ -416,7 +399,7 @@
     out = [
         arr((MEL, g.win, g.cm), F32),
         arr((MEL, g.win, 3 * g.ci_all), BF),
-        arr((16, 128), F32),
+        arr((1, 2 * g.cm + 5 * 128), F32),
     ]
     args = [lens, gains, *keep_near(w, maps)]
     ins = [SMEM] + [VMEM] * 3
@@ -437,14 +420,13 @@
     here = Here(g, lens)
     c = g.cm
     valid, own = row_masks(g, here, c)
-    one, two = total_of(g, got)
-    misc = misc_of(g, got)
+    one, two, rest = total_of(g, got)
+    misc = rest[:, :128]
     count = MEL * pick(misc, 0) / g.nch
     pairs = (MEL // 2) * pick(misc, 1) / g.nch
-    at = 2 * (c // 128) + 1
+    at = [2 * c + 128 * (1 + i) for i in range(4)]
     vectors = [
-        jnp.concatenate([got[zz, at + i : at + i + 1, : g.co] for zz in range(g.nch)], axis=1)
-        for i in range(4)
+        jnp.concatenate([got[zz, :, i : i + g.co] for zz in range(g.nch)], axis=1) for i in at
     ]
     mean = one / count
     inverse = lax.rsqrt(two / count - mean * mean + 1e-05)
@@ -469,8 +451,8 @@
     for m in range(MEL):
         square = activate(m, square)
     one, two = convolve_sums(g, here, x3, w, pre, True)
-    pay[...] = payload(8, lanes(one), lanes(two))
-    misc_out[...] = payload(8, misc_row(jnp.sum(square, axis=1, keepdims=True)))
+    pay[...] = payload(one, two)
+    misc_out[...] = misc_row(jnp.sum(square, axis=1, keepdims=True))
 
 
 def second(g, lens, got, pre1, w):
@@ -479,8 +461,8 @@
         arr((MEL, g.win, g.cm), F32),
         arr((MEL, g.win, 3 * g.cm), BF),
         arr((TABLE, g.cm), F32),
-        arr((8, 128), F32),
-        arr((8, 128), F32),
+        arr((1, 2 * g.cm), F32),
+        arr((1, 128), F32),
     ]
     args = [lens, *keep_near(got, pre1, w)]
     flops = 2 * 9 * MEL * g.win * g.cm * g.cm
@@ -505,7 +487,7 @@
         block = dot(spread, cells, ((1,), (1,)))
         grads[:, pl.ds(aligned(64 * j), 64), :] = block.reshape(MEL // 2, 64, c)
 
-    one, two = total_of(g, got)
+    one, two, _ = total_of(g, got)
     old = old_ref[...]
     count = old[COUNT : COUNT + 1]
     mean = one / count
@@ -514,40 +496,56 @@
     table[...] = jnp.concatenate([old[:MEAN2], mean, inverse] + [wide] * (TABLE - 11), axis=0)
     half_gamma, half_beta = 0.5 * old[GAMMA2 : GAMMA2 + 1], 0.5 * old[BETA2 : BETA2 + 1]
     less = -mean * inverse
-    valid, own = row_masks(g, here, c)
-    r = lax.broadcasted_iota(jnp.int32, (g.win, 128), 0) + here.start
-    share = widen(jnp.where(here.length - r // 2 * 2 >= 2, 0.25, 0.5), c)
-    half_share = 0.5 * share * valid
-    window = pl.ds(aligned(here.qoff), g.win)
-    out_row = lax.broadcasted_iota(jnp.int32, (g.win, 2 * g.seg), 0) - here.off
-    out_cell = lax.broadcasted_iota(jnp.int32, (g.win, 2 * g.seg), 1)
-    first_cell = jnp.where(out_row >= 0, out_row // 2 * 4, -MEL)
+    side = g.win - g.seg
+    segment = pl.ds(aligned(here.off), g.seg)
+    sides = [
+        aligned(jnp.where(16 * j < here.off, 16 * j, 16 * j + g.seg)) for j in range(side // 16)
+    ]
+
+    def weights(rows, start, width):
+        frame = lax.broadcasted_iota(jnp.int32, (rows, 128), 0) + (here.start + start)
+        valid = (frame < here.length).astype(F32)
+        share = jnp.where(here.length - frame // 2 * 2 >= 2, 0.25, 0.5)
+        return widen(0.5 * share * valid, width), widen(valid, width)
+
+    half_share, valid = weights(g.seg, here.off, c)
+    side_shares = [weights(16, start, c)[0] for start in sides]
+    out_row = lax.broadcasted_iota(jnp.int32, (g.seg, 2 * g.seg), 0)
+    out_cell = lax.broadcasted_iota(jnp.int32, (g.seg, 2 * g.seg), 1)
+    first_cell = out_row // 2 * 4
+    frame = out_row + (here.start + here.off)
+    out_share = jnp.where(here.length - frame // 2 * 2 >= 2, 0.25, 0.5)
     total[...] = jnp.zeros(total.shape, F32)
+
+    def bent(pre):
+        scaled = pre * inverse + less
+        half = scaled * half_gamma + half_beta
+        bend = jnp.tanh(half)
+        twice = 1.0 + bend
+        whole = half * twice
+        return scaled, whole, twice + whole * (1.0 - bend)
 
     def step(k, sums):
         beta_sum, gamma_sum, square = sums
-        given = grads[k, window, :] * half_share
+        given = grads[k, pl.ds(aligned(here.qoff + here.off), g.seg), :] * half_share
         pair = None
         for i in range(2):
             m = 2 * k + i
-            scaled = pre2[m] * inverse + less
-            half = scaled * half_gamma + half_beta
-            bend = jnp.tanh(half)
-            twice = 1.0 + bend
-            whole = half * twice
-            act = whole * own
+            scaled, whole, slope = bent(pre2[m, segment, :])
+            act = whole * valid
             square = square + sum_rows(act * act)
-            local = given * (twice + whole * (1.0 - bend))
-            local_ref[m] = local
-            kept = local * own
-            beta_sum = beta_sum + sum_rows(kept)
-            gamma_sum = gamma_sum + sum_rows(kept * scaled)
+            local = given * slope
+            local_ref[m, segment, :] = local
+            beta_sum = beta_sum + sum_rows(local)
+            gamma_sum = gamma_sum + sum_rows(local * scaled)
             pair = act if pair is None else pair + act
-        pair = pair * share
-        high = pair.astype(BF)
-        low = (pair - high.astype(F32)).astype(BF)
-        gather = (out_cell == first_cell + k).astype(BF)
-        total[...] += dot(high, gather, ((0,), (0,))) + dot(low, gather, ((0,), (0,)))
+            for start, side_share in zip(sides, side_shares, strict=True):
+                rows = pl.ds(start, 16)
+                _, _, slope = bent(pre2[m, rows, :])
+                given_side = grads[k, pl.ds(aligned(here.qoff + start), 16), :] * side_share
+                local_ref[m, rows, :] = given_side * slope
+        gather = jnp.where(out_cell == first_cell + k, out_share, 0.0).astype(BF)
+        total[...] += dot(pair.astype(BF), gather, ((0,), (0,)))
         return beta_sum, gamma_sum, square
 
     zero = jnp.zeros((1, c), F32)
@@ -557,9 +555,8 @@
     for k in range(n):
         outs[k][...] = flat[pl.ds(aligned((here.z ^ k) * g.co), g.co), :]
     pooled_square = sum_rows(jnp.sum(pooled * pooled, axis=1, keepdims=True))
-    block = payload(8, lanes(beta_sum), lanes(gamma_sum))
-    pay[...] = jnp.broadcast_to(block[None], pay.shape)
-    misc_out[...] = payload(8, misc_row(jnp.sum(square, axis=1, keepdims=True), pooled_square))
+    pay[...] = jnp.broadcast_to(payload(beta_sum, gamma_sum)[None], pay.shape)
+    misc_out[...] = misc_row(jnp.sum(square, axis=1, keepdims=True), pooled_square)
 
 
 def pool(g, lens, got, table, pre2, cs):
@@ -568,8 +565,8 @@
     out = [arr((g.co, 2 * g.seg), BF)] * n + [
         arr((MEL, g.win, g.cm), F32),
         arr((TABLE, g.cm), F32),
-        arr((g.ndev, 8, 128), F32),
-        arr((8, 128), F32),
+        arr((g.ndev, 1, 2 * g.cm), F32),
+        arr((1, 128), F32),
     ]
     scratch = [
         pltpu.VMEM((g.cm, g.cwin * 2), BF),
@@ -583,21 +580,21 @@
     return out[:n], *out[n:]
 
 
-def terms_kernel(g, depth, norm, lens, got, table, pre, local, x3, after, *rest):
-    grad, sums, roots, terms, give = rest
+def terms_kernel(g, depth, norm, lens, got, table, pre, local, x3, after, *refs):
+    grad, sums, roots, terms, give = refs
     here = Here(g, lens)
     c = g.cm
     valid, _ = row_masks(g, here, c)
-    beta_sum, gamma_sum = total_of(g, got)
+    beta_sum, gamma_sum, rest = total_of(g, got)
     t = table[...]
     mean, inverse, gamma = (t[i : i + 1] for i in norm)
     count = t[COUNT : COUNT + 1]
     sums[...] = jnp.concatenate([beta_sum, gamma_sum] + [jnp.zeros((1, c), F32)] * 6, axis=0)
-    if got.shape[1] > 8:
-        at = 2 * (c // 128)
-        square1 = pick(jnp.sum(got[:, at, :], axis=0, keepdims=True), 0)
-        later = jnp.sum(got[:, at + 1, :], axis=0, keepdims=True)
-        tops = misc_row(pick(t[SQ0 : SQ0 + 1, :128], 0), square1, pick(later, 0), pick(later, 1))
+    if rest.shape[1]:
+        second, third = rest[:, :128], rest[:, 128:]
+        tops = misc_row(
+            pick(t[SQ0 : SQ0 + 1, :128], 0), pick(second, 0), pick(third, 0), pick(third, 1)
+        )
         lane = lax.broadcasted_iota(jnp.int32, (1, 128), 1)
         cells, pairs = count[:, :128], t[PAIRS : PAIRS + 1, :128]
         under = jnp.where(lane == 0, cells * g.ci_all, jnp.where(lane == 3, pairs * c, cells * c))
@@ -679,13 +676,12 @@
 
     zero = jnp.zeros((1, c), F32)
     beta_sum, gamma_sum = convolve(g3, w, local1, True, finish, (zero, zero), True)
-    squares = jnp.concatenate([misc2[0:1], misc3[0:1]], axis=0)
-    pay[...] = payload(16, lanes(beta_sum), lanes(gamma_sum), squares)
+    pay[...] = payload(beta_sum, gamma_sum, misc2[...], misc3[...])
 
 
 def back(g, lens, table, grad, pre1, w, misc2, misc3, after):
     body = functools.partial(back_kernel, g)
-    out = [arr((MEL, g.win, g.cm), F32), arr((16, 128), F32)]
+    out = [arr((MEL, g.win, g.cm), F32), arr((1, 2 * g.cm + 2 * 128), F32)]
     scratch = [pltpu.VMEM((MEL, g.win, 3 * g.cm), BF)]
     args = [lens, *keep_near(table, grad, pre1, w, misc2, misc3), after]
     flops = 2 * 9 * MEL * g.win * g.cm * g.cm

time: 229 us -> 225 us (0.983)
  starting transfers between devices: 51.1 us -> 47.2 us
  waiting for transfers between devices: 60.1 us -> 63.1 us
  blocking collectives: 48.5 us -> 46.2 us
    all_to_all x4, blocking collectives: 48.5 us -> 46.2 us  [everyone(): return lax.all_to_all(x, ('dp', 'chan'), 0, 0)]
    ppermute x16, starting transfers between devices: 23 us -> 20.7 us  [chan(): return lax.ppermute(x, 'chan', [(i, i ^ k) for i in range(self.g.nch)])]
  transfers between devices with their start and end apart: 46 -> 46, of which waited for: 21 -> 22; matrix products, arithmetic and copies ran while one was open for 1% -> 1% of each run, Pallas kernels for 17% -> 18%
where the time goes in v2:
time: 225 us; the launch traced here: 224 us
  Pallas kernels  63.4 us (28%)
  waiting for transfers between devices  63.1 us (28%)
  starting transfers between devices  47.2 us (21%)
  blocking collectives  46.2 us (21%)
  local copies, waits for them, and re-layouts  3.45 us (2%)
    pallas_call x23, Pallas kernels, call(): pl.pallas_call(body, out_shape=[pltpu.VMEM(o.shape, o.dtype) if isinstanc...  57 us
    all_to_all x4, blocking collectives, everyone(): return lax.all_to_all(x, ('dp', 'chan'), 0, 0)  46.2 us
    ppermute x16, waiting for transfers between devices, chan(): return lax.ppermute(x, 'chan', [(i, i ^ k) for i in range(self.g.nch)])  33.6 us
    ppermute x17, waiting for transfers between devices, plane(): lax.ppermute(x, 'dp', [(i, i ^ 2 * g.mask(i & 1, turn)) for i in range(g....  27.1 us
    ppermute x16, starting transfers between devices, chan(): return lax.ppermute(x, 'chan', [(i, i ^ k) for i in range(self.g.nch)])  20.7 us
    ppermute x17, starting transfers between devices, plane(): lax.ppermute(x, 'dp', [(i, i ^ 2 * g.mask(i & 1, turn)) for i in range(g....  17.6 us
    all_to_all x1, starting transfers between devices, body(): maps = lax.all_to_all(release_far([pieces_in], cells), 'chan', 0, 0)  6.3 us
  transfers between devices with their start and end apart: 46, of which 22 were waited for; matrix products, arithmetic and copies ran while one was open for 1% of the time, Pallas kernels for 18%

profile of v2, /device:TPU:0, one launch (start us, length us, event | category | flops | bytes accessed | tf_op | source)
XLA Modules:
  0.0 224.4 jit_solution(10651990249967726443)
XLA Ops:
  0.6 1.0 cut_weights.1.after
  1.6 3.1 %collective-permute-start = (bf16[9,16,768]{2,1,0:T(8,128)(2,1)S(1)}, bf16[9,16,768]{2,1,0:T(8,128)(2,1)S(1)}, u32[]{:S(2)}, u32[]{:S(2)}) collective-permute-start(bf16[9,16,768]{2,1,0:T(8,128)(2,1)S(1)} %cut_weights.1.after), channel_id=1, source_target_pairs={{0,1},{1,0},{2,3},{3,2},{4,5},{5,4},{6,7},{7,6},{8,9},{9,8},{10,11... | collective-permute-start | bytes 663560 | tf_op jit(solution)/shard_map/ppermute | solution.py:943
  4.7 2.6 %collective-permute-start.1 = (bf16[9,16,768]{2,1,0:T(8,128)(2,1)S(1)}, bf16[9,16,768]{2,1,0:T(8,128)(2,1)S(1)}, u32[]{:S(2)}, u32[]{:S(2)}) collective-permute-start(bf16[9,16,768]{2,1,0:T(8,128)(2,1)S(1)} %cut_weights.1.after), channel_id=1, source_target_pairs={{0,2},{1,3},{2,0},{3,1},{4,6},{5,7},{6,4},{7,5},{8,10},{9,11},{10,... | collective-permute-start | bytes 663560 | tf_op jit(solution)/shard_map/ppermute | solution.py:943
  7.3 2.0 cut_maps.1.after.refs_1_
  9.3 1.1 copy-done
  10.5 1.1 cut_cotangent.1
  12.3 1.8 collective-permute-done.rest_0_
  14.1 9.3 %collective-permute-done.1.rest_1_ = bf16[9,16,768]{2,1,0:T(8,128)(2,1)S(1)} collective-permute-done((bf16[9,16,768]{2,1,0:T(8,128)(2,1)S(1)}, bf16[9,16,768]{2,1,0:T(8,128)(2,1)S(1)}, u32[]{:S(2)}, u32[]{:S(2)}) %collective-permute-start.1) | collective-permute-done | bytes 221216 | tf_op jit(solution)/shard_map/ppermute | solution.py:943
  23.5 0.7 sort_pieces.1
  24.2 6.3 %all-to-all-start = ((bf16[4,64,1664]{2,1,0:T(8,128)(2,1)}), bf16[4,64,1664]{2,1,0:T(8,128)(2,1)S(1)}, u32[]{:S(2)}, u32[]{:S(2)}) async-start(bf16[4,64,1664]{2,1,0:T(8,128)(2,1)} %release_far.1), calls=%async_computation | async-start | bytes 1703936 | tf_op jit(solution)/shard_map/all_to_all | solution.py:993
  30.5 1.5 collective-permute-start.3
  32.6 1.5 collective-permute-start.11
  34.6 4.6 %collective-permute-done.3.rest_1_ = bf16[3,9,16,256]{3,2,1,0:T(8,128)(2,1)} collective-permute-done((bf16[3,9,16,256]{3,2,1,0:T(8,128)(2,1)}, bf16[3,9,16,256]{3,2,1,0:T(8,128)(2,1)}, u32[]{:S(2)}, u32[]{:S(2)}) %collective-permute-start.3) | collective-permute-done | bytes 221216 | tf_op jit(solution)/shard_map/ppermute | solution.py:940
  39.2 1.5 collective-permute-start.5
  40.7 5.4 %collective-permute-done.4.rest_2_ = bf16[3,9,16,256]{3,2,1,0:T(8,128)(2,1)} collective-permute-done((bf16[3,9,16,256]{3,2,1,0:T(8,128)(2,1)}, bf16[3,9,16,256]{3,2,1,0:T(8,128)(2,1)}, u32[]{:S(2)}, u32[]{:S(2)}) %collective-permute-start.4) | collective-permute-done | bytes 221216 | tf_op jit(solution)/shard_map/ppermute | solution.py:940
  46.1 2.3 %collective-permute-done.5.rest_3_ = bf16[3,9,16,256]{3,2,1,0:T(8,128)(2,1)} collective-permute-done((bf16[3,9,16,256]{3,2,1,0:T(8,128)(2,1)}, bf16[3,9,16,256]{3,2,1,0:T(8,128)(2,1)}, u32[]{:S(2)}, u32[]{:S(2)}) %collective-permute-start.5) | collective-permute-done | bytes 221216 | tf_op jit(solution)/shard_map/ppermute | solution.py:940
  48.4 1.3 collective-permute-start.8
  49.8 1.1 all-to-all-done.maps.refs_0_
  50.9 1.5 collective-permute-start.12
  52.5 1.7 join_in.1.w
  54.2 5.1 %first_conv.1 = (f32[8,208,512]{2,1,0:T(8,128)S(1)}, bf16[8,208,768]{2,1,0:T(8,128)(2,1)S(1)}, f32[1,1664]{1,0:T(1,128)S(1)}) custom-call(s32[2]{0:T(128)S(1)} %copy-done.7, f32[4,128]{1,0:T(4,128)S(1)} %pad_maximum_fusion.gains, bf16[9,512,256]{2,1,0:T(8,128)(2,1)S(1)} %join_in.1.w, bf16[4,64,1664]{2,1,0:T(8,128)(2,1)S(1)} %all-to-all-done.maps.refs_0_), custom_call_target="tpu_custom_call" | custom-call | flops 3925868544 | bytes 10485760 | tf_op jit(solution)/shard_map/first_conv/pallas_call | solution.py:90
  59.4 14.0 %all_to_all.25.refs_0_.got = f32[32,1,1664]{2,1,0:T(1,128)S(1)} all-to-all(f32[32,1,1664]{2,1,0:T(1,128)S(1)} %fan.3), channel_id=1, replica_groups=mesh['dp'=8,'chan'=4] {'dp','chan'}, dimensions={0} | all-to-all | bytes 425984 | tf_op jit(solution)/shard_map/all_to_all | solution.py:968
  75.2 1.3 collective-permute-start.18
  76.5 2.3 %collective-permute-start.19 = (bf16[128,512]{1,0:T(8,128)(2,1)S(1)}, bf16[128,512]{1,0:T(8,128)(2,1)S(1)}, u32[]{:S(2)}, u32[]{:S(2)}) collective-permute-start(bf16[128,512]{1,0:T(8,128)(2,1)S(1)} %get-tuple-element.93), channel_id=1, source_target_pairs={{0,3},{1,2},{2,1},{3,0},{4,7},{5,6},{6,5},{7,4},{8,11},{9,10},{10,... | collective-permute-start | bytes 393224 | tf_op jit(solution)/shard_map/ppermute | solution.py:943
  79.2 9.5 %second_conv.1 = (f32[8,208,512]{2,1,0:T(8,128)S(1)}, bf16[8,208,1536]{2,1,0:T(8,128)(2,1)S(1)}, f32[16,512]{1,0:T(8,128)S(1)}, f32[1,1024]{1,0:T(1,128)S(1)}, f32[1,128]{1,0:T(1,128)S(1)}) custom-call(s32[2]{0:T(128)S(1)} %copy-done.7, f32[32,1,1664]{2,1,0:T(1,128)S(1)} %all_to_all.25.refs_0_.got, f32[8,208,512]{2,1,0:T(8,128)S(1)} %get-tuple-element.82.pre1.pre, ...), custom_call_target="tpu_custom_call" | custom-call | flops 7851737088 | bytes 17825792 | tf_op jit(solution)/shard_map/second_conv/pallas_call | solution.py:90
  88.8 11.0 %all_to_all.26.got = f32[32,1,1024]{2,1,0:T(1,128)S(1)} all-to-all(f32[32,1,1024]{2,1,0:T(1,128)S(1)} %fan.4), channel_id=1, replica_groups=mesh['dp'=8,'chan'=4] {'dp','chan'}, dimensions={0} | all-to-all | bytes 262144 | tf_op jit(solution)/shard_map/all_to_all | solution.py:968
  99.7 5.2 %pool.1 = (bf16[128,384]{1,0:T(8,128)(2,1)S(1)}, bf16[128,384]{1,0:T(8,128)(2,1)S(1)}, bf16[128,384]{1,0:T(8,128)(2,1)S(1)}, bf16[128,384]{1,0:T(8,128)(2,1)S(1)...) custom-call(s32[2]{0:T(128)S(1)} %copy-done.7, ...), custom_call_target="tpu_custom_call" | custom-call | flops 4000000000 | bytes 8388608 | tf_op jit(solution)/shard_map/pool/pallas_call | solution.py:90
  105.0 10.1 %all_to_all.27.refs_0_.got.after = f32[32,1,1024]{2,1,0:T(1,128)S(1)} all-to-all(f32[32,1,1024]{2,1,0:T(1,128)S(1)} %get-tuple-element.97), channel_id=1, replica_groups=mesh['dp'=8,'chan'=4] {'dp','chan'}, dimensions={0} | all-to-all | bytes 262144 | tf_op jit(solution)/shard_map/all_to_all | solution.py:968
  115.1 9.5 %weight_mid_terms.1 = (bf16[8,208,512]{2,1,0:T(8,128)(2,1)S(1)}, f32[8,512]{1,0:T(8,128)S(1)}, f32[8,128]{1,0:T(8,128)}, bf16[2,4,4,9,16,512]{5,4,3,2,1,0:T(8,128)(2,1)S(1)}, bf16[4,4,9,16,512]{4,3,2,1,0:T(8,128)(2,1)S(1)}) custom-call(s32[2]{0:T(128)S(1)} %copy-done.7, f32[32,1,1024]{2,1,0:T(1,128)S(1)} %all_to_all.27.refs_0_.got.after, ...), custom_call_target="tpu_custom_call" | custom-call | flops 7851737088 | bytes 15728640 | tf_op jit(solution)/shard_map/weight_mid_terms/pallas_call | solution.py:90
  124.9 1.5 collective-permute-start.21
  126.4 2.7 %collective-permute-start.22 = (bf16[128,384]{1,0:T(8,128)(2,1)S(1)}, bf16[128,384]{1,0:T(8,128)(2,1)S(1)}, u32[]{:S(2)}, u32[]{:S(2)}) collective-permute-start(bf16[128,384]{1,0:T(8,128)(2,1)S(1)} %get-tuple-element.105), channel_id=1, source_target_pairs={{0,3},{1,2},{2,1},{3,0},{4,7},{5,6},{6,5},{7,4},{8,11},{9,10},{10,... | collective-permute-start | bytes 294920 | tf_op jit(solution)/shard_map/ppermute | solution.py:943
  129.7 0.8 collective-permute-start.24
  130.5 9.3 %second_back.1 = (f32[8,208,512]{2,1,0:T(8,128)S(1)}, f32[1,1280]{1,0:T(1,128)S(1)}) custom-call(s32[2]{0:T(128)S(1)} %copy-done.7, f32[16,512]{1,0:T(8,128)S(1)} %get-tuple-element.107.table, bf16[8,208,512]{2,1,0:T(8,128)(2,1)S(1)} %get-tuple-element.110.grad, f32[8,208,512]{2,1,0:T(8,128)S(1)} %get-tuple-element.82.pre1.pre, ...), custom_call_target="tpu_custom_call" | custom-call | flops 7851737088 | bytes 20971520 | tf_op jit(solution)/shard_map/second_back/pallas_call | solution.py:90
  139.9 11.1 %all_to_all.28.got.after.refs_0_.rest_2_ = f32[32,1,1280]{2,1,0:T(1,128)S(1)} all-to-all(f32[32,1,1280]{2,1,0:T(1,128)S(1)} %fan.5), channel_id=1, replica_groups=mesh['dp'=8,'chan'=4] {'dp','chan'}, dimensions={0} | all-to-all | bytes 327680 | tf_op jit(solution)/shard_map/all_to_all | solution.py:968
  151.0 5.8 %weight_in_terms.1 = (bf16[8,208,512]{2,1,0:T(8,128)(2,1)S(1)}, f32[8,512]{1,0:T(8,128)S(1)}, f32[8,128]{1,0:T(8,128)S(1)}, bf16[2,4,4,9,16,256]{5,4,3,2,1,0:T(8,128)(2,1)S(1)}, bf16[4,4,9,16,256]{4,3,2,1,0:T(8,128)(2,1)S(1)}) custom-call(s32[2]{0:T(128)S(1)} %copy-done.7, f32[32,1,1280]{2,1,0:T(1,128)S(1)} %all_to_all.28.got.after.refs_0_.rest_2_, ...), custom_call_target="tpu_custom_call" | custom-call | flops 3925868544 | bytes 15728640 | tf_op jit(solution)/shard_map/weight_in_terms/pallas_call | solution.py:90
  157.0 0.9 collective-permute-start.31
  158.4 5.6 %spectra_back.1 = (bf16[64,1536]{1,0:T(8,128)(2,1)S(1)}, bf16[64,1536]{1,0:T(8,128)(2,1)S(1)}, bf16[64,1536]{1,0:T(8,128)(2,1)S(1)}, bf16[64,1536]{1,0:T(8,128)(2,1)S(1)}) custom-call(s32[2]{0:T(128)S(1)} %copy-done.7, bf16[8,208,512]{2,1,0:T(8,128)(2,1)S(1)} %get-tuple-element.119.grad.after, bf16[8,208,512]{2,1,0:T(8,128)(2,1)S(1)} %get-tuple-element.119.grad.after, ...), custom_call_target="tpu_custom_call" | custom-call | flops 3925868544 | bytes 5242880 | tf_op jit(solution)/shard_map/spectra_back/pallas_call | solution.py:90
  164.4 1.6 collective-permute-start.29
  166.2 1.6 collective-permute-start.26
  167.8 5.4 %collective-permute-done.31.rest_2_ = bf16[4,9,16,512]{3,2,1,0:T(8,128)(2,1)S(1)} collective-permute-done((bf16[4,9,16,512]{3,2,1,0:T(8,128)(2,1)S(1)}, bf16[4,9,16,512]{3,2,1,0:T(8,128)(2,1)S(1)}, u32[]{:S(2)}, u32[]{:S(2)}) %collective-permute-start.31) | collective-permute-done | bytes 589856 | tf_op jit(solution)/shard_map/ppermute | solution.py:940
  173.7 1.7 collective-permute-done.25.rest_1_
  175.5 2.2 collective-permute-done.26.rest_2_
  177.6 1.5 collective-permute-done.29.got
  179.3 0.9 collective-permute-start.32
  180.2 1.3 collective-permute-start.27
  181.5 0.8 place_pooled.1
  182.3 1.3 collective-permute-done.33.got
  183.7 5.5 %collective-permute-done.27.rest_3_.rest_1_ = bf16[64,1536]{1,0:T(8,128)(2,1)S(1)} collective-permute-done((bf16[64,1536]{1,0:T(8,128)(2,1)S(1)}, bf16[64,1536]{1,0:T(8,128)(2,1)S(1)}, u32[]{:S(2)}, u32[]{:S(2)}) %collective-permute-start.27) | collective-permute-done | bytes 196640 | tf_op jit(solution)/shard_map/ppermute | solution.py:943
  189.2 2.6 %collective-permute-start.34 = (bf16[2,9,16,256]{3,2,1,0:T(8,128)(2,1)S(1)}, bf16[2,9,16,256]{3,2,1,0:T(8,128)(2,1)S(1)}, u32[]{:S(2)}, u32[]{:S(2)}) collective-permute-start(bf16[2,9,16,256]{3,2,1,0:T(8,128)(2,1)S(1)} %get-tuple-element.139), channel_id=1, source_target_pairs={{0,1},{1,0},{2,3},{3,2},{4,5},{5,4},{6,7},{7,6},{8,9},{9,8},{10,11... | collective-permute-start | bytes 442376 | tf_op jit(solution)/shard_map/ppermute | solution.py:943
  192.1 1.3 place_spectra.1
  193.4 3.7 %collective-permute-done.34.got = bf16[2,9,16,256]{3,2,1,0:T(8,128)(2,1)S(1)} collective-permute-done((bf16[2,9,16,256]{3,2,1,0:T(8,128)(2,1)S(1)}, bf16[2,9,16,256]{3,2,1,0:T(8,128)(2,1)S(1)}, u32[]{:S(2)}, u32[]{:S(2)}) %collective-permute-start.34) | collective-permute-done | bytes 147488 | tf_op jit(solution)/shard_map/ppermute | solution.py:943
  197.1 4.1 %collective-permute-done.36.got = bf16[1,9,16,512]{3,2,1,0:T(8,128)(2,1)S(1)} collective-permute-done((bf16[1,9,16,512]{3,2,1,0:T(8,128)(2,1)S(1)}, bf16[1,9,16,512]{3,2,1,0:T(8,128)(2,1)S(1)}, u32[]{:S(2)}, u32[]{:S(2)}) %collective-permute-start.36) | collective-permute-done | bytes 147488 | tf_op jit(solution)/shard_map/ppermute | solution.py:943
  201.8 1.3 collective-permute-start.42
  203.1 4.0 %collective-permute-done.35.got = bf16[1,9,16,256]{3,2,1,0:T(8,128)(2,1)S(1)} collective-permute-done((bf16[1,9,16,256]{3,2,1,0:T(8,128)(2,1)S(1)}, bf16[1,9,16,256]{3,2,1,0:T(8,128)(2,1)S(1)}, u32[]{:S(2)}, u32[]{:S(2)}) %collective-permute-start.35) | collective-permute-done | bytes 73760 | tf_op jit(solution)/shard_map/ppermute | solution.py:943
  207.1 1.6 collective-permute-start.37
  208.7 1.2 collective-permute-start.38
  209.9 0.8 collective-permute-start.43
  210.7 1.6 collective-permute-done.37.refs_1_.refs_4_
  212.4 0.7 collective-permute-done.38.refs_2_.refs_5_
  213.1 2.0 collective-permute-done.43.refs_3_
  215.7 0.8 collective-permute-start.39
  216.5 3.6 %collective-permute-done.39.refs_3_ = bf16[9,16,256]{2,1,0:T(8,128)(2,1)S(1)} collective-permute-done((bf16[9,16,256]{2,1,0:T(8,128)(2,1)S(1)}, bf16[9,16,256]{2,1,0:T(8,128)(2,1)S(1)}, u32[]{:S(2)}, u32[]{:S(2)}) %collective-permute-start.39) | collective-permute-done | bytes 73760 | tf_op jit(solution)/shard_map/ppermute | solution.py:940
  221.8 1.1 in_out.1
  222.9 1.6 mid_out.1
  (101 shorter events, 10.3 us)
Async XLA Ops:
  1.6 12.5 %collective-permute-start = (bf16[9,16,768]{2,1,0:T(8,128)(2,1)S(1)}, bf16[9,16,768]{2,1,0:T(8,128)(2,1)S(1)}, u32[]{:S(2)}, u32[]{:S(2)}) collective-permute-start(bf16[9,16,768]{2,1,0:T(8,128)(2,1)S(1)} %cut_weights.1.after), channel_id=1, source_target_pairs={{0,1},{1,0},{2,3},{3,2},{4,5},{5,4},{6,7},{7,6},{8,9},{9,8},{10,11... | collective-permute-start | bytes 663560 | tf_op jit(solution)/shard_map/ppermute | solution.py:943
  4.7 18.7 %collective-permute-start.1 = (bf16[9,16,768]{2,1,0:T(8,128)(2,1)S(1)}, bf16[9,16,768]{2,1,0:T(8,128)(2,1)S(1)}, u32[]{:S(2)}, u32[]{:S(2)}) collective-permute-start(bf16[9,16,768]{2,1,0:T(8,128)(2,1)S(1)} %cut_weights.1.after), channel_id=1, source_target_pairs={{0,2},{1,3},{2,0},{3,1},{4,6},{5,7},{6,4},{7,5},{8,10},{9,11},{10,... | collective-permute-start | bytes 663560 | tf_op jit(solution)/shard_map/ppermute | solution.py:943
  7.3 16.1 %collective-permute-start.2 = (bf16[9,16,768]{2,1,0:T(8,128)(2,1)S(1)}, bf16[9,16,768]{2,1,0:T(8,128)(2,1)S(1)}, u32[]{:S(2)}, u32[]{:S(2)}) collective-permute-start(bf16[9,16,768]{2,1,0:T(8,128)(2,1)S(1)} %cut_weights.1.after), channel_id=1, source_target_pairs={{0,3},{1,2},{2,1},{3,0},{4,7},{5,6},{6,5},{7,4},{8,11},{9,10},{10,... | collective-permute-start | bytes 663560 | tf_op jit(solution)/shard_map/ppermute | solution.py:943
  9.3 1.2 copy-start
  11.6 0.7 copy-start.5
  12.3 11.9 %copy-start.3 = (bf16[128,512]{1,0:T(8,128)(2,1)}, bf16[128,512]{1,0:T(8,128)(2,1)S(1)}, u32[]{:S(2)}) copy-start(bf16[128,512]{1,0:T(8,128)(2,1)S(1)} %get-tuple-element.89.refs_3_) | copy-start | bytes 393220
  24.2 28.2 %copy-start.8 = (f32[128]{0:T(128)S(1)}, f32[128]{0:T(128)}, u32[]{:S(2)}) copy-start(f32[128]{0:T(128)} %param.16) | copy-start | bytes 1540
  24.2 28.2 %copy-start.9 = (f32[128]{0:T(128)S(1)}, f32[128]{0:T(128)}, u32[]{:S(2)}) copy-start(f32[128]{0:T(128)} %param.15) | copy-start | bytes 1540
  24.2 28.2 %copy-start.10 = (f32[128]{0:T(128)S(1)}, f32[128]{0:T(128)}, u32[]{:S(2)}) copy-start(f32[128]{0:T(128)} %param.13) | copy-start | bytes 1540
  24.2 28.2 %copy-start.11 = (f32[128]{0:T(128)S(1)}, f32[128]{0:T(128)}, u32[]{:S(2)}) copy-start(f32[128]{0:T(128)} %param.12) | copy-start | bytes 1540
  24.2 28.3 %copy-start.2 = (bf16[9,128,256]{2,1,0:T(8,128)(2,1)S(1)}, bf16[9,128,256]{2,1,0:T(8,128)(2,1)}, u32[]{:S(2)}) copy-start(bf16[9,128,256]{2,1,0:T(8,128)(2,1)} %own.2) | copy-start | bytes 1769476
  24.2 26.7 %all-to-all-start = ((bf16[4,64,1664]{2,1,0:T(8,128)(2,1)}), bf16[4,64,1664]{2,1,0:T(8,128)(2,1)S(1)}, u32[]{:S(2)}, u32[]{:S(2)}) async-start(bf16[4,64,1664]{2,1,0:T(8,128)(2,1)} %release_far.1), calls=%async_computation | async-start | bytes 1703936 | tf_op jit(solution)/shard_map/all_to_all | solution.py:993
  30.5 8.7 %collective-permute-start.3 = (bf16[3,9,16,256]{3,2,1,0:T(8,128)(2,1)}, bf16[3,9,16,256]{3,2,1,0:T(8,128)(2,1)}, u32[]{:S(2)}, u32[]{:S(2)}) collective-permute-start(bf16[3,9,16,256]{3,2,1,0:T(8,128)(2,1)} %get-tuple-element.79.rest_0_.refs_0_), channel_id=1, source_target_pairs={{0,16},{4,12},{8,24},{12,4},{16,0},{20,28},{24,8},{28,20},{1,17},{... | collective-permute-start | bytes 663560 | tf_op jit(solution)/shard_map/ppermute | solution.py:940
  32.1 17.7 %collective-permute-start.10 = (bf16[3,9,16,512]{3,2,1,0:T(8,128)(2,1)S(1)}, bf16[3,9,16,512]{3,2,1,0:T(8,128)(2,1)S(1)}, u32[]{:S(2)}, u32[]{:S(2)}) collective-permute-start(bf16[3,9,16,512]{3,2,1,0:T(8,128)(2,1)S(1)} %get-tuple-element.81.refs_1_), channel_id=1, source_target_pairs={{0,16},{4,12},{8,24},{12,4},{16,0},{20,28},{24,8},{28,20},{1,17},{... | collective-permute-start | bytes 1327112 | tf_op jit(solution)/shard_map/ppermute | solution.py:940
  32.6 17.2 %collective-permute-start.11 = (bf16[3,9,16,512]{3,2,1,0:T(8,128)(2,1)S(1)}, bf16[3,9,16,512]{3,2,1,0:T(8,128)(2,1)S(1)}, u32[]{:S(2)}, u32[]{:S(2)}) collective-permute-start(bf16[3,9,16,512]{3,2,1,0:T(8,128)(2,1)S(1)} %get-tuple-element.81.refs_1_), channel_id=1, source_target_pairs={{0,8},{4,20},{8,0},{12,28},{16,24},{20,4},{24,16},{28,12},{1,9},{5... | collective-permute-start | bytes 1327112 | tf_op jit(solution)/shard_map/ppermute | solution.py:940
  34.1 12.0 %collective-permute-start.4 = (bf16[3,9,16,256]{3,2,1,0:T(8,128)(2,1)}, bf16[3,9,16,256]{3,2,1,0:T(8,128)(2,1)}, u32[]{:S(2)}, u32[]{:S(2)}) collective-permute-start(bf16[3,9,16,256]{3,2,1,0:T(8,128)(2,1)} %get-tuple-element.79.rest_0_.refs_0_), channel_id=1, source_target_pairs={{0,8},{4,20},{8,0},{12,28},{16,24},{20,4},{24,16},{28,12},{1,9},{5... | collective-permute-start | bytes 663560 | tf_op jit(solution)/shard_map/ppermute | solution.py:940
  39.2 9.3 %collective-permute-start.5 = (bf16[3,9,16,256]{3,2,1,0:T(8,128)(2,1)}, bf16[3,9,16,256]{3,2,1,0:T(8,128)(2,1)}, u32[]{:S(2)}, u32[]{:S(2)}) collective-permute-start(bf16[3,9,16,256]{3,2,1,0:T(8,128)(2,1)} %collective-permute-done.3.rest_1_), channel_id=1, source_target_pairs={{0,8},{4,20},{8,0},{12,28},{16,24},{20,4},{24,16},{28,12},{1,9},{5... | collective-permute-start | bytes 663560 | tf_op jit(solution)/shard_map/ppermute | solution.py:940
  40.7 11.8 %collective-permute-start.6 = (bf16[3,9,16,256]{3,2,1,0:T(8,128)(2,1)}, bf16[3,9,16,256]{3,2,1,0:T(8,128)(2,1)}, u32[]{:S(2)}, u32[]{:S(2)}) collective-permute-start(bf16[3,9,16,256]{3,2,1,0:T(8,128)(2,1)} %get-tuple-element.79.rest_0_.refs_0_), channel_id=1, source_target_pairs={{0,4},{4,0},{8,12},{12,8},{16,20},{20,16},{24,28},{28,24},{1,5},{5... | collective-permute-start | bytes 663560 | tf_op jit(solution)/shard_map/ppermute | solution.py:933
  46.1 6.4 %collective-permute-start.7 = (bf16[3,9,16,256]{3,2,1,0:T(8,128)(2,1)}, bf16[3,9,16,256]{3,2,1,0:T(8,128)(2,1)}, u32[]{:S(2)}, u32[]{:S(2)}) collective-permute-start(bf16[3,9,16,256]{3,2,1,0:T(8,128)(2,1)} %collective-permute-done.3.rest_1_), channel_id=1, source_target_pairs={{0,4},{4,0},{8,12},{12,8},{16,20},{20,16},{24,28},{28,24},{1,5},{5... | collective-permute-start | bytes 663560 | tf_op jit(solution)/shard_map/ppermute | solution.py:933
  48.4 4.0 %collective-permute-start.8 = (bf16[3,9,16,256]{3,2,1,0:T(8,128)(2,1)}, bf16[3,9,16,256]{3,2,1,0:T(8,128)(2,1)}, u32[]{:S(2)}, u32[]{:S(2)}) collective-permute-start(bf16[3,9,16,256]{3,2,1,0:T(8,128)(2,1)} %collective-permute-done.4.rest_2_), channel_id=1, source_target_pairs={{0,4},{4,0},{8,12},{12,8},{16,20},{20,16},{24,28},{28,24},{1,5},{5... | collective-permute-start | bytes 663560 | tf_op jit(solution)/shard_map/ppermute | solution.py:933
  49.7 2.8 %collective-permute-start.9 = (bf16[3,9,16,256]{3,2,1,0:T(8,128)(2,1)}, bf16[3,9,16,256]{3,2,1,0:T(8,128)(2,1)}, u32[]{:S(2)}, u32[]{:S(2)}) collective-permute-start(bf16[3,9,16,256]{3,2,1,0:T(8,128)(2,1)} %collective-permute-done.5.rest_3_), channel_id=1, source_target_pairs={{0,4},{4,0},{8,12},{12,8},{16,20},{20,16},{24,28},{28,24},{1,5},{5... | collective-permute-start | bytes 663560 | tf_op jit(solution)/shard_map/ppermute | solution.py:933
  50.9 8.4 %collective-permute-start.12 = (bf16[3,9,16,512]{3,2,1,0:T(8,128)(2,1)S(1)}, bf16[3,9,16,512]{3,2,1,0:T(8,128)(2,1)S(1)}, u32[]{:S(2)}, u32[]{:S(2)}) collective-permute-start(bf16[3,9,16,512]{3,2,1,0:T(8,128)(2,1)S(1)} %release.5), channel_id=1, source_target_pairs={{0,8},{4,20},{8,0},{12,28},{16,24},{20,4},{24,16},{28,12},{1,9},{5... | collective-permute-start | bytes 1327112 | tf_op jit(solution)/shard_map/ppermute | solution.py:940
  52.4 1.8 copy-start.7
  59.3 15.1 %copy-start.4 = (bf16[128,512]{1,0:T(8,128)(2,1)S(1)}, bf16[128,512]{1,0:T(8,128)(2,1)}, u32[]{:S(2)}) copy-start(bf16[128,512]{1,0:T(8,128)(2,1)} %copy-done.3) | copy-start | bytes 393220
  59.3 15.1 %copy-start.6 = (bf16[128,512]{1,0:T(8,128)(2,1)S(1)}, bf16[128,512]{1,0:T(8,128)(2,1)}, u32[]{:S(2)}) copy-start(bf16[128,512]{1,0:T(8,128)(2,1)} %copy-done.5) | copy-start | bytes 393220
  59.4 19.5 %copy-start.1 = (bf16[9,128,512]{2,1,0:T(8,128)(2,1)S(1)}, bf16[9,128,512]{2,1,0:T(8,128)(2,1)}, u32[]{:S(2)}) copy-start(bf16[9,128,512]{2,1,0:T(8,128)(2,1)} %own.3) | copy-start | bytes 3538948
  73.4 1.8 collective-permute-start.13
  73.4 3.1 %collective-permute-start.14 = (bf16[3,9,16,512]{3,2,1,0:T(8,128)(2,1)S(1)}, bf16[3,9,16,512]{3,2,1,0:T(8,128)(2,1)S(1)}, u32[]{:S(2)}, u32[]{:S(2)}) collective-permute-start(bf16[3,9,16,512]{3,2,1,0:T(8,128)(2,1)S(1)} %get-tuple-element.84.rest_1_), channel_id=1, source_target_pairs={{0,4},{4,0},{8,12},{12,8},{16,20},{20,16},{24,28},{28,24},{1,5},{5... | collective-permute-start | bytes 1327112 | tf_op jit(solution)/shard_map/ppermute | solution.py:933
  73.9 4.9 %collective-permute-start.15 = (bf16[3,9,16,512]{3,2,1,0:T(8,128)(2,1)S(1)}, bf16[3,9,16,512]{3,2,1,0:T(8,128)(2,1)S(1)}, u32[]{:S(2)}, u32[]{:S(2)}) collective-permute-start(bf16[3,9,16,512]{3,2,1,0:T(8,128)(2,1)S(1)} %get-tuple-element.85.rest_2_), channel_id=1, source_target_pairs={{0,4},{4,0},{8,12},{12,8},{16,20},{20,16},{24,28},{28,24},{1,5},{5... | collective-permute-start | bytes 1327112 | tf_op jit(solution)/shard_map/ppermute | solution.py:933
  73.9 4.9 %collective-permute-start.16 = (bf16[3,9,16,512]{3,2,1,0:T(8,128)(2,1)S(1)}, bf16[3,9,16,512]{3,2,1,0:T(8,128)(2,1)S(1)}, u32[]{:S(2)}, u32[]{:S(2)}) collective-permute-start(bf16[3,9,16,512]{3,2,1,0:T(8,128)(2,1)S(1)} %get-tuple-element.86.rest_3_), channel_id=1, source_target_pairs={{0,4},{4,0},{8,12},{12,8},{16,20},{20,16},{24,28},{28,24},{1,5},{5... | collective-permute-start | bytes 1327112 | tf_op jit(solution)/shard_map/ppermute | solution.py:933
  74.4 14.3 %collective-permute-start.17 = (bf16[128,512]{1,0:T(8,128)(2,1)S(1)}, bf16[128,512]{1,0:T(8,128)(2,1)S(1)}, u32[]{:S(2)}, u32[]{:S(2)}) collective-permute-start(bf16[128,512]{1,0:T(8,128)(2,1)S(1)} %get-tuple-element.91), channel_id=1, source_target_pairs={{0,1},{1,0},{2,3},{3,2},{4,5},{5,4},{6,7},{7,6},{8,9},{9,8},{10,11... | collective-permute-start | bytes 393224 | tf_op jit(solution)/shard_map/ppermute | solution.py:943
  75.2 13.5 %collective-permute-start.18 = (bf16[128,512]{1,0:T(8,128)(2,1)S(1)}, bf16[128,512]{1,0:T(8,128)(2,1)S(1)}, u32[]{:S(2)}, u32[]{:S(2)}) collective-permute-start(bf16[128,512]{1,0:T(8,128)(2,1)S(1)} %get-tuple-element.92), channel_id=1, source_target_pairs={{0,2},{1,3},{2,0},{3,1},{4,6},{5,7},{6,4},{7,5},{8,10},{9,11},{10,... | collective-permute-start | bytes 393224 | tf_op jit(solution)/shard_map/ppermute | solution.py:943
  76.5 12.2 %collective-permute-start.19 = (bf16[128,512]{1,0:T(8,128)(2,1)S(1)}, bf16[128,512]{1,0:T(8,128)(2,1)S(1)}, u32[]{:S(2)}, u32[]{:S(2)}) collective-permute-start(bf16[128,512]{1,0:T(8,128)(2,1)S(1)} %get-tuple-element.93), channel_id=1, source_target_pairs={{0,3},{1,2},{2,1},{3,0},{4,7},{5,6},{6,5},{7,4},{8,11},{9,10},{10,... | collective-permute-start | bytes 393224 | tf_op jit(solution)/shard_map/ppermute | solution.py:943
  124.6 4.6 %collective-permute-start.23 = (bf16[4,4,9,16,512]{4,3,2,1,0:T(8,128)(2,1)S(1)}, bf16[4,4,9,16,512]{4,3,2,1,0:T(8,128)(2,1)S(1)}, u32[]{:S(2)}, u32[]{:S(2)}) collective-permute-start(bf16[4,4,9,16,512]{4,3,2,1,0:T(8,128)(2,1)S(1)} %get-tuple-element.114), channel_id=1, source_target_pairs={{0,4},{4,0},{8,12},{12,8},{16,20},{20,16},{24,28},{28,24},{1,5},{5... | collective-permute-start | bytes 7077896 | tf_op jit(solution)/shard_map/ppermute | solution.py:933
  124.6 15.2 %collective-permute-start.20 = (bf16[128,384]{1,0:T(8,128)(2,1)S(1)}, bf16[128,384]{1,0:T(8,128)(2,1)S(1)}, u32[]{:S(2)}, u32[]{:S(2)}) collective-permute-start(bf16[128,384]{1,0:T(8,128)(2,1)S(1)} %get-tuple-element.103), channel_id=1, source_target_pairs={{0,1},{1,0},{2,3},{3,2},{4,5},{5,4},{6,7},{7,6},{8,9},{9,8},{10,11... | collective-permute-start | bytes 294920 | tf_op jit(solution)/shard_map/ppermute | solution.py:943
  124.9 14.9 %collective-permute-start.21 = (bf16[128,384]{1,0:T(8,128)(2,1)S(1)}, bf16[128,384]{1,0:T(8,128)(2,1)S(1)}, u32[]{:S(2)}, u32[]{:S(2)}) collective-permute-start(bf16[128,384]{1,0:T(8,128)(2,1)S(1)} %get-tuple-element.104), channel_id=1, source_target_pairs={{0,2},{1,3},{2,0},{3,1},{4,6},{5,7},{6,4},{7,5},{8,10},{9,11},{10,... | collective-permute-start | bytes 294920 | tf_op jit(solution)/shard_map/ppermute | solution.py:943
  126.4 13.4 %collective-permute-start.22 = (bf16[128,384]{1,0:T(8,128)(2,1)S(1)}, bf16[128,384]{1,0:T(8,128)(2,1)S(1)}, u32[]{:S(2)}, u32[]{:S(2)}) collective-permute-start(bf16[128,384]{1,0:T(8,128)(2,1)S(1)} %get-tuple-element.105), channel_id=1, source_target_pairs={{0,3},{1,2},{2,1},{3,0},{4,7},{5,6},{6,5},{7,4},{8,11},{9,10},{10,... | collective-permute-start | bytes 294920 | tf_op jit(solution)/shard_map/ppermute | solution.py:943
  129.7 10.2 %collective-permute-start.24 = (bf16[4,9,16,512]{3,2,1,0:T(8,128)(2,1)S(1)}, bf16[4,9,16,512]{3,2,1,0:T(8,128)(2,1)S(1)}, u32[]{:S(2)}, u32[]{:S(2)}) collective-permute-start(bf16[4,9,16,512]{3,2,1,0:T(8,128)(2,1)S(1)} %get-tuple-element.115.after), channel_id=1, source_target_pairs={{0,8},{4,20},{8,0},{12,28},{16,24},{20,4},{24,16},{28,12},{1,9},{5... | collective-permute-start | bytes 1769480 | tf_op jit(solution)/shard_map/ppermute | solution.py:940
  156.8 7.3 %collective-permute-start.28 = (bf16[4,4,9,16,256]{4,3,2,1,0:T(8,128)(2,1)S(1)}, bf16[4,4,9,16,256]{4,3,2,1,0:T(8,128)(2,1)S(1)}, u32[]{:S(2)}, u32[]{:S(2)}) collective-permute-start(bf16[4,4,9,16,256]{4,3,2,1,0:T(8,128)(2,1)S(1)} %get-tuple-element.126), channel_id=1, source_target_pairs={{0,4},{4,0},{8,12},{12,8},{16,20},{20,16},{24,28},{28,24},{1,5},{5... | collective-permute-start | bytes 3538952 | tf_op jit(solution)/shard_map/ppermute | solution.py:933
  157.0 16.2 %collective-permute-start.31 = (bf16[4,9,16,512]{3,2,1,0:T(8,128)(2,1)S(1)}, bf16[4,9,16,512]{3,2,1,0:T(8,128)(2,1)S(1)}, u32[]{:S(2)}, u32[]{:S(2)}) collective-permute-start(bf16[4,9,16,512]{3,2,1,0:T(8,128)(2,1)S(1)} %mid_sum_b.1), channel_id=1, source_target_pairs={{0,16},{4,12},{8,24},{12,4},{16,0},{20,28},{24,8},{28,20},{1,17},{... | collective-permute-start | bytes 1769480 | tf_op jit(solution)/shard_map/ppermute | solution.py:940
  157.9 15.3 %collective-permute-start.30 = (bf16[4,9,16,512]{3,2,1,0:T(8,128)(2,1)S(1)}, bf16[4,9,16,512]{3,2,1,0:T(8,128)(2,1)S(1)}, u32[]{:S(2)}, u32[]{:S(2)}) collective-permute-start(bf16[4,9,16,512]{3,2,1,0:T(8,128)(2,1)S(1)} %release.9), channel_id=1, source_target_pairs={{0,8},{4,20},{8,0},{12,28},{16,24},{20,4},{24,16},{28,12},{1,9},{5... | collective-permute-start | bytes 1769480 | tf_op jit(solution)/shard_map/ppermute | solution.py:940
  164.4 14.8 %collective-permute-start.29 = (bf16[8,9,16,256]{3,2,1,0:T(8,128)(2,1)S(1)}, bf16[8,9,16,256]{3,2,1,0:T(8,128)(2,1)S(1)}, u32[]{:S(2)}, u32[]{:S(2)}) collective-permute-start(bf16[8,9,16,256]{3,2,1,0:T(8,128)(2,1)S(1)} %get-tuple-element.128), channel_id=1, source_target_pairs={{0,8},{4,20},{8,0},{12,28},{16,24},{20,4},{24,16},{28,12},{1,9},{5... | collective-permute-start | bytes 1769480 | tf_op jit(solution)/shard_map/ppermute | solution.py:940
  165.9 9.5 %collective-permute-start.25 = (bf16[64,1536]{1,0:T(8,128)(2,1)S(1)}, bf16[64,1536]{1,0:T(8,128)(2,1)S(1)}, u32[]{:S(2)}, u32[]{:S(2)}) collective-permute-start(bf16[64,1536]{1,0:T(8,128)(2,1)S(1)} %get-tuple-element.121), channel_id=1, source_target_pairs={{0,1},{1,0},{2,3},{3,2},{4,5},{5,4},{6,7},{7,6},{8,9},{9,8},{10,11... | collective-permute-start | bytes 589832 | tf_op jit(solution)/shard_map/ppermute | solution.py:943
  166.2 11.4 %collective-permute-start.26 = (bf16[64,1536]{1,0:T(8,128)(2,1)S(1)}, bf16[64,1536]{1,0:T(8,128)(2,1)S(1)}, u32[]{:S(2)}, u32[]{:S(2)}) collective-permute-start(bf16[64,1536]{1,0:T(8,128)(2,1)S(1)} %get-tuple-element.122), channel_id=1, source_target_pairs={{0,2},{1,3},{2,0},{3,1},{4,6},{5,7},{6,4},{7,5},{8,10},{9,11},{10,... | collective-permute-start | bytes 589832 | tf_op jit(solution)/shard_map/ppermute | solution.py:943
  173.5 10.2 %collective-permute-start.33 = (bf16[2,9,16,512]{3,2,1,0:T(8,128)(2,1)S(1)}, bf16[2,9,16,512]{3,2,1,0:T(8,128)(2,1)S(1)}, u32[]{:S(2)}, u32[]{:S(2)}) collective-permute-start(bf16[2,9,16,512]{3,2,1,0:T(8,128)(2,1)S(1)} %get-tuple-element.135), channel_id=1, source_target_pairs={{0,1},{1,0},{2,3},{3,2},{4,5},{5,4},{6,7},{7,6},{8,9},{9,8},{10,11... | collective-permute-start | bytes 884744 | tf_op jit(solution)/shard_map/ppermute | solution.py:943
  179.3 9.9 %collective-permute-start.32 = (bf16[4,9,16,256]{3,2,1,0:T(8,128)(2,1)S(1)}, bf16[4,9,16,256]{3,2,1,0:T(8,128)(2,1)S(1)}, u32[]{:S(2)}, u32[]{:S(2)}) collective-permute-start(bf16[4,9,16,256]{3,2,1,0:T(8,128)(2,1)S(1)} %get-tuple-element.134), channel_id=1, source_target_pairs={{0,16},{4,12},{8,24},{12,4},{16,0},{20,28},{24,8},{28,20},{1,17},{... | collective-permute-start | bytes 884744 | tf_op jit(solution)/shard_map/ppermute | solution.py:940
  180.2 9.0 %collective-permute-start.27 = (bf16[64,1536]{1,0:T(8,128)(2,1)S(1)}, bf16[64,1536]{1,0:T(8,128)(2,1)S(1)}, u32[]{:S(2)}, u32[]{:S(2)}) collective-permute-start(bf16[64,1536]{1,0:T(8,128)(2,1)S(1)} %get-tuple-element.123), channel_id=1, source_target_pairs={{0,3},{1,2},{2,1},{3,0},{4,7},{5,6},{6,5},{7,4},{8,11},{9,10},{10,... | collective-permute-start | bytes 589832 | tf_op jit(solution)/shard_map/ppermute | solution.py:943
  189.2 7.8 %collective-permute-start.34 = (bf16[2,9,16,256]{3,2,1,0:T(8,128)(2,1)S(1)}, bf16[2,9,16,256]{3,2,1,0:T(8,128)(2,1)S(1)}, u32[]{:S(2)}, u32[]{:S(2)}) collective-permute-start(bf16[2,9,16,256]{3,2,1,0:T(8,128)(2,1)S(1)} %get-tuple-element.139), channel_id=1, source_target_pairs={{0,1},{1,0},{2,3},{3,2},{4,5},{5,4},{6,7},{7,6},{8,9},{9,8},{10,11... | collective-permute-start | bytes 442376 | tf_op jit(solution)/shard_map/ppermute | solution.py:943
  191.8 9.4 %collective-permute-start.36 = (bf16[1,9,16,512]{3,2,1,0:T(8,128)(2,1)S(1)}, bf16[1,9,16,512]{3,2,1,0:T(8,128)(2,1)S(1)}, u32[]{:S(2)}, u32[]{:S(2)}) collective-permute-start(bf16[1,9,16,512]{3,2,1,0:T(8,128)(2,1)S(1)} %get-tuple-element.143), channel_id=1, source_target_pairs={{0,2},{1,3},{2,0},{3,1},{4,6},{5,7},{6,4},{7,5},{8,10},{9,11},{10,... | collective-permute-start | bytes 442376 | tf_op jit(solution)/shard_map/ppermute | solution.py:943
  201.3 8.7 %collective-permute-start.41 = (bf16[9,16,512]{2,1,0:T(8,128)(2,1)S(1)}, bf16[9,16,512]{2,1,0:T(8,128)(2,1)S(1)}, u32[]{:S(2)}, u32[]{:S(2)}) collective-permute-start(bf16[9,16,512]{2,1,0:T(8,128)(2,1)S(1)} %mid_sum_3.1.rest_0_.refs_0_), channel_id=1, source_target_pairs={{0,16},{4,12},{8,24},{12,4},{16,0},{20,28},{24,8},{28,20},{1,17},{... | collective-permute-start | bytes 442376 | tf_op jit(solution)/shard_map/ppermute | solution.py:940
  201.4 5.7 %collective-permute-start.35 = (bf16[1,9,16,256]{3,2,1,0:T(8,128)(2,1)S(1)}, bf16[1,9,16,256]{3,2,1,0:T(8,128)(2,1)S(1)}, u32[]{:S(2)}, u32[]{:S(2)}) collective-permute-start(bf16[1,9,16,256]{3,2,1,0:T(8,128)(2,1)S(1)} %get-tuple-element.142), channel_id=1, source_target_pairs={{0,2},{1,3},{2,0},{3,1},{4,6},{5,7},{6,4},{7,5},{8,10},{9,11},{10,... | collective-permute-start | bytes 221192 | tf_op jit(solution)/shard_map/ppermute | solution.py:943
  201.8 8.9 %collective-permute-start.42 = (bf16[9,16,512]{2,1,0:T(8,128)(2,1)S(1)}, bf16[9,16,512]{2,1,0:T(8,128)(2,1)S(1)}, u32[]{:S(2)}, u32[]{:S(2)}) collective-permute-start(bf16[9,16,512]{2,1,0:T(8,128)(2,1)S(1)} %mid_sum_3.1.rest_0_.refs_0_), channel_id=1, source_target_pairs={{0,8},{4,20},{8,0},{12,28},{16,24},{20,4},{24,16},{28,12},{1,9},{5... | collective-permute-start | bytes 442376 | tf_op jit(solution)/shard_map/ppermute | solution.py:940
  207.1 5.2 %collective-permute-start.37 = (bf16[9,16,256]{2,1,0:T(8,128)(2,1)S(1)}, bf16[9,16,256]{2,1,0:T(8,128)(2,1)S(1)}, u32[]{:S(2)}, u32[]{:S(2)}) collective-permute-start(bf16[9,16,256]{2,1,0:T(8,128)(2,1)S(1)} %in_sum_3.1.refs_0_), channel_id=1, source_target_pairs={{0,16},{4,12},{8,24},{12,4},{16,0},{20,28},{24,8},{28,20},{1,17},{... | collective-permute-start | bytes 221192 | tf_op jit(solution)/shard_map/ppermute | solution.py:940
  208.7 4.4 %collective-permute-start.38 = (bf16[9,16,256]{2,1,0:T(8,128)(2,1)S(1)}, bf16[9,16,256]{2,1,0:T(8,128)(2,1)S(1)}, u32[]{:S(2)}, u32[]{:S(2)}) collective-permute-start(bf16[9,16,256]{2,1,0:T(8,128)(2,1)S(1)} %in_sum_3.1.refs_0_), channel_id=1, source_target_pairs={{0,8},{4,20},{8,0},{12,28},{16,24},{20,4},{24,16},{28,12},{1,9},{5... | collective-permute-start | bytes 221192 | tf_op jit(solution)/shard_map/ppermute | solution.py:940
  209.9 5.1 %collective-permute-start.43 = (bf16[9,16,512]{2,1,0:T(8,128)(2,1)S(1)}, bf16[9,16,512]{2,1,0:T(8,128)(2,1)S(1)}, u32[]{:S(2)}, u32[]{:S(2)}) collective-permute-start(bf16[9,16,512]{2,1,0:T(8,128)(2,1)S(1)} %collective-permute-done.41.refs_1_), channel_id=1, source_target_pairs={{0,8},{4,20},{8,0},{12,28},{16,24},{20,4},{24,16},{28,12},{1,9},{5... | collective-permute-start | bytes 442376 | tf_op jit(solution)/shard_map/ppermute | solution.py:940
  215.1 7.7 %collective-permute-start.44 = (bf16[4,9,16,512]{3,2,1,0:T(8,128)(2,1)S(1)}, bf16[4,9,16,512]{3,2,1,0:T(8,128)(2,1)S(1)}, u32[]{:S(2)}, u32[]{:S(2)}) collective-permute-start(bf16[4,9,16,512]{3,2,1,0:T(8,128)(2,1)S(1)} %mid_stack.1.mine), channel_id=1, source_target_pairs={{0,4},{4,0},{8,12},{12,8},{16,20},{20,16},{24,28},{28,24},{1,5},{5... | collective-permute-start | bytes 1769480 | tf_op jit(solution)/shard_map/ppermute | solution.py:933
  215.7 4.4 %collective-permute-start.39 = (bf16[9,16,256]{2,1,0:T(8,128)(2,1)S(1)}, bf16[9,16,256]{2,1,0:T(8,128)(2,1)S(1)}, u32[]{:S(2)}, u32[]{:S(2)}) collective-permute-start(bf16[9,16,256]{2,1,0:T(8,128)(2,1)S(1)} %collective-permute-done.37.refs_1_.refs_4_), channel_id=1, source_target_pairs={{0,8},{4,20},{8,0},{12,28},{16,24},{20,4},{24,16},{28,12},{1,9},{5... | collective-permute-start | bytes 221192 | tf_op jit(solution)/shard_map/ppermute | solution.py:940
  220.1 1.6 collective-permute-start.40

commit v3 on v2

--- a/solution.py
+++ b/solution.py
@@ -891,7 +891,8 @@
     )(stay, got, *gates)
 
 
-def spread_kernel(g, mine, other, out):
+def spread_kernel(g, mine, other, out, done):
+    done[...] = jnp.zeros(done.shape, F32)
     d = lax.axis_index("dp")
     core, plane = lax.rem(d, 2), lax.rem(d, g.pieces) // 2
     for side, part in enumerate((mine, other)):
@@ -904,9 +905,12 @@
 def spread_out(g, mine, other, depth, name):
     return pl.pallas_call(
         functools.partial(spread_kernel, g),
-        out_shape=jax.ShapeDtypeStruct((9, g.co, depth), F32),
+        out_shape=[
+            jax.ShapeDtypeStruct((9, g.co, depth), F32),
+            jax.ShapeDtypeStruct((8, 128), F32),
+        ],
         in_specs=[VMEM] * 2,
-        out_specs=VMEM,
+        out_specs=[VMEM] * 2,
         compiler_params=pltpu.CompilerParams(vmem_limit_bytes=12 * MIB),
         name=name,
     )(mine, other)
@@ -1066,21 +1070,21 @@
             mid = Chain(stay_mid, go_mid, g.cm, "mid")
             for i in range(g.turns):
                 mid.turn(i, stay_in)
-        gates = [parts[1 : nch - 1], [*parts[nch - 1 :], pooled_done]]
+        gates = [parts[1 : nch - 1], [pooled_done]]
         at = mid.stay
         for i in range(g.turns):
             at = inner.turn(i, at, *(gates[i] if i < 2 else []))
             if i == 0:
                 at = mid.turn(g.turns, at)
         for i in range(g.turns, turns):
-            at = inner.turn(i, at, *([spectra_done] if i == g.turns else []))
+            at = inner.turn(i, at, *(parts[nch - 1 :] if i == g.turns else []))
             if i + 1 < turns:
                 at = mid.turn(i + 1, at)
         inner.rest()
         mid.rest()
         planes_in = links.gather_planes(inner.stay)
-        weight_mid_grad = mid.out(links.gather_planes(mid.stay), *planes_in[1:3])
-        weight_in_grad = inner.out(planes_in)
+        weight_mid_grad, mid_done = mid.out(links.gather_direct(mid.stay), *planes_in[1:3])
+        weight_in_grad, _ = inner.out(planes_in, mid_done, spectra_done)
         z = lax.axis_index("chan")
 
         def share(sums, i):

time: 225 us -> 218 us (0.969)
  waiting for transfers between devices: 63.1 us -> 57 us
    ppermute x16, waiting for transfers between devices: 33.6 us -> 27.5 us  [chan(): return lax.ppermute(x, 'chan', [(i, i ^ k) for i in range(self.g.nch)])]
    ppermute x0 -> x3, waiting for transfers between devices: none -> 4.28 us  [gather_direct(): return [x] + [lax.ppermute(x, 'dp', p) for p in pairs[1:]]]
    ppermute x17 -> x14, waiting for transfers between devices: 27.1 us -> 22.9 us  [plane(): lax.ppermute(x, 'dp', [(i, i ^ 2 * g.mask(i & 1, turn)) for i in range(g....]
    ppermute x0 -> x3, starting transfers between devices: none -> 3.55 us  [gather_direct(): return [x] + [lax.ppermute(x, 'dp', p) for p in pairs[1:]]]
    ppermute x17 -> x14, starting transfers between devices: 17.6 us -> 14.9 us  [plane(): lax.ppermute(x, 'dp', [(i, i ^ 2 * g.mask(i & 1, turn)) for i in range(g....]
  transfers between devices with their start and end apart: 46 -> 46, of which waited for: 22 -> 21; matrix products, arithmetic and copies ran while one was open for 1% -> 1% of each run, Pallas kernels for 18% -> 18%
where the time goes in v3:
time: 218 us
  Pallas kernels  63.4 us (29%)
  waiting for transfers between devices  57 us (26%)
  starting transfers between devices  46.7 us (21%)
  blocking collectives  46.2 us (21%)
  local copies, waits for them, and re-layouts  3.46 us (2%)
    pallas_call x23, Pallas kernels, call(): pl.pallas_call(body, out_shape=[pltpu.VMEM(o.shape, o.dtype) if isinstanc...  57 us
    all_to_all x4, blocking collectives, everyone(): return lax.all_to_all(x, ('dp', 'chan'), 0, 0)  46.2 us
    ppermute x16, waiting for transfers between devices, chan(): return lax.ppermute(x, 'chan', [(i, i ^ k) for i in range(self.g.nch)])  27.5 us
    ppermute x14, waiting for transfers between devices, plane(): lax.ppermute(x, 'dp', [(i, i ^ 2 * g.mask(i & 1, turn)) for i in range(g....  22.9 us
    ppermute x16, starting transfers between devices, chan(): return lax.ppermute(x, 'chan', [(i, i ^ k) for i in range(self.g.nch)])  19.4 us
    ppermute x14, starting transfers between devices, plane(): lax.ppermute(x, 'dp', [(i, i ^ 2 * g.mask(i & 1, turn)) for i in range(g....  14.9 us
    all_to_all x1, starting transfers between devices, body(): maps = lax.all_to_all(release_far([pieces_in], cells), 'chan', 0, 0)  6.3 us
  transfers between devices with their start and end apart: 46, of which 21 were waited for; matrix products, arithmetic and copies ran while one was open for 1% of the time, Pallas kernels for 18%

profile of v3, /device:TPU:0, one launch (start us, length us, event | category | flops | bytes accessed | tf_op | source)
XLA Modules:
  0.0 218.0 jit_solution(4637936735932513411)
XLA Ops:
  0.6 1.0 cut_weights.1.after
  1.6 3.1 %collective-permute-start = (bf16[9,16,768]{2,1,0:T(8,128)(2,1)S(1)}, bf16[9,16,768]{2,1,0:T(8,128)(2,1)S(1)}, u32[]{:S(2)}, u32[]{:S(2)}) collective-permute-start(bf16[9,16,768]{2,1,0:T(8,128)(2,1)S(1)} %cut_weights.1.after), channel_id=1, source_target_pairs={{0,1},{1,0},{2,3},{3,2},{4,5},{5,4},{6,7},{7,6},{8,9},{9,8},{10,11... | collective-permute-start | bytes 663560 | tf_op jit(solution)/shard_map/ppermute | solution.py:947
  4.7 2.6 %collective-permute-start.1 = (bf16[9,16,768]{2,1,0:T(8,128)(2,1)S(1)}, bf16[9,16,768]{2,1,0:T(8,128)(2,1)S(1)}, u32[]{:S(2)}, u32[]{:S(2)}) collective-permute-start(bf16[9,16,768]{2,1,0:T(8,128)(2,1)S(1)} %cut_weights.1.after), channel_id=1, source_target_pairs={{0,2},{1,3},{2,0},{3,1},{4,6},{5,7},{6,4},{7,5},{8,10},{9,11},{10,... | collective-permute-start | bytes 663560 | tf_op jit(solution)/shard_map/ppermute | solution.py:947
  7.3 2.0 cut_maps.1.after.refs_1_
  9.3 1.1 copy-done
  10.5 1.1 cut_cotangent.1
  11.6 0.6 copy-done.5
  12.3 1.8 collective-permute-done.rest_0_
  14.1 9.3 %collective-permute-done.1.rest_1_ = bf16[9,16,768]{2,1,0:T(8,128)(2,1)S(1)} collective-permute-done((bf16[9,16,768]{2,1,0:T(8,128)(2,1)S(1)}, bf16[9,16,768]{2,1,0:T(8,128)(2,1)S(1)}, u32[]{:S(2)}, u32[]{:S(2)}) %collective-permute-start.1) | collective-permute-done | bytes 221216 | tf_op jit(solution)/shard_map/ppermute | solution.py:947
  23.5 0.7 sort_pieces.1
  24.2 6.3 %all-to-all-start = ((bf16[4,64,1664]{2,1,0:T(8,128)(2,1)}), bf16[4,64,1664]{2,1,0:T(8,128)(2,1)S(1)}, u32[]{:S(2)}, u32[]{:S(2)}) async-start(bf16[4,64,1664]{2,1,0:T(8,128)(2,1)} %release_far.1), calls=%async_computation | async-start | bytes 1703936 | tf_op jit(solution)/shard_map/all_to_all | solution.py:997
  30.5 1.5 collective-permute-start.3
  32.6 1.5 collective-permute-start.11
  34.6 4.6 %collective-permute-done.3.rest_1_ = bf16[3,9,16,256]{3,2,1,0:T(8,128)(2,1)} collective-permute-done((bf16[3,9,16,256]{3,2,1,0:T(8,128)(2,1)}, bf16[3,9,16,256]{3,2,1,0:T(8,128)(2,1)}, u32[]{:S(2)}, u32[]{:S(2)}) %collective-permute-start.3) | collective-permute-done | bytes 221216 | tf_op jit(solution)/shard_map/ppermute | solution.py:944
  39.2 1.5 collective-permute-start.5
  40.7 5.4 %collective-permute-done.4.rest_2_ = bf16[3,9,16,256]{3,2,1,0:T(8,128)(2,1)} collective-permute-done((bf16[3,9,16,256]{3,2,1,0:T(8,128)(2,1)}, bf16[3,9,16,256]{3,2,1,0:T(8,128)(2,1)}, u32[]{:S(2)}, u32[]{:S(2)}) %collective-permute-start.4) | collective-permute-done | bytes 221216 | tf_op jit(solution)/shard_map/ppermute | solution.py:944
  46.1 2.3 %collective-permute-done.5.rest_3_ = bf16[3,9,16,256]{3,2,1,0:T(8,128)(2,1)} collective-permute-done((bf16[3,9,16,256]{3,2,1,0:T(8,128)(2,1)}, bf16[3,9,16,256]{3,2,1,0:T(8,128)(2,1)}, u32[]{:S(2)}, u32[]{:S(2)}) %collective-permute-start.5) | collective-permute-done | bytes 221216 | tf_op jit(solution)/shard_map/ppermute | solution.py:944
  48.4 1.3 collective-permute-start.8
  49.8 1.1 all-to-all-done.maps.refs_0_
  50.9 1.5 collective-permute-start.12
  52.5 1.7 join_in.1.w
  54.2 5.1 %first_conv.1 = (f32[8,208,512]{2,1,0:T(8,128)S(1)}, bf16[8,208,768]{2,1,0:T(8,128)(2,1)S(1)}, f32[1,1664]{1,0:T(1,128)S(1)}) custom-call(s32[2]{0:T(128)S(1)} %copy-done.7, f32[4,128]{1,0:T(4,128)S(1)} %pad_maximum_fusion.gains, bf16[9,512,256]{2,1,0:T(8,128)(2,1)S(1)} %join_in.1.w, bf16[4,64,1664]{2,1,0:T(8,128)(2,1)S(1)} %all-to-all-done.maps.refs_0_), custom_call_target="tpu_custom_call" | custom-call | flops 3925868544 | bytes 10485760 | tf_op jit(solution)/shard_map/first_conv/pallas_call | solution.py:90
  59.4 14.0 %all_to_all.25.refs_0_.got = f32[32,1,1664]{2,1,0:T(1,128)S(1)} all-to-all(f32[32,1,1664]{2,1,0:T(1,128)S(1)} %fan.3), channel_id=1, replica_groups=mesh['dp'=8,'chan'=4] {'dp','chan'}, dimensions={0} | all-to-all | bytes 425984 | tf_op jit(solution)/shard_map/all_to_all | solution.py:972
  75.2 1.3 collective-permute-start.18
  76.5 2.3 %collective-permute-start.19 = (bf16[128,512]{1,0:T(8,128)(2,1)S(1)}, bf16[128,512]{1,0:T(8,128)(2,1)S(1)}, u32[]{:S(2)}, u32[]{:S(2)}) collective-permute-start(bf16[128,512]{1,0:T(8,128)(2,1)S(1)} %get-tuple-element.96), channel_id=1, source_target_pairs={{0,3},{1,2},{2,1},{3,0},{4,7},{5,6},{6,5},{7,4},{8,11},{9,10},{10,... | collective-permute-start | bytes 393224 | tf_op jit(solution)/shard_map/ppermute | solution.py:947
  79.2 9.5 %second_conv.1 = (f32[8,208,512]{2,1,0:T(8,128)S(1)}, bf16[8,208,1536]{2,1,0:T(8,128)(2,1)S(1)}, f32[16,512]{1,0:T(8,128)S(1)}, f32[1,1024]{1,0:T(1,128)S(1)}, f32[1,128]{1,0:T(1,128)S(1)}) custom-call(s32[2]{0:T(128)S(1)} %copy-done.7, f32[32,1,1664]{2,1,0:T(1,128)S(1)} %all_to_all.25.refs_0_.got, f32[8,208,512]{2,1,0:T(8,128)S(1)} %get-tuple-element.85.pre1.pre, ...), custom_call_target="tpu_custom_call" | custom-call | flops 7851737088 | bytes 17825792 | tf_op jit(solution)/shard_map/second_conv/pallas_call | solution.py:90
  88.8 11.0 %all_to_all.26.got = f32[32,1,1024]{2,1,0:T(1,128)S(1)} all-to-all(f32[32,1,1024]{2,1,0:T(1,128)S(1)} %fan.4), channel_id=1, replica_groups=mesh['dp'=8,'chan'=4] {'dp','chan'}, dimensions={0} | all-to-all | bytes 262144 | tf_op jit(solution)/shard_map/all_to_all | solution.py:972
  99.7 5.2 %pool.1 = (bf16[128,384]{1,0:T(8,128)(2,1)S(1)}, bf16[128,384]{1,0:T(8,128)(2,1)S(1)}, bf16[128,384]{1,0:T(8,128)(2,1)S(1)}, bf16[128,384]{1,0:T(8,128)(2,1)S(1)...) custom-call(s32[2]{0:T(128)S(1)} %copy-done.7, ...), custom_call_target="tpu_custom_call" | custom-call | flops 4000000000 | bytes 8388608 | tf_op jit(solution)/shard_map/pool/pallas_call | solution.py:90
  105.0 10.1 %all_to_all.27.refs_0_.got.after = f32[32,1,1024]{2,1,0:T(1,128)S(1)} all-to-all(f32[32,1,1024]{2,1,0:T(1,128)S(1)} %get-tuple-element.100), channel_id=1, replica_groups=mesh['dp'=8,'chan'=4] {'dp','chan'}, dimensions={0} | all-to-all | bytes 262144 | tf_op jit(solution)/shard_map/all_to_all | solution.py:972
  115.1 9.5 %weight_mid_terms.1 = (bf16[8,208,512]{2,1,0:T(8,128)(2,1)S(1)}, f32[8,512]{1,0:T(8,128)S(1)}, f32[8,128]{1,0:T(8,128)}, bf16[2,4,4,9,16,512]{5,4,3,2,1,0:T(8,128)(2,1)S(1)}, bf16[4,4,9,16,512]{4,3,2,1,0:T(8,128)(2,1)S(1)}) custom-call(s32[2]{0:T(128)S(1)} %copy-done.7, f32[32,1,1024]{2,1,0:T(1,128)S(1)} %all_to_all.27.refs_0_.got.after, ...), custom_call_target="tpu_custom_call" | custom-call | flops 7851737088 | bytes 15728640 | tf_op jit(solution)/shard_map/weight_mid_terms/pallas_call | solution.py:90
  124.9 1.5 collective-permute-start.21
  126.4 2.7 %collective-permute-start.22 = (bf16[128,384]{1,0:T(8,128)(2,1)S(1)}, bf16[128,384]{1,0:T(8,128)(2,1)S(1)}, u32[]{:S(2)}, u32[]{:S(2)}) collective-permute-start(bf16[128,384]{1,0:T(8,128)(2,1)S(1)} %get-tuple-element.108), channel_id=1, source_target_pairs={{0,3},{1,2},{2,1},{3,0},{4,7},{5,6},{6,5},{7,4},{8,11},{9,10},{10,... | collective-permute-start | bytes 294920 | tf_op jit(solution)/shard_map/ppermute | solution.py:947
  129.7 0.8 collective-permute-start.24
  130.5 9.3 %second_back.1 = (f32[8,208,512]{2,1,0:T(8,128)S(1)}, f32[1,1280]{1,0:T(1,128)S(1)}) custom-call(s32[2]{0:T(128)S(1)} %copy-done.7, f32[16,512]{1,0:T(8,128)S(1)} %get-tuple-element.110.table, bf16[8,208,512]{2,1,0:T(8,128)(2,1)S(1)} %get-tuple-element.113.grad, f32[8,208,512]{2,1,0:T(8,128)S(1)} %get-tuple-element.85.pre1.pre, ...), custom_call_target="tpu_custom_call" | custom-call | flops 7851737088 | bytes 20971520 | tf_op jit(solution)/shard_map/second_back/pallas_call | solution.py:90
  139.9 11.1 %all_to_all.28.got.after.refs_0_.rest_2_ = f32[32,1,1280]{2,1,0:T(1,128)S(1)} all-to-all(f32[32,1,1280]{2,1,0:T(1,128)S(1)} %fan.5), channel_id=1, replica_groups=mesh['dp'=8,'chan'=4] {'dp','chan'}, dimensions={0} | all-to-all | bytes 327680 | tf_op jit(solution)/shard_map/all_to_all | solution.py:972
  151.0 5.8 %weight_in_terms.1 = (bf16[8,208,512]{2,1,0:T(8,128)(2,1)S(1)}, f32[8,512]{1,0:T(8,128)S(1)}, f32[8,128]{1,0:T(8,128)S(1)}, bf16[2,4,4,9,16,256]{5,4,3,2,1,0:T(8,128)(2,1)S(1)}, bf16[4,4,9,16,256]{4,3,2,1,0:T(8,128)(2,1)S(1)}) custom-call(s32[2]{0:T(128)S(1)} %copy-done.7, f32[32,1,1280]{2,1,0:T(1,128)S(1)} %all_to_all.28.got.after.refs_0_.rest_2_, ...), custom_call_target="tpu_custom_call" | custom-call | flops 3925868544 | bytes 15728640 | tf_op jit(solution)/shard_map/weight_in_terms/pallas_call | solution.py:90
  157.0 0.9 collective-permute-start.31
  158.4 5.6 %spectra_back.1 = (bf16[64,1536]{1,0:T(8,128)(2,1)S(1)}, bf16[64,1536]{1,0:T(8,128)(2,1)S(1)}, bf16[64,1536]{1,0:T(8,128)(2,1)S(1)}, bf16[64,1536]{1,0:T(8,128)(2,1)S(1)}) custom-call(s32[2]{0:T(128)S(1)} %copy-done.7, bf16[8,208,512]{2,1,0:T(8,128)(2,1)S(1)} %get-tuple-element.122.grad.after, bf16[8,208,512]{2,1,0:T(8,128)(2,1)S(1)} %get-tuple-element.122.grad.after, ...), custom_call_target="tpu_custom_call" | custom-call | flops 3925868544 | bytes 5242880 | tf_op jit(solution)/shard_map/spectra_back/pallas_call | solution.py:90
  164.4 1.6 collective-permute-start.29
  166.2 1.6 collective-permute-start.26
  167.8 5.4 %collective-permute-done.31.rest_2_ = bf16[4,9,16,512]{3,2,1,0:T(8,128)(2,1)S(1)} collective-permute-done((bf16[4,9,16,512]{3,2,1,0:T(8,128)(2,1)S(1)}, bf16[4,9,16,512]{3,2,1,0:T(8,128)(2,1)S(1)}, u32[]{:S(2)}, u32[]{:S(2)}) %collective-permute-start.31) | collective-permute-done | bytes 589856 | tf_op jit(solution)/shard_map/ppermute | solution.py:944
  173.7 1.8 collective-permute-done.25.rest_1_
  175.5 2.2 collective-permute-done.26.rest_2_
  177.6 1.5 collective-permute-done.29.got
  179.3 0.9 collective-permute-start.32
  180.2 1.3 collective-permute-start.27
  181.5 0.8 place_pooled.1
  182.3 1.3 collective-permute-done.33.got
  183.7 2.4 %collective-permute-done.32.got = bf16[4,9,16,256]{3,2,1,0:T(8,128)(2,1)S(1)} collective-permute-done((bf16[4,9,16,256]{3,2,1,0:T(8,128)(2,1)S(1)}, bf16[4,9,16,256]{3,2,1,0:T(8,128)(2,1)S(1)}, u32[]{:S(2)}, u32[]{:S(2)}) %collective-permute-start.32) | collective-permute-done | bytes 294944 | tf_op jit(solution)/shard_map/ppermute | solution.py:944
  186.2 1.9 collective-permute-start.36
  188.1 1.6 collective-permute-done.27.rest_3_.rest_1_
  189.7 3.8 %collective-permute-done.34.got = bf16[2,9,16,256]{3,2,1,0:T(8,128)(2,1)S(1)} collective-permute-done((bf16[2,9,16,256]{3,2,1,0:T(8,128)(2,1)S(1)}, bf16[2,9,16,256]{3,2,1,0:T(8,128)(2,1)S(1)}, u32[]{:S(2)}, u32[]{:S(2)}) %collective-permute-start.34) | collective-permute-done | bytes 147488 | tf_op jit(solution)/shard_map/ppermute | solution.py:947
  193.7 5.7 %collective-permute-done.36.got = bf16[1,9,16,512]{3,2,1,0:T(8,128)(2,1)S(1)} collective-permute-done((bf16[1,9,16,512]{3,2,1,0:T(8,128)(2,1)S(1)}, bf16[1,9,16,512]{3,2,1,0:T(8,128)(2,1)S(1)}, u32[]{:S(2)}, u32[]{:S(2)}) %collective-permute-start.36) | collective-permute-done | bytes 147488 | tf_op jit(solution)/shard_map/ppermute | solution.py:947
  199.3 1.2 collective-permute-start.40
  200.5 0.9 collective-permute-start.41
  201.4 1.5 collective-permute-start.42
  202.9 1.2 collective-permute-start.37
  204.1 0.9 collective-permute-start.38
  205.0 4.3 %collective-permute-done.40.refs_1_ = bf16[9,16,512]{2,1,0:T(8,128)(2,1)S(1)} collective-permute-done((bf16[9,16,512]{2,1,0:T(8,128)(2,1)S(1)}, bf16[9,16,512]{2,1,0:T(8,128)(2,1)S(1)}, u32[]{:S(2)}, u32[]{:S(2)}) %collective-permute-start.40) | collective-permute-done | bytes 147488 | tf_op jit(solution)/shard_map/ppermute | solution.py:968
  209.3 0.9 collective-permute-done.37.refs_4_.refs_1_
  210.8 1.1 collective-permute-start.39
  211.9 1.3 place_spectra.1
  213.2 1.6 mid_out.1
  216.9 1.1 in_out.1
  (101 shorter events, 9.4 us)
Async XLA Ops:
  1.6 12.5 %collective-permute-start = (bf16[9,16,768]{2,1,0:T(8,128)(2,1)S(1)}, bf16[9,16,768]{2,1,0:T(8,128)(2,1)S(1)}, u32[]{:S(2)}, u32[]{:S(2)}) collective-permute-start(bf16[9,16,768]{2,1,0:T(8,128)(2,1)S(1)} %cut_weights.1.after), channel_id=1, source_target_pairs={{0,1},{1,0},{2,3},{3,2},{4,5},{5,4},{6,7},{7,6},{8,9},{9,8},{10,11... | collective-permute-start | bytes 663560 | tf_op jit(solution)/shard_map/ppermute | solution.py:947
  4.7 18.7 %collective-permute-start.1 = (bf16[9,16,768]{2,1,0:T(8,128)(2,1)S(1)}, bf16[9,16,768]{2,1,0:T(8,128)(2,1)S(1)}, u32[]{:S(2)}, u32[]{:S(2)}) collective-permute-start(bf16[9,16,768]{2,1,0:T(8,128)(2,1)S(1)} %cut_weights.1.after), channel_id=1, source_target_pairs={{0,2},{1,3},{2,0},{3,1},{4,6},{5,7},{6,4},{7,5},{8,10},{9,11},{10,... | collective-permute-start | bytes 663560 | tf_op jit(solution)/shard_map/ppermute | solution.py:947
  7.3 16.1 %collective-permute-start.2 = (bf16[9,16,768]{2,1,0:T(8,128)(2,1)S(1)}, bf16[9,16,768]{2,1,0:T(8,128)(2,1)S(1)}, u32[]{:S(2)}, u32[]{:S(2)}) collective-permute-start(bf16[9,16,768]{2,1,0:T(8,128)(2,1)S(1)} %cut_weights.1.after), channel_id=1, source_target_pairs={{0,3},{1,2},{2,1},{3,0},{4,7},{5,6},{6,5},{7,4},{8,11},{9,10},{10,... | collective-permute-start | bytes 663560 | tf_op jit(solution)/shard_map/ppermute | solution.py:947
  9.3 1.2 copy-start
  11.6 0.7 copy-start.5
  12.3 11.9 %copy-start.3 = (bf16[128,512]{1,0:T(8,128)(2,1)}, bf16[128,512]{1,0:T(8,128)(2,1)S(1)}, u32[]{:S(2)}) copy-start(bf16[128,512]{1,0:T(8,128)(2,1)S(1)} %get-tuple-element.92.refs_3_) | copy-start | bytes 393220
  24.2 28.2 %copy-start.8 = (f32[128]{0:T(128)S(1)}, f32[128]{0:T(128)}, u32[]{:S(2)}) copy-start(f32[128]{0:T(128)} %param.16) | copy-start | bytes 1540
  24.2 28.2 %copy-start.9 = (f32[128]{0:T(128)S(1)}, f32[128]{0:T(128)}, u32[]{:S(2)}) copy-start(f32[128]{0:T(128)} %param.15) | copy-start | bytes 1540
  24.2 28.2 %copy-start.10 = (f32[128]{0:T(128)S(1)}, f32[128]{0:T(128)}, u32[]{:S(2)}) copy-start(f32[128]{0:T(128)} %param.13) | copy-start | bytes 1540
  24.2 28.2 %copy-start.11 = (f32[128]{0:T(128)S(1)}, f32[128]{0:T(128)}, u32[]{:S(2)}) copy-start(f32[128]{0:T(128)} %param.12) | copy-start | bytes 1540
  24.2 28.3 %copy-start.2 = (bf16[9,128,256]{2,1,0:T(8,128)(2,1)S(1)}, bf16[9,128,256]{2,1,0:T(8,128)(2,1)}, u32[]{:S(2)}) copy-start(bf16[9,128,256]{2,1,0:T(8,128)(2,1)} %own.2) | copy-start | bytes 1769476
  24.2 26.7 %all-to-all-start = ((bf16[4,64,1664]{2,1,0:T(8,128)(2,1)}), bf16[4,64,1664]{2,1,0:T(8,128)(2,1)S(1)}, u32[]{:S(2)}, u32[]{:S(2)}) async-start(bf16[4,64,1664]{2,1,0:T(8,128)(2,1)} %release_far.1), calls=%async_computation | async-start | bytes 1703936 | tf_op jit(solution)/shard_map/all_to_all | solution.py:997
  30.5 8.7 %collective-permute-start.3 = (bf16[3,9,16,256]{3,2,1,0:T(8,128)(2,1)}, bf16[3,9,16,256]{3,2,1,0:T(8,128)(2,1)}, u32[]{:S(2)}, u32[]{:S(2)}) collective-permute-start(bf16[3,9,16,256]{3,2,1,0:T(8,128)(2,1)} %get-tuple-element.82.rest_0_.refs_0_), channel_id=1, source_target_pairs={{0,16},{4,12},{8,24},{12,4},{16,0},{20,28},{24,8},{28,20},{1,17},{... | collective-permute-start | bytes 663560 | tf_op jit(solution)/shard_map/ppermute | solution.py:944
  32.1 17.7 %collective-permute-start.10 = (bf16[3,9,16,512]{3,2,1,0:T(8,128)(2,1)S(1)}, bf16[3,9,16,512]{3,2,1,0:T(8,128)(2,1)S(1)}, u32[]{:S(2)}, u32[]{:S(2)}) collective-permute-start(bf16[3,9,16,512]{3,2,1,0:T(8,128)(2,1)S(1)} %get-tuple-element.84.refs_1_), channel_id=1, source_target_pairs={{0,16},{4,12},{8,24},{12,4},{16,0},{20,28},{24,8},{28,20},{1,17},{... | collective-permute-start | bytes 1327112 | tf_op jit(solution)/shard_map/ppermute | solution.py:944
  32.6 17.2 %collective-permute-start.11 = (bf16[3,9,16,512]{3,2,1,0:T(8,128)(2,1)S(1)}, bf16[3,9,16,512]{3,2,1,0:T(8,128)(2,1)S(1)}, u32[]{:S(2)}, u32[]{:S(2)}) collective-permute-start(bf16[3,9,16,512]{3,2,1,0:T(8,128)(2,1)S(1)} %get-tuple-element.84.refs_1_), channel_id=1, source_target_pairs={{0,8},{4,20},{8,0},{12,28},{16,24},{20,4},{24,16},{28,12},{1,9},{5... | collective-permute-start | bytes 1327112 | tf_op jit(solution)/shard_map/ppermute | solution.py:944
  34.1 12.0 %collective-permute-start.4 = (bf16[3,9,16,256]{3,2,1,0:T(8,128)(2,1)}, bf16[3,9,16,256]{3,2,1,0:T(8,128)(2,1)}, u32[]{:S(2)}, u32[]{:S(2)}) collective-permute-start(bf16[3,9,16,256]{3,2,1,0:T(8,128)(2,1)} %get-tuple-element.82.rest_0_.refs_0_), channel_id=1, source_target_pairs={{0,8},{4,20},{8,0},{12,28},{16,24},{20,4},{24,16},{28,12},{1,9},{5... | collective-permute-start | bytes 663560 | tf_op jit(solution)/shard_map/ppermute | solution.py:944
  39.2 9.3 %collective-permute-start.5 = (bf16[3,9,16,256]{3,2,1,0:T(8,128)(2,1)}, bf16[3,9,16,256]{3,2,1,0:T(8,128)(2,1)}, u32[]{:S(2)}, u32[]{:S(2)}) collective-permute-start(bf16[3,9,16,256]{3,2,1,0:T(8,128)(2,1)} %collective-permute-done.3.rest_1_), channel_id=1, source_target_pairs={{0,8},{4,20},{8,0},{12,28},{16,24},{20,4},{24,16},{28,12},{1,9},{5... | collective-permute-start | bytes 663560 | tf_op jit(solution)/shard_map/ppermute | solution.py:944
  40.7 11.8 %collective-permute-start.6 = (bf16[3,9,16,256]{3,2,1,0:T(8,128)(2,1)}, bf16[3,9,16,256]{3,2,1,0:T(8,128)(2,1)}, u32[]{:S(2)}, u32[]{:S(2)}) collective-permute-start(bf16[3,9,16,256]{3,2,1,0:T(8,128)(2,1)} %get-tuple-element.82.rest_0_.refs_0_), channel_id=1, source_target_pairs={{0,4},{4,0},{8,12},{12,8},{16,20},{20,16},{24,28},{28,24},{1,5},{5... | collective-permute-start | bytes 663560 | tf_op jit(solution)/shard_map/ppermute | solution.py:937
  46.1 6.4 %collective-permute-start.7 = (bf16[3,9,16,256]{3,2,1,0:T(8,128)(2,1)}, bf16[3,9,16,256]{3,2,1,0:T(8,128)(2,1)}, u32[]{:S(2)}, u32[]{:S(2)}) collective-permute-start(bf16[3,9,16,256]{3,2,1,0:T(8,128)(2,1)} %collective-permute-done.3.rest_1_), channel_id=1, source_target_pairs={{0,4},{4,0},{8,12},{12,8},{16,20},{20,16},{24,28},{28,24},{1,5},{5... | collective-permute-start | bytes 663560 | tf_op jit(solution)/shard_map/ppermute | solution.py:937
  48.4 4.0 %collective-permute-start.8 = (bf16[3,9,16,256]{3,2,1,0:T(8,128)(2,1)}, bf16[3,9,16,256]{3,2,1,0:T(8,128)(2,1)}, u32[]{:S(2)}, u32[]{:S(2)}) collective-permute-start(bf16[3,9,16,256]{3,2,1,0:T(8,128)(2,1)} %collective-permute-done.4.rest_2_), channel_id=1, source_target_pairs={{0,4},{4,0},{8,12},{12,8},{16,20},{20,16},{24,28},{28,24},{1,5},{5... | collective-permute-start | bytes 663560 | tf_op jit(solution)/shard_map/ppermute | solution.py:937
  49.7 2.8 %collective-permute-start.9 = (bf16[3,9,16,256]{3,2,1,0:T(8,128)(2,1)}, bf16[3,9,16,256]{3,2,1,0:T(8,128)(2,1)}, u32[]{:S(2)}, u32[]{:S(2)}) collective-permute-start(bf16[3,9,16,256]{3,2,1,0:T(8,128)(2,1)} %collective-permute-done.5.rest_3_), channel_id=1, source_target_pairs={{0,4},{4,0},{8,12},{12,8},{16,20},{20,16},{24,28},{28,24},{1,5},{5... | collective-permute-start | bytes 663560 | tf_op jit(solution)/shard_map/ppermute | solution.py:937
  50.9 8.4 %collective-permute-start.12 = (bf16[3,9,16,512]{3,2,1,0:T(8,128)(2,1)S(1)}, bf16[3,9,16,512]{3,2,1,0:T(8,128)(2,1)S(1)}, u32[]{:S(2)}, u32[]{:S(2)}) collective-permute-start(bf16[3,9,16,512]{3,2,1,0:T(8,128)(2,1)S(1)} %release.5), channel_id=1, source_target_pairs={{0,8},{4,20},{8,0},{12,28},{16,24},{20,4},{24,16},{28,12},{1,9},{5... | collective-permute-start | bytes 1327112 | tf_op jit(solution)/shard_map/ppermute | solution.py:944
  52.4 1.8 copy-start.7
  59.3 15.1 %copy-start.4 = (bf16[128,512]{1,0:T(8,128)(2,1)S(1)}, bf16[128,512]{1,0:T(8,128)(2,1)}, u32[]{:S(2)}) copy-start(bf16[128,512]{1,0:T(8,128)(2,1)} %copy-done.3) | copy-start | bytes 393220
  59.3 15.1 %copy-start.6 = (bf16[128,512]{1,0:T(8,128)(2,1)S(1)}, bf16[128,512]{1,0:T(8,128)(2,1)}, u32[]{:S(2)}) copy-start(bf16[128,512]{1,0:T(8,128)(2,1)} %copy-done.5) | copy-start | bytes 393220
  59.4 19.5 %copy-start.1 = (bf16[9,128,512]{2,1,0:T(8,128)(2,1)S(1)}, bf16[9,128,512]{2,1,0:T(8,128)(2,1)}, u32[]{:S(2)}) copy-start(bf16[9,128,512]{2,1,0:T(8,128)(2,1)} %own.3) | copy-start | bytes 3538948
  73.4 1.8 collective-permute-start.13
  73.4 3.1 %collective-permute-start.14 = (bf16[3,9,16,512]{3,2,1,0:T(8,128)(2,1)S(1)}, bf16[3,9,16,512]{3,2,1,0:T(8,128)(2,1)S(1)}, u32[]{:S(2)}, u32[]{:S(2)}) collective-permute-start(bf16[3,9,16,512]{3,2,1,0:T(8,128)(2,1)S(1)} %get-tuple-element.87.rest_1_), channel_id=1, source_target_pairs={{0,4},{4,0},{8,12},{12,8},{16,20},{20,16},{24,28},{28,24},{1,5},{5... | collective-permute-start | bytes 1327112 | tf_op jit(solution)/shard_map/ppermute | solution.py:937
  73.9 4.9 %collective-permute-start.15 = (bf16[3,9,16,512]{3,2,1,0:T(8,128)(2,1)S(1)}, bf16[3,9,16,512]{3,2,1,0:T(8,128)(2,1)S(1)}, u32[]{:S(2)}, u32[]{:S(2)}) collective-permute-start(bf16[3,9,16,512]{3,2,1,0:T(8,128)(2,1)S(1)} %get-tuple-element.88.rest_2_), channel_id=1, source_target_pairs={{0,4},{4,0},{8,12},{12,8},{16,20},{20,16},{24,28},{28,24},{1,5},{5... | collective-permute-start | bytes 1327112 | tf_op jit(solution)/shard_map/ppermute | solution.py:937
  73.9 4.9 %collective-permute-start.16 = (bf16[3,9,16,512]{3,2,1,0:T(8,128)(2,1)S(1)}, bf16[3,9,16,512]{3,2,1,0:T(8,128)(2,1)S(1)}, u32[]{:S(2)}, u32[]{:S(2)}) collective-permute-start(bf16[3,9,16,512]{3,2,1,0:T(8,128)(2,1)S(1)} %get-tuple-element.89.rest_3_), channel_id=1, source_target_pairs={{0,4},{4,0},{8,12},{12,8},{16,20},{20,16},{24,28},{28,24},{1,5},{5... | collective-permute-start | bytes 1327112 | tf_op jit(solution)/shard_map/ppermute | solution.py:937
  74.4 14.3 %collective-permute-start.17 = (bf16[128,512]{1,0:T(8,128)(2,1)S(1)}, bf16[128,512]{1,0:T(8,128)(2,1)S(1)}, u32[]{:S(2)}, u32[]{:S(2)}) collective-permute-start(bf16[128,512]{1,0:T(8,128)(2,1)S(1)} %get-tuple-element.94), channel_id=1, source_target_pairs={{0,1},{1,0},{2,3},{3,2},{4,5},{5,4},{6,7},{7,6},{8,9},{9,8},{10,11... | collective-permute-start | bytes 393224 | tf_op jit(solution)/shard_map/ppermute | solution.py:947
  75.2 13.5 %collective-permute-start.18 = (bf16[128,512]{1,0:T(8,128)(2,1)S(1)}, bf16[128,512]{1,0:T(8,128)(2,1)S(1)}, u32[]{:S(2)}, u32[]{:S(2)}) collective-permute-start(bf16[128,512]{1,0:T(8,128)(2,1)S(1)} %get-tuple-element.95), channel_id=1, source_target_pairs={{0,2},{1,3},{2,0},{3,1},{4,6},{5,7},{6,4},{7,5},{8,10},{9,11},{10,... | collective-permute-start | bytes 393224 | tf_op jit(solution)/shard_map/ppermute | solution.py:947
  76.5 12.2 %collective-permute-start.19 = (bf16[128,512]{1,0:T(8,128)(2,1)S(1)}, bf16[128,512]{1,0:T(8,128)(2,1)S(1)}, u32[]{:S(2)}, u32[]{:S(2)}) collective-permute-start(bf16[128,512]{1,0:T(8,128)(2,1)S(1)} %get-tuple-element.96), channel_id=1, source_target_pairs={{0,3},{1,2},{2,1},{3,0},{4,7},{5,6},{6,5},{7,4},{8,11},{9,10},{10,... | collective-permute-start | bytes 393224 | tf_op jit(solution)/shard_map/ppermute | solution.py:947
  124.6 4.6 %collective-permute-start.23 = (bf16[4,4,9,16,512]{4,3,2,1,0:T(8,128)(2,1)S(1)}, bf16[4,4,9,16,512]{4,3,2,1,0:T(8,128)(2,1)S(1)}, u32[]{:S(2)}, u32[]{:S(2)}) collective-permute-start(bf16[4,4,9,16,512]{4,3,2,1,0:T(8,128)(2,1)S(1)} %get-tuple-element.117), channel_id=1, source_target_pairs={{0,4},{4,0},{8,12},{12,8},{16,20},{20,16},{24,28},{28,24},{1,5},{5... | collective-permute-start | bytes 7077896 | tf_op jit(solution)/shard_map/ppermute | solution.py:937
  124.6 15.2 %collective-permute-start.20 = (bf16[128,384]{1,0:T(8,128)(2,1)S(1)}, bf16[128,384]{1,0:T(8,128)(2,1)S(1)}, u32[]{:S(2)}, u32[]{:S(2)}) collective-permute-start(bf16[128,384]{1,0:T(8,128)(2,1)S(1)} %get-tuple-element.106), channel_id=1, source_target_pairs={{0,1},{1,0},{2,3},{3,2},{4,5},{5,4},{6,7},{7,6},{8,9},{9,8},{10,11... | collective-permute-start | bytes 294920 | tf_op jit(solution)/shard_map/ppermute | solution.py:947
  124.9 14.9 %collective-permute-start.21 = (bf16[128,384]{1,0:T(8,128)(2,1)S(1)}, bf16[128,384]{1,0:T(8,128)(2,1)S(1)}, u32[]{:S(2)}, u32[]{:S(2)}) collective-permute-start(bf16[128,384]{1,0:T(8,128)(2,1)S(1)} %get-tuple-element.107), channel_id=1, source_target_pairs={{0,2},{1,3},{2,0},{3,1},{4,6},{5,7},{6,4},{7,5},{8,10},{9,11},{10,... | collective-permute-start | bytes 294920 | tf_op jit(solution)/shard_map/ppermute | solution.py:947
  126.4 13.4 %collective-permute-start.22 = (bf16[128,384]{1,0:T(8,128)(2,1)S(1)}, bf16[128,384]{1,0:T(8,128)(2,1)S(1)}, u32[]{:S(2)}, u32[]{:S(2)}) collective-permute-start(bf16[128,384]{1,0:T(8,128)(2,1)S(1)} %get-tuple-element.108), channel_id=1, source_target_pairs={{0,3},{1,2},{2,1},{3,0},{4,7},{5,6},{6,5},{7,4},{8,11},{9,10},{10,... | collective-permute-start | bytes 294920 | tf_op jit(solution)/shard_map/ppermute | solution.py:947
  129.7 10.2 %collective-permute-start.24 = (bf16[4,9,16,512]{3,2,1,0:T(8,128)(2,1)S(1)}, bf16[4,9,16,512]{3,2,1,0:T(8,128)(2,1)S(1)}, u32[]{:S(2)}, u32[]{:S(2)}) collective-permute-start(bf16[4,9,16,512]{3,2,1,0:T(8,128)(2,1)S(1)} %get-tuple-element.118.after), channel_id=1, source_target_pairs={{0,8},{4,20},{8,0},{12,28},{16,24},{20,4},{24,16},{28,12},{1,9},{5... | collective-permute-start | bytes 1769480 | tf_op jit(solution)/shard_map/ppermute | solution.py:944
  156.8 7.3 %collective-permute-start.28 = (bf16[4,4,9,16,256]{4,3,2,1,0:T(8,128)(2,1)S(1)}, bf16[4,4,9,16,256]{4,3,2,1,0:T(8,128)(2,1)S(1)}, u32[]{:S(2)}, u32[]{:S(2)}) collective-permute-start(bf16[4,4,9,16,256]{4,3,2,1,0:T(8,128)(2,1)S(1)} %get-tuple-element.129), channel_id=1, source_target_pairs={{0,4},{4,0},{8,12},{12,8},{16,20},{20,16},{24,28},{28,24},{1,5},{5... | collective-permute-start | bytes 3538952 | tf_op jit(solution)/shard_map/ppermute | solution.py:937
  157.0 16.2 %collective-permute-start.31 = (bf16[4,9,16,512]{3,2,1,0:T(8,128)(2,1)S(1)}, bf16[4,9,16,512]{3,2,1,0:T(8,128)(2,1)S(1)}, u32[]{:S(2)}, u32[]{:S(2)}) collective-permute-start(bf16[4,9,16,512]{3,2,1,0:T(8,128)(2,1)S(1)} %mid_sum_b.1), channel_id=1, source_target_pairs={{0,16},{4,12},{8,24},{12,4},{16,0},{20,28},{24,8},{28,20},{1,17},{... | collective-permute-start | bytes 1769480 | tf_op jit(solution)/shard_map/ppermute | solution.py:944
  157.9 15.3 %collective-permute-start.30 = (bf16[4,9,16,512]{3,2,1,0:T(8,128)(2,1)S(1)}, bf16[4,9,16,512]{3,2,1,0:T(8,128)(2,1)S(1)}, u32[]{:S(2)}, u32[]{:S(2)}) collective-permute-start(bf16[4,9,16,512]{3,2,1,0:T(8,128)(2,1)S(1)} %release.9), channel_id=1, source_target_pairs={{0,8},{4,20},{8,0},{12,28},{16,24},{20,4},{24,16},{28,12},{1,9},{5... | collective-permute-start | bytes 1769480 | tf_op jit(solution)/shard_map/ppermute | solution.py:944
  164.4 14.8 %collective-permute-start.29 = (bf16[8,9,16,256]{3,2,1,0:T(8,128)(2,1)S(1)}, bf16[8,9,16,256]{3,2,1,0:T(8,128)(2,1)S(1)}, u32[]{:S(2)}, u32[]{:S(2)}) collective-permute-start(bf16[8,9,16,256]{3,2,1,0:T(8,128)(2,1)S(1)} %get-tuple-element.131), channel_id=1, source_target_pairs={{0,8},{4,20},{8,0},{12,28},{16,24},{20,4},{24,16},{28,12},{1,9},{5... | collective-permute-start | bytes 1769480 | tf_op jit(solution)/shard_map/ppermute | solution.py:944
  165.9 9.5 %collective-permute-start.25 = (bf16[64,1536]{1,0:T(8,128)(2,1)S(1)}, bf16[64,1536]{1,0:T(8,128)(2,1)S(1)}, u32[]{:S(2)}, u32[]{:S(2)}) collective-permute-start(bf16[64,1536]{1,0:T(8,128)(2,1)S(1)} %get-tuple-element.124), channel_id=1, source_target_pairs={{0,1},{1,0},{2,3},{3,2},{4,5},{5,4},{6,7},{7,6},{8,9},{9,8},{10,11... | collective-permute-start | bytes 589832 | tf_op jit(solution)/shard_map/ppermute | solution.py:947
  166.2 11.4 %collective-permute-start.26 = (bf16[64,1536]{1,0:T(8,128)(2,1)S(1)}, bf16[64,1536]{1,0:T(8,128)(2,1)S(1)}, u32[]{:S(2)}, u32[]{:S(2)}) collective-permute-start(bf16[64,1536]{1,0:T(8,128)(2,1)S(1)} %get-tuple-element.125), channel_id=1, source_target_pairs={{0,2},{1,3},{2,0},{3,1},{4,6},{5,7},{6,4},{7,5},{8,10},{9,11},{10,... | collective-permute-start | bytes 589832 | tf_op jit(solution)/shard_map/ppermute | solution.py:947
  173.4 10.2 %collective-permute-start.33 = (bf16[2,9,16,512]{3,2,1,0:T(8,128)(2,1)S(1)}, bf16[2,9,16,512]{3,2,1,0:T(8,128)(2,1)S(1)}, u32[]{:S(2)}, u32[]{:S(2)}) collective-permute-start(bf16[2,9,16,512]{3,2,1,0:T(8,128)(2,1)S(1)} %get-tuple-element.138), channel_id=1, source_target_pairs={{0,1},{1,0},{2,3},{3,2},{4,5},{5,4},{6,7},{7,6},{8,9},{9,8},{10,11... | collective-permute-start | bytes 884744 | tf_op jit(solution)/shard_map/ppermute | solution.py:947
  179.3 6.8 %collective-permute-start.32 = (bf16[4,9,16,256]{3,2,1,0:T(8,128)(2,1)S(1)}, bf16[4,9,16,256]{3,2,1,0:T(8,128)(2,1)S(1)}, u32[]{:S(2)}, u32[]{:S(2)}) collective-permute-start(bf16[4,9,16,256]{3,2,1,0:T(8,128)(2,1)S(1)} %get-tuple-element.137), channel_id=1, source_target_pairs={{0,16},{4,12},{8,24},{12,4},{16,0},{20,28},{24,8},{28,20},{1,17},{... | collective-permute-start | bytes 884744 | tf_op jit(solution)/shard_map/ppermute | solution.py:944
  180.2 9.6 %collective-permute-start.27 = (bf16[64,1536]{1,0:T(8,128)(2,1)S(1)}, bf16[64,1536]{1,0:T(8,128)(2,1)S(1)}, u32[]{:S(2)}, u32[]{:S(2)}) collective-permute-start(bf16[64,1536]{1,0:T(8,128)(2,1)S(1)} %get-tuple-element.126), channel_id=1, source_target_pairs={{0,3},{1,2},{2,1},{3,0},{4,7},{5,6},{6,5},{7,4},{8,11},{9,10},{10,... | collective-permute-start | bytes 589832 | tf_op jit(solution)/shard_map/ppermute | solution.py:947
  186.1 7.4 %collective-permute-start.34 = (bf16[2,9,16,256]{3,2,1,0:T(8,128)(2,1)S(1)}, bf16[2,9,16,256]{3,2,1,0:T(8,128)(2,1)S(1)}, u32[]{:S(2)}, u32[]{:S(2)}) collective-permute-start(bf16[2,9,16,256]{3,2,1,0:T(8,128)(2,1)S(1)} %get-tuple-element.142), channel_id=1, source_target_pairs={{0,1},{1,0},{2,3},{3,2},{4,5},{5,4},{6,7},{7,6},{8,9},{9,8},{10,11... | collective-permute-start | bytes 442376 | tf_op jit(solution)/shard_map/ppermute | solution.py:947
  186.2 13.1 %collective-permute-start.36 = (bf16[1,9,16,512]{3,2,1,0:T(8,128)(2,1)S(1)}, bf16[1,9,16,512]{3,2,1,0:T(8,128)(2,1)S(1)}, u32[]{:S(2)}, u32[]{:S(2)}) collective-permute-start(bf16[1,9,16,512]{3,2,1,0:T(8,128)(2,1)S(1)} %get-tuple-element.145), channel_id=1, source_target_pairs={{0,2},{1,3},{2,0},{3,1},{4,6},{5,7},{6,4},{7,5},{8,10},{9,11},{10,... | collective-permute-start | bytes 442376 | tf_op jit(solution)/shard_map/ppermute | solution.py:947
  193.6 9.3 %collective-permute-start.35 = (bf16[1,9,16,256]{3,2,1,0:T(8,128)(2,1)S(1)}, bf16[1,9,16,256]{3,2,1,0:T(8,128)(2,1)S(1)}, u32[]{:S(2)}, u32[]{:S(2)}) collective-permute-start(bf16[1,9,16,256]{3,2,1,0:T(8,128)(2,1)S(1)} %get-tuple-element.144), channel_id=1, source_target_pairs={{0,2},{1,3},{2,0},{3,1},{4,6},{5,7},{6,4},{7,5},{8,10},{9,11},{10,... | collective-permute-start | bytes 221192 | tf_op jit(solution)/shard_map/ppermute | solution.py:947
  199.3 9.9 %collective-permute-start.40 = (bf16[9,16,512]{2,1,0:T(8,128)(2,1)S(1)}, bf16[9,16,512]{2,1,0:T(8,128)(2,1)S(1)}, u32[]{:S(2)}, u32[]{:S(2)}) collective-permute-start(bf16[9,16,512]{2,1,0:T(8,128)(2,1)S(1)} %mid_sum_3.1.rest_0_.refs_0_), channel_id=1, source_target_pairs={{0,16},{4,12},{8,24},{12,4},{16,0},{20,28},{24,8},{28,20},{1,17},{... | collective-permute-start | bytes 442376 | tf_op jit(solution)/shard_map/ppermute | solution.py:968
  200.5 8.7 %collective-permute-start.41 = (bf16[9,16,512]{2,1,0:T(8,128)(2,1)S(1)}, bf16[9,16,512]{2,1,0:T(8,128)(2,1)S(1)}, u32[]{:S(2)}, u32[]{:S(2)}) collective-permute-start(bf16[9,16,512]{2,1,0:T(8,128)(2,1)S(1)} %mid_sum_3.1.rest_0_.refs_0_), channel_id=1, source_target_pairs={{0,8},{4,20},{8,0},{12,28},{16,24},{20,4},{24,16},{28,12},{1,9},{5... | collective-permute-start | bytes 442376 | tf_op jit(solution)/shard_map/ppermute | solution.py:968
  201.4 7.9 %collective-permute-start.42 = (bf16[9,16,512]{2,1,0:T(8,128)(2,1)S(1)}, bf16[9,16,512]{2,1,0:T(8,128)(2,1)S(1)}, u32[]{:S(2)}, u32[]{:S(2)}) collective-permute-start(bf16[9,16,512]{2,1,0:T(8,128)(2,1)S(1)} %mid_sum_3.1.rest_0_.refs_0_), channel_id=1, source_target_pairs={{0,24},{4,28},{8,16},{12,20},{16,8},{20,12},{24,0},{28,4},{1,25},{... | collective-permute-start | bytes 442376 | tf_op jit(solution)/shard_map/ppermute | solution.py:968
  202.9 7.2 %collective-permute-start.37 = (bf16[9,16,256]{2,1,0:T(8,128)(2,1)S(1)}, bf16[9,16,256]{2,1,0:T(8,128)(2,1)S(1)}, u32[]{:S(2)}, u32[]{:S(2)}) collective-permute-start(bf16[9,16,256]{2,1,0:T(8,128)(2,1)S(1)} %in_sum_3.1.refs_0_), channel_id=1, source_target_pairs={{0,16},{4,12},{8,24},{12,4},{16,0},{20,28},{24,8},{28,20},{1,17},{... | collective-permute-start | bytes 221192 | tf_op jit(solution)/shard_map/ppermute | solution.py:944
  204.1 6.1 %collective-permute-start.38 = (bf16[9,16,256]{2,1,0:T(8,128)(2,1)S(1)}, bf16[9,16,256]{2,1,0:T(8,128)(2,1)S(1)}, u32[]{:S(2)}, u32[]{:S(2)}) collective-permute-start(bf16[9,16,256]{2,1,0:T(8,128)(2,1)S(1)} %in_sum_3.1.refs_0_), channel_id=1, source_target_pairs={{0,8},{4,20},{8,0},{12,28},{16,24},{20,4},{24,16},{28,12},{1,9},{5... | collective-permute-start | bytes 221192 | tf_op jit(solution)/shard_map/ppermute | solution.py:944
  210.2 3.0 %collective-permute-start.43 = (bf16[4,9,16,512]{3,2,1,0:T(8,128)(2,1)S(1)}, bf16[4,9,16,512]{3,2,1,0:T(8,128)(2,1)S(1)}, u32[]{:S(2)}, u32[]{:S(2)}) collective-permute-start(bf16[4,9,16,512]{3,2,1,0:T(8,128)(2,1)S(1)} %mid_stack.1.mine), channel_id=1, source_target_pairs={{0,4},{4,0},{8,12},{12,8},{16,20},{20,16},{24,28},{28,24},{1,5},{5... | collective-permute-start | bytes 1769480 | tf_op jit(solution)/shard_map/ppermute | solution.py:937
  210.8 4.4 %collective-permute-start.39 = (bf16[9,16,256]{2,1,0:T(8,128)(2,1)S(1)}, bf16[9,16,256]{2,1,0:T(8,128)(2,1)S(1)}, u32[]{:S(2)}, u32[]{:S(2)}) collective-permute-start(bf16[9,16,256]{2,1,0:T(8,128)(2,1)S(1)} %collective-permute-done.37.refs_4_.refs_1_), channel_id=1, source_target_pairs={{0,8},{4,20},{8,0},{12,28},{16,24},{20,4},{24,16},{28,12},{1,9},{5... | collective-permute-start | bytes 221192 | tf_op jit(solution)/shard_map/ppermute | solution.py:944
  215.2 1.6 collective-permute-start.44

commit v4 on v3

--- a/solution.py
+++ b/solution.py
@@ -1070,7 +1070,7 @@
             mid = Chain(stay_mid, go_mid, g.cm, "mid")
             for i in range(g.turns):
                 mid.turn(i, stay_in)
-        gates = [parts[1 : nch - 1], [pooled_done]]
+        gates = [parts[2 : nch - 1], [pooled_done]]
         at = mid.stay
         for i in range(g.turns):
             at = inner.turn(i, at, *(gates[i] if i < 2 else []))
@@ -1083,7 +1083,7 @@
         inner.rest()
         mid.rest()
         planes_in = links.gather_planes(inner.stay)
-        weight_mid_grad, mid_done = mid.out(links.gather_direct(mid.stay), *planes_in[1:3])
+        weight_mid_grad, mid_done = mid.out(links.gather_direct(mid.stay), *planes_in[1:3], parts[1])
         weight_in_grad, _ = inner.out(planes_in, mid_done, spectra_done)
         z = lax.axis_index("chan")
 

time: 218 us -> 217 us (level)
    ppermute x16, waiting for transfers between devices: 27.5 us -> 24.1 us  [chan(): return lax.ppermute(x, 'chan', [(i, i ^ k) for i in range(self.g.nch)])]
    ppermute x14, waiting for transfers between devices: 22.9 us -> 25.8 us  [plane(): lax.ppermute(x, 'dp', [(i, i ^ 2 * g.mask(i & 1, turn)) for i in range(g....]
  transfers between devices with their start and end apart: 46 -> 46, of which waited for: 21 -> 20; matrix products, arithmetic and copies ran while one was open for 1% -> 1% of each run, Pallas kernels for 18% -> 18%
where the time goes in v4:
time: 217 us; the launch traced here: 216 us
  Pallas kernels  63.4 us (29%)
  waiting for transfers between devices  56.6 us (26%)
  blocking collectives  46.2 us (21%)
  starting transfers between devices  45.7 us (21%)
  local copies, waits for them, and re-layouts  3.46 us (2%)
    pallas_call x23, Pallas kernels, call(): pl.pallas_call(body, out_shape=[pltpu.VMEM(o.shape, o.dtype) if isinstanc...  57 us
    all_to_all x4, blocking collectives, everyone(): return lax.all_to_all(x, ('dp', 'chan'), 0, 0)  46.2 us
    ppermute x14, waiting for transfers between devices, plane(): lax.ppermute(x, 'dp', [(i, i ^ 2 * g.mask(i & 1, turn)) for i in range(g....  25.8 us
    ppermute x16, waiting for transfers between devices, chan(): return lax.ppermute(x, 'chan', [(i, i ^ k) for i in range(self.g.nch)])  24.1 us
    ppermute x16, starting transfers between devices, chan(): return lax.ppermute(x, 'chan', [(i, i ^ k) for i in range(self.g.nch)])  18.3 us
    ppermute x14, starting transfers between devices, plane(): lax.ppermute(x, 'dp', [(i, i ^ 2 * g.mask(i & 1, turn)) for i in range(g....  14.9 us
    all_to_all x1, starting transfers between devices, body(): maps = lax.all_to_all(release_far([pieces_in], cells), 'chan', 0, 0)  6.3 us
  transfers between devices with their start and end apart: 46, of which 20 were waited for; matrix products, arithmetic and copies ran while one was open for 1% of the time, Pallas kernels for 18%

profile of v4, /device:TPU:0, one launch (start us, length us, event | category | flops | bytes accessed | tf_op | source)
XLA Modules:
  0.0 216.4 jit_solution(4279972299899733675)
XLA Ops:
  0.6 1.0 cut_weights.1.after
  1.6 3.1 %collective-permute-start = (bf16[9,16,768]{2,1,0:T(8,128)(2,1)S(1)}, bf16[9,16,768]{2,1,0:T(8,128)(2,1)S(1)}, u32[]{:S(2)}, u32[]{:S(2)}) collective-permute-start(bf16[9,16,768]{2,1,0:T(8,128)(2,1)S(1)} %cut_weights.1.after), channel_id=1, source_target_pairs={{0,1},{1,0},{2,3},{3,2},{4,5},{5,4},{6,7},{7,6},{8,9},{9,8},{10,11... | collective-permute-start | bytes 663560 | tf_op jit(solution)/shard_map/ppermute | solution.py:947
  4.7 2.6 %collective-permute-start.1 = (bf16[9,16,768]{2,1,0:T(8,128)(2,1)S(1)}, bf16[9,16,768]{2,1,0:T(8,128)(2,1)S(1)}, u32[]{:S(2)}, u32[]{:S(2)}) collective-permute-start(bf16[9,16,768]{2,1,0:T(8,128)(2,1)S(1)} %cut_weights.1.after), channel_id=1, source_target_pairs={{0,2},{1,3},{2,0},{3,1},{4,6},{5,7},{6,4},{7,5},{8,10},{9,11},{10,... | collective-permute-start | bytes 663560 | tf_op jit(solution)/shard_map/ppermute | solution.py:947
  7.3 2.0 cut_maps.1.after.refs_1_
  9.3 1.1 copy-done
  10.5 1.1 cut_cotangent.1
  11.6 0.6 copy-done.5
  12.3 1.8 collective-permute-done.rest_0_
  14.1 9.3 %collective-permute-done.1.rest_1_ = bf16[9,16,768]{2,1,0:T(8,128)(2,1)S(1)} collective-permute-done((bf16[9,16,768]{2,1,0:T(8,128)(2,1)S(1)}, bf16[9,16,768]{2,1,0:T(8,128)(2,1)S(1)}, u32[]{:S(2)}, u32[]{:S(2)}) %collective-permute-start.1) | collective-permute-done | bytes 221216 | tf_op jit(solution)/shard_map/ppermute | solution.py:947
  23.5 0.7 sort_pieces.1
  24.2 6.3 %all-to-all-start = ((bf16[4,64,1664]{2,1,0:T(8,128)(2,1)}), bf16[4,64,1664]{2,1,0:T(8,128)(2,1)S(1)}, u32[]{:S(2)}, u32[]{:S(2)}) async-start(bf16[4,64,1664]{2,1,0:T(8,128)(2,1)} %release_far.1), calls=%async_computation | async-start | bytes 1703936 | tf_op jit(solution)/shard_map/all_to_all | solution.py:997
  30.5 1.5 collective-permute-start.3
  32.6 1.5 collective-permute-start.11
  34.6 4.6 %collective-permute-done.3.rest_1_ = bf16[3,9,16,256]{3,2,1,0:T(8,128)(2,1)} collective-permute-done((bf16[3,9,16,256]{3,2,1,0:T(8,128)(2,1)}, bf16[3,9,16,256]{3,2,1,0:T(8,128)(2,1)}, u32[]{:S(2)}, u32[]{:S(2)}) %collective-permute-start.3) | collective-permute-done | bytes 221216 | tf_op jit(solution)/shard_map/ppermute | solution.py:944
  39.2 1.5 collective-permute-start.5
  40.7 5.4 %collective-permute-done.4.rest_2_ = bf16[3,9,16,256]{3,2,1,0:T(8,128)(2,1)} collective-permute-done((bf16[3,9,16,256]{3,2,1,0:T(8,128)(2,1)}, bf16[3,9,16,256]{3,2,1,0:T(8,128)(2,1)}, u32[]{:S(2)}, u32[]{:S(2)}) %collective-permute-start.4) | collective-permute-done | bytes 221216 | tf_op jit(solution)/shard_map/ppermute | solution.py:944
  46.1 2.3 %collective-permute-done.5.rest_3_ = bf16[3,9,16,256]{3,2,1,0:T(8,128)(2,1)} collective-permute-done((bf16[3,9,16,256]{3,2,1,0:T(8,128)(2,1)}, bf16[3,9,16,256]{3,2,1,0:T(8,128)(2,1)}, u32[]{:S(2)}, u32[]{:S(2)}) %collective-permute-start.5) | collective-permute-done | bytes 221216 | tf_op jit(solution)/shard_map/ppermute | solution.py:944
  48.4 1.3 collective-permute-start.8
  49.8 1.1 all-to-all-done.maps.refs_0_
  50.9 1.5 collective-permute-start.12
  52.5 1.7 join_in.1.w
  54.2 5.1 %first_conv.1 = (f32[8,208,512]{2,1,0:T(8,128)S(1)}, bf16[8,208,768]{2,1,0:T(8,128)(2,1)S(1)}, f32[1,1664]{1,0:T(1,128)S(1)}) custom-call(s32[2]{0:T(128)S(1)} %copy-done.7, f32[4,128]{1,0:T(4,128)S(1)} %pad_maximum_fusion.gains, bf16[9,512,256]{2,1,0:T(8,128)(2,1)S(1)} %join_in.1.w, bf16[4,64,1664]{2,1,0:T(8,128)(2,1)S(1)} %all-to-all-done.maps.refs_0_), custom_call_target="tpu_custom_call" | custom-call | flops 3925868544 | bytes 10485760 | tf_op jit(solution)/shard_map/first_conv/pallas_call | solution.py:90
  59.4 14.0 %all_to_all.25.refs_0_.got = f32[32,1,1664]{2,1,0:T(1,128)S(1)} all-to-all(f32[32,1,1664]{2,1,0:T(1,128)S(1)} %fan.3), channel_id=1, replica_groups=mesh['dp'=8,'chan'=4] {'dp','chan'}, dimensions={0} | all-to-all | bytes 425984 | tf_op jit(solution)/shard_map/all_to_all | solution.py:972
  74.6 0.6 collective-permute-done.13.rest_4_
  75.2 1.3 collective-permute-start.18
  76.5 2.3 %collective-permute-start.19 = (bf16[128,512]{1,0:T(8,128)(2,1)S(1)}, bf16[128,512]{1,0:T(8,128)(2,1)S(1)}, u32[]{:S(2)}, u32[]{:S(2)}) collective-permute-start(bf16[128,512]{1,0:T(8,128)(2,1)S(1)} %get-tuple-element.96), channel_id=1, source_target_pairs={{0,3},{1,2},{2,1},{3,0},{4,7},{5,6},{6,5},{7,4},{8,11},{9,10},{10,... | collective-permute-start | bytes 393224 | tf_op jit(solution)/shard_map/ppermute | solution.py:947
  79.2 9.5 %second_conv.1 = (f32[8,208,512]{2,1,0:T(8,128)S(1)}, bf16[8,208,1536]{2,1,0:T(8,128)(2,1)S(1)}, f32[16,512]{1,0:T(8,128)S(1)}, f32[1,1024]{1,0:T(1,128)S(1)}, f32[1,128]{1,0:T(1,128)S(1)}) custom-call(s32[2]{0:T(128)S(1)} %copy-done.7, f32[32,1,1664]{2,1,0:T(1,128)S(1)} %all_to_all.25.refs_0_.got, f32[8,208,512]{2,1,0:T(8,128)S(1)} %get-tuple-element.85.pre1.pre, ...), custom_call_target="tpu_custom_call" | custom-call | flops 7851737088 | bytes 17825792 | tf_op jit(solution)/shard_map/second_conv/pallas_call | solution.py:90
  88.8 11.0 %all_to_all.26.got = f32[32,1,1024]{2,1,0:T(1,128)S(1)} all-to-all(f32[32,1,1024]{2,1,0:T(1,128)S(1)} %fan.4), channel_id=1, replica_groups=mesh['dp'=8,'chan'=4] {'dp','chan'}, dimensions={0} | all-to-all | bytes 262144 | tf_op jit(solution)/shard_map/all_to_all | solution.py:972
  99.7 5.2 %pool.1 = (bf16[128,384]{1,0:T(8,128)(2,1)S(1)}, bf16[128,384]{1,0:T(8,128)(2,1)S(1)}, bf16[128,384]{1,0:T(8,128)(2,1)S(1)}, bf16[128,384]{1,0:T(8,128)(2,1)S(1)...) custom-call(s32[2]{0:T(128)S(1)} %copy-done.7, ...), custom_call_target="tpu_custom_call" | custom-call | flops 4000000000 | bytes 8388608 | tf_op jit(solution)/shard_map/pool/pallas_call | solution.py:90
  105.0 10.1 %all_to_all.27.refs_0_.got.after = f32[32,1,1024]{2,1,0:T(1,128)S(1)} all-to-all(f32[32,1,1024]{2,1,0:T(1,128)S(1)} %get-tuple-element.100), channel_id=1, replica_groups=mesh['dp'=8,'chan'=4] {'dp','chan'}, dimensions={0} | all-to-all | bytes 262144 | tf_op jit(solution)/shard_map/all_to_all | solution.py:972
  115.1 9.5 %weight_mid_terms.1 = (bf16[8,208,512]{2,1,0:T(8,128)(2,1)S(1)}, f32[8,512]{1,0:T(8,128)S(1)}, f32[8,128]{1,0:T(8,128)}, bf16[2,4,4,9,16,512]{5,4,3,2,1,0:T(8,128)(2,1)S(1)}, bf16[4,4,9,16,512]{4,3,2,1,0:T(8,128)(2,1)S(1)}) custom-call(s32[2]{0:T(128)S(1)} %copy-done.7, f32[32,1,1024]{2,1,0:T(1,128)S(1)} %all_to_all.27.refs_0_.got.after, ...), custom_call_target="tpu_custom_call" | custom-call | flops 7851737088 | bytes 15728640 | tf_op jit(solution)/shard_map/weight_mid_terms/pallas_call | solution.py:90
  124.9 1.5 collective-permute-start.21
  126.4 2.7 %collective-permute-start.22 = (bf16[128,384]{1,0:T(8,128)(2,1)S(1)}, bf16[128,384]{1,0:T(8,128)(2,1)S(1)}, u32[]{:S(2)}, u32[]{:S(2)}) collective-permute-start(bf16[128,384]{1,0:T(8,128)(2,1)S(1)} %get-tuple-element.108), channel_id=1, source_target_pairs={{0,3},{1,2},{2,1},{3,0},{4,7},{5,6},{6,5},{7,4},{8,11},{9,10},{10,... | collective-permute-start | bytes 294920 | tf_op jit(solution)/shard_map/ppermute | solution.py:947
  129.7 0.8 collective-permute-start.24
  130.5 9.3 %second_back.1 = (f32[8,208,512]{2,1,0:T(8,128)S(1)}, f32[1,1280]{1,0:T(1,128)S(1)}) custom-call(s32[2]{0:T(128)S(1)} %copy-done.7, f32[16,512]{1,0:T(8,128)S(1)} %get-tuple-element.110.table, bf16[8,208,512]{2,1,0:T(8,128)(2,1)S(1)} %get-tuple-element.113.grad, f32[8,208,512]{2,1,0:T(8,128)S(1)} %get-tuple-element.85.pre1.pre, ...), custom_call_target="tpu_custom_call" | custom-call | flops 7851737088 | bytes 20971520 | tf_op jit(solution)/shard_map/second_back/pallas_call | solution.py:90
  139.9 11.1 %all_to_all.28.got.after.refs_0_.rest_2_ = f32[32,1,1280]{2,1,0:T(1,128)S(1)} all-to-all(f32[32,1,1280]{2,1,0:T(1,128)S(1)} %fan.5), channel_id=1, replica_groups=mesh['dp'=8,'chan'=4] {'dp','chan'}, dimensions={0} | all-to-all | bytes 327680 | tf_op jit(solution)/shard_map/all_to_all | solution.py:972
  151.0 5.8 %weight_in_terms.1 = (bf16[8,208,512]{2,1,0:T(8,128)(2,1)S(1)}, f32[8,512]{1,0:T(8,128)S(1)}, f32[8,128]{1,0:T(8,128)S(1)}, bf16[2,4,4,9,16,256]{5,4,3,2,1,0:T(8,128)(2,1)S(1)}, bf16[4,4,9,16,256]{4,3,2,1,0:T(8,128)(2,1)S(1)}) custom-call(s32[2]{0:T(128)S(1)} %copy-done.7, f32[32,1,1280]{2,1,0:T(1,128)S(1)} %all_to_all.28.got.after.refs_0_.rest_2_, ...), custom_call_target="tpu_custom_call" | custom-call | flops 3925868544 | bytes 15728640 | tf_op jit(solution)/shard_map/weight_in_terms/pallas_call | solution.py:90
  157.0 0.9 collective-permute-start.31
  158.4 5.6 %spectra_back.1 = (bf16[64,1536]{1,0:T(8,128)(2,1)S(1)}, bf16[64,1536]{1,0:T(8,128)(2,1)S(1)}, bf16[64,1536]{1,0:T(8,128)(2,1)S(1)}, bf16[64,1536]{1,0:T(8,128)(2,1)S(1)}) custom-call(s32[2]{0:T(128)S(1)} %copy-done.7, bf16[8,208,512]{2,1,0:T(8,128)(2,1)S(1)} %get-tuple-element.122.grad.after, bf16[8,208,512]{2,1,0:T(8,128)(2,1)S(1)} %get-tuple-element.122.grad.after, ...), custom_call_target="tpu_custom_call" | custom-call | flops 3925868544 | bytes 5242880 | tf_op jit(solution)/shard_map/spectra_back/pallas_call | solution.py:90
  164.4 1.6 collective-permute-start.29
  166.2 7.0 %collective-permute-done.31.rest_2_ = bf16[4,9,16,512]{3,2,1,0:T(8,128)(2,1)S(1)} collective-permute-done((bf16[4,9,16,512]{3,2,1,0:T(8,128)(2,1)S(1)}, bf16[4,9,16,512]{3,2,1,0:T(8,128)(2,1)S(1)}, u32[]{:S(2)}, u32[]{:S(2)}) %collective-permute-start.31) | collective-permute-done | bytes 589856 | tf_op jit(solution)/shard_map/ppermute | solution.py:944
  173.7 3.1 %collective-permute-done.26.rest_2_.rest_1_ = bf16[64,1536]{1,0:T(8,128)(2,1)S(1)} collective-permute-done((bf16[64,1536]{1,0:T(8,128)(2,1)S(1)}, bf16[64,1536]{1,0:T(8,128)(2,1)S(1)}, u32[]{:S(2)}, u32[]{:S(2)}) %collective-permute-start.26) | collective-permute-done | bytes 196640 | tf_op jit(solution)/shard_map/ppermute | solution.py:947
  176.8 2.3 %collective-permute-done.29.got = bf16[8,9,16,256]{3,2,1,0:T(8,128)(2,1)S(1)} collective-permute-done((bf16[8,9,16,256]{3,2,1,0:T(8,128)(2,1)S(1)}, bf16[8,9,16,256]{3,2,1,0:T(8,128)(2,1)S(1)}, u32[]{:S(2)}, u32[]{:S(2)}) %collective-permute-start.29) | collective-permute-done | bytes 589856 | tf_op jit(solution)/shard_map/ppermute | solution.py:944
  179.3 0.9 collective-permute-start.32
  180.2 1.3 collective-permute-start.27
  181.5 0.8 place_pooled.1
  182.3 0.7 collective-permute-done.33.got
  183.2 2.9 %collective-permute-done.32.got = bf16[4,9,16,256]{3,2,1,0:T(8,128)(2,1)S(1)} collective-permute-done((bf16[4,9,16,256]{3,2,1,0:T(8,128)(2,1)S(1)}, bf16[4,9,16,256]{3,2,1,0:T(8,128)(2,1)S(1)}, u32[]{:S(2)}, u32[]{:S(2)}) %collective-permute-start.32) | collective-permute-done | bytes 294944 | tf_op jit(solution)/shard_map/ppermute | solution.py:944
  186.2 1.9 collective-permute-start.36
  188.1 0.5 collective-permute-start.25
  188.6 1.1 collective-permute-done.27.rest_3_.rest_1_
  189.7 4.4 %collective-permute-done.34.got = bf16[2,9,16,256]{3,2,1,0:T(8,128)(2,1)S(1)} collective-permute-done((bf16[2,9,16,256]{3,2,1,0:T(8,128)(2,1)S(1)}, bf16[2,9,16,256]{3,2,1,0:T(8,128)(2,1)S(1)}, u32[]{:S(2)}, u32[]{:S(2)}) %collective-permute-start.34) | collective-permute-done | bytes 147488 | tf_op jit(solution)/shard_map/ppermute | solution.py:947
  194.3 3.6 %collective-permute-done.36.got = bf16[1,9,16,512]{3,2,1,0:T(8,128)(2,1)S(1)} collective-permute-done((bf16[1,9,16,512]{3,2,1,0:T(8,128)(2,1)S(1)}, bf16[1,9,16,512]{3,2,1,0:T(8,128)(2,1)S(1)}, u32[]{:S(2)}, u32[]{:S(2)}) %collective-permute-start.36) | collective-permute-done | bytes 147488 | tf_op jit(solution)/shard_map/ppermute | solution.py:947
  197.9 1.2 collective-permute-start.40
  199.0 0.9 collective-permute-start.41
  199.9 1.5 collective-permute-start.42
  201.5 1.2 collective-permute-start.37
  202.6 0.9 collective-permute-start.38
  203.5 4.3 %collective-permute-done.40.refs_1_ = bf16[9,16,512]{2,1,0:T(8,128)(2,1)S(1)} collective-permute-done((bf16[9,16,512]{2,1,0:T(8,128)(2,1)S(1)}, bf16[9,16,512]{2,1,0:T(8,128)(2,1)S(1)}, u32[]{:S(2)}, u32[]{:S(2)}) %collective-permute-start.40) | collective-permute-done | bytes 147488 | tf_op jit(solution)/shard_map/ppermute | solution.py:968
  207.8 0.8 collective-permute-done.37.refs_4_.refs_1_
  209.3 1.1 collective-permute-start.39
  210.4 1.3 place_spectra.1
  211.7 1.6 mid_out.1
  215.3 1.1 in_out.1
  (101 shorter events, 8.7 us)
Async XLA Ops:
  1.6 12.5 %collective-permute-start = (bf16[9,16,768]{2,1,0:T(8,128)(2,1)S(1)}, bf16[9,16,768]{2,1,0:T(8,128)(2,1)S(1)}, u32[]{:S(2)}, u32[]{:S(2)}) collective-permute-start(bf16[9,16,768]{2,1,0:T(8,128)(2,1)S(1)} %cut_weights.1.after), channel_id=1, source_target_pairs={{0,1},{1,0},{2,3},{3,2},{4,5},{5,4},{6,7},{7,6},{8,9},{9,8},{10,11... | collective-permute-start | bytes 663560 | tf_op jit(solution)/shard_map/ppermute | solution.py:947
  4.7 18.7 %collective-permute-start.1 = (bf16[9,16,768]{2,1,0:T(8,128)(2,1)S(1)}, bf16[9,16,768]{2,1,0:T(8,128)(2,1)S(1)}, u32[]{:S(2)}, u32[]{:S(2)}) collective-permute-start(bf16[9,16,768]{2,1,0:T(8,128)(2,1)S(1)} %cut_weights.1.after), channel_id=1, source_target_pairs={{0,2},{1,3},{2,0},{3,1},{4,6},{5,7},{6,4},{7,5},{8,10},{9,11},{10,... | collective-permute-start | bytes 663560 | tf_op jit(solution)/shard_map/ppermute | solution.py:947
  7.3 16.1 %collective-permute-start.2 = (bf16[9,16,768]{2,1,0:T(8,128)(2,1)S(1)}, bf16[9,16,768]{2,1,0:T(8,128)(2,1)S(1)}, u32[]{:S(2)}, u32[]{:S(2)}) collective-permute-start(bf16[9,16,768]{2,1,0:T(8,128)(2,1)S(1)} %cut_weights.1.after), channel_id=1, source_target_pairs={{0,3},{1,2},{2,1},{3,0},{4,7},{5,6},{6,5},{7,4},{8,11},{9,10},{10,... | collective-permute-start | bytes 663560 | tf_op jit(solution)/shard_map/ppermute | solution.py:947
  9.3 1.2 copy-start
  11.6 0.7 copy-start.5
  12.3 11.9 %copy-start.3 = (bf16[128,512]{1,0:T(8,128)(2,1)}, bf16[128,512]{1,0:T(8,128)(2,1)S(1)}, u32[]{:S(2)}) copy-start(bf16[128,512]{1,0:T(8,128)(2,1)S(1)} %get-tuple-element.92.refs_3_) | copy-start | bytes 393220
  24.2 28.2 %copy-start.8 = (f32[128]{0:T(128)S(1)}, f32[128]{0:T(128)}, u32[]{:S(2)}) copy-start(f32[128]{0:T(128)} %param.16) | copy-start | bytes 1540
  24.2 28.2 %copy-start.9 = (f32[128]{0:T(128)S(1)}, f32[128]{0:T(128)}, u32[]{:S(2)}) copy-start(f32[128]{0:T(128)} %param.15) | copy-start | bytes 1540
  24.2 28.2 %copy-start.10 = (f32[128]{0:T(128)S(1)}, f32[128]{0:T(128)}, u32[]{:S(2)}) copy-start(f32[128]{0:T(128)} %param.13) | copy-start | bytes 1540
  24.2 28.2 %copy-start.11 = (f32[128]{0:T(128)S(1)}, f32[128]{0:T(128)}, u32[]{:S(2)}) copy-start(f32[128]{0:T(128)} %param.12) | copy-start | bytes 1540
  24.2 28.3 %copy-start.2 = (bf16[9,128,256]{2,1,0:T(8,128)(2,1)S(1)}, bf16[9,128,256]{2,1,0:T(8,128)(2,1)}, u32[]{:S(2)}) copy-start(bf16[9,128,256]{2,1,0:T(8,128)(2,1)} %own.2) | copy-start | bytes 1769476
  24.2 26.7 %all-to-all-start = ((bf16[4,64,1664]{2,1,0:T(8,128)(2,1)}), bf16[4,64,1664]{2,1,0:T(8,128)(2,1)S(1)}, u32[]{:S(2)}, u32[]{:S(2)}) async-start(bf16[4,64,1664]{2,1,0:T(8,128)(2,1)} %release_far.1), calls=%async_computation | async-start | bytes 1703936 | tf_op jit(solution)/shard_map/all_to_all | solution.py:997
  30.5 8.7 %collective-permute-start.3 = (bf16[3,9,16,256]{3,2,1,0:T(8,128)(2,1)}, bf16[3,9,16,256]{3,2,1,0:T(8,128)(2,1)}, u32[]{:S(2)}, u32[]{:S(2)}) collective-permute-start(bf16[3,9,16,256]{3,2,1,0:T(8,128)(2,1)} %get-tuple-element.82.rest_0_.refs_0_), channel_id=1, source_target_pairs={{0,16},{4,12},{8,24},{12,4},{16,0},{20,28},{24,8},{28,20},{1,17},{... | collective-permute-start | bytes 663560 | tf_op jit(solution)/shard_map/ppermute | solution.py:944
  32.1 17.7 %collective-permute-start.10 = (bf16[3,9,16,512]{3,2,1,0:T(8,128)(2,1)S(1)}, bf16[3,9,16,512]{3,2,1,0:T(8,128)(2,1)S(1)}, u32[]{:S(2)}, u32[]{:S(2)}) collective-permute-start(bf16[3,9,16,512]{3,2,1,0:T(8,128)(2,1)S(1)} %get-tuple-element.84.refs_1_), channel_id=1, source_target_pairs={{0,16},{4,12},{8,24},{12,4},{16,0},{20,28},{24,8},{28,20},{1,17},{... | collective-permute-start | bytes 1327112 | tf_op jit(solution)/shard_map/ppermute | solution.py:944
  32.6 17.2 %collective-permute-start.11 = (bf16[3,9,16,512]{3,2,1,0:T(8,128)(2,1)S(1)}, bf16[3,9,16,512]{3,2,1,0:T(8,128)(2,1)S(1)}, u32[]{:S(2)}, u32[]{:S(2)}) collective-permute-start(bf16[3,9,16,512]{3,2,1,0:T(8,128)(2,1)S(1)} %get-tuple-element.84.refs_1_), channel_id=1, source_target_pairs={{0,8},{4,20},{8,0},{12,28},{16,24},{20,4},{24,16},{28,12},{1,9},{5... | collective-permute-start | bytes 1327112 | tf_op jit(solution)/shard_map/ppermute | solution.py:944
  34.1 12.0 %collective-permute-start.4 = (bf16[3,9,16,256]{3,2,1,0:T(8,128)(2,1)}, bf16[3,9,16,256]{3,2,1,0:T(8,128)(2,1)}, u32[]{:S(2)}, u32[]{:S(2)}) collective-permute-start(bf16[3,9,16,256]{3,2,1,0:T(8,128)(2,1)} %get-tuple-element.82.rest_0_.refs_0_), channel_id=1, source_target_pairs={{0,8},{4,20},{8,0},{12,28},{16,24},{20,4},{24,16},{28,12},{1,9},{5... | collective-permute-start | bytes 663560 | tf_op jit(solution)/shard_map/ppermute | solution.py:944
  39.2 9.3 %collective-permute-start.5 = (bf16[3,9,16,256]{3,2,1,0:T(8,128)(2,1)}, bf16[3,9,16,256]{3,2,1,0:T(8,128)(2,1)}, u32[]{:S(2)}, u32[]{:S(2)}) collective-permute-start(bf16[3,9,16,256]{3,2,1,0:T(8,128)(2,1)} %collective-permute-done.3.rest_1_), channel_id=1, source_target_pairs={{0,8},{4,20},{8,0},{12,28},{16,24},{20,4},{24,16},{28,12},{1,9},{5... | collective-permute-start | bytes 663560 | tf_op jit(solution)/shard_map/ppermute | solution.py:944
  40.7 11.8 %collective-permute-start.6 = (bf16[3,9,16,256]{3,2,1,0:T(8,128)(2,1)}, bf16[3,9,16,256]{3,2,1,0:T(8,128)(2,1)}, u32[]{:S(2)}, u32[]{:S(2)}) collective-permute-start(bf16[3,9,16,256]{3,2,1,0:T(8,128)(2,1)} %get-tuple-element.82.rest_0_.refs_0_), channel_id=1, source_target_pairs={{0,4},{4,0},{8,12},{12,8},{16,20},{20,16},{24,28},{28,24},{1,5},{5... | collective-permute-start | bytes 663560 | tf_op jit(solution)/shard_map/ppermute | solution.py:937
  46.1 6.4 %collective-permute-start.7 = (bf16[3,9,16,256]{3,2,1,0:T(8,128)(2,1)}, bf16[3,9,16,256]{3,2,1,0:T(8,128)(2,1)}, u32[]{:S(2)}, u32[]{:S(2)}) collective-permute-start(bf16[3,9,16,256]{3,2,1,0:T(8,128)(2,1)} %collective-permute-done.3.rest_1_), channel_id=1, source_target_pairs={{0,4},{4,0},{8,12},{12,8},{16,20},{20,16},{24,28},{28,24},{1,5},{5... | collective-permute-start | bytes 663560 | tf_op jit(solution)/shard_map/ppermute | solution.py:937
  48.4 4.0 %collective-permute-start.8 = (bf16[3,9,16,256]{3,2,1,0:T(8,128)(2,1)}, bf16[3,9,16,256]{3,2,1,0:T(8,128)(2,1)}, u32[]{:S(2)}, u32[]{:S(2)}) collective-permute-start(bf16[3,9,16,256]{3,2,1,0:T(8,128)(2,1)} %collective-permute-done.4.rest_2_), channel_id=1, source_target_pairs={{0,4},{4,0},{8,12},{12,8},{16,20},{20,16},{24,28},{28,24},{1,5},{5... | collective-permute-start | bytes 663560 | tf_op jit(solution)/shard_map/ppermute | solution.py:937
  49.7 2.8 %collective-permute-start.9 = (bf16[3,9,16,256]{3,2,1,0:T(8,128)(2,1)}, bf16[3,9,16,256]{3,2,1,0:T(8,128)(2,1)}, u32[]{:S(2)}, u32[]{:S(2)}) collective-permute-start(bf16[3,9,16,256]{3,2,1,0:T(8,128)(2,1)} %collective-permute-done.5.rest_3_), channel_id=1, source_target_pairs={{0,4},{4,0},{8,12},{12,8},{16,20},{20,16},{24,28},{28,24},{1,5},{5... | collective-permute-start | bytes 663560 | tf_op jit(solution)/shard_map/ppermute | solution.py:937
  50.9 8.4 %collective-permute-start.12 = (bf16[3,9,16,512]{3,2,1,0:T(8,128)(2,1)S(1)}, bf16[3,9,16,512]{3,2,1,0:T(8,128)(2,1)S(1)}, u32[]{:S(2)}, u32[]{:S(2)}) collective-permute-start(bf16[3,9,16,512]{3,2,1,0:T(8,128)(2,1)S(1)} %release.5), channel_id=1, source_target_pairs={{0,8},{4,20},{8,0},{12,28},{16,24},{20,4},{24,16},{28,12},{1,9},{5... | collective-permute-start | bytes 1327112 | tf_op jit(solution)/shard_map/ppermute | solution.py:944
  52.4 1.8 copy-start.7
  59.3 15.1 %copy-start.4 = (bf16[128,512]{1,0:T(8,128)(2,1)S(1)}, bf16[128,512]{1,0:T(8,128)(2,1)}, u32[]{:S(2)}) copy-start(bf16[128,512]{1,0:T(8,128)(2,1)} %copy-done.3) | copy-start | bytes 393220
  59.3 15.1 %copy-start.6 = (bf16[128,512]{1,0:T(8,128)(2,1)S(1)}, bf16[128,512]{1,0:T(8,128)(2,1)}, u32[]{:S(2)}) copy-start(bf16[128,512]{1,0:T(8,128)(2,1)} %copy-done.5) | copy-start | bytes 393220
  59.4 19.5 %copy-start.1 = (bf16[9,128,512]{2,1,0:T(8,128)(2,1)S(1)}, bf16[9,128,512]{2,1,0:T(8,128)(2,1)}, u32[]{:S(2)}) copy-start(bf16[9,128,512]{2,1,0:T(8,128)(2,1)} %own.3) | copy-start | bytes 3538948
  73.4 1.8 collective-permute-start.13
  73.4 3.1 %collective-permute-start.14 = (bf16[3,9,16,512]{3,2,1,0:T(8,128)(2,1)S(1)}, bf16[3,9,16,512]{3,2,1,0:T(8,128)(2,1)S(1)}, u32[]{:S(2)}, u32[]{:S(2)}) collective-permute-start(bf16[3,9,16,512]{3,2,1,0:T(8,128)(2,1)S(1)} %get-tuple-element.87.rest_1_), channel_id=1, source_target_pairs={{0,4},{4,0},{8,12},{12,8},{16,20},{20,16},{24,28},{28,24},{1,5},{5... | collective-permute-start | bytes 1327112 | tf_op jit(solution)/shard_map/ppermute | solution.py:937
  73.9 4.9 %collective-permute-start.15 = (bf16[3,9,16,512]{3,2,1,0:T(8,128)(2,1)S(1)}, bf16[3,9,16,512]{3,2,1,0:T(8,128)(2,1)S(1)}, u32[]{:S(2)}, u32[]{:S(2)}) collective-permute-start(bf16[3,9,16,512]{3,2,1,0:T(8,128)(2,1)S(1)} %get-tuple-element.88.rest_2_), channel_id=1, source_target_pairs={{0,4},{4,0},{8,12},{12,8},{16,20},{20,16},{24,28},{28,24},{1,5},{5... | collective-permute-start | bytes 1327112 | tf_op jit(solution)/shard_map/ppermute | solution.py:937
  73.9 4.9 %collective-permute-start.16 = (bf16[3,9,16,512]{3,2,1,0:T(8,128)(2,1)S(1)}, bf16[3,9,16,512]{3,2,1,0:T(8,128)(2,1)S(1)}, u32[]{:S(2)}, u32[]{:S(2)}) collective-permute-start(bf16[3,9,16,512]{3,2,1,0:T(8,128)(2,1)S(1)} %get-tuple-element.89.rest_3_), channel_id=1, source_target_pairs={{0,4},{4,0},{8,12},{12,8},{16,20},{20,16},{24,28},{28,24},{1,5},{5... | collective-permute-start | bytes 1327112 | tf_op jit(solution)/shard_map/ppermute | solution.py:937
  74.4 14.3 %collective-permute-start.17 = (bf16[128,512]{1,0:T(8,128)(2,1)S(1)}, bf16[128,512]{1,0:T(8,128)(2,1)S(1)}, u32[]{:S(2)}, u32[]{:S(2)}) collective-permute-start(bf16[128,512]{1,0:T(8,128)(2,1)S(1)} %get-tuple-element.94), channel_id=1, source_target_pairs={{0,1},{1,0},{2,3},{3,2},{4,5},{5,4},{6,7},{7,6},{8,9},{9,8},{10,11... | collective-permute-start | bytes 393224 | tf_op jit(solution)/shard_map/ppermute | solution.py:947
  75.2 13.5 %collective-permute-start.18 = (bf16[128,512]{1,0:T(8,128)(2,1)S(1)}, bf16[128,512]{1,0:T(8,128)(2,1)S(1)}, u32[]{:S(2)}, u32[]{:S(2)}) collective-permute-start(bf16[128,512]{1,0:T(8,128)(2,1)S(1)} %get-tuple-element.95), channel_id=1, source_target_pairs={{0,2},{1,3},{2,0},{3,1},{4,6},{5,7},{6,4},{7,5},{8,10},{9,11},{10,... | collective-permute-start | bytes 393224 | tf_op jit(solution)/shard_map/ppermute | solution.py:947
  76.5 12.2 %collective-permute-start.19 = (bf16[128,512]{1,0:T(8,128)(2,1)S(1)}, bf16[128,512]{1,0:T(8,128)(2,1)S(1)}, u32[]{:S(2)}, u32[]{:S(2)}) collective-permute-start(bf16[128,512]{1,0:T(8,128)(2,1)S(1)} %get-tuple-element.96), channel_id=1, source_target_pairs={{0,3},{1,2},{2,1},{3,0},{4,7},{5,6},{6,5},{7,4},{8,11},{9,10},{10,... | collective-permute-start | bytes 393224 | tf_op jit(solution)/shard_map/ppermute | solution.py:947
  124.6 4.6 %collective-permute-start.23 = (bf16[4,4,9,16,512]{4,3,2,1,0:T(8,128)(2,1)S(1)}, bf16[4,4,9,16,512]{4,3,2,1,0:T(8,128)(2,1)S(1)}, u32[]{:S(2)}, u32[]{:S(2)}) collective-permute-start(bf16[4,4,9,16,512]{4,3,2,1,0:T(8,128)(2,1)S(1)} %get-tuple-element.117), channel_id=1, source_target_pairs={{0,4},{4,0},{8,12},{12,8},{16,20},{20,16},{24,28},{28,24},{1,5},{5... | collective-permute-start | bytes 7077896 | tf_op jit(solution)/shard_map/ppermute | solution.py:937
  124.6 15.2 %collective-permute-start.20 = (bf16[128,384]{1,0:T(8,128)(2,1)S(1)}, bf16[128,384]{1,0:T(8,128)(2,1)S(1)}, u32[]{:S(2)}, u32[]{:S(2)}) collective-permute-start(bf16[128,384]{1,0:T(8,128)(2,1)S(1)} %get-tuple-element.106), channel_id=1, source_target_pairs={{0,1},{1,0},{2,3},{3,2},{4,5},{5,4},{6,7},{7,6},{8,9},{9,8},{10,11... | collective-permute-start | bytes 294920 | tf_op jit(solution)/shard_map/ppermute | solution.py:947
  124.9 14.9 %collective-permute-start.21 = (bf16[128,384]{1,0:T(8,128)(2,1)S(1)}, bf16[128,384]{1,0:T(8,128)(2,1)S(1)}, u32[]{:S(2)}, u32[]{:S(2)}) collective-permute-start(bf16[128,384]{1,0:T(8,128)(2,1)S(1)} %get-tuple-element.107), channel_id=1, source_target_pairs={{0,2},{1,3},{2,0},{3,1},{4,6},{5,7},{6,4},{7,5},{8,10},{9,11},{10,... | collective-permute-start | bytes 294920 | tf_op jit(solution)/shard_map/ppermute | solution.py:947
  126.4 13.4 %collective-permute-start.22 = (bf16[128,384]{1,0:T(8,128)(2,1)S(1)}, bf16[128,384]{1,0:T(8,128)(2,1)S(1)}, u32[]{:S(2)}, u32[]{:S(2)}) collective-permute-start(bf16[128,384]{1,0:T(8,128)(2,1)S(1)} %get-tuple-element.108), channel_id=1, source_target_pairs={{0,3},{1,2},{2,1},{3,0},{4,7},{5,6},{6,5},{7,4},{8,11},{9,10},{10,... | collective-permute-start | bytes 294920 | tf_op jit(solution)/shard_map/ppermute | solution.py:947
  129.7 10.2 %collective-permute-start.24 = (bf16[4,9,16,512]{3,2,1,0:T(8,128)(2,1)S(1)}, bf16[4,9,16,512]{3,2,1,0:T(8,128)(2,1)S(1)}, u32[]{:S(2)}, u32[]{:S(2)}) collective-permute-start(bf16[4,9,16,512]{3,2,1,0:T(8,128)(2,1)S(1)} %get-tuple-element.118.after), channel_id=1, source_target_pairs={{0,8},{4,20},{8,0},{12,28},{16,24},{20,4},{24,16},{28,12},{1,9},{5... | collective-permute-start | bytes 1769480 | tf_op jit(solution)/shard_map/ppermute | solution.py:944
  156.8 7.3 %collective-permute-start.28 = (bf16[4,4,9,16,256]{4,3,2,1,0:T(8,128)(2,1)S(1)}, bf16[4,4,9,16,256]{4,3,2,1,0:T(8,128)(2,1)S(1)}, u32[]{:S(2)}, u32[]{:S(2)}) collective-permute-start(bf16[4,4,9,16,256]{4,3,2,1,0:T(8,128)(2,1)S(1)} %get-tuple-element.129), channel_id=1, source_target_pairs={{0,4},{4,0},{8,12},{12,8},{16,20},{20,16},{24,28},{28,24},{1,5},{5... | collective-permute-start | bytes 3538952 | tf_op jit(solution)/shard_map/ppermute | solution.py:937
  157.0 16.2 %collective-permute-start.31 = (bf16[4,9,16,512]{3,2,1,0:T(8,128)(2,1)S(1)}, bf16[4,9,16,512]{3,2,1,0:T(8,128)(2,1)S(1)}, u32[]{:S(2)}, u32[]{:S(2)}) collective-permute-start(bf16[4,9,16,512]{3,2,1,0:T(8,128)(2,1)S(1)} %mid_sum_b.1), channel_id=1, source_target_pairs={{0,16},{4,12},{8,24},{12,4},{16,0},{20,28},{24,8},{28,20},{1,17},{... | collective-permute-start | bytes 1769480 | tf_op jit(solution)/shard_map/ppermute | solution.py:944
  157.9 15.3 %collective-permute-start.30 = (bf16[4,9,16,512]{3,2,1,0:T(8,128)(2,1)S(1)}, bf16[4,9,16,512]{3,2,1,0:T(8,128)(2,1)S(1)}, u32[]{:S(2)}, u32[]{:S(2)}) collective-permute-start(bf16[4,9,16,512]{3,2,1,0:T(8,128)(2,1)S(1)} %release.9), channel_id=1, source_target_pairs={{0,8},{4,20},{8,0},{12,28},{16,24},{20,4},{24,16},{28,12},{1,9},{5... | collective-permute-start | bytes 1769480 | tf_op jit(solution)/shard_map/ppermute | solution.py:944
  164.4 14.8 %collective-permute-start.29 = (bf16[8,9,16,256]{3,2,1,0:T(8,128)(2,1)S(1)}, bf16[8,9,16,256]{3,2,1,0:T(8,128)(2,1)S(1)}, u32[]{:S(2)}, u32[]{:S(2)}) collective-permute-start(bf16[8,9,16,256]{3,2,1,0:T(8,128)(2,1)S(1)} %get-tuple-element.131), channel_id=1, source_target_pairs={{0,8},{4,20},{8,0},{12,28},{16,24},{20,4},{24,16},{28,12},{1,9},{5... | collective-permute-start | bytes 1769480 | tf_op jit(solution)/shard_map/ppermute | solution.py:944
  165.9 10.9 %collective-permute-start.26 = (bf16[64,1536]{1,0:T(8,128)(2,1)S(1)}, bf16[64,1536]{1,0:T(8,128)(2,1)S(1)}, u32[]{:S(2)}, u32[]{:S(2)}) collective-permute-start(bf16[64,1536]{1,0:T(8,128)(2,1)S(1)} %get-tuple-element.125), channel_id=1, source_target_pairs={{0,2},{1,3},{2,0},{3,1},{4,6},{5,7},{6,4},{7,5},{8,10},{9,11},{10,... | collective-permute-start | bytes 589832 | tf_op jit(solution)/shard_map/ppermute | solution.py:947
  173.4 9.6 %collective-permute-start.33 = (bf16[2,9,16,512]{3,2,1,0:T(8,128)(2,1)S(1)}, bf16[2,9,16,512]{3,2,1,0:T(8,128)(2,1)S(1)}, u32[]{:S(2)}, u32[]{:S(2)}) collective-permute-start(bf16[2,9,16,512]{3,2,1,0:T(8,128)(2,1)S(1)} %get-tuple-element.138), channel_id=1, source_target_pairs={{0,1},{1,0},{2,3},{3,2},{4,5},{5,4},{6,7},{7,6},{8,9},{9,8},{10,11... | collective-permute-start | bytes 884744 | tf_op jit(solution)/shard_map/ppermute | solution.py:947
  179.3 6.8 %collective-permute-start.32 = (bf16[4,9,16,256]{3,2,1,0:T(8,128)(2,1)S(1)}, bf16[4,9,16,256]{3,2,1,0:T(8,128)(2,1)S(1)}, u32[]{:S(2)}, u32[]{:S(2)}) collective-permute-start(bf16[4,9,16,256]{3,2,1,0:T(8,128)(2,1)S(1)} %get-tuple-element.137), channel_id=1, source_target_pairs={{0,16},{4,12},{8,24},{12,4},{16,0},{20,28},{24,8},{28,20},{1,17},{... | collective-permute-start | bytes 884744 | tf_op jit(solution)/shard_map/ppermute | solution.py:944
  180.2 9.6 %collective-permute-start.27 = (bf16[64,1536]{1,0:T(8,128)(2,1)S(1)}, bf16[64,1536]{1,0:T(8,128)(2,1)S(1)}, u32[]{:S(2)}, u32[]{:S(2)}) collective-permute-start(bf16[64,1536]{1,0:T(8,128)(2,1)S(1)} %get-tuple-element.126), channel_id=1, source_target_pairs={{0,3},{1,2},{2,1},{3,0},{4,7},{5,6},{6,5},{7,4},{8,11},{9,10},{10,... | collective-permute-start | bytes 589832 | tf_op jit(solution)/shard_map/ppermute | solution.py:947
  186.1 8.0 %collective-permute-start.34 = (bf16[2,9,16,256]{3,2,1,0:T(8,128)(2,1)S(1)}, bf16[2,9,16,256]{3,2,1,0:T(8,128)(2,1)S(1)}, u32[]{:S(2)}, u32[]{:S(2)}) collective-permute-start(bf16[2,9,16,256]{3,2,1,0:T(8,128)(2,1)S(1)} %get-tuple-element.142), channel_id=1, source_target_pairs={{0,1},{1,0},{2,3},{3,2},{4,5},{5,4},{6,7},{7,6},{8,9},{9,8},{10,11... | collective-permute-start | bytes 442376 | tf_op jit(solution)/shard_map/ppermute | solution.py:947
  186.2 11.6 %collective-permute-start.36 = (bf16[1,9,16,512]{3,2,1,0:T(8,128)(2,1)S(1)}, bf16[1,9,16,512]{3,2,1,0:T(8,128)(2,1)S(1)}, u32[]{:S(2)}, u32[]{:S(2)}) collective-permute-start(bf16[1,9,16,512]{3,2,1,0:T(8,128)(2,1)S(1)} %get-tuple-element.145), channel_id=1, source_target_pairs={{0,2},{1,3},{2,0},{3,1},{4,6},{5,7},{6,4},{7,5},{8,10},{9,11},{10,... | collective-permute-start | bytes 442376 | tf_op jit(solution)/shard_map/ppermute | solution.py:947
  188.1 14.6 %collective-permute-start.25 = (bf16[64,1536]{1,0:T(8,128)(2,1)S(1)}, bf16[64,1536]{1,0:T(8,128)(2,1)S(1)}, u32[]{:S(2)}, u32[]{:S(2)}) collective-permute-start(bf16[64,1536]{1,0:T(8,128)(2,1)S(1)} %get-tuple-element.124), channel_id=1, source_target_pairs={{0,1},{1,0},{2,3},{3,2},{4,5},{5,4},{6,7},{7,6},{8,9},{9,8},{10,11... | collective-permute-start | bytes 589832 | tf_op jit(solution)/shard_map/ppermute | solution.py:947
  194.2 7.2 %collective-permute-start.35 = (bf16[1,9,16,256]{3,2,1,0:T(8,128)(2,1)S(1)}, bf16[1,9,16,256]{3,2,1,0:T(8,128)(2,1)S(1)}, u32[]{:S(2)}, u32[]{:S(2)}) collective-permute-start(bf16[1,9,16,256]{3,2,1,0:T(8,128)(2,1)S(1)} %get-tuple-element.144), channel_id=1, source_target_pairs={{0,2},{1,3},{2,0},{3,1},{4,6},{5,7},{6,4},{7,5},{8,10},{9,11},{10,... | collective-permute-start | bytes 221192 | tf_op jit(solution)/shard_map/ppermute | solution.py:947
  197.9 9.9 %collective-permute-start.40 = (bf16[9,16,512]{2,1,0:T(8,128)(2,1)S(1)}, bf16[9,16,512]{2,1,0:T(8,128)(2,1)S(1)}, u32[]{:S(2)}, u32[]{:S(2)}) collective-permute-start(bf16[9,16,512]{2,1,0:T(8,128)(2,1)S(1)} %mid_sum_3.1.rest_0_.refs_0_), channel_id=1, source_target_pairs={{0,16},{4,12},{8,24},{12,4},{16,0},{20,28},{24,8},{28,20},{1,17},{... | collective-permute-start | bytes 442376 | tf_op jit(solution)/shard_map/ppermute | solution.py:968
  199.0 8.7 %collective-permute-start.41 = (bf16[9,16,512]{2,1,0:T(8,128)(2,1)S(1)}, bf16[9,16,512]{2,1,0:T(8,128)(2,1)S(1)}, u32[]{:S(2)}, u32[]{:S(2)}) collective-permute-start(bf16[9,16,512]{2,1,0:T(8,128)(2,1)S(1)} %mid_sum_3.1.rest_0_.refs_0_), channel_id=1, source_target_pairs={{0,8},{4,20},{8,0},{12,28},{16,24},{20,4},{24,16},{28,12},{1,9},{5... | collective-permute-start | bytes 442376 | tf_op jit(solution)/shard_map/ppermute | solution.py:968
  199.9 7.9 %collective-permute-start.42 = (bf16[9,16,512]{2,1,0:T(8,128)(2,1)S(1)}, bf16[9,16,512]{2,1,0:T(8,128)(2,1)S(1)}, u32[]{:S(2)}, u32[]{:S(2)}) collective-permute-start(bf16[9,16,512]{2,1,0:T(8,128)(2,1)S(1)} %mid_sum_3.1.rest_0_.refs_0_), channel_id=1, source_target_pairs={{0,24},{4,28},{8,16},{12,20},{16,8},{20,12},{24,0},{28,4},{1,25},{... | collective-permute-start | bytes 442376 | tf_op jit(solution)/shard_map/ppermute | solution.py:968
  201.5 7.2 %collective-permute-start.37 = (bf16[9,16,256]{2,1,0:T(8,128)(2,1)S(1)}, bf16[9,16,256]{2,1,0:T(8,128)(2,1)S(1)}, u32[]{:S(2)}, u32[]{:S(2)}) collective-permute-start(bf16[9,16,256]{2,1,0:T(8,128)(2,1)S(1)} %in_sum_3.1.refs_0_), channel_id=1, source_target_pairs={{0,16},{4,12},{8,24},{12,4},{16,0},{20,28},{24,8},{28,20},{1,17},{... | collective-permute-start | bytes 221192 | tf_op jit(solution)/shard_map/ppermute | solution.py:944
  202.6 6.0 %collective-permute-start.38 = (bf16[9,16,256]{2,1,0:T(8,128)(2,1)S(1)}, bf16[9,16,256]{2,1,0:T(8,128)(2,1)S(1)}, u32[]{:S(2)}, u32[]{:S(2)}) collective-permute-start(bf16[9,16,256]{2,1,0:T(8,128)(2,1)S(1)} %in_sum_3.1.refs_0_), channel_id=1, source_target_pairs={{0,8},{4,20},{8,0},{12,28},{16,24},{20,4},{24,16},{28,12},{1,9},{5... | collective-permute-start | bytes 221192 | tf_op jit(solution)/shard_map/ppermute | solution.py:944
  208.7 3.0 %collective-permute-start.43 = (bf16[4,9,16,512]{3,2,1,0:T(8,128)(2,1)S(1)}, bf16[4,9,16,512]{3,2,1,0:T(8,128)(2,1)S(1)}, u32[]{:S(2)}, u32[]{:S(2)}) collective-permute-start(bf16[4,9,16,512]{3,2,1,0:T(8,128)(2,1)S(1)} %mid_stack.1.mine), channel_id=1, source_target_pairs={{0,4},{4,0},{8,12},{12,8},{16,20},{20,16},{24,28},{28,24},{1,5},{5... | collective-permute-start | bytes 1769480 | tf_op jit(solution)/shard_map/ppermute | solution.py:937
  209.3 4.4 %collective-permute-start.39 = (bf16[9,16,256]{2,1,0:T(8,128)(2,1)S(1)}, bf16[9,16,256]{2,1,0:T(8,128)(2,1)S(1)}, u32[]{:S(2)}, u32[]{:S(2)}) collective-permute-start(bf16[9,16,256]{2,1,0:T(8,128)(2,1)S(1)} %collective-permute-done.37.refs_4_.refs_1_), channel_id=1, source_target_pairs={{0,8},{4,20},{8,0},{12,28},{16,24},{20,4},{24,16},{28,12},{1,9},{5... | collective-permute-start | bytes 221192 | tf_op jit(solution)/shard_map/ppermute | solution.py:944
  213.7 1.6 collective-permute-start.44

commit v5 on v4

--- a/solution.py
+++ b/solution.py
@@ -1024,13 +1024,14 @@
         got = everyone(fan(g, pay, got_b, *pooled[1:]))
         block_out, pooled_done = place(g, pooled, BF, "place_pooled")
         if split:
-            (go_1,) = add_up([stay_b, got_b], 1, [got], "mid_sum_b")
-            got_1 = links.plane(go_1, 1)
+            (go_1,) = add_up([stay_b, got_b], 1, [pay, *pooled[1:]], "mid_sum_b")
+            got_1 = early = links.plane(go_1, 1)
             got_a = links.plane(release([got], [go_a])[0], 0)
         else:
             (go_mid,) = release([got], [go_b])
+            early = got
         grad1, sums1, roots, terms_in, give_in = terms_of(
-            g, lengths, got, table, pre1, local1, x3_in, got, g.ci_all, (MEAN1, INV1, GAMMA1), "weight_in_terms"
+            g, lengths, got, table, pre1, local1, x3_in, early, g.ci_all, (MEAN1, INV1, GAMMA1), "weight_in_terms"
         )
         got_in = links.core(give_in)
 

time: 217 us -> 213 us (0.982)
  waiting for transfers between devices: 56.6 us -> 51.3 us
    ppermute x14, waiting for transfers between devices: 25.8 us -> 18.7 us  [plane(): lax.ppermute(x, 'dp', [(i, i ^ 2 * g.mask(i & 1, turn)) for i in range(g....]
    ppermute x16, waiting for transfers between devices: 24.1 us -> 28.9 us  [chan(): return lax.ppermute(x, 'chan', [(i, i ^ k) for i in range(self.g.nch)])]
    ppermute x3, waiting for transfers between devices: 4.28 us -> 1.32 us  [gather_direct(): return [x] + [lax.ppermute(x, 'dp', p) for p in pairs[1:]]]
  transfers between devices with their start and end apart: 46 -> 46, of which waited for: 20 -> 18; matrix products, arithmetic and copies ran while one was open for 1% -> 1% of each run, Pallas kernels for 18% -> 19%
where the time goes in v5:
time: 213 us
  Pallas kernels  63.4 us (30%)
  waiting for transfers between devices  51.3 us (24%)
  blocking collectives  46.9 us (22%)
  starting transfers between devices  46.8 us (22%)
  local copies, waits for them, and re-layouts  3.46 us (2%)
    pallas_call x23, Pallas kernels, call(): pl.pallas_call(body, out_shape=[pltpu.VMEM(o.shape, o.dtype) if isinstanc...  57 us
    all_to_all x4, blocking collectives, everyone(): return lax.all_to_all(x, ('dp', 'chan'), 0, 0)  46.9 us
    ppermute x16, waiting for transfers between devices, chan(): return lax.ppermute(x, 'chan', [(i, i ^ k) for i in range(self.g.nch)])  28.9 us
    ppermute x16, starting transfers between devices, chan(): return lax.ppermute(x, 'chan', [(i, i ^ k) for i in range(self.g.nch)])  19.2 us
    ppermute x14, waiting for transfers between devices, plane(): lax.ppermute(x, 'dp', [(i, i ^ 2 * g.mask(i & 1, turn)) for i in range(g....  18.7 us
    ppermute x14, starting transfers between devices, plane(): lax.ppermute(x, 'dp', [(i, i ^ 2 * g.mask(i & 1, turn)) for i in range(g....  15.1 us
    all_to_all x1, starting transfers between devices, body(): maps = lax.all_to_all(release_far([pieces_in], cells), 'chan', 0, 0)  6.3 us
  transfers between devices with their start and end apart: 46, of which 18 were waited for; matrix products, arithmetic and copies ran while one was open for 1% of the time, Pallas kernels for 19%

profile of v5, /device:TPU:0, one launch (start us, length us, event | category | flops | bytes accessed | tf_op | source)
XLA Modules:
  0.0 213.0 jit_solution(15311398525624460876)
XLA Ops:
  0.6 1.0 cut_weights.1.after
  1.6 3.1 %collective-permute-start = (bf16[9,16,768]{2,1,0:T(8,128)(2,1)S(1)}, bf16[9,16,768]{2,1,0:T(8,128)(2,1)S(1)}, u32[]{:S(2)}, u32[]{:S(2)}) collective-permute-start(bf16[9,16,768]{2,1,0:T(8,128)(2,1)S(1)} %cut_weights.1.after), channel_id=1, source_target_pairs={{0,1},{1,0},{2,3},{3,2},{4,5},{5,4},{6,7},{7,6},{8,9},{9,8},{10,11... | collective-permute-start | bytes 663560 | tf_op jit(solution)/shard_map/ppermute | solution.py:947
  4.7 2.6 %collective-permute-start.1 = (bf16[9,16,768]{2,1,0:T(8,128)(2,1)S(1)}, bf16[9,16,768]{2,1,0:T(8,128)(2,1)S(1)}, u32[]{:S(2)}, u32[]{:S(2)}) collective-permute-start(bf16[9,16,768]{2,1,0:T(8,128)(2,1)S(1)} %cut_weights.1.after), channel_id=1, source_target_pairs={{0,2},{1,3},{2,0},{3,1},{4,6},{5,7},{6,4},{7,5},{8,10},{9,11},{10,... | collective-permute-start | bytes 663560 | tf_op jit(solution)/shard_map/ppermute | solution.py:947
  7.3 2.0 cut_maps.1.after.refs_1_
  9.3 1.1 copy-done
  10.5 1.1 cut_cotangent.1
  11.6 0.6 copy-done.5
  12.3 1.8 collective-permute-done.rest_0_
  14.1 9.3 %collective-permute-done.1.rest_1_ = bf16[9,16,768]{2,1,0:T(8,128)(2,1)S(1)} collective-permute-done((bf16[9,16,768]{2,1,0:T(8,128)(2,1)S(1)}, bf16[9,16,768]{2,1,0:T(8,128)(2,1)S(1)}, u32[]{:S(2)}, u32[]{:S(2)}) %collective-permute-start.1) | collective-permute-done | bytes 221216 | tf_op jit(solution)/shard_map/ppermute | solution.py:947
  23.5 0.7 sort_pieces.1
  24.2 6.3 %all-to-all-start = ((bf16[4,64,1664]{2,1,0:T(8,128)(2,1)}), bf16[4,64,1664]{2,1,0:T(8,128)(2,1)S(1)}, u32[]{:S(2)}, u32[]{:S(2)}) async-start(bf16[4,64,1664]{2,1,0:T(8,128)(2,1)} %release_far.1), calls=%async_computation | async-start | bytes 1703936 | tf_op jit(solution)/shard_map/all_to_all | solution.py:997
  30.5 1.5 collective-permute-start.3
  32.6 1.5 collective-permute-start.11
  34.1 0.5 collective-permute-start.4
  34.6 4.6 %collective-permute-done.3.rest_1_ = bf16[3,9,16,256]{3,2,1,0:T(8,128)(2,1)} collective-permute-done((bf16[3,9,16,256]{3,2,1,0:T(8,128)(2,1)}, bf16[3,9,16,256]{3,2,1,0:T(8,128)(2,1)}, u32[]{:S(2)}, u32[]{:S(2)}) %collective-permute-start.3) | collective-permute-done | bytes 221216 | tf_op jit(solution)/shard_map/ppermute | solution.py:944
  39.2 1.5 collective-permute-start.5
  40.7 5.4 %collective-permute-done.4.rest_2_ = bf16[3,9,16,256]{3,2,1,0:T(8,128)(2,1)} collective-permute-done((bf16[3,9,16,256]{3,2,1,0:T(8,128)(2,1)}, bf16[3,9,16,256]{3,2,1,0:T(8,128)(2,1)}, u32[]{:S(2)}, u32[]{:S(2)}) %collective-permute-start.4) | collective-permute-done | bytes 221216 | tf_op jit(solution)/shard_map/ppermute | solution.py:944
  46.1 2.3 %collective-permute-done.5.rest_3_ = bf16[3,9,16,256]{3,2,1,0:T(8,128)(2,1)} collective-permute-done((bf16[3,9,16,256]{3,2,1,0:T(8,128)(2,1)}, bf16[3,9,16,256]{3,2,1,0:T(8,128)(2,1)}, u32[]{:S(2)}, u32[]{:S(2)}) %collective-permute-start.5) | collective-permute-done | bytes 221216 | tf_op jit(solution)/shard_map/ppermute | solution.py:944
  48.4 1.3 collective-permute-start.8
  49.8 1.1 all-to-all-done.maps.refs_0_
  50.9 1.5 collective-permute-start.12
  52.5 1.7 join_in.1.w
  54.2 5.1 %first_conv.1 = (f32[8,208,512]{2,1,0:T(8,128)S(1)}, bf16[8,208,768]{2,1,0:T(8,128)(2,1)S(1)}, f32[1,1664]{1,0:T(1,128)S(1)}) custom-call(s32[2]{0:T(128)S(1)} %copy-done.7, f32[4,128]{1,0:T(4,128)S(1)} %pad_maximum_fusion.gains, bf16[9,512,256]{2,1,0:T(8,128)(2,1)S(1)} %join_in.1.w, bf16[4,64,1664]{2,1,0:T(8,128)(2,1)S(1)} %all-to-all-done.maps.refs_0_), custom_call_target="tpu_custom_call" | custom-call | flops 3925868544 | bytes 10485760 | tf_op jit(solution)/shard_map/first_conv/pallas_call | solution.py:90
  59.4 14.0 %all_to_all.25.refs_0_.got = f32[32,1,1664]{2,1,0:T(1,128)S(1)} all-to-all(f32[32,1,1664]{2,1,0:T(1,128)S(1)} %fan.3), channel_id=1, replica_groups=mesh['dp'=8,'chan'=4] {'dp','chan'}, dimensions={0} | all-to-all | bytes 425984 | tf_op jit(solution)/shard_map/all_to_all | solution.py:972
  74.6 0.6 collective-permute-done.13.rest_4_
  75.2 1.3 collective-permute-start.18
  76.5 2.3 %collective-permute-start.19 = (bf16[128,512]{1,0:T(8,128)(2,1)S(1)}, bf16[128,512]{1,0:T(8,128)(2,1)S(1)}, u32[]{:S(2)}, u32[]{:S(2)}) collective-permute-start(bf16[128,512]{1,0:T(8,128)(2,1)S(1)} %get-tuple-element.96), channel_id=1, source_target_pairs={{0,3},{1,2},{2,1},{3,0},{4,7},{5,6},{6,5},{7,4},{8,11},{9,10},{10,... | collective-permute-start | bytes 393224 | tf_op jit(solution)/shard_map/ppermute | solution.py:947
  79.2 9.5 %second_conv.1 = (f32[8,208,512]{2,1,0:T(8,128)S(1)}, bf16[8,208,1536]{2,1,0:T(8,128)(2,1)S(1)}, f32[16,512]{1,0:T(8,128)S(1)}, f32[1,1024]{1,0:T(1,128)S(1)}, f32[1,128]{1,0:T(1,128)S(1)}) custom-call(s32[2]{0:T(128)S(1)} %copy-done.7, f32[32,1,1664]{2,1,0:T(1,128)S(1)} %all_to_all.25.refs_0_.got, f32[8,208,512]{2,1,0:T(8,128)S(1)} %get-tuple-element.85.pre1.pre, ...), custom_call_target="tpu_custom_call" | custom-call | flops 7851737088 | bytes 17825792 | tf_op jit(solution)/shard_map/second_conv/pallas_call | solution.py:90
  88.8 11.0 %all_to_all.26.got = f32[32,1,1024]{2,1,0:T(1,128)S(1)} all-to-all(f32[32,1,1024]{2,1,0:T(1,128)S(1)} %fan.4), channel_id=1, replica_groups=mesh['dp'=8,'chan'=4] {'dp','chan'}, dimensions={0} | all-to-all | bytes 262144 | tf_op jit(solution)/shard_map/all_to_all | solution.py:972
  99.7 5.2 %pool.1 = (bf16[128,384]{1,0:T(8,128)(2,1)S(1)}, bf16[128,384]{1,0:T(8,128)(2,1)S(1)}, bf16[128,384]{1,0:T(8,128)(2,1)S(1)}, bf16[128,384]{1,0:T(8,128)(2,1)S(1)...) custom-call(s32[2]{0:T(128)S(1)} %copy-done.7, ...), custom_call_target="tpu_custom_call" | custom-call | flops 4000000000 | bytes 8388608 | tf_op jit(solution)/shard_map/pool/pallas_call | solution.py:90
  105.0 10.1 %all_to_all.27.refs_0_.got.after = f32[32,1,1024]{2,1,0:T(1,128)S(1)} all-to-all(f32[32,1,1024]{2,1,0:T(1,128)S(1)} %get-tuple-element.100), channel_id=1, replica_groups=mesh['dp'=8,'chan'=4] {'dp','chan'}, dimensions={0} | all-to-all | bytes 262144 | tf_op jit(solution)/shard_map/all_to_all | solution.py:972
  115.1 9.5 %weight_mid_terms.1 = (bf16[8,208,512]{2,1,0:T(8,128)(2,1)S(1)}, f32[8,512]{1,0:T(8,128)S(1)}, f32[8,128]{1,0:T(8,128)}, bf16[2,4,4,9,16,512]{5,4,3,2,1,0:T(8,128)(2,1)S(1)}, bf16[4,4,9,16,512]{4,3,2,1,0:T(8,128)(2,1)S(1)}) custom-call(s32[2]{0:T(128)S(1)} %copy-done.7, f32[32,1,1024]{2,1,0:T(1,128)S(1)} %all_to_all.27.refs_0_.got.after, ...), custom_call_target="tpu_custom_call" | custom-call | flops 7851737088 | bytes 15728640 | tf_op jit(solution)/shard_map/weight_mid_terms/pallas_call | solution.py:90
  124.9 1.5 collective-permute-start.21
  126.4 2.7 %collective-permute-start.22 = (bf16[128,384]{1,0:T(8,128)(2,1)S(1)}, bf16[128,384]{1,0:T(8,128)(2,1)S(1)}, u32[]{:S(2)}, u32[]{:S(2)}) collective-permute-start(bf16[128,384]{1,0:T(8,128)(2,1)S(1)} %get-tuple-element.108), channel_id=1, source_target_pairs={{0,3},{1,2},{2,1},{3,0},{4,7},{5,6},{6,5},{7,4},{8,11},{9,10},{10,... | collective-permute-start | bytes 294920 | tf_op jit(solution)/shard_map/ppermute | solution.py:947
  129.2 0.5 mid_core_sum.1
  129.7 0.8 collective-permute-start.24
  130.5 9.3 %second_back.1 = (f32[8,208,512]{2,1,0:T(8,128)S(1)}, f32[1,1280]{1,0:T(1,128)S(1)}) custom-call(s32[2]{0:T(128)S(1)} %copy-done.7, f32[16,512]{1,0:T(8,128)S(1)} %get-tuple-element.110.table, bf16[8,208,512]{2,1,0:T(8,128)(2,1)S(1)} %get-tuple-element.113.grad, f32[8,208,512]{2,1,0:T(8,128)S(1)} %get-tuple-element.85.pre1.pre, ...), custom_call_target="tpu_custom_call" | custom-call | flops 7851737088 | bytes 20971520 | tf_op jit(solution)/shard_map/second_back/pallas_call | solution.py:90
  140.0 0.6 collective-permute-start.25
  140.7 11.8 %all_to_all.28.got.refs_0_ = f32[32,1,1280]{2,1,0:T(1,128)S(1)} all-to-all(f32[32,1,1280]{2,1,0:T(1,128)S(1)} %fan.5), channel_id=1, replica_groups=mesh['dp'=8,'chan'=4] {'dp','chan'}, dimensions={0} | all-to-all | bytes 327680 | tf_op jit(solution)/shard_map/all_to_all | solution.py:972
  152.5 5.8 %weight_in_terms.1 = (bf16[8,208,512]{2,1,0:T(8,128)(2,1)S(1)}, f32[8,512]{1,0:T(8,128)S(1)}, f32[8,128]{1,0:T(8,128)S(1)}, bf16[2,4,4,9,16,256]{5,4,3,2,1,0:T(8,128)(2,1)S(1)}, bf16[4,4,9,16,256]{4,3,2,1,0:T(8,128)(2,1)S(1)}) custom-call(s32[2]{0:T(128)S(1)} %copy-done.7, f32[32,1,1280]{2,1,0:T(1,128)S(1)} %all_to_all.28.got.refs_0_, ...), custom_call_target="tpu_custom_call" | custom-call | flops 3925868544 | bytes 15728640 | tf_op jit(solution)/shard_map/weight_in_terms/pallas_call | solution.py:90
  158.4 0.9 collective-permute-start.31
  159.2 5.6 %spectra_back.1 = (bf16[64,1536]{1,0:T(8,128)(2,1)S(1)}, bf16[64,1536]{1,0:T(8,128)(2,1)S(1)}, bf16[64,1536]{1,0:T(8,128)(2,1)S(1)}, bf16[64,1536]{1,0:T(8,128)(2,1)S(1)}) custom-call(s32[2]{0:T(128)S(1)} %copy-done.7, bf16[8,208,512]{2,1,0:T(8,128)(2,1)S(1)} %get-tuple-element.123.grad.after, bf16[8,208,512]{2,1,0:T(8,128)(2,1)S(1)} %get-tuple-element.123.grad.after, ...), custom_call_target="tpu_custom_call" | custom-call | flops 3925868544 | bytes 5242880 | tf_op jit(solution)/shard_map/spectra_back/pallas_call | solution.py:90
  165.2 1.3 collective-permute-start.30
  166.9 1.4 collective-permute-done.31.rest_1_
  168.8 8.8 %collective-permute-done.27.rest_2_.rest_1_ = bf16[64,1536]{1,0:T(8,128)(2,1)S(1)} collective-permute-done((bf16[64,1536]{1,0:T(8,128)(2,1)S(1)}, bf16[64,1536]{1,0:T(8,128)(2,1)S(1)}, u32[]{:S(2)}, u32[]{:S(2)}) %collective-permute-start.27) | collective-permute-done | bytes 196640 | tf_op jit(solution)/shard_map/ppermute | solution.py:947
  177.8 1.0 collective-permute-start.32
  178.7 1.8 collective-permute-start.28
  180.6 0.8 place_pooled.1
  181.5 3.1 %collective-permute-done.32.got = bf16[4,9,16,256]{3,2,1,0:T(8,128)(2,1)S(1)} collective-permute-done((bf16[4,9,16,256]{3,2,1,0:T(8,128)(2,1)S(1)}, bf16[4,9,16,256]{3,2,1,0:T(8,128)(2,1)S(1)}, u32[]{:S(2)}, u32[]{:S(2)}) %collective-permute-start.32) | collective-permute-done | bytes 294944 | tf_op jit(solution)/shard_map/ppermute | solution.py:944
  184.7 2.6 %collective-permute-start.36 = (bf16[1,9,16,512]{3,2,1,0:T(8,128)(2,1)S(1)}, bf16[1,9,16,512]{3,2,1,0:T(8,128)(2,1)S(1)}, u32[]{:S(2)}, u32[]{:S(2)}) collective-permute-start(bf16[1,9,16,512]{3,2,1,0:T(8,128)(2,1)S(1)} %get-tuple-element.145), channel_id=1, source_target_pairs={{0,2},{1,3},{2,0},{3,1},{4,6},{5,7},{6,4},{7,5},{8,10},{9,11},{10,... | collective-permute-start | bytes 442376 | tf_op jit(solution)/shard_map/ppermute | solution.py:947
  187.4 6.9 %collective-permute-done.34.got = bf16[2,9,16,256]{3,2,1,0:T(8,128)(2,1)S(1)} collective-permute-done((bf16[2,9,16,256]{3,2,1,0:T(8,128)(2,1)S(1)}, bf16[2,9,16,256]{3,2,1,0:T(8,128)(2,1)S(1)}, u32[]{:S(2)}, u32[]{:S(2)}) %collective-permute-start.34) | collective-permute-done | bytes 147488 | tf_op jit(solution)/shard_map/ppermute | solution.py:947
  194.4 0.7 collective-permute-start.40
  195.1 1.3 collective-permute-start.41
  196.4 1.5 collective-permute-start.42
  198.0 2.0 collective-permute-done.35.got
  200.0 0.8 collective-permute-start.37
  200.8 1.3 collective-permute-start.38
  202.1 1.3 collective-permute-done.42.refs_3_
  203.4 0.9 collective-permute-done.37.refs_4_.refs_1_
  204.4 0.8 collective-permute-done.38.refs_5_.refs_2_
  205.8 1.3 collective-permute-start.39
  207.1 1.3 place_spectra.1
  208.4 1.6 mid_out.1
  211.8 1.1 in_out.1
  (101 shorter events, 7.1 us)
Async XLA Ops:
  1.6 12.5 %collective-permute-start = (bf16[9,16,768]{2,1,0:T(8,128)(2,1)S(1)}, bf16[9,16,768]{2,1,0:T(8,128)(2,1)S(1)}, u32[]{:S(2)}, u32[]{:S(2)}) collective-permute-start(bf16[9,16,768]{2,1,0:T(8,128)(2,1)S(1)} %cut_weights.1.after), channel_id=1, source_target_pairs={{0,1},{1,0},{2,3},{3,2},{4,5},{5,4},{6,7},{7,6},{8,9},{9,8},{10,11... | collective-permute-start | bytes 663560 | tf_op jit(solution)/shard_map/ppermute | solution.py:947
  4.7 18.7 %collective-permute-start.1 = (bf16[9,16,768]{2,1,0:T(8,128)(2,1)S(1)}, bf16[9,16,768]{2,1,0:T(8,128)(2,1)S(1)}, u32[]{:S(2)}, u32[]{:S(2)}) collective-permute-start(bf16[9,16,768]{2,1,0:T(8,128)(2,1)S(1)} %cut_weights.1.after), channel_id=1, source_target_pairs={{0,2},{1,3},{2,0},{3,1},{4,6},{5,7},{6,4},{7,5},{8,10},{9,11},{10,... | collective-permute-start | bytes 663560 | tf_op jit(solution)/shard_map/ppermute | solution.py:947
  7.3 16.1 %collective-permute-start.2 = (bf16[9,16,768]{2,1,0:T(8,128)(2,1)S(1)}, bf16[9,16,768]{2,1,0:T(8,128)(2,1)S(1)}, u32[]{:S(2)}, u32[]{:S(2)}) collective-permute-start(bf16[9,16,768]{2,1,0:T(8,128)(2,1)S(1)} %cut_weights.1.after), channel_id=1, source_target_pairs={{0,3},{1,2},{2,1},{3,0},{4,7},{5,6},{6,5},{7,4},{8,11},{9,10},{10,... | collective-permute-start | bytes 663560 | tf_op jit(solution)/shard_map/ppermute | solution.py:947
  9.3 1.2 copy-start
  11.6 0.7 copy-start.5
  12.3 11.9 %copy-start.3 = (bf16[128,512]{1,0:T(8,128)(2,1)}, bf16[128,512]{1,0:T(8,128)(2,1)S(1)}, u32[]{:S(2)}) copy-start(bf16[128,512]{1,0:T(8,128)(2,1)S(1)} %get-tuple-element.92.refs_3_) | copy-start | bytes 393220
  24.2 28.2 %copy-start.8 = (f32[128]{0:T(128)S(1)}, f32[128]{0:T(128)}, u32[]{:S(2)}) copy-start(f32[128]{0:T(128)} %param.16) | copy-start | bytes 1540
  24.2 28.2 %copy-start.9 = (f32[128]{0:T(128)S(1)}, f32[128]{0:T(128)}, u32[]{:S(2)}) copy-start(f32[128]{0:T(128)} %param.15) | copy-start | bytes 1540
  24.2 28.2 %copy-start.10 = (f32[128]{0:T(128)S(1)}, f32[128]{0:T(128)}, u32[]{:S(2)}) copy-start(f32[128]{0:T(128)} %param.13) | copy-start | bytes 1540
  24.2 28.2 %copy-start.11 = (f32[128]{0:T(128)S(1)}, f32[128]{0:T(128)}, u32[]{:S(2)}) copy-start(f32[128]{0:T(128)} %param.12) | copy-start | bytes 1540
  24.2 28.3 %copy-start.2 = (bf16[9,128,256]{2,1,0:T(8,128)(2,1)S(1)}, bf16[9,128,256]{2,1,0:T(8,128)(2,1)}, u32[]{:S(2)}) copy-start(bf16[9,128,256]{2,1,0:T(8,128)(2,1)} %own.2) | copy-start | bytes 1769476
  24.2 26.7 %all-to-all-start = ((bf16[4,64,1664]{2,1,0:T(8,128)(2,1)}), bf16[4,64,1664]{2,1,0:T(8,128)(2,1)S(1)}, u32[]{:S(2)}, u32[]{:S(2)}) async-start(bf16[4,64,1664]{2,1,0:T(8,128)(2,1)} %release_far.1), calls=%async_computation | async-start | bytes 1703936 | tf_op jit(solution)/shard_map/all_to_all | solution.py:997
  30.5 8.7 %collective-permute-start.3 = (bf16[3,9,16,256]{3,2,1,0:T(8,128)(2,1)}, bf16[3,9,16,256]{3,2,1,0:T(8,128)(2,1)}, u32[]{:S(2)}, u32[]{:S(2)}) collective-permute-start(bf16[3,9,16,256]{3,2,1,0:T(8,128)(2,1)} %get-tuple-element.82.rest_0_.refs_0_), channel_id=1, source_target_pairs={{0,16},{4,12},{8,24},{12,4},{16,0},{20,28},{24,8},{28,20},{1,17},{... | collective-permute-start | bytes 663560 | tf_op jit(solution)/shard_map/ppermute | solution.py:944
  32.1 17.7 %collective-permute-start.10 = (bf16[3,9,16,512]{3,2,1,0:T(8,128)(2,1)S(1)}, bf16[3,9,16,512]{3,2,1,0:T(8,128)(2,1)S(1)}, u32[]{:S(2)}, u32[]{:S(2)}) collective-permute-start(bf16[3,9,16,512]{3,2,1,0:T(8,128)(2,1)S(1)} %get-tuple-element.84.refs_1_), channel_id=1, source_target_pairs={{0,16},{4,12},{8,24},{12,4},{16,0},{20,28},{24,8},{28,20},{1,17},{... | collective-permute-start | bytes 1327112 | tf_op jit(solution)/shard_map/ppermute | solution.py:944
  32.6 17.2 %collective-permute-start.11 = (bf16[3,9,16,512]{3,2,1,0:T(8,128)(2,1)S(1)}, bf16[3,9,16,512]{3,2,1,0:T(8,128)(2,1)S(1)}, u32[]{:S(2)}, u32[]{:S(2)}) collective-permute-start(bf16[3,9,16,512]{3,2,1,0:T(8,128)(2,1)S(1)} %get-tuple-element.84.refs_1_), channel_id=1, source_target_pairs={{0,8},{4,20},{8,0},{12,28},{16,24},{20,4},{24,16},{28,12},{1,9},{5... | collective-permute-start | bytes 1327112 | tf_op jit(solution)/shard_map/ppermute | solution.py:944
  34.1 12.0 %collective-permute-start.4 = (bf16[3,9,16,256]{3,2,1,0:T(8,128)(2,1)}, bf16[3,9,16,256]{3,2,1,0:T(8,128)(2,1)}, u32[]{:S(2)}, u32[]{:S(2)}) collective-permute-start(bf16[3,9,16,256]{3,2,1,0:T(8,128)(2,1)} %get-tuple-element.82.rest_0_.refs_0_), channel_id=1, source_target_pairs={{0,8},{4,20},{8,0},{12,28},{16,24},{20,4},{24,16},{28,12},{1,9},{5... | collective-permute-start | bytes 663560 | tf_op jit(solution)/shard_map/ppermute | solution.py:944
  39.2 9.3 %collective-permute-start.5 = (bf16[3,9,16,256]{3,2,1,0:T(8,128)(2,1)}, bf16[3,9,16,256]{3,2,1,0:T(8,128)(2,1)}, u32[]{:S(2)}, u32[]{:S(2)}) collective-permute-start(bf16[3,9,16,256]{3,2,1,0:T(8,128)(2,1)} %collective-permute-done.3.rest_1_), channel_id=1, source_target_pairs={{0,8},{4,20},{8,0},{12,28},{16,24},{20,4},{24,16},{28,12},{1,9},{5... | collective-permute-start | bytes 663560 | tf_op jit(solution)/shard_map/ppermute | solution.py:944
  40.7 11.8 %collective-permute-start.6 = (bf16[3,9,16,256]{3,2,1,0:T(8,128)(2,1)}, bf16[3,9,16,256]{3,2,1,0:T(8,128)(2,1)}, u32[]{:S(2)}, u32[]{:S(2)}) collective-permute-start(bf16[3,9,16,256]{3,2,1,0:T(8,128)(2,1)} %get-tuple-element.82.rest_0_.refs_0_), channel_id=1, source_target_pairs={{0,4},{4,0},{8,12},{12,8},{16,20},{20,16},{24,28},{28,24},{1,5},{5... | collective-permute-start | bytes 663560 | tf_op jit(solution)/shard_map/ppermute | solution.py:937
  46.1 6.4 %collective-permute-start.7 = (bf16[3,9,16,256]{3,2,1,0:T(8,128)(2,1)}, bf16[3,9,16,256]{3,2,1,0:T(8,128)(2,1)}, u32[]{:S(2)}, u32[]{:S(2)}) collective-permute-start(bf16[3,9,16,256]{3,2,1,0:T(8,128)(2,1)} %collective-permute-done.3.rest_1_), channel_id=1, source_target_pairs={{0,4},{4,0},{8,12},{12,8},{16,20},{20,16},{24,28},{28,24},{1,5},{5... | collective-permute-start | bytes 663560 | tf_op jit(solution)/shard_map/ppermute | solution.py:937
  48.4 4.0 %collective-permute-start.8 = (bf16[3,9,16,256]{3,2,1,0:T(8,128)(2,1)}, bf16[3,9,16,256]{3,2,1,0:T(8,128)(2,1)}, u32[]{:S(2)}, u32[]{:S(2)}) collective-permute-start(bf16[3,9,16,256]{3,2,1,0:T(8,128)(2,1)} %collective-permute-done.4.rest_2_), channel_id=1, source_target_pairs={{0,4},{4,0},{8,12},{12,8},{16,20},{20,16},{24,28},{28,24},{1,5},{5... | collective-permute-start | bytes 663560 | tf_op jit(solution)/shard_map/ppermute | solution.py:937
  49.7 2.8 %collective-permute-start.9 = (bf16[3,9,16,256]{3,2,1,0:T(8,128)(2,1)}, bf16[3,9,16,256]{3,2,1,0:T(8,128)(2,1)}, u32[]{:S(2)}, u32[]{:S(2)}) collective-permute-start(bf16[3,9,16,256]{3,2,1,0:T(8,128)(2,1)} %collective-permute-done.5.rest_3_), channel_id=1, source_target_pairs={{0,4},{4,0},{8,12},{12,8},{16,20},{20,16},{24,28},{28,24},{1,5},{5... | collective-permute-start | bytes 663560 | tf_op jit(solution)/shard_map/ppermute | solution.py:937
  50.9 8.4 %collective-permute-start.12 = (bf16[3,9,16,512]{3,2,1,0:T(8,128)(2,1)S(1)}, bf16[3,9,16,512]{3,2,1,0:T(8,128)(2,1)S(1)}, u32[]{:S(2)}, u32[]{:S(2)}) collective-permute-start(bf16[3,9,16,512]{3,2,1,0:T(8,128)(2,1)S(1)} %release.5), channel_id=1, source_target_pairs={{0,8},{4,20},{8,0},{12,28},{16,24},{20,4},{24,16},{28,12},{1,9},{5... | collective-permute-start | bytes 1327112 | tf_op jit(solution)/shard_map/ppermute | solution.py:944
  52.4 1.8 copy-start.7
  59.3 15.1 %copy-start.4 = (bf16[128,512]{1,0:T(8,128)(2,1)S(1)}, bf16[128,512]{1,0:T(8,128)(2,1)}, u32[]{:S(2)}) copy-start(bf16[128,512]{1,0:T(8,128)(2,1)} %copy-done.3) | copy-start | bytes 393220
  59.3 15.1 %copy-start.6 = (bf16[128,512]{1,0:T(8,128)(2,1)S(1)}, bf16[128,512]{1,0:T(8,128)(2,1)}, u32[]{:S(2)}) copy-start(bf16[128,512]{1,0:T(8,128)(2,1)} %copy-done.5) | copy-start | bytes 393220
  59.4 19.5 %copy-start.1 = (bf16[9,128,512]{2,1,0:T(8,128)(2,1)S(1)}, bf16[9,128,512]{2,1,0:T(8,128)(2,1)}, u32[]{:S(2)}) copy-start(bf16[9,128,512]{2,1,0:T(8,128)(2,1)} %own.3) | copy-start | bytes 3538948
  73.4 1.8 collective-permute-start.13
  73.4 3.1 %collective-permute-start.14 = (bf16[3,9,16,512]{3,2,1,0:T(8,128)(2,1)S(1)}, bf16[3,9,16,512]{3,2,1,0:T(8,128)(2,1)S(1)}, u32[]{:S(2)}, u32[]{:S(2)}) collective-permute-start(bf16[3,9,16,512]{3,2,1,0:T(8,128)(2,1)S(1)} %get-tuple-element.87.rest_1_), channel_id=1, source_target_pairs={{0,4},{4,0},{8,12},{12,8},{16,20},{20,16},{24,28},{28,24},{1,5},{5... | collective-permute-start | bytes 1327112 | tf_op jit(solution)/shard_map/ppermute | solution.py:937
  73.9 4.9 %collective-permute-start.15 = (bf16[3,9,16,512]{3,2,1,0:T(8,128)(2,1)S(1)}, bf16[3,9,16,512]{3,2,1,0:T(8,128)(2,1)S(1)}, u32[]{:S(2)}, u32[]{:S(2)}) collective-permute-start(bf16[3,9,16,512]{3,2,1,0:T(8,128)(2,1)S(1)} %get-tuple-element.88.rest_2_), channel_id=1, source_target_pairs={{0,4},{4,0},{8,12},{12,8},{16,20},{20,16},{24,28},{28,24},{1,5},{5... | collective-permute-start | bytes 1327112 | tf_op jit(solution)/shard_map/ppermute | solution.py:937
  73.9 4.9 %collective-permute-start.16 = (bf16[3,9,16,512]{3,2,1,0:T(8,128)(2,1)S(1)}, bf16[3,9,16,512]{3,2,1,0:T(8,128)(2,1)S(1)}, u32[]{:S(2)}, u32[]{:S(2)}) collective-permute-start(bf16[3,9,16,512]{3,2,1,0:T(8,128)(2,1)S(1)} %get-tuple-element.89.rest_3_), channel_id=1, source_target_pairs={{0,4},{4,0},{8,12},{12,8},{16,20},{20,16},{24,28},{28,24},{1,5},{5... | collective-permute-start | bytes 1327112 | tf_op jit(solution)/shard_map/ppermute | solution.py:937
  74.4 14.3 %collective-permute-start.17 = (bf16[128,512]{1,0:T(8,128)(2,1)S(1)}, bf16[128,512]{1,0:T(8,128)(2,1)S(1)}, u32[]{:S(2)}, u32[]{:S(2)}) collective-permute-start(bf16[128,512]{1,0:T(8,128)(2,1)S(1)} %get-tuple-element.94), channel_id=1, source_target_pairs={{0,1},{1,0},{2,3},{3,2},{4,5},{5,4},{6,7},{7,6},{8,9},{9,8},{10,11... | collective-permute-start | bytes 393224 | tf_op jit(solution)/shard_map/ppermute | solution.py:947
  75.2 13.5 %collective-permute-start.18 = (bf16[128,512]{1,0:T(8,128)(2,1)S(1)}, bf16[128,512]{1,0:T(8,128)(2,1)S(1)}, u32[]{:S(2)}, u32[]{:S(2)}) collective-permute-start(bf16[128,512]{1,0:T(8,128)(2,1)S(1)} %get-tuple-element.95), channel_id=1, source_target_pairs={{0,2},{1,3},{2,0},{3,1},{4,6},{5,7},{6,4},{7,5},{8,10},{9,11},{10,... | collective-permute-start | bytes 393224 | tf_op jit(solution)/shard_map/ppermute | solution.py:947
  76.5 12.2 %collective-permute-start.19 = (bf16[128,512]{1,0:T(8,128)(2,1)S(1)}, bf16[128,512]{1,0:T(8,128)(2,1)S(1)}, u32[]{:S(2)}, u32[]{:S(2)}) collective-permute-start(bf16[128,512]{1,0:T(8,128)(2,1)S(1)} %get-tuple-element.96), channel_id=1, source_target_pairs={{0,3},{1,2},{2,1},{3,0},{4,7},{5,6},{6,5},{7,4},{8,11},{9,10},{10,... | collective-permute-start | bytes 393224 | tf_op jit(solution)/shard_map/ppermute | solution.py:947
  124.6 4.6 %collective-permute-start.23 = (bf16[4,4,9,16,512]{4,3,2,1,0:T(8,128)(2,1)S(1)}, bf16[4,4,9,16,512]{4,3,2,1,0:T(8,128)(2,1)S(1)}, u32[]{:S(2)}, u32[]{:S(2)}) collective-permute-start(bf16[4,4,9,16,512]{4,3,2,1,0:T(8,128)(2,1)S(1)} %get-tuple-element.117), channel_id=1, source_target_pairs={{0,4},{4,0},{8,12},{12,8},{16,20},{20,16},{24,28},{28,24},{1,5},{5... | collective-permute-start | bytes 7077896 | tf_op jit(solution)/shard_map/ppermute | solution.py:937
  124.6 15.2 %collective-permute-start.20 = (bf16[128,384]{1,0:T(8,128)(2,1)S(1)}, bf16[128,384]{1,0:T(8,128)(2,1)S(1)}, u32[]{:S(2)}, u32[]{:S(2)}) collective-permute-start(bf16[128,384]{1,0:T(8,128)(2,1)S(1)} %get-tuple-element.106), channel_id=1, source_target_pairs={{0,1},{1,0},{2,3},{3,2},{4,5},{5,4},{6,7},{7,6},{8,9},{9,8},{10,11... | collective-permute-start | bytes 294920 | tf_op jit(solution)/shard_map/ppermute | solution.py:947
  124.9 14.9 %collective-permute-start.21 = (bf16[128,384]{1,0:T(8,128)(2,1)S(1)}, bf16[128,384]{1,0:T(8,128)(2,1)S(1)}, u32[]{:S(2)}, u32[]{:S(2)}) collective-permute-start(bf16[128,384]{1,0:T(8,128)(2,1)S(1)} %get-tuple-element.107), channel_id=1, source_target_pairs={{0,2},{1,3},{2,0},{3,1},{4,6},{5,7},{6,4},{7,5},{8,10},{9,11},{10,... | collective-permute-start | bytes 294920 | tf_op jit(solution)/shard_map/ppermute | solution.py:947
  126.4 13.4 %collective-permute-start.22 = (bf16[128,384]{1,0:T(8,128)(2,1)S(1)}, bf16[128,384]{1,0:T(8,128)(2,1)S(1)}, u32[]{:S(2)}, u32[]{:S(2)}) collective-permute-start(bf16[128,384]{1,0:T(8,128)(2,1)S(1)} %get-tuple-element.108), channel_id=1, source_target_pairs={{0,3},{1,2},{2,1},{3,0},{4,7},{5,6},{6,5},{7,4},{8,11},{9,10},{10,... | collective-permute-start | bytes 294920 | tf_op jit(solution)/shard_map/ppermute | solution.py:947
  129.7 10.2 %collective-permute-start.24 = (bf16[4,9,16,512]{3,2,1,0:T(8,128)(2,1)S(1)}, bf16[4,9,16,512]{3,2,1,0:T(8,128)(2,1)S(1)}, u32[]{:S(2)}, u32[]{:S(2)}) collective-permute-start(bf16[4,9,16,512]{3,2,1,0:T(8,128)(2,1)S(1)} %get-tuple-element.118.after), channel_id=1, source_target_pairs={{0,8},{4,20},{8,0},{12,28},{16,24},{20,4},{24,16},{28,12},{1,9},{5... | collective-permute-start | bytes 1769480 | tf_op jit(solution)/shard_map/ppermute | solution.py:944
  140.0 12.4 %collective-permute-start.25 = (bf16[4,9,16,512]{3,2,1,0:T(8,128)(2,1)S(1)}, bf16[4,9,16,512]{3,2,1,0:T(8,128)(2,1)S(1)}, u32[]{:S(2)}, u32[]{:S(2)}) collective-permute-start(bf16[4,9,16,512]{3,2,1,0:T(8,128)(2,1)S(1)} %mid_sum_b.1), channel_id=1, source_target_pairs={{0,16},{4,12},{8,24},{12,4},{16,0},{20,28},{24,8},{28,20},{1,17},{... | collective-permute-start | bytes 1769480 | tf_op jit(solution)/shard_map/ppermute | solution.py:944
  158.3 6.6 %collective-permute-start.29 = (bf16[4,4,9,16,256]{4,3,2,1,0:T(8,128)(2,1)S(1)}, bf16[4,4,9,16,256]{4,3,2,1,0:T(8,128)(2,1)S(1)}, u32[]{:S(2)}, u32[]{:S(2)}) collective-permute-start(bf16[4,4,9,16,256]{4,3,2,1,0:T(8,128)(2,1)S(1)} %get-tuple-element.130), channel_id=1, source_target_pairs={{0,4},{4,0},{8,12},{12,8},{16,20},{20,16},{24,28},{28,24},{1,5},{5... | collective-permute-start | bytes 3538952 | tf_op jit(solution)/shard_map/ppermute | solution.py:937
  158.4 9.9 %collective-permute-start.31 = (bf16[4,9,16,512]{3,2,1,0:T(8,128)(2,1)S(1)}, bf16[4,9,16,512]{3,2,1,0:T(8,128)(2,1)S(1)}, u32[]{:S(2)}, u32[]{:S(2)}) collective-permute-start(bf16[4,9,16,512]{3,2,1,0:T(8,128)(2,1)S(1)} %release.9), channel_id=1, source_target_pairs={{0,8},{4,20},{8,0},{12,28},{16,24},{20,4},{24,16},{28,12},{1,9},{5... | collective-permute-start | bytes 1769480 | tf_op jit(solution)/shard_map/ppermute | solution.py:944
  165.2 12.4 %collective-permute-start.30 = (bf16[8,9,16,256]{3,2,1,0:T(8,128)(2,1)S(1)}, bf16[8,9,16,256]{3,2,1,0:T(8,128)(2,1)S(1)}, u32[]{:S(2)}, u32[]{:S(2)}) collective-permute-start(bf16[8,9,16,256]{3,2,1,0:T(8,128)(2,1)S(1)} %get-tuple-element.132), channel_id=1, source_target_pairs={{0,8},{4,20},{8,0},{12,28},{16,24},{20,4},{24,16},{28,12},{1,9},{5... | collective-permute-start | bytes 1769480 | tf_op jit(solution)/shard_map/ppermute | solution.py:944
  166.5 11.2 %collective-permute-start.27 = (bf16[64,1536]{1,0:T(8,128)(2,1)S(1)}, bf16[64,1536]{1,0:T(8,128)(2,1)S(1)}, u32[]{:S(2)}, u32[]{:S(2)}) collective-permute-start(bf16[64,1536]{1,0:T(8,128)(2,1)S(1)} %get-tuple-element.126), channel_id=1, source_target_pairs={{0,2},{1,3},{2,0},{3,1},{4,6},{5,7},{6,4},{7,5},{8,10},{9,11},{10,... | collective-permute-start | bytes 589832 | tf_op jit(solution)/shard_map/ppermute | solution.py:947
  168.5 12.9 %collective-permute-start.33 = (bf16[2,9,16,512]{3,2,1,0:T(8,128)(2,1)S(1)}, bf16[2,9,16,512]{3,2,1,0:T(8,128)(2,1)S(1)}, u32[]{:S(2)}, u32[]{:S(2)}) collective-permute-start(bf16[2,9,16,512]{3,2,1,0:T(8,128)(2,1)S(1)} %get-tuple-element.138), channel_id=1, source_target_pairs={{0,1},{1,0},{2,3},{3,2},{4,5},{5,4},{6,7},{7,6},{8,9},{9,8},{10,11... | collective-permute-start | bytes 884744 | tf_op jit(solution)/shard_map/ppermute | solution.py:947
  177.8 6.8 %collective-permute-start.32 = (bf16[4,9,16,256]{3,2,1,0:T(8,128)(2,1)S(1)}, bf16[4,9,16,256]{3,2,1,0:T(8,128)(2,1)S(1)}, u32[]{:S(2)}, u32[]{:S(2)}) collective-permute-start(bf16[4,9,16,256]{3,2,1,0:T(8,128)(2,1)S(1)} %get-tuple-element.137), channel_id=1, source_target_pairs={{0,16},{4,12},{8,24},{12,4},{16,0},{20,28},{24,8},{28,20},{1,17},{... | collective-permute-start | bytes 884744 | tf_op jit(solution)/shard_map/ppermute | solution.py:944
  178.7 8.6 %collective-permute-start.28 = (bf16[64,1536]{1,0:T(8,128)(2,1)S(1)}, bf16[64,1536]{1,0:T(8,128)(2,1)S(1)}, u32[]{:S(2)}, u32[]{:S(2)}) collective-permute-start(bf16[64,1536]{1,0:T(8,128)(2,1)S(1)} %get-tuple-element.127), channel_id=1, source_target_pairs={{0,3},{1,2},{2,1},{3,0},{4,7},{5,6},{6,5},{7,4},{8,11},{9,10},{10,... | collective-permute-start | bytes 589832 | tf_op jit(solution)/shard_map/ppermute | solution.py:947
  184.6 9.6 %collective-permute-start.34 = (bf16[2,9,16,256]{3,2,1,0:T(8,128)(2,1)S(1)}, bf16[2,9,16,256]{3,2,1,0:T(8,128)(2,1)S(1)}, u32[]{:S(2)}, u32[]{:S(2)}) collective-permute-start(bf16[2,9,16,256]{3,2,1,0:T(8,128)(2,1)S(1)} %get-tuple-element.142), channel_id=1, source_target_pairs={{0,1},{1,0},{2,3},{3,2},{4,5},{5,4},{6,7},{7,6},{8,9},{9,8},{10,11... | collective-permute-start | bytes 442376 | tf_op jit(solution)/shard_map/ppermute | solution.py:947
  184.7 9.6 %collective-permute-start.36 = (bf16[1,9,16,512]{3,2,1,0:T(8,128)(2,1)S(1)}, bf16[1,9,16,512]{3,2,1,0:T(8,128)(2,1)S(1)}, u32[]{:S(2)}, u32[]{:S(2)}) collective-permute-start(bf16[1,9,16,512]{3,2,1,0:T(8,128)(2,1)S(1)} %get-tuple-element.145), channel_id=1, source_target_pairs={{0,2},{1,3},{2,0},{3,1},{4,6},{5,7},{6,4},{7,5},{8,10},{9,11},{10,... | collective-permute-start | bytes 442376 | tf_op jit(solution)/shard_map/ppermute | solution.py:947
  187.3 13.5 %collective-permute-start.26 = (bf16[64,1536]{1,0:T(8,128)(2,1)S(1)}, bf16[64,1536]{1,0:T(8,128)(2,1)S(1)}, u32[]{:S(2)}, u32[]{:S(2)}) collective-permute-start(bf16[64,1536]{1,0:T(8,128)(2,1)S(1)} %get-tuple-element.125), channel_id=1, source_target_pairs={{0,1},{1,0},{2,3},{3,2},{4,5},{5,4},{6,7},{7,6},{8,9},{9,8},{10,11... | collective-permute-start | bytes 589832 | tf_op jit(solution)/shard_map/ppermute | solution.py:947
  194.3 5.7 %collective-permute-start.35 = (bf16[1,9,16,256]{3,2,1,0:T(8,128)(2,1)S(1)}, bf16[1,9,16,256]{3,2,1,0:T(8,128)(2,1)S(1)}, u32[]{:S(2)}, u32[]{:S(2)}) collective-permute-start(bf16[1,9,16,256]{3,2,1,0:T(8,128)(2,1)S(1)} %get-tuple-element.144), channel_id=1, source_target_pairs={{0,2},{1,3},{2,0},{3,1},{4,6},{5,7},{6,4},{7,5},{8,10},{9,11},{10,... | collective-permute-start | bytes 221192 | tf_op jit(solution)/shard_map/ppermute | solution.py:947
  194.4 7.7 %collective-permute-start.40 = (bf16[9,16,512]{2,1,0:T(8,128)(2,1)S(1)}, bf16[9,16,512]{2,1,0:T(8,128)(2,1)S(1)}, u32[]{:S(2)}, u32[]{:S(2)}) collective-permute-start(bf16[9,16,512]{2,1,0:T(8,128)(2,1)S(1)} %mid_sum_3.1.rest_0_.refs_0_), channel_id=1, source_target_pairs={{0,16},{4,12},{8,24},{12,4},{16,0},{20,28},{24,8},{28,20},{1,17},{... | collective-permute-start | bytes 442376 | tf_op jit(solution)/shard_map/ppermute | solution.py:968
  195.1 7.0 %collective-permute-start.41 = (bf16[9,16,512]{2,1,0:T(8,128)(2,1)S(1)}, bf16[9,16,512]{2,1,0:T(8,128)(2,1)S(1)}, u32[]{:S(2)}, u32[]{:S(2)}) collective-permute-start(bf16[9,16,512]{2,1,0:T(8,128)(2,1)S(1)} %mid_sum_3.1.rest_0_.refs_0_), channel_id=1, source_target_pairs={{0,8},{4,20},{8,0},{12,28},{16,24},{20,4},{24,16},{28,12},{1,9},{5... | collective-permute-start | bytes 442376 | tf_op jit(solution)/shard_map/ppermute | solution.py:968
  196.4 7.0 %collective-permute-start.42 = (bf16[9,16,512]{2,1,0:T(8,128)(2,1)S(1)}, bf16[9,16,512]{2,1,0:T(8,128)(2,1)S(1)}, u32[]{:S(2)}, u32[]{:S(2)}) collective-permute-start(bf16[9,16,512]{2,1,0:T(8,128)(2,1)S(1)} %mid_sum_3.1.rest_0_.refs_0_), channel_id=1, source_target_pairs={{0,24},{4,28},{8,16},{12,20},{16,8},{20,12},{24,0},{28,4},{1,25},{... | collective-permute-start | bytes 442376 | tf_op jit(solution)/shard_map/ppermute | solution.py:968
  200.0 4.4 %collective-permute-start.37 = (bf16[9,16,256]{2,1,0:T(8,128)(2,1)S(1)}, bf16[9,16,256]{2,1,0:T(8,128)(2,1)S(1)}, u32[]{:S(2)}, u32[]{:S(2)}) collective-permute-start(bf16[9,16,256]{2,1,0:T(8,128)(2,1)S(1)} %in_sum_3.1.refs_0_), channel_id=1, source_target_pairs={{0,16},{4,12},{8,24},{12,4},{16,0},{20,28},{24,8},{28,20},{1,17},{... | collective-permute-start | bytes 221192 | tf_op jit(solution)/shard_map/ppermute | solution.py:944
  200.8 4.4 %collective-permute-start.38 = (bf16[9,16,256]{2,1,0:T(8,128)(2,1)S(1)}, bf16[9,16,256]{2,1,0:T(8,128)(2,1)S(1)}, u32[]{:S(2)}, u32[]{:S(2)}) collective-permute-start(bf16[9,16,256]{2,1,0:T(8,128)(2,1)S(1)} %in_sum_3.1.refs_0_), channel_id=1, source_target_pairs={{0,8},{4,20},{8,0},{12,28},{16,24},{20,4},{24,16},{28,12},{1,9},{5... | collective-permute-start | bytes 221192 | tf_op jit(solution)/shard_map/ppermute | solution.py:944
  205.2 3.3 %collective-permute-start.43 = (bf16[4,9,16,512]{3,2,1,0:T(8,128)(2,1)S(1)}, bf16[4,9,16,512]{3,2,1,0:T(8,128)(2,1)S(1)}, u32[]{:S(2)}, u32[]{:S(2)}) collective-permute-start(bf16[4,9,16,512]{3,2,1,0:T(8,128)(2,1)S(1)} %mid_stack.1.mine), channel_id=1, source_target_pairs={{0,4},{4,0},{8,12},{12,8},{16,20},{20,16},{24,28},{28,24},{1,5},{5... | collective-permute-start | bytes 1769480 | tf_op jit(solution)/shard_map/ppermute | solution.py:937
  205.8 4.4 %collective-permute-start.39 = (bf16[9,16,256]{2,1,0:T(8,128)(2,1)S(1)}, bf16[9,16,256]{2,1,0:T(8,128)(2,1)S(1)}, u32[]{:S(2)}, u32[]{:S(2)}) collective-permute-start(bf16[9,16,256]{2,1,0:T(8,128)(2,1)S(1)} %collective-permute-done.37.refs_4_.refs_1_), channel_id=1, source_target_pairs={{0,8},{4,20},{8,0},{12,28},{16,24},{20,4},{24,16},{28,12},{1,9},{5... | collective-permute-start | bytes 221192 | tf_op jit(solution)/shard_map/ppermute | solution.py:944
  210.2 1.6 collective-permute-start.44

commit v6 on v5

--- a/solution.py
+++ b/solution.py
@@ -1000,7 +1000,7 @@
         planes_mid = links.gather_planes(pieces_mid, [maps])
 
         pre1, x3_in, pay = first(g, lengths, gains, maps, w_in)
-        got = everyone(fan(g, pay, cots[0], *planes_mid[1:]))
+        got = everyone(fan(g, pay, cots[0], *planes_mid[1:-1]))
         planes_mid = release([got], planes_mid)
         w_mid = join(g, weight_mid, links.gather_cores(planes_mid), g.cm, "join_mid")
         cs = links.exchange(release([got], cots))

time: 213 us -> 212 us (level)
  local copies, waits for them, and re-layouts: 3.46 us -> 6.53 us
  waiting for transfers between devices: 51.3 us -> 48.5 us
    ppermute x14, waiting for transfers between devices: 18.7 us -> 15.3 us  [plane(): lax.ppermute(x, 'dp', [(i, i ^ 2 * g.mask(i & 1, turn)) for i in range(g....]
    unnamed x25 -> x31, local copies, waits for them, and re-layouts: 1.88 us -> 4.96 us
  transfers between devices with their start and end apart: 46 -> 46, of which waited for: 18 -> 19; matrix products, arithmetic and copies ran while one was open for 1% -> 1% of each run, Pallas kernels for 19% -> 19%
where the time goes in v6:
time: 212 us; the launch traced here: 211 us
  Pallas kernels  62.9 us (30%)
  waiting for transfers between devices  48.5 us (23%)
  starting transfers between devices  47 us (22%)
  blocking collectives  45.4 us (21%)
  local copies, waits for them, and re-layouts  6.53 us (3%)
    pallas_call x23, Pallas kernels, call(): pl.pallas_call(body, out_shape=[pltpu.VMEM(o.shape, o.dtype) if isinstanc...  56.5 us
    all_to_all x4, blocking collectives, everyone(): return lax.all_to_all(x, ('dp', 'chan'), 0, 0)  45.4 us
    ppermute x16, waiting for transfers between devices, chan(): return lax.ppermute(x, 'chan', [(i, i ^ k) for i in range(self.g.nch)])  28.9 us
    ppermute x16, starting transfers between devices, chan(): return lax.ppermute(x, 'chan', [(i, i ^ k) for i in range(self.g.nch)])  19.2 us
    ppermute x14, starting transfers between devices, plane(): lax.ppermute(x, 'dp', [(i, i ^ 2 * g.mask(i & 1, turn)) for i in range(g....  16.1 us
    ppermute x14, waiting for transfers between devices, plane(): lax.ppermute(x, 'dp', [(i, i ^ 2 * g.mask(i & 1, turn)) for i in range(g....  15.3 us
    all_to_all x1, starting transfers between devices, body(): maps = lax.all_to_all(release_far([pieces_in], cells), 'chan', 0, 0)  6.29 us
    unnamed x31, local copies, waits for them, and re-layouts  4.96 us
  transfers between devices with their start and end apart: 46, of which 19 were waited for; matrix products, arithmetic and copies ran while one was open for 1% of the time, Pallas kernels for 19%

profile of v6, /device:TPU:0, one launch (start us, length us, event | category | flops | bytes accessed | tf_op | source)
XLA Modules:
  0.0 211.3 jit_solution(15460591181529898887)
XLA Ops:
  0.6 1.0 cut_weights.1.after
  1.6 3.1 %collective-permute-start = (bf16[9,16,768]{2,1,0:T(8,128)(2,1)S(1)}, bf16[9,16,768]{2,1,0:T(8,128)(2,1)S(1)}, u32[]{:S(2)}, u32[]{:S(2)}) collective-permute-start(bf16[9,16,768]{2,1,0:T(8,128)(2,1)S(1)} %cut_weights.1.after), channel_id=1, source_target_pairs={{0,1},{1,0},{2,3},{3,2},{4,5},{5,4},{6,7},{7,6},{8,9},{9,8},{10,11... | collective-permute-start | bytes 663560 | tf_op jit(solution)/shard_map/ppermute | solution.py:947
  4.7 2.6 %collective-permute-start.1 = (bf16[9,16,768]{2,1,0:T(8,128)(2,1)S(1)}, bf16[9,16,768]{2,1,0:T(8,128)(2,1)S(1)}, u32[]{:S(2)}, u32[]{:S(2)}) collective-permute-start(bf16[9,16,768]{2,1,0:T(8,128)(2,1)S(1)} %cut_weights.1.after), channel_id=1, source_target_pairs={{0,2},{1,3},{2,0},{3,1},{4,6},{5,7},{6,4},{7,5},{8,10},{9,11},{10,... | collective-permute-start | bytes 663560 | tf_op jit(solution)/shard_map/ppermute | solution.py:947
  7.3 2.0 cut_maps.1.after.refs_1_
  9.3 1.1 copy-done
  10.5 1.1 cut_cotangent.1
  11.6 0.7 copy-done.8
  12.3 1.8 collective-permute-done.rest_0_
  14.1 9.3 %collective-permute-done.1.rest_1_ = bf16[9,16,768]{2,1,0:T(8,128)(2,1)S(1)} collective-permute-done((bf16[9,16,768]{2,1,0:T(8,128)(2,1)S(1)}, bf16[9,16,768]{2,1,0:T(8,128)(2,1)S(1)}, u32[]{:S(2)}, u32[]{:S(2)}) %collective-permute-start.1) | collective-permute-done | bytes 221216 | tf_op jit(solution)/shard_map/ppermute | solution.py:947
  23.5 0.7 sort_pieces.1
  24.2 6.3 %all-to-all-start = ((bf16[4,64,1664]{2,1,0:T(8,128)(2,1)}), bf16[4,64,1664]{2,1,0:T(8,128)(2,1)S(1)}, u32[]{:S(2)}, u32[]{:S(2)}) async-start(bf16[4,64,1664]{2,1,0:T(8,128)(2,1)} %release_far.1), calls=%async_computation | async-start | bytes 1703936 | tf_op jit(solution)/shard_map/all_to_all | solution.py:997
  30.5 1.5 collective-permute-start.3
  32.5 1.5 collective-permute-start.4
  34.0 5.0 %collective-permute-done.3.rest_1_ = bf16[3,9,16,256]{3,2,1,0:T(8,128)(2,1)S(1)} collective-permute-done((bf16[3,9,16,256]{3,2,1,0:T(8,128)(2,1)}, bf16[3,9,16,256]{3,2,1,0:T(8,128)(2,1)S(1)}, u32[]{:S(2)}, u32[]{:S(2)}) %collective-permute-start.3) | collective-permute-done | bytes 221216 | tf_op jit(solution)/shard_map/ppermute | solution.py:944
  39.0 1.5 collective-permute-start.5
  41.1 3.8 %collective-permute-done.5.rest_3_ = bf16[3,9,16,256]{3,2,1,0:T(8,128)(2,1)S(1)} collective-permute-done((bf16[3,9,16,256]{3,2,1,0:T(8,128)(2,1)S(1)}, bf16[3,9,16,256]{3,2,1,0:T(8,128)(2,1)S(1)}, u32[]{:S(2)}, u32[]{:S(2)}) %collective-permute-start.5) | collective-permute-done | bytes 221216 | tf_op jit(solution)/shard_map/ppermute | solution.py:944
  45.0 1.5 collective-permute-start.11
  46.6 1.1 join_in.1.w
  47.8 1.4 copy-done.3
  49.2 1.7 all-to-all-done.maps.refs_0_
  50.9 1.7 copy-done.4
  52.5 5.1 %first_conv.1 = (f32[8,208,512]{2,1,0:T(8,128)S(1)}, bf16[8,208,768]{2,1,0:T(8,128)(2,1)S(1)}, f32[1,1664]{1,0:T(1,128)S(1)}) custom-call(s32[2]{0:T(128)S(1)} %copy-done.10, f32[4,128]{1,0:T(4,128)S(1)} %pad_maximum_fusion.gains, bf16[9,512,256]{2,1,0:T(8,128)(2,1)S(1)} %copy-done.4, bf16[4,64,1664]{2,1,0:T(8,128)(2,1)S(1)} %all-to-all-done.maps.refs_0_), custom_call_target="tpu_custom_call" | custom-call | flops 3925868544 | bytes 10485760 | tf_op jit(solution)/shard_map/first_conv/pallas_call | solution.py:90
  57.7 1.6 collective-permute-start.12
  59.3 12.5 %all_to_all.25.refs_0_.got = f32[32,1,1664]{2,1,0:T(1,128)S(1)} all-to-all(f32[32,1,1664]{2,1,0:T(1,128)S(1)} %fan.3), channel_id=1, replica_groups=mesh['dp'=8,'chan'=4] {'dp','chan'}, dimensions={0} | all-to-all | bytes 425984 | tf_op jit(solution)/shard_map/all_to_all | solution.py:972
  73.0 0.6 collective-permute-done.13.rest_4_
  73.6 1.3 collective-permute-start.18
  74.9 2.3 %collective-permute-start.19 = (bf16[128,512]{1,0:T(8,128)(2,1)S(1)}, bf16[128,512]{1,0:T(8,128)(2,1)S(1)}, u32[]{:S(2)}, u32[]{:S(2)}) collective-permute-start(bf16[128,512]{1,0:T(8,128)(2,1)S(1)} %get-tuple-element.96), channel_id=1, source_target_pairs={{0,3},{1,2},{2,1},{3,0},{4,7},{5,6},{6,5},{7,4},{8,11},{9,10},{10,... | collective-permute-start | bytes 393224 | tf_op jit(solution)/shard_map/ppermute | solution.py:947
  77.6 9.5 %second_conv.1 = (f32[8,208,512]{2,1,0:T(8,128)S(1)}, bf16[8,208,1536]{2,1,0:T(8,128)(2,1)S(1)}, f32[16,512]{1,0:T(8,128)S(1)}, f32[1,1024]{1,0:T(1,128)S(1)}, f32[1,128]{1,0:T(1,128)S(1)}) custom-call(s32[2]{0:T(128)S(1)} %copy-done.10, f32[32,1,1664]{2,1,0:T(1,128)S(1)} %all_to_all.25.refs_0_.got, f32[8,208,512]{2,1,0:T(8,128)S(1)} %get-tuple-element.85.pre1.pre, ...), custom_call_target="tpu_custom_call" | custom-call | flops 7851737088 | bytes 17825792 | tf_op jit(solution)/shard_map/second_conv/pallas_call | solution.py:90
  87.1 11.0 %all_to_all.26.got = f32[32,1,1024]{2,1,0:T(1,128)S(1)} all-to-all(f32[32,1,1024]{2,1,0:T(1,128)S(1)} %fan.4), channel_id=1, replica_groups=mesh['dp'=8,'chan'=4] {'dp','chan'}, dimensions={0} | all-to-all | bytes 262144 | tf_op jit(solution)/shard_map/all_to_all | solution.py:972
  98.1 5.2 %pool.1 = (bf16[128,384]{1,0:T(8,128)(2,1)S(1)}, bf16[128,384]{1,0:T(8,128)(2,1)S(1)}, bf16[128,384]{1,0:T(8,128)(2,1)S(1)}, bf16[128,384]{1,0:T(8,128)(2,1)S(1)...) custom-call(s32[2]{0:T(128)S(1)} %copy-done.10, ...), custom_call_target="tpu_custom_call" | custom-call | flops 4000000000 | bytes 8388608 | tf_op jit(solution)/shard_map/pool/pallas_call | solution.py:90
  103.4 10.1 %all_to_all.27.refs_0_.got.after = f32[32,1,1024]{2,1,0:T(1,128)S(1)} all-to-all(f32[32,1,1024]{2,1,0:T(1,128)S(1)} %get-tuple-element.100), channel_id=1, replica_groups=mesh['dp'=8,'chan'=4] {'dp','chan'}, dimensions={0} | all-to-all | bytes 262144 | tf_op jit(solution)/shard_map/all_to_all | solution.py:972
  113.5 9.5 %weight_mid_terms.1 = (bf16[8,208,512]{2,1,0:T(8,128)(2,1)S(1)}, f32[8,512]{1,0:T(8,128)S(1)}, f32[8,128]{1,0:T(8,128)}, bf16[2,4,4,9,16,512]{5,4,3,2,1,0:T(8,128)(2,1)S(1)}, bf16[4,4,9,16,512]{4,3,2,1,0:T(8,128)(2,1)S(1)}) custom-call(s32[2]{0:T(128)S(1)} %copy-done.10, f32[32,1,1024]{2,1,0:T(1,128)S(1)} %all_to_all.27.refs_0_.got.after, ...), custom_call_target="tpu_custom_call" | custom-call | flops 7851737088 | bytes 15728640 | tf_op jit(solution)/shard_map/weight_mid_terms/pallas_call | solution.py:90
  123.3 1.5 collective-permute-start.21
  124.8 2.7 %collective-permute-start.22 = (bf16[128,384]{1,0:T(8,128)(2,1)S(1)}, bf16[128,384]{1,0:T(8,128)(2,1)S(1)}, u32[]{:S(2)}, u32[]{:S(2)}) collective-permute-start(bf16[128,384]{1,0:T(8,128)(2,1)S(1)} %get-tuple-element.108), channel_id=1, source_target_pairs={{0,3},{1,2},{2,1},{3,0},{4,7},{5,6},{6,5},{7,4},{8,11},{9,10},{10,... | collective-permute-start | bytes 294920 | tf_op jit(solution)/shard_map/ppermute | solution.py:947
  127.5 0.5 mid_core_sum.1
  128.1 0.8 collective-permute-start.24
  128.9 9.3 %second_back.1 = (f32[8,208,512]{2,1,0:T(8,128)S(1)}, f32[1,1280]{1,0:T(1,128)S(1)}) custom-call(s32[2]{0:T(128)S(1)} %copy-done.10, f32[16,512]{1,0:T(8,128)S(1)} %get-tuple-element.110.table, bf16[8,208,512]{2,1,0:T(8,128)(2,1)S(1)} %get-tuple-element.113.grad, f32[8,208,512]{2,1,0:T(8,128)S(1)} %get-tuple-element.85.pre1.pre, ...), custom_call_target="tpu_custom_call" | custom-call | flops 7851737088 | bytes 20971520 | tf_op jit(solution)/shard_map/second_back/pallas_call | solution.py:90
  138.4 0.6 collective-permute-start.25
  139.0 11.8 %all_to_all.28.got.refs_0_ = f32[32,1,1280]{2,1,0:T(1,128)S(1)} all-to-all(f32[32,1,1280]{2,1,0:T(1,128)S(1)} %fan.5), channel_id=1, replica_groups=mesh['dp'=8,'chan'=4] {'dp','chan'}, dimensions={0} | all-to-all | bytes 327680 | tf_op jit(solution)/shard_map/all_to_all | solution.py:972
  150.8 5.8 %weight_in_terms.1 = (bf16[8,208,512]{2,1,0:T(8,128)(2,1)S(1)}, f32[8,512]{1,0:T(8,128)S(1)}, f32[8,128]{1,0:T(8,128)S(1)}, bf16[2,4,4,9,16,256]{5,4,3,2,1,0:T(8,128)(2,1)S(1)}, bf16[4,4,9,16,256]{4,3,2,1,0:T(8,128)(2,1)S(1)}) custom-call(s32[2]{0:T(128)S(1)} %copy-done.10, f32[32,1,1280]{2,1,0:T(1,128)S(1)} %all_to_all.28.got.refs_0_, ...), custom_call_target="tpu_custom_call" | custom-call | flops 3925868544 | bytes 15728640 | tf_op jit(solution)/shard_map/weight_in_terms/pallas_call | solution.py:90
  156.7 0.9 collective-permute-start.31
  157.6 5.6 %spectra_back.1 = (bf16[64,1536]{1,0:T(8,128)(2,1)S(1)}, bf16[64,1536]{1,0:T(8,128)(2,1)S(1)}, bf16[64,1536]{1,0:T(8,128)(2,1)S(1)}, bf16[64,1536]{1,0:T(8,128)(2,1)S(1)}) custom-call(s32[2]{0:T(128)S(1)} %copy-done.10, bf16[8,208,512]{2,1,0:T(8,128)(2,1)S(1)} %get-tuple-element.123.grad.after, bf16[8,208,512]{2,1,0:T(8,128)(2,1)S(1)} %get-tuple-element.123.grad.after, ...), custom_call_target="tpu_custom_call" | custom-call | flops 3925868544 | bytes 5242880 | tf_op jit(solution)/shard_map/spectra_back/pallas_call | solution.py:90
  163.6 1.3 collective-permute-start.30
  165.3 1.4 collective-permute-done.31.rest_1_
  167.2 8.8 %collective-permute-done.27.rest_2_.rest_1_ = bf16[64,1536]{1,0:T(8,128)(2,1)S(1)} collective-permute-done((bf16[64,1536]{1,0:T(8,128)(2,1)S(1)}, bf16[64,1536]{1,0:T(8,128)(2,1)S(1)}, u32[]{:S(2)}, u32[]{:S(2)}) %collective-permute-start.27) | collective-permute-done | bytes 196640 | tf_op jit(solution)/shard_map/ppermute | solution.py:947
  176.2 1.0 collective-permute-start.32
  177.1 1.8 collective-permute-start.28
  179.0 0.8 place_pooled.1
  179.9 3.1 %collective-permute-done.32.got = bf16[4,9,16,256]{3,2,1,0:T(8,128)(2,1)S(1)} collective-permute-done((bf16[4,9,16,256]{3,2,1,0:T(8,128)(2,1)S(1)}, bf16[4,9,16,256]{3,2,1,0:T(8,128)(2,1)S(1)}, u32[]{:S(2)}, u32[]{:S(2)}) %collective-permute-start.32) | collective-permute-done | bytes 294944 | tf_op jit(solution)/shard_map/ppermute | solution.py:944
  183.1 2.6 %collective-permute-start.36 = (bf16[1,9,16,512]{3,2,1,0:T(8,128)(2,1)S(1)}, bf16[1,9,16,512]{3,2,1,0:T(8,128)(2,1)S(1)}, u32[]{:S(2)}, u32[]{:S(2)}) collective-permute-start(bf16[1,9,16,512]{3,2,1,0:T(8,128)(2,1)S(1)} %get-tuple-element.145), channel_id=1, source_target_pairs={{0,2},{1,3},{2,0},{3,1},{4,6},{5,7},{6,4},{7,5},{8,10},{9,11},{10,... | collective-permute-start | bytes 442376 | tf_op jit(solution)/shard_map/ppermute | solution.py:947
  185.8 6.9 %collective-permute-done.34.got = bf16[2,9,16,256]{3,2,1,0:T(8,128)(2,1)S(1)} collective-permute-done((bf16[2,9,16,256]{3,2,1,0:T(8,128)(2,1)S(1)}, bf16[2,9,16,256]{3,2,1,0:T(8,128)(2,1)S(1)}, u32[]{:S(2)}, u32[]{:S(2)}) %collective-permute-start.34) | collective-permute-done | bytes 147488 | tf_op jit(solution)/shard_map/ppermute | solution.py:947
  192.8 0.7 collective-permute-start.40
  193.5 1.3 collective-permute-start.41
  194.8 1.5 collective-permute-start.42
  196.3 2.0 collective-permute-done.35.got
  198.4 0.8 collective-permute-start.37
  199.2 1.3 collective-permute-start.38
  200.5 1.3 collective-permute-done.42.refs_3_
  201.8 0.9 collective-permute-done.37.refs_4_.refs_1_
  202.8 0.8 collective-permute-done.38.refs_5_.refs_2_
  204.2 1.3 collective-permute-start.39
  205.5 1.3 place_spectra.1
  206.8 1.6 mid_out.1
  210.2 1.1 in_out.1
  (107 shorter events, 7.7 us)
Async XLA Ops:
  1.6 12.5 %collective-permute-start = (bf16[9,16,768]{2,1,0:T(8,128)(2,1)S(1)}, bf16[9,16,768]{2,1,0:T(8,128)(2,1)S(1)}, u32[]{:S(2)}, u32[]{:S(2)}) collective-permute-start(bf16[9,16,768]{2,1,0:T(8,128)(2,1)S(1)} %cut_weights.1.after), channel_id=1, source_target_pairs={{0,1},{1,0},{2,3},{3,2},{4,5},{5,4},{6,7},{7,6},{8,9},{9,8},{10,11... | collective-permute-start | bytes 663560 | tf_op jit(solution)/shard_map/ppermute | solution.py:947
  4.7 18.7 %collective-permute-start.1 = (bf16[9,16,768]{2,1,0:T(8,128)(2,1)S(1)}, bf16[9,16,768]{2,1,0:T(8,128)(2,1)S(1)}, u32[]{:S(2)}, u32[]{:S(2)}) collective-permute-start(bf16[9,16,768]{2,1,0:T(8,128)(2,1)S(1)} %cut_weights.1.after), channel_id=1, source_target_pairs={{0,2},{1,3},{2,0},{3,1},{4,6},{5,7},{6,4},{7,5},{8,10},{9,11},{10,... | collective-permute-start | bytes 663560 | tf_op jit(solution)/shard_map/ppermute | solution.py:947
  7.3 16.1 %collective-permute-start.2 = (bf16[9,16,768]{2,1,0:T(8,128)(2,1)S(1)}, bf16[9,16,768]{2,1,0:T(8,128)(2,1)S(1)}, u32[]{:S(2)}, u32[]{:S(2)}) collective-permute-start(bf16[9,16,768]{2,1,0:T(8,128)(2,1)S(1)} %cut_weights.1.after), channel_id=1, source_target_pairs={{0,3},{1,2},{2,1},{3,0},{4,7},{5,6},{6,5},{7,4},{8,11},{9,10},{10,... | collective-permute-start | bytes 663560 | tf_op jit(solution)/shard_map/ppermute | solution.py:947
  9.3 1.2 copy-start
  11.6 0.7 copy-start.8
  12.3 11.9 %copy-start.6 = (bf16[128,512]{1,0:T(8,128)(2,1)}, bf16[128,512]{1,0:T(8,128)(2,1)S(1)}, u32[]{:S(2)}) copy-start(bf16[128,512]{1,0:T(8,128)(2,1)S(1)} %get-tuple-element.92.refs_3_) | copy-start | bytes 393220
  12.3 34.2 %copy-start.11 = (f32[128]{0:T(128)S(1)}, f32[128]{0:T(128)}, u32[]{:S(2)}) copy-start(f32[128]{0:T(128)} %param.16) | copy-start | bytes 1540
  12.3 34.2 %copy-start.12 = (f32[128]{0:T(128)S(1)}, f32[128]{0:T(128)}, u32[]{:S(2)}) copy-start(f32[128]{0:T(128)} %param.15) | copy-start | bytes 1540
  12.3 34.2 %copy-start.13 = (f32[128]{0:T(128)S(1)}, f32[128]{0:T(128)}, u32[]{:S(2)}) copy-start(f32[128]{0:T(128)} %param.13) | copy-start | bytes 1540
  12.3 34.2 %copy-start.14 = (f32[128]{0:T(128)S(1)}, f32[128]{0:T(128)}, u32[]{:S(2)}) copy-start(f32[128]{0:T(128)} %param.12) | copy-start | bytes 1540
  24.2 22.4 %copy-start.2 = (bf16[9,128,256]{2,1,0:T(8,128)(2,1)S(1)}, bf16[9,128,256]{2,1,0:T(8,128)(2,1)}, u32[]{:S(2)}) copy-start(bf16[9,128,256]{2,1,0:T(8,128)(2,1)} %own.2) | copy-start | bytes 1769476
  24.2 26.7 %all-to-all-start = ((bf16[4,64,1664]{2,1,0:T(8,128)(2,1)}), bf16[4,64,1664]{2,1,0:T(8,128)(2,1)S(1)}, u32[]{:S(2)}, u32[]{:S(2)}) async-start(bf16[4,64,1664]{2,1,0:T(8,128)(2,1)} %release_far.1), calls=%async_computation | async-start | bytes 1703936 | tf_op jit(solution)/shard_map/all_to_all | solution.py:997
  30.5 8.5 %collective-permute-start.3 = (bf16[3,9,16,256]{3,2,1,0:T(8,128)(2,1)}, bf16[3,9,16,256]{3,2,1,0:T(8,128)(2,1)S(1)}, u32[]{:S(2)}, u32[]{:S(2)}) collective-permute-start(bf16[3,9,16,256]{3,2,1,0:T(8,128)(2,1)} %get-tuple-element.82.rest_0_.refs_0_), channel_id=1, source_target_pairs={{0,16},{4,12},{8,24},{12,4},{16,0},{20,28},{24,8},{28,20},{1,17},{... | collective-permute-start | bytes 663560 | tf_op jit(solution)/shard_map/ppermute | solution.py:944
  32.0 13.0 %collective-permute-start.10 = (bf16[3,9,16,512]{3,2,1,0:T(8,128)(2,1)S(1)}, bf16[3,9,16,512]{3,2,1,0:T(8,128)(2,1)S(1)}, u32[]{:S(2)}, u32[]{:S(2)}) collective-permute-start(bf16[3,9,16,512]{3,2,1,0:T(8,128)(2,1)S(1)} %get-tuple-element.84.refs_1_), channel_id=1, source_target_pairs={{0,16},{4,12},{8,24},{12,4},{16,0},{20,28},{24,8},{28,20},{1,17},{... | collective-permute-start | bytes 1327112 | tf_op jit(solution)/shard_map/ppermute | solution.py:944
  32.5 8.6 %collective-permute-start.4 = (bf16[3,9,16,256]{3,2,1,0:T(8,128)(2,1)}, bf16[3,9,16,256]{3,2,1,0:T(8,128)(2,1)S(1)}, u32[]{:S(2)}, u32[]{:S(2)}) collective-permute-start(bf16[3,9,16,256]{3,2,1,0:T(8,128)(2,1)} %get-tuple-element.82.rest_0_.refs_0_), channel_id=1, source_target_pairs={{0,8},{4,20},{8,0},{12,28},{16,24},{20,4},{24,16},{28,12},{1,9},{5... | collective-permute-start | bytes 663560 | tf_op jit(solution)/shard_map/ppermute | solution.py:944
  39.0 5.9 %collective-permute-start.5 = (bf16[3,9,16,256]{3,2,1,0:T(8,128)(2,1)S(1)}, bf16[3,9,16,256]{3,2,1,0:T(8,128)(2,1)S(1)}, u32[]{:S(2)}, u32[]{:S(2)}) collective-permute-start(bf16[3,9,16,256]{3,2,1,0:T(8,128)(2,1)S(1)} %collective-permute-done.3.rest_1_), channel_id=1, source_target_pairs={{0,8},{4,20},{8,0},{12,28},{16,24},{20,4},{24,16},{28,12},{1,9},{5... | collective-permute-start | bytes 663560 | tf_op jit(solution)/shard_map/ppermute | solution.py:944
  40.5 6.1 %collective-permute-start.6 = (bf16[3,9,16,256]{3,2,1,0:T(8,128)(2,1)}, bf16[3,9,16,256]{3,2,1,0:T(8,128)(2,1)S(1)}, u32[]{:S(2)}, u32[]{:S(2)}) collective-permute-start(bf16[3,9,16,256]{3,2,1,0:T(8,128)(2,1)} %get-tuple-element.82.rest_0_.refs_0_), channel_id=1, source_target_pairs={{0,4},{4,0},{8,12},{12,8},{16,20},{20,16},{24,28},{28,24},{1,5},{5... | collective-permute-start | bytes 663560 | tf_op jit(solution)/shard_map/ppermute | solution.py:937
  40.5 6.1 %collective-permute-start.7 = (bf16[3,9,16,256]{3,2,1,0:T(8,128)(2,1)S(1)}, bf16[3,9,16,256]{3,2,1,0:T(8,128)(2,1)S(1)}, u32[]{:S(2)}, u32[]{:S(2)}) collective-permute-start(bf16[3,9,16,256]{3,2,1,0:T(8,128)(2,1)S(1)} %collective-permute-done.3.rest_1_), channel_id=1, source_target_pairs={{0,4},{4,0},{8,12},{12,8},{16,20},{20,16},{24,28},{28,24},{1,5},{5... | collective-permute-start | bytes 663560 | tf_op jit(solution)/shard_map/ppermute | solution.py:937
  41.1 5.5 %collective-permute-start.8 = (bf16[3,9,16,256]{3,2,1,0:T(8,128)(2,1)S(1)}, bf16[3,9,16,256]{3,2,1,0:T(8,128)(2,1)S(1)}, u32[]{:S(2)}, u32[]{:S(2)}) collective-permute-start(bf16[3,9,16,256]{3,2,1,0:T(8,128)(2,1)S(1)} %collective-permute-done.4.rest_2_), channel_id=1, source_target_pairs={{0,4},{4,0},{8,12},{12,8},{16,20},{20,16},{24,28},{28,24},{1,5},{5... | collective-permute-start | bytes 663560 | tf_op jit(solution)/shard_map/ppermute | solution.py:937
  44.9 1.7 collective-permute-start.9
  45.0 12.6 %collective-permute-start.11 = (bf16[3,9,16,512]{3,2,1,0:T(8,128)(2,1)S(1)}, bf16[3,9,16,512]{3,2,1,0:T(8,128)(2,1)S(1)}, u32[]{:S(2)}, u32[]{:S(2)}) collective-permute-start(bf16[3,9,16,512]{3,2,1,0:T(8,128)(2,1)S(1)} %get-tuple-element.84.refs_1_), channel_id=1, source_target_pairs={{0,8},{4,20},{8,0},{12,28},{16,24},{20,4},{24,16},{28,12},{1,9},{5... | collective-permute-start | bytes 1327112 | tf_op jit(solution)/shard_map/ppermute | solution.py:944
  46.6 4.3 %copy-start.10 = (s32[2]{0:T(128)S(1)}, s32[2]{0:T(128)}, u32[]{:S(2)}) copy-start(s32[2]{0:T(128)} %lens.13) | copy-start | bytes 28
  47.8 1.4 copy-start.3
  50.9 1.7 copy-start.4
  57.7 15.1 %copy-start.7 = (bf16[128,512]{1,0:T(8,128)(2,1)S(1)}, bf16[128,512]{1,0:T(8,128)(2,1)}, u32[]{:S(2)}) copy-start(bf16[128,512]{1,0:T(8,128)(2,1)} %copy-done.6) | copy-start | bytes 393220
  57.7 15.1 %copy-start.9 = (bf16[128,512]{1,0:T(8,128)(2,1)S(1)}, bf16[128,512]{1,0:T(8,128)(2,1)}, u32[]{:S(2)}) copy-start(bf16[128,512]{1,0:T(8,128)(2,1)} %copy-done.8) | copy-start | bytes 393220
  57.7 19.5 %copy-start.1 = (bf16[9,128,512]{2,1,0:T(8,128)(2,1)S(1)}, bf16[9,128,512]{2,1,0:T(8,128)(2,1)}, u32[]{:S(2)}) copy-start(bf16[9,128,512]{2,1,0:T(8,128)(2,1)} %own.3) | copy-start | bytes 3538948
  57.7 14.1 %collective-permute-start.12 = (bf16[3,9,16,512]{3,2,1,0:T(8,128)(2,1)S(1)}, bf16[3,9,16,512]{3,2,1,0:T(8,128)(2,1)S(1)}, u32[]{:S(2)}, u32[]{:S(2)}) collective-permute-start(bf16[3,9,16,512]{3,2,1,0:T(8,128)(2,1)S(1)} %release.5), channel_id=1, source_target_pairs={{0,8},{4,20},{8,0},{12,28},{16,24},{20,4},{24,16},{28,12},{1,9},{5... | collective-permute-start | bytes 1327112 | tf_op jit(solution)/shard_map/ppermute | solution.py:944
  71.8 1.8 collective-permute-start.13
  71.8 3.1 %collective-permute-start.14 = (bf16[3,9,16,512]{3,2,1,0:T(8,128)(2,1)S(1)}, bf16[3,9,16,512]{3,2,1,0:T(8,128)(2,1)S(1)}, u32[]{:S(2)}, u32[]{:S(2)}) collective-permute-start(bf16[3,9,16,512]{3,2,1,0:T(8,128)(2,1)S(1)} %get-tuple-element.87.rest_1_), channel_id=1, source_target_pairs={{0,4},{4,0},{8,12},{12,8},{16,20},{20,16},{24,28},{28,24},{1,5},{5... | collective-permute-start | bytes 1327112 | tf_op jit(solution)/shard_map/ppermute | solution.py:937
  72.3 4.9 %collective-permute-start.15 = (bf16[3,9,16,512]{3,2,1,0:T(8,128)(2,1)S(1)}, bf16[3,9,16,512]{3,2,1,0:T(8,128)(2,1)S(1)}, u32[]{:S(2)}, u32[]{:S(2)}) collective-permute-start(bf16[3,9,16,512]{3,2,1,0:T(8,128)(2,1)S(1)} %get-tuple-element.88.rest_2_), channel_id=1, source_target_pairs={{0,4},{4,0},{8,12},{12,8},{16,20},{20,16},{24,28},{28,24},{1,5},{5... | collective-permute-start | bytes 1327112 | tf_op jit(solution)/shard_map/ppermute | solution.py:937
  72.4 4.9 %collective-permute-start.16 = (bf16[3,9,16,512]{3,2,1,0:T(8,128)(2,1)S(1)}, bf16[3,9,16,512]{3,2,1,0:T(8,128)(2,1)S(1)}, u32[]{:S(2)}, u32[]{:S(2)}) collective-permute-start(bf16[3,9,16,512]{3,2,1,0:T(8,128)(2,1)S(1)} %get-tuple-element.89.rest_3_), channel_id=1, source_target_pairs={{0,4},{4,0},{8,12},{12,8},{16,20},{20,16},{24,28},{28,24},{1,5},{5... | collective-permute-start | bytes 1327112 | tf_op jit(solution)/shard_map/ppermute | solution.py:937
  72.8 14.3 %collective-permute-start.17 = (bf16[128,512]{1,0:T(8,128)(2,1)S(1)}, bf16[128,512]{1,0:T(8,128)(2,1)S(1)}, u32[]{:S(2)}, u32[]{:S(2)}) collective-permute-start(bf16[128,512]{1,0:T(8,128)(2,1)S(1)} %get-tuple-element.94), channel_id=1, source_target_pairs={{0,1},{1,0},{2,3},{3,2},{4,5},{5,4},{6,7},{7,6},{8,9},{9,8},{10,11... | collective-permute-start | bytes 393224 | tf_op jit(solution)/shard_map/ppermute | solution.py:947
  73.6 13.5 %collective-permute-start.18 = (bf16[128,512]{1,0:T(8,128)(2,1)S(1)}, bf16[128,512]{1,0:T(8,128)(2,1)S(1)}, u32[]{:S(2)}, u32[]{:S(2)}) collective-permute-start(bf16[128,512]{1,0:T(8,128)(2,1)S(1)} %get-tuple-element.95), channel_id=1, source_target_pairs={{0,2},{1,3},{2,0},{3,1},{4,6},{5,7},{6,4},{7,5},{8,10},{9,11},{10,... | collective-permute-start | bytes 393224 | tf_op jit(solution)/shard_map/ppermute | solution.py:947
  74.9 12.2 %collective-permute-start.19 = (bf16[128,512]{1,0:T(8,128)(2,1)S(1)}, bf16[128,512]{1,0:T(8,128)(2,1)S(1)}, u32[]{:S(2)}, u32[]{:S(2)}) collective-permute-start(bf16[128,512]{1,0:T(8,128)(2,1)S(1)} %get-tuple-element.96), channel_id=1, source_target_pairs={{0,3},{1,2},{2,1},{3,0},{4,7},{5,6},{6,5},{7,4},{8,11},{9,10},{10,... | collective-permute-start | bytes 393224 | tf_op jit(solution)/shard_map/ppermute | solution.py:947
  122.9 4.6 %collective-permute-start.23 = (bf16[4,4,9,16,512]{4,3,2,1,0:T(8,128)(2,1)S(1)}, bf16[4,4,9,16,512]{4,3,2,1,0:T(8,128)(2,1)S(1)}, u32[]{:S(2)}, u32[]{:S(2)}) collective-permute-start(bf16[4,4,9,16,512]{4,3,2,1,0:T(8,128)(2,1)S(1)} %get-tuple-element.117), channel_id=1, source_target_pairs={{0,4},{4,0},{8,12},{12,8},{16,20},{20,16},{24,28},{28,24},{1,5},{5... | collective-permute-start | bytes 7077896 | tf_op jit(solution)/shard_map/ppermute | solution.py:937
  123.0 15.2 %collective-permute-start.20 = (bf16[128,384]{1,0:T(8,128)(2,1)S(1)}, bf16[128,384]{1,0:T(8,128)(2,1)S(1)}, u32[]{:S(2)}, u32[]{:S(2)}) collective-permute-start(bf16[128,384]{1,0:T(8,128)(2,1)S(1)} %get-tuple-element.106), channel_id=1, source_target_pairs={{0,1},{1,0},{2,3},{3,2},{4,5},{5,4},{6,7},{7,6},{8,9},{9,8},{10,11... | collective-permute-start | bytes 294920 | tf_op jit(solution)/shard_map/ppermute | solution.py:947
  123.3 14.9 %collective-permute-start.21 = (bf16[128,384]{1,0:T(8,128)(2,1)S(1)}, bf16[128,384]{1,0:T(8,128)(2,1)S(1)}, u32[]{:S(2)}, u32[]{:S(2)}) collective-permute-start(bf16[128,384]{1,0:T(8,128)(2,1)S(1)} %get-tuple-element.107), channel_id=1, source_target_pairs={{0,2},{1,3},{2,0},{3,1},{4,6},{5,7},{6,4},{7,5},{8,10},{9,11},{10,... | collective-permute-start | bytes 294920 | tf_op jit(solution)/shard_map/ppermute | solution.py:947
  124.8 13.5 %collective-permute-start.22 = (bf16[128,384]{1,0:T(8,128)(2,1)S(1)}, bf16[128,384]{1,0:T(8,128)(2,1)S(1)}, u32[]{:S(2)}, u32[]{:S(2)}) collective-permute-start(bf16[128,384]{1,0:T(8,128)(2,1)S(1)} %get-tuple-element.108), channel_id=1, source_target_pairs={{0,3},{1,2},{2,1},{3,0},{4,7},{5,6},{6,5},{7,4},{8,11},{9,10},{10,... | collective-permute-start | bytes 294920 | tf_op jit(solution)/shard_map/ppermute | solution.py:947
  128.1 10.2 %collective-permute-start.24 = (bf16[4,9,16,512]{3,2,1,0:T(8,128)(2,1)S(1)}, bf16[4,9,16,512]{3,2,1,0:T(8,128)(2,1)S(1)}, u32[]{:S(2)}, u32[]{:S(2)}) collective-permute-start(bf16[4,9,16,512]{3,2,1,0:T(8,128)(2,1)S(1)} %get-tuple-element.118.after), channel_id=1, source_target_pairs={{0,8},{4,20},{8,0},{12,28},{16,24},{20,4},{24,16},{28,12},{1,9},{5... | collective-permute-start | bytes 1769480 | tf_op jit(solution)/shard_map/ppermute | solution.py:944
  138.4 12.4 %collective-permute-start.25 = (bf16[4,9,16,512]{3,2,1,0:T(8,128)(2,1)S(1)}, bf16[4,9,16,512]{3,2,1,0:T(8,128)(2,1)S(1)}, u32[]{:S(2)}, u32[]{:S(2)}) collective-permute-start(bf16[4,9,16,512]{3,2,1,0:T(8,128)(2,1)S(1)} %mid_sum_b.1), channel_id=1, source_target_pairs={{0,16},{4,12},{8,24},{12,4},{16,0},{20,28},{24,8},{28,20},{1,17},{... | collective-permute-start | bytes 1769480 | tf_op jit(solution)/shard_map/ppermute | solution.py:944
  150.8 6.8 %copy-start.5 = (bf16[9,512,256]{2,1,0:T(8,128)(2,1)S(1)}, bf16[9,512,256]{2,1,0:T(8,128)(2,1)}, u32[]{:S(2)}) copy-start(bf16[9,512,256]{2,1,0:T(8,128)(2,1)} %copy-done.3) | copy-start | bytes 7077892
  156.7 6.6 %collective-permute-start.29 = (bf16[4,4,9,16,256]{4,3,2,1,0:T(8,128)(2,1)S(1)}, bf16[4,4,9,16,256]{4,3,2,1,0:T(8,128)(2,1)S(1)}, u32[]{:S(2)}, u32[]{:S(2)}) collective-permute-start(bf16[4,4,9,16,256]{4,3,2,1,0:T(8,128)(2,1)S(1)} %get-tuple-element.130), channel_id=1, source_target_pairs={{0,4},{4,0},{8,12},{12,8},{16,20},{20,16},{24,28},{28,24},{1,5},{5... | collective-permute-start | bytes 3538952 | tf_op jit(solution)/shard_map/ppermute | solution.py:937
  156.7 9.9 %collective-permute-start.31 = (bf16[4,9,16,512]{3,2,1,0:T(8,128)(2,1)S(1)}, bf16[4,9,16,512]{3,2,1,0:T(8,128)(2,1)S(1)}, u32[]{:S(2)}, u32[]{:S(2)}) collective-permute-start(bf16[4,9,16,512]{3,2,1,0:T(8,128)(2,1)S(1)} %release.9), channel_id=1, source_target_pairs={{0,8},{4,20},{8,0},{12,28},{16,24},{20,4},{24,16},{28,12},{1,9},{5... | collective-permute-start | bytes 1769480 | tf_op jit(solution)/shard_map/ppermute | solution.py:944
  163.6 12.5 %collective-permute-start.30 = (bf16[8,9,16,256]{3,2,1,0:T(8,128)(2,1)S(1)}, bf16[8,9,16,256]{3,2,1,0:T(8,128)(2,1)S(1)}, u32[]{:S(2)}, u32[]{:S(2)}) collective-permute-start(bf16[8,9,16,256]{3,2,1,0:T(8,128)(2,1)S(1)} %get-tuple-element.132), channel_id=1, source_target_pairs={{0,8},{4,20},{8,0},{12,28},{16,24},{20,4},{24,16},{28,12},{1,9},{5... | collective-permute-start | bytes 1769480 | tf_op jit(solution)/shard_map/ppermute | solution.py:944
  164.8 11.2 %collective-permute-start.27 = (bf16[64,1536]{1,0:T(8,128)(2,1)S(1)}, bf16[64,1536]{1,0:T(8,128)(2,1)S(1)}, u32[]{:S(2)}, u32[]{:S(2)}) collective-permute-start(bf16[64,1536]{1,0:T(8,128)(2,1)S(1)} %get-tuple-element.126), channel_id=1, source_target_pairs={{0,2},{1,3},{2,0},{3,1},{4,6},{5,7},{6,4},{7,5},{8,10},{9,11},{10,... | collective-permute-start | bytes 589832 | tf_op jit(solution)/shard_map/ppermute | solution.py:947
  166.9 12.9 %collective-permute-start.33 = (bf16[2,9,16,512]{3,2,1,0:T(8,128)(2,1)S(1)}, bf16[2,9,16,512]{3,2,1,0:T(8,128)(2,1)S(1)}, u32[]{:S(2)}, u32[]{:S(2)}) collective-permute-start(bf16[2,9,16,512]{3,2,1,0:T(8,128)(2,1)S(1)} %get-tuple-element.138), channel_id=1, source_target_pairs={{0,1},{1,0},{2,3},{3,2},{4,5},{5,4},{6,7},{7,6},{8,9},{9,8},{10,11... | collective-permute-start | bytes 884744 | tf_op jit(solution)/shard_map/ppermute | solution.py:947
  176.2 6.8 %collective-permute-start.32 = (bf16[4,9,16,256]{3,2,1,0:T(8,128)(2,1)S(1)}, bf16[4,9,16,256]{3,2,1,0:T(8,128)(2,1)S(1)}, u32[]{:S(2)}, u32[]{:S(2)}) collective-permute-start(bf16[4,9,16,256]{3,2,1,0:T(8,128)(2,1)S(1)} %get-tuple-element.137), channel_id=1, source_target_pairs={{0,16},{4,12},{8,24},{12,4},{16,0},{20,28},{24,8},{28,20},{1,17},{... | collective-permute-start | bytes 884744 | tf_op jit(solution)/shard_map/ppermute | solution.py:944
  177.1 8.6 %collective-permute-start.28 = (bf16[64,1536]{1,0:T(8,128)(2,1)S(1)}, bf16[64,1536]{1,0:T(8,128)(2,1)S(1)}, u32[]{:S(2)}, u32[]{:S(2)}) collective-permute-start(bf16[64,1536]{1,0:T(8,128)(2,1)S(1)} %get-tuple-element.127), channel_id=1, source_target_pairs={{0,3},{1,2},{2,1},{3,0},{4,7},{5,6},{6,5},{7,4},{8,11},{9,10},{10,... | collective-permute-start | bytes 589832 | tf_op jit(solution)/shard_map/ppermute | solution.py:947
  183.0 9.6 %collective-permute-start.34 = (bf16[2,9,16,256]{3,2,1,0:T(8,128)(2,1)S(1)}, bf16[2,9,16,256]{3,2,1,0:T(8,128)(2,1)S(1)}, u32[]{:S(2)}, u32[]{:S(2)}) collective-permute-start(bf16[2,9,16,256]{3,2,1,0:T(8,128)(2,1)S(1)} %get-tuple-element.142), channel_id=1, source_target_pairs={{0,1},{1,0},{2,3},{3,2},{4,5},{5,4},{6,7},{7,6},{8,9},{9,8},{10,11... | collective-permute-start | bytes 442376 | tf_op jit(solution)/shard_map/ppermute | solution.py:947
  183.1 9.6 %collective-permute-start.36 = (bf16[1,9,16,512]{3,2,1,0:T(8,128)(2,1)S(1)}, bf16[1,9,16,512]{3,2,1,0:T(8,128)(2,1)S(1)}, u32[]{:S(2)}, u32[]{:S(2)}) collective-permute-start(bf16[1,9,16,512]{3,2,1,0:T(8,128)(2,1)S(1)} %get-tuple-element.145), channel_id=1, source_target_pairs={{0,2},{1,3},{2,0},{3,1},{4,6},{5,7},{6,4},{7,5},{8,10},{9,11},{10,... | collective-permute-start | bytes 442376 | tf_op jit(solution)/shard_map/ppermute | solution.py:947
  185.7 13.5 %collective-permute-start.26 = (bf16[64,1536]{1,0:T(8,128)(2,1)S(1)}, bf16[64,1536]{1,0:T(8,128)(2,1)S(1)}, u32[]{:S(2)}, u32[]{:S(2)}) collective-permute-start(bf16[64,1536]{1,0:T(8,128)(2,1)S(1)} %get-tuple-element.125), channel_id=1, source_target_pairs={{0,1},{1,0},{2,3},{3,2},{4,5},{5,4},{6,7},{7,6},{8,9},{9,8},{10,11... | collective-permute-start | bytes 589832 | tf_op jit(solution)/shard_map/ppermute | solution.py:947
  192.7 5.7 %collective-permute-start.35 = (bf16[1,9,16,256]{3,2,1,0:T(8,128)(2,1)S(1)}, bf16[1,9,16,256]{3,2,1,0:T(8,128)(2,1)S(1)}, u32[]{:S(2)}, u32[]{:S(2)}) collective-permute-start(bf16[1,9,16,256]{3,2,1,0:T(8,128)(2,1)S(1)} %get-tuple-element.144), channel_id=1, source_target_pairs={{0,2},{1,3},{2,0},{3,1},{4,6},{5,7},{6,4},{7,5},{8,10},{9,11},{10,... | collective-permute-start | bytes 221192 | tf_op jit(solution)/shard_map/ppermute | solution.py:947
  192.8 7.7 %collective-permute-start.40 = (bf16[9,16,512]{2,1,0:T(8,128)(2,1)S(1)}, bf16[9,16,512]{2,1,0:T(8,128)(2,1)S(1)}, u32[]{:S(2)}, u32[]{:S(2)}) collective-permute-start(bf16[9,16,512]{2,1,0:T(8,128)(2,1)S(1)} %mid_sum_3.1.rest_0_.refs_0_), channel_id=1, source_target_pairs={{0,16},{4,12},{8,24},{12,4},{16,0},{20,28},{24,8},{28,20},{1,17},{... | collective-permute-start | bytes 442376 | tf_op jit(solution)/shard_map/ppermute | solution.py:968
  193.5 7.0 %collective-permute-start.41 = (bf16[9,16,512]{2,1,0:T(8,128)(2,1)S(1)}, bf16[9,16,512]{2,1,0:T(8,128)(2,1)S(1)}, u32[]{:S(2)}, u32[]{:S(2)}) collective-permute-start(bf16[9,16,512]{2,1,0:T(8,128)(2,1)S(1)} %mid_sum_3.1.rest_0_.refs_0_), channel_id=1, source_target_pairs={{0,8},{4,20},{8,0},{12,28},{16,24},{20,4},{24,16},{28,12},{1,9},{5... | collective-permute-start | bytes 442376 | tf_op jit(solution)/shard_map/ppermute | solution.py:968
  194.8 7.0 %collective-permute-start.42 = (bf16[9,16,512]{2,1,0:T(8,128)(2,1)S(1)}, bf16[9,16,512]{2,1,0:T(8,128)(2,1)S(1)}, u32[]{:S(2)}, u32[]{:S(2)}) collective-permute-start(bf16[9,16,512]{2,1,0:T(8,128)(2,1)S(1)} %mid_sum_3.1.rest_0_.refs_0_), channel_id=1, source_target_pairs={{0,24},{4,28},{8,16},{12,20},{16,8},{20,12},{24,0},{28,4},{1,25},{... | collective-permute-start | bytes 442376 | tf_op jit(solution)/shard_map/ppermute | solution.py:968
  198.4 4.4 %collective-permute-start.37 = (bf16[9,16,256]{2,1,0:T(8,128)(2,1)S(1)}, bf16[9,16,256]{2,1,0:T(8,128)(2,1)S(1)}, u32[]{:S(2)}, u32[]{:S(2)}) collective-permute-start(bf16[9,16,256]{2,1,0:T(8,128)(2,1)S(1)} %in_sum_3.1.refs_0_), channel_id=1, source_target_pairs={{0,16},{4,12},{8,24},{12,4},{16,0},{20,28},{24,8},{28,20},{1,17},{... | collective-permute-start | bytes 221192 | tf_op jit(solution)/shard_map/ppermute | solution.py:944
  199.2 4.4 %collective-permute-start.38 = (bf16[9,16,256]{2,1,0:T(8,128)(2,1)S(1)}, bf16[9,16,256]{2,1,0:T(8,128)(2,1)S(1)}, u32[]{:S(2)}, u32[]{:S(2)}) collective-permute-start(bf16[9,16,256]{2,1,0:T(8,128)(2,1)S(1)} %in_sum_3.1.refs_0_), channel_id=1, source_target_pairs={{0,8},{4,20},{8,0},{12,28},{16,24},{20,4},{24,16},{28,12},{1,9},{5... | collective-permute-start | bytes 221192 | tf_op jit(solution)/shard_map/ppermute | solution.py:944
  203.6 3.3 %collective-permute-start.43 = (bf16[4,9,16,512]{3,2,1,0:T(8,128)(2,1)S(1)}, bf16[4,9,16,512]{3,2,1,0:T(8,128)(2,1)S(1)}, u32[]{:S(2)}, u32[]{:S(2)}) collective-permute-start(bf16[4,9,16,512]{3,2,1,0:T(8,128)(2,1)S(1)} %mid_stack.1.mine), channel_id=1, source_target_pairs={{0,4},{4,0},{8,12},{12,8},{16,20},{20,16},{24,28},{28,24},{1,5},{5... | collective-permute-start | bytes 1769480 | tf_op jit(solution)/shard_map/ppermute | solution.py:937
  204.2 4.4 %collective-permute-start.39 = (bf16[9,16,256]{2,1,0:T(8,128)(2,1)S(1)}, bf16[9,16,256]{2,1,0:T(8,128)(2,1)S(1)}, u32[]{:S(2)}, u32[]{:S(2)}) collective-permute-start(bf16[9,16,256]{2,1,0:T(8,128)(2,1)S(1)} %collective-permute-done.37.refs_4_.refs_1_), channel_id=1, source_target_pairs={{0,8},{4,20},{8,0},{12,28},{16,24},{20,4},{24,16},{28,12},{1,9},{5... | collective-permute-start | bytes 221192 | tf_op jit(solution)/shard_map/ppermute | solution.py:944
  208.6 1.6 collective-permute-start.44

commit v7 on v6

--- a/solution.py
+++ b/solution.py
@@ -733,7 +733,7 @@
         rows[m] = (total * valid).astype(BF)
         return carry
 
-    convolve(g3, w, part, True, finish, 0, False, pl.ds(aligned(here.off), g.seg))
+    convolve(g3, w, part, True, finish, 0, True, pl.ds(aligned(here.off), g.seg))
     order = grid_order()
 
     for j in range(g.seg // 16):

time: 212 us -> 211 us (level)
  transfers between devices with their start and end apart: 46 -> 46, of which waited for: 19 -> 19; matrix products, arithmetic and copies ran while one was open for 1% -> 1% of each run, Pallas kernels for 19% -> 18%
where the time goes in v7:
time: 211 us
  Pallas kernels  62.6 us (30%)
  waiting for transfers between devices  48.4 us (23%)
  starting transfers between devices  47 us (22%)
  blocking collectives  45.4 us (22%)
  local copies, waits for them, and re-layouts  6.53 us (3%)
    pallas_call x23, Pallas kernels, call(): pl.pallas_call(body, out_shape=[pltpu.VMEM(o.shape, o.dtype) if isinstanc...  56.2 us
    all_to_all x4, blocking collectives, everyone(): return lax.all_to_all(x, ('dp', 'chan'), 0, 0)  45.4 us
    ppermute x16, waiting for transfers between devices, chan(): return lax.ppermute(x, 'chan', [(i, i ^ k) for i in range(self.g.nch)])  28.6 us
    ppermute x16, starting transfers between devices, chan(): return lax.ppermute(x, 'chan', [(i, i ^ k) for i in range(self.g.nch)])  19.2 us
    ppermute x14, starting transfers between devices, plane(): lax.ppermute(x, 'dp', [(i, i ^ 2 * g.mask(i & 1, turn)) for i in range(g....  16.1 us
    ppermute x14, waiting for transfers between devices, plane(): lax.ppermute(x, 'dp', [(i, i ^ 2 * g.mask(i & 1, turn)) for i in range(g....  15.6 us
    all_to_all x1, starting transfers between devices, body(): maps = lax.all_to_all(release_far([pieces_in], cells), 'chan', 0, 0)  6.29 us
    unnamed x31, local copies, waits for them, and re-layouts  4.96 us
  transfers between devices with their start and end apart: 46, of which 19 were waited for; matrix products, arithmetic and copies ran while one was open for 1% of the time, Pallas kernels for 18%

profile of v7, /device:TPU:0, one launch (start us, length us, event | category | flops | bytes accessed | tf_op | source)
XLA Modules:
  0.0 211.1 jit_solution(1362050069155703464)
XLA Ops:
  0.6 1.0 cut_weights.1.after
  1.6 3.1 %collective-permute-start = (bf16[9,16,768]{2,1,0:T(8,128)(2,1)S(1)}, bf16[9,16,768]{2,1,0:T(8,128)(2,1)S(1)}, u32[]{:S(2)}, u32[]{:S(2)}) collective-permute-start(bf16[9,16,768]{2,1,0:T(8,128)(2,1)S(1)} %cut_weights.1.after), channel_id=1, source_target_pairs={{0,1},{1,0},{2,3},{3,2},{4,5},{5,4},{6,7},{7,6},{8,9},{9,8},{10,11... | collective-permute-start | bytes 663560 | tf_op jit(solution)/shard_map/ppermute | solution.py:947
  4.7 2.6 %collective-permute-start.1 = (bf16[9,16,768]{2,1,0:T(8,128)(2,1)S(1)}, bf16[9,16,768]{2,1,0:T(8,128)(2,1)S(1)}, u32[]{:S(2)}, u32[]{:S(2)}) collective-permute-start(bf16[9,16,768]{2,1,0:T(8,128)(2,1)S(1)} %cut_weights.1.after), channel_id=1, source_target_pairs={{0,2},{1,3},{2,0},{3,1},{4,6},{5,7},{6,4},{7,5},{8,10},{9,11},{10,... | collective-permute-start | bytes 663560 | tf_op jit(solution)/shard_map/ppermute | solution.py:947
  7.3 2.0 cut_maps.1.after.refs_1_
  9.3 1.1 copy-done
  10.5 1.1 cut_cotangent.1
  11.6 0.7 copy-done.8
  12.3 1.8 collective-permute-done.rest_0_
  14.1 9.3 %collective-permute-done.1.rest_1_ = bf16[9,16,768]{2,1,0:T(8,128)(2,1)S(1)} collective-permute-done((bf16[9,16,768]{2,1,0:T(8,128)(2,1)S(1)}, bf16[9,16,768]{2,1,0:T(8,128)(2,1)S(1)}, u32[]{:S(2)}, u32[]{:S(2)}) %collective-permute-start.1) | collective-permute-done | bytes 221216 | tf_op jit(solution)/shard_map/ppermute | solution.py:947
  23.5 0.7 sort_pieces.1
  24.2 6.3 %all-to-all-start = ((bf16[4,64,1664]{2,1,0:T(8,128)(2,1)}), bf16[4,64,1664]{2,1,0:T(8,128)(2,1)S(1)}, u32[]{:S(2)}, u32[]{:S(2)}) async-start(bf16[4,64,1664]{2,1,0:T(8,128)(2,1)} %release_far.1), calls=%async_computation | async-start | bytes 1703936 | tf_op jit(solution)/shard_map/all_to_all | solution.py:997
  30.5 1.5 collective-permute-start.3
  32.5 1.5 collective-permute-start.4
  34.0 5.0 %collective-permute-done.3.rest_1_ = bf16[3,9,16,256]{3,2,1,0:T(8,128)(2,1)S(1)} collective-permute-done((bf16[3,9,16,256]{3,2,1,0:T(8,128)(2,1)}, bf16[3,9,16,256]{3,2,1,0:T(8,128)(2,1)S(1)}, u32[]{:S(2)}, u32[]{:S(2)}) %collective-permute-start.3) | collective-permute-done | bytes 221216 | tf_op jit(solution)/shard_map/ppermute | solution.py:944
  39.0 1.5 collective-permute-start.5
  41.1 3.8 %collective-permute-done.5.rest_3_ = bf16[3,9,16,256]{3,2,1,0:T(8,128)(2,1)S(1)} collective-permute-done((bf16[3,9,16,256]{3,2,1,0:T(8,128)(2,1)S(1)}, bf16[3,9,16,256]{3,2,1,0:T(8,128)(2,1)S(1)}, u32[]{:S(2)}, u32[]{:S(2)}) %collective-permute-start.5) | collective-permute-done | bytes 221216 | tf_op jit(solution)/shard_map/ppermute | solution.py:944
  45.0 1.5 collective-permute-start.11
  46.6 1.1 join_in.1.w
  47.8 1.4 copy-done.3
  49.2 1.7 all-to-all-done.maps.refs_0_
  50.9 1.7 copy-done.4
  52.5 5.1 %first_conv.1 = (f32[8,208,512]{2,1,0:T(8,128)S(1)}, bf16[8,208,768]{2,1,0:T(8,128)(2,1)S(1)}, f32[1,1664]{1,0:T(1,128)S(1)}) custom-call(s32[2]{0:T(128)S(1)} %copy-done.10, f32[4,128]{1,0:T(4,128)S(1)} %pad_maximum_fusion.gains, bf16[9,512,256]{2,1,0:T(8,128)(2,1)S(1)} %copy-done.4, bf16[4,64,1664]{2,1,0:T(8,128)(2,1)S(1)} %all-to-all-done.maps.refs_0_), custom_call_target="tpu_custom_call" | custom-call | flops 3925868544 | bytes 10485760 | tf_op jit(solution)/shard_map/first_conv/pallas_call | solution.py:90
  57.7 1.6 collective-permute-start.12
  59.3 12.5 %all_to_all.25.refs_0_.got = f32[32,1,1664]{2,1,0:T(1,128)S(1)} all-to-all(f32[32,1,1664]{2,1,0:T(1,128)S(1)} %fan.3), channel_id=1, replica_groups=mesh['dp'=8,'chan'=4] {'dp','chan'}, dimensions={0} | all-to-all | bytes 425984 | tf_op jit(solution)/shard_map/all_to_all | solution.py:972
  73.0 0.6 collective-permute-done.13.rest_4_
  73.6 1.3 collective-permute-start.18
  74.9 2.3 %collective-permute-start.19 = (bf16[128,512]{1,0:T(8,128)(2,1)S(1)}, bf16[128,512]{1,0:T(8,128)(2,1)S(1)}, u32[]{:S(2)}, u32[]{:S(2)}) collective-permute-start(bf16[128,512]{1,0:T(8,128)(2,1)S(1)} %get-tuple-element.96), channel_id=1, source_target_pairs={{0,3},{1,2},{2,1},{3,0},{4,7},{5,6},{6,5},{7,4},{8,11},{9,10},{10,... | collective-permute-start | bytes 393224 | tf_op jit(solution)/shard_map/ppermute | solution.py:947
  77.6 9.5 %second_conv.1 = (f32[8,208,512]{2,1,0:T(8,128)S(1)}, bf16[8,208,1536]{2,1,0:T(8,128)(2,1)S(1)}, f32[16,512]{1,0:T(8,128)S(1)}, f32[1,1024]{1,0:T(1,128)S(1)}, f32[1,128]{1,0:T(1,128)S(1)}) custom-call(s32[2]{0:T(128)S(1)} %copy-done.10, f32[32,1,1664]{2,1,0:T(1,128)S(1)} %all_to_all.25.refs_0_.got, f32[8,208,512]{2,1,0:T(8,128)S(1)} %get-tuple-element.85.pre1.pre, ...), custom_call_target="tpu_custom_call" | custom-call | flops 7851737088 | bytes 17825792 | tf_op jit(solution)/shard_map/second_conv/pallas_call | solution.py:90
  87.1 11.0 %all_to_all.26.got = f32[32,1,1024]{2,1,0:T(1,128)S(1)} all-to-all(f32[32,1,1024]{2,1,0:T(1,128)S(1)} %fan.4), channel_id=1, replica_groups=mesh['dp'=8,'chan'=4] {'dp','chan'}, dimensions={0} | all-to-all | bytes 262144 | tf_op jit(solution)/shard_map/all_to_all | solution.py:972
  98.1 5.2 %pool.1 = (bf16[128,384]{1,0:T(8,128)(2,1)S(1)}, bf16[128,384]{1,0:T(8,128)(2,1)S(1)}, bf16[128,384]{1,0:T(8,128)(2,1)S(1)}, bf16[128,384]{1,0:T(8,128)(2,1)S(1)...) custom-call(s32[2]{0:T(128)S(1)} %copy-done.10, ...), custom_call_target="tpu_custom_call" | custom-call | flops 4000000000 | bytes 8388608 | tf_op jit(solution)/shard_map/pool/pallas_call | solution.py:90
  103.4 10.1 %all_to_all.27.refs_0_.got.after = f32[32,1,1024]{2,1,0:T(1,128)S(1)} all-to-all(f32[32,1,1024]{2,1,0:T(1,128)S(1)} %get-tuple-element.100), channel_id=1, replica_groups=mesh['dp'=8,'chan'=4] {'dp','chan'}, dimensions={0} | all-to-all | bytes 262144 | tf_op jit(solution)/shard_map/all_to_all | solution.py:972
  113.5 9.5 %weight_mid_terms.1 = (bf16[8,208,512]{2,1,0:T(8,128)(2,1)S(1)}, f32[8,512]{1,0:T(8,128)S(1)}, f32[8,128]{1,0:T(8,128)}, bf16[2,4,4,9,16,512]{5,4,3,2,1,0:T(8,128)(2,1)S(1)}, bf16[4,4,9,16,512]{4,3,2,1,0:T(8,128)(2,1)S(1)}) custom-call(s32[2]{0:T(128)S(1)} %copy-done.10, f32[32,1,1024]{2,1,0:T(1,128)S(1)} %all_to_all.27.refs_0_.got.after, ...), custom_call_target="tpu_custom_call" | custom-call | flops 7851737088 | bytes 15728640 | tf_op jit(solution)/shard_map/weight_mid_terms/pallas_call | solution.py:90
  123.3 1.5 collective-permute-start.21
  124.8 2.7 %collective-permute-start.22 = (bf16[128,384]{1,0:T(8,128)(2,1)S(1)}, bf16[128,384]{1,0:T(8,128)(2,1)S(1)}, u32[]{:S(2)}, u32[]{:S(2)}) collective-permute-start(bf16[128,384]{1,0:T(8,128)(2,1)S(1)} %get-tuple-element.108), channel_id=1, source_target_pairs={{0,3},{1,2},{2,1},{3,0},{4,7},{5,6},{6,5},{7,4},{8,11},{9,10},{10,... | collective-permute-start | bytes 294920 | tf_op jit(solution)/shard_map/ppermute | solution.py:947
  127.5 0.5 mid_core_sum.1
  128.1 0.8 collective-permute-start.24
  128.9 9.3 %second_back.1 = (f32[8,208,512]{2,1,0:T(8,128)S(1)}, f32[1,1280]{1,0:T(1,128)S(1)}) custom-call(s32[2]{0:T(128)S(1)} %copy-done.10, f32[16,512]{1,0:T(8,128)S(1)} %get-tuple-element.110.table, bf16[8,208,512]{2,1,0:T(8,128)(2,1)S(1)} %get-tuple-element.113.grad, f32[8,208,512]{2,1,0:T(8,128)S(1)} %get-tuple-element.85.pre1.pre, ...), custom_call_target="tpu_custom_call" | custom-call | flops 7851737088 | bytes 20971520 | tf_op jit(solution)/shard_map/second_back/pallas_call | solution.py:90
  138.4 0.6 collective-permute-start.25
  139.0 11.8 %all_to_all.28.got.refs_0_ = f32[32,1,1280]{2,1,0:T(1,128)S(1)} all-to-all(f32[32,1,1280]{2,1,0:T(1,128)S(1)} %fan.5), channel_id=1, replica_groups=mesh['dp'=8,'chan'=4] {'dp','chan'}, dimensions={0} | all-to-all | bytes 327680 | tf_op jit(solution)/shard_map/all_to_all | solution.py:972
  150.8 5.8 %weight_in_terms.1 = (bf16[8,208,512]{2,1,0:T(8,128)(2,1)S(1)}, f32[8,512]{1,0:T(8,128)S(1)}, f32[8,128]{1,0:T(8,128)S(1)}, bf16[2,4,4,9,16,256]{5,4,3,2,1,0:T(8,128)(2,1)S(1)}, bf16[4,4,9,16,256]{4,3,2,1,0:T(8,128)(2,1)S(1)}) custom-call(s32[2]{0:T(128)S(1)} %copy-done.10, f32[32,1,1280]{2,1,0:T(1,128)S(1)} %all_to_all.28.got.refs_0_, ...), custom_call_target="tpu_custom_call" | custom-call | flops 3925868544 | bytes 15728640 | tf_op jit(solution)/shard_map/weight_in_terms/pallas_call | solution.py:90
  156.7 0.9 collective-permute-start.31
  157.6 5.3 %spectra_back.1 = (bf16[64,1536]{1,0:T(8,128)(2,1)S(1)}, bf16[64,1536]{1,0:T(8,128)(2,1)S(1)}, bf16[64,1536]{1,0:T(8,128)(2,1)S(1)}, bf16[64,1536]{1,0:T(8,128)(2,1)S(1)}) custom-call(s32[2]{0:T(128)S(1)} %copy-done.10, bf16[8,208,512]{2,1,0:T(8,128)(2,1)S(1)} %get-tuple-element.123.grad.after, bf16[8,208,512]{2,1,0:T(8,128)(2,1)S(1)} %get-tuple-element.123.grad.after, ...), custom_call_target="tpu_custom_call" | custom-call | flops 3925868544 | bytes 5242880 | tf_op jit(solution)/shard_map/spectra_back/pallas_call | solution.py:90
  163.3 1.3 collective-permute-start.30
  165.0 1.7 collective-permute-done.31.rest_1_
  167.2 8.6 %collective-permute-done.27.rest_2_.rest_1_ = bf16[64,1536]{1,0:T(8,128)(2,1)S(1)} collective-permute-done((bf16[64,1536]{1,0:T(8,128)(2,1)S(1)}, bf16[64,1536]{1,0:T(8,128)(2,1)S(1)}, u32[]{:S(2)}, u32[]{:S(2)}) %collective-permute-start.27) | collective-permute-done | bytes 196640 | tf_op jit(solution)/shard_map/ppermute | solution.py:947
  175.9 1.0 collective-permute-start.32
  176.8 1.8 collective-permute-start.28
  178.7 0.8 place_pooled.1
  179.6 3.0 %collective-permute-done.32.got = bf16[4,9,16,256]{3,2,1,0:T(8,128)(2,1)S(1)} collective-permute-done((bf16[4,9,16,256]{3,2,1,0:T(8,128)(2,1)S(1)}, bf16[4,9,16,256]{3,2,1,0:T(8,128)(2,1)S(1)}, u32[]{:S(2)}, u32[]{:S(2)}) %collective-permute-start.32) | collective-permute-done | bytes 294944 | tf_op jit(solution)/shard_map/ppermute | solution.py:944
  182.8 2.6 %collective-permute-start.36 = (bf16[1,9,16,512]{3,2,1,0:T(8,128)(2,1)S(1)}, bf16[1,9,16,512]{3,2,1,0:T(8,128)(2,1)S(1)}, u32[]{:S(2)}, u32[]{:S(2)}) collective-permute-start(bf16[1,9,16,512]{3,2,1,0:T(8,128)(2,1)S(1)} %get-tuple-element.145), channel_id=1, source_target_pairs={{0,2},{1,3},{2,0},{3,1},{4,6},{5,7},{6,4},{7,5},{8,10},{9,11},{10,... | collective-permute-start | bytes 442376 | tf_op jit(solution)/shard_map/ppermute | solution.py:947
  185.5 6.9 %collective-permute-done.34.got = bf16[2,9,16,256]{3,2,1,0:T(8,128)(2,1)S(1)} collective-permute-done((bf16[2,9,16,256]{3,2,1,0:T(8,128)(2,1)S(1)}, bf16[2,9,16,256]{3,2,1,0:T(8,128)(2,1)S(1)}, u32[]{:S(2)}, u32[]{:S(2)}) %collective-permute-start.34) | collective-permute-done | bytes 147488 | tf_op jit(solution)/shard_map/ppermute | solution.py:947
  192.5 0.7 collective-permute-start.40
  193.3 1.3 collective-permute-start.41
  194.6 1.5 collective-permute-start.42
  196.1 2.0 collective-permute-done.35.got
  198.1 0.8 collective-permute-start.37
  198.9 1.3 collective-permute-start.38
  200.2 1.3 collective-permute-done.42.refs_3_
  201.6 0.9 collective-permute-done.37.refs_4_.refs_1_
  202.5 0.8 collective-permute-done.38.refs_5_.refs_2_
  203.9 1.3 collective-permute-start.39
  205.3 1.3 place_spectra.1
  206.6 1.6 mid_out.1
  210.0 1.1 in_out.1
  (107 shorter events, 7.8 us)
Async XLA Ops:
  1.6 12.5 %collective-permute-start = (bf16[9,16,768]{2,1,0:T(8,128)(2,1)S(1)}, bf16[9,16,768]{2,1,0:T(8,128)(2,1)S(1)}, u32[]{:S(2)}, u32[]{:S(2)}) collective-permute-start(bf16[9,16,768]{2,1,0:T(8,128)(2,1)S(1)} %cut_weights.1.after), channel_id=1, source_target_pairs={{0,1},{1,0},{2,3},{3,2},{4,5},{5,4},{6,7},{7,6},{8,9},{9,8},{10,11... | collective-permute-start | bytes 663560 | tf_op jit(solution)/shard_map/ppermute | solution.py:947
  4.7 18.7 %collective-permute-start.1 = (bf16[9,16,768]{2,1,0:T(8,128)(2,1)S(1)}, bf16[9,16,768]{2,1,0:T(8,128)(2,1)S(1)}, u32[]{:S(2)}, u32[]{:S(2)}) collective-permute-start(bf16[9,16,768]{2,1,0:T(8,128)(2,1)S(1)} %cut_weights.1.after), channel_id=1, source_target_pairs={{0,2},{1,3},{2,0},{3,1},{4,6},{5,7},{6,4},{7,5},{8,10},{9,11},{10,... | collective-permute-start | bytes 663560 | tf_op jit(solution)/shard_map/ppermute | solution.py:947
  7.3 16.1 %collective-permute-start.2 = (bf16[9,16,768]{2,1,0:T(8,128)(2,1)S(1)}, bf16[9,16,768]{2,1,0:T(8,128)(2,1)S(1)}, u32[]{:S(2)}, u32[]{:S(2)}) collective-permute-start(bf16[9,16,768]{2,1,0:T(8,128)(2,1)S(1)} %cut_weights.1.after), channel_id=1, source_target_pairs={{0,3},{1,2},{2,1},{3,0},{4,7},{5,6},{6,5},{7,4},{8,11},{9,10},{10,... | collective-permute-start | bytes 663560 | tf_op jit(solution)/shard_map/ppermute | solution.py:947
  9.3 1.2 copy-start
  11.6 0.7 copy-start.8
  12.3 11.9 %copy-start.6 = (bf16[128,512]{1,0:T(8,128)(2,1)}, bf16[128,512]{1,0:T(8,128)(2,1)S(1)}, u32[]{:S(2)}) copy-start(bf16[128,512]{1,0:T(8,128)(2,1)S(1)} %get-tuple-element.92.refs_3_) | copy-start | bytes 393220
  12.3 34.2 %copy-start.11 = (f32[128]{0:T(128)S(1)}, f32[128]{0:T(128)}, u32[]{:S(2)}) copy-start(f32[128]{0:T(128)} %param.16) | copy-start | bytes 1540
  12.3 34.2 %copy-start.12 = (f32[128]{0:T(128)S(1)}, f32[128]{0:T(128)}, u32[]{:S(2)}) copy-start(f32[128]{0:T(128)} %param.15) | copy-start | bytes 1540
  12.3 34.2 %copy-start.13 = (f32[128]{0:T(128)S(1)}, f32[128]{0:T(128)}, u32[]{:S(2)}) copy-start(f32[128]{0:T(128)} %param.13) | copy-start | bytes 1540
  12.3 34.2 %copy-start.14 = (f32[128]{0:T(128)S(1)}, f32[128]{0:T(128)}, u32[]{:S(2)}) copy-start(f32[128]{0:T(128)} %param.12) | copy-start | bytes 1540
  24.2 22.4 %copy-start.2 = (bf16[9,128,256]{2,1,0:T(8,128)(2,1)S(1)}, bf16[9,128,256]{2,1,0:T(8,128)(2,1)}, u32[]{:S(2)}) copy-start(bf16[9,128,256]{2,1,0:T(8,128)(2,1)} %own.2) | copy-start | bytes 1769476
  24.2 26.7 %all-to-all-start = ((bf16[4,64,1664]{2,1,0:T(8,128)(2,1)}), bf16[4,64,1664]{2,1,0:T(8,128)(2,1)S(1)}, u32[]{:S(2)}, u32[]{:S(2)}) async-start(bf16[4,64,1664]{2,1,0:T(8,128)(2,1)} %release_far.1), calls=%async_computation | async-start | bytes 1703936 | tf_op jit(solution)/shard_map/all_to_all | solution.py:997
  30.5 8.5 %collective-permute-start.3 = (bf16[3,9,16,256]{3,2,1,0:T(8,128)(2,1)}, bf16[3,9,16,256]{3,2,1,0:T(8,128)(2,1)S(1)}, u32[]{:S(2)}, u32[]{:S(2)}) collective-permute-start(bf16[3,9,16,256]{3,2,1,0:T(8,128)(2,1)} %get-tuple-element.82.rest_0_.refs_0_), channel_id=1, source_target_pairs={{0,16},{4,12},{8,24},{12,4},{16,0},{20,28},{24,8},{28,20},{1,17},{... | collective-permute-start | bytes 663560 | tf_op jit(solution)/shard_map/ppermute | solution.py:944
  32.0 13.0 %collective-permute-start.10 = (bf16[3,9,16,512]{3,2,1,0:T(8,128)(2,1)S(1)}, bf16[3,9,16,512]{3,2,1,0:T(8,128)(2,1)S(1)}, u32[]{:S(2)}, u32[]{:S(2)}) collective-permute-start(bf16[3,9,16,512]{3,2,1,0:T(8,128)(2,1)S(1)} %get-tuple-element.84.refs_1_), channel_id=1, source_target_pairs={{0,16},{4,12},{8,24},{12,4},{16,0},{20,28},{24,8},{28,20},{1,17},{... | collective-permute-start | bytes 1327112 | tf_op jit(solution)/shard_map/ppermute | solution.py:944
  32.5 8.6 %collective-permute-start.4 = (bf16[3,9,16,256]{3,2,1,0:T(8,128)(2,1)}, bf16[3,9,16,256]{3,2,1,0:T(8,128)(2,1)S(1)}, u32[]{:S(2)}, u32[]{:S(2)}) collective-permute-start(bf16[3,9,16,256]{3,2,1,0:T(8,128)(2,1)} %get-tuple-element.82.rest_0_.refs_0_), channel_id=1, source_target_pairs={{0,8},{4,20},{8,0},{12,28},{16,24},{20,4},{24,16},{28,12},{1,9},{5... | collective-permute-start | bytes 663560 | tf_op jit(solution)/shard_map/ppermute | solution.py:944
  39.0 5.9 %collective-permute-start.5 = (bf16[3,9,16,256]{3,2,1,0:T(8,128)(2,1)S(1)}, bf16[3,9,16,256]{3,2,1,0:T(8,128)(2,1)S(1)}, u32[]{:S(2)}, u32[]{:S(2)}) collective-permute-start(bf16[3,9,16,256]{3,2,1,0:T(8,128)(2,1)S(1)} %collective-permute-done.3.rest_1_), channel_id=1, source_target_pairs={{0,8},{4,20},{8,0},{12,28},{16,24},{20,4},{24,16},{28,12},{1,9},{5... | collective-permute-start | bytes 663560 | tf_op jit(solution)/shard_map/ppermute | solution.py:944
  40.5 6.1 %collective-permute-start.6 = (bf16[3,9,16,256]{3,2,1,0:T(8,128)(2,1)}, bf16[3,9,16,256]{3,2,1,0:T(8,128)(2,1)S(1)}, u32[]{:S(2)}, u32[]{:S(2)}) collective-permute-start(bf16[3,9,16,256]{3,2,1,0:T(8,128)(2,1)} %get-tuple-element.82.rest_0_.refs_0_), channel_id=1, source_target_pairs={{0,4},{4,0},{8,12},{12,8},{16,20},{20,16},{24,28},{28,24},{1,5},{5... | collective-permute-start | bytes 663560 | tf_op jit(solution)/shard_map/ppermute | solution.py:937
  40.5 6.1 %collective-permute-start.7 = (bf16[3,9,16,256]{3,2,1,0:T(8,128)(2,1)S(1)}, bf16[3,9,16,256]{3,2,1,0:T(8,128)(2,1)S(1)}, u32[]{:S(2)}, u32[]{:S(2)}) collective-permute-start(bf16[3,9,16,256]{3,2,1,0:T(8,128)(2,1)S(1)} %collective-permute-done.3.rest_1_), channel_id=1, source_target_pairs={{0,4},{4,0},{8,12},{12,8},{16,20},{20,16},{24,28},{28,24},{1,5},{5... | collective-permute-start | bytes 663560 | tf_op jit(solution)/shard_map/ppermute | solution.py:937
  41.1 5.5 %collective-permute-start.8 = (bf16[3,9,16,256]{3,2,1,0:T(8,128)(2,1)S(1)}, bf16[3,9,16,256]{3,2,1,0:T(8,128)(2,1)S(1)}, u32[]{:S(2)}, u32[]{:S(2)}) collective-permute-start(bf16[3,9,16,256]{3,2,1,0:T(8,128)(2,1)S(1)} %collective-permute-done.4.rest_2_), channel_id=1, source_target_pairs={{0,4},{4,0},{8,12},{12,8},{16,20},{20,16},{24,28},{28,24},{1,5},{5... | collective-permute-start | bytes 663560 | tf_op jit(solution)/shard_map/ppermute | solution.py:937
  44.9 1.7 collective-permute-start.9
  45.0 12.6 %collective-permute-start.11 = (bf16[3,9,16,512]{3,2,1,0:T(8,128)(2,1)S(1)}, bf16[3,9,16,512]{3,2,1,0:T(8,128)(2,1)S(1)}, u32[]{:S(2)}, u32[]{:S(2)}) collective-permute-start(bf16[3,9,16,512]{3,2,1,0:T(8,128)(2,1)S(1)} %get-tuple-element.84.refs_1_), channel_id=1, source_target_pairs={{0,8},{4,20},{8,0},{12,28},{16,24},{20,4},{24,16},{28,12},{1,9},{5... | collective-permute-start | bytes 1327112 | tf_op jit(solution)/shard_map/ppermute | solution.py:944
  46.6 4.3 %copy-start.10 = (s32[2]{0:T(128)S(1)}, s32[2]{0:T(128)}, u32[]{:S(2)}) copy-start(s32[2]{0:T(128)} %lens.13) | copy-start | bytes 28
  47.8 1.4 copy-start.3
  50.9 1.7 copy-start.4
  57.7 15.1 %copy-start.7 = (bf16[128,512]{1,0:T(8,128)(2,1)S(1)}, bf16[128,512]{1,0:T(8,128)(2,1)}, u32[]{:S(2)}) copy-start(bf16[128,512]{1,0:T(8,128)(2,1)} %copy-done.6) | copy-start | bytes 393220
  57.7 15.1 %copy-start.9 = (bf16[128,512]{1,0:T(8,128)(2,1)S(1)}, bf16[128,512]{1,0:T(8,128)(2,1)}, u32[]{:S(2)}) copy-start(bf16[128,512]{1,0:T(8,128)(2,1)} %copy-done.8) | copy-start | bytes 393220
  57.7 19.5 %copy-start.1 = (bf16[9,128,512]{2,1,0:T(8,128)(2,1)S(1)}, bf16[9,128,512]{2,1,0:T(8,128)(2,1)}, u32[]{:S(2)}) copy-start(bf16[9,128,512]{2,1,0:T(8,128)(2,1)} %own.3) | copy-start | bytes 3538948
  57.7 14.1 %collective-permute-start.12 = (bf16[3,9,16,512]{3,2,1,0:T(8,128)(2,1)S(1)}, bf16[3,9,16,512]{3,2,1,0:T(8,128)(2,1)S(1)}, u32[]{:S(2)}, u32[]{:S(2)}) collective-permute-start(bf16[3,9,16,512]{3,2,1,0:T(8,128)(2,1)S(1)} %release.5), channel_id=1, source_target_pairs={{0,8},{4,20},{8,0},{12,28},{16,24},{20,4},{24,16},{28,12},{1,9},{5... | collective-permute-start | bytes 1327112 | tf_op jit(solution)/shard_map/ppermute | solution.py:944
  71.8 1.8 collective-permute-start.13
  71.8 3.1 %collective-permute-start.14 = (bf16[3,9,16,512]{3,2,1,0:T(8,128)(2,1)S(1)}, bf16[3,9,16,512]{3,2,1,0:T(8,128)(2,1)S(1)}, u32[]{:S(2)}, u32[]{:S(2)}) collective-permute-start(bf16[3,9,16,512]{3,2,1,0:T(8,128)(2,1)S(1)} %get-tuple-element.87.rest_1_), channel_id=1, source_target_pairs={{0,4},{4,0},{8,12},{12,8},{16,20},{20,16},{24,28},{28,24},{1,5},{5... | collective-permute-start | bytes 1327112 | tf_op jit(solution)/shard_map/ppermute | solution.py:937
  72.3 4.9 %collective-permute-start.15 = (bf16[3,9,16,512]{3,2,1,0:T(8,128)(2,1)S(1)}, bf16[3,9,16,512]{3,2,1,0:T(8,128)(2,1)S(1)}, u32[]{:S(2)}, u32[]{:S(2)}) collective-permute-start(bf16[3,9,16,512]{3,2,1,0:T(8,128)(2,1)S(1)} %get-tuple-element.88.rest_2_), channel_id=1, source_target_pairs={{0,4},{4,0},{8,12},{12,8},{16,20},{20,16},{24,28},{28,24},{1,5},{5... | collective-permute-start | bytes 1327112 | tf_op jit(solution)/shard_map/ppermute | solution.py:937
  72.4 4.9 %collective-permute-start.16 = (bf16[3,9,16,512]{3,2,1,0:T(8,128)(2,1)S(1)}, bf16[3,9,16,512]{3,2,1,0:T(8,128)(2,1)S(1)}, u32[]{:S(2)}, u32[]{:S(2)}) collective-permute-start(bf16[3,9,16,512]{3,2,1,0:T(8,128)(2,1)S(1)} %get-tuple-element.89.rest_3_), channel_id=1, source_target_pairs={{0,4},{4,0},{8,12},{12,8},{16,20},{20,16},{24,28},{28,24},{1,5},{5... | collective-permute-start | bytes 1327112 | tf_op jit(solution)/shard_map/ppermute | solution.py:937
  72.8 14.3 %collective-permute-start.17 = (bf16[128,512]{1,0:T(8,128)(2,1)S(1)}, bf16[128,512]{1,0:T(8,128)(2,1)S(1)}, u32[]{:S(2)}, u32[]{:S(2)}) collective-permute-start(bf16[128,512]{1,0:T(8,128)(2,1)S(1)} %get-tuple-element.94), channel_id=1, source_target_pairs={{0,1},{1,0},{2,3},{3,2},{4,5},{5,4},{6,7},{7,6},{8,9},{9,8},{10,11... | collective-permute-start | bytes 393224 | tf_op jit(solution)/shard_map/ppermute | solution.py:947
  73.6 13.5 %collective-permute-start.18 = (bf16[128,512]{1,0:T(8,128)(2,1)S(1)}, bf16[128,512]{1,0:T(8,128)(2,1)S(1)}, u32[]{:S(2)}, u32[]{:S(2)}) collective-permute-start(bf16[128,512]{1,0:T(8,128)(2,1)S(1)} %get-tuple-element.95), channel_id=1, source_target_pairs={{0,2},{1,3},{2,0},{3,1},{4,6},{5,7},{6,4},{7,5},{8,10},{9,11},{10,... | collective-permute-start | bytes 393224 | tf_op jit(solution)/shard_map/ppermute | solution.py:947
  74.9 12.2 %collective-permute-start.19 = (bf16[128,512]{1,0:T(8,128)(2,1)S(1)}, bf16[128,512]{1,0:T(8,128)(2,1)S(1)}, u32[]{:S(2)}, u32[]{:S(2)}) collective-permute-start(bf16[128,512]{1,0:T(8,128)(2,1)S(1)} %get-tuple-element.96), channel_id=1, source_target_pairs={{0,3},{1,2},{2,1},{3,0},{4,7},{5,6},{6,5},{7,4},{8,11},{9,10},{10,... | collective-permute-start | bytes 393224 | tf_op jit(solution)/shard_map/ppermute | solution.py:947
  122.9 4.6 %collective-permute-start.23 = (bf16[4,4,9,16,512]{4,3,2,1,0:T(8,128)(2,1)S(1)}, bf16[4,4,9,16,512]{4,3,2,1,0:T(8,128)(2,1)S(1)}, u32[]{:S(2)}, u32[]{:S(2)}) collective-permute-start(bf16[4,4,9,16,512]{4,3,2,1,0:T(8,128)(2,1)S(1)} %get-tuple-element.117), channel_id=1, source_target_pairs={{0,4},{4,0},{8,12},{12,8},{16,20},{20,16},{24,28},{28,24},{1,5},{5... | collective-permute-start | bytes 7077896 | tf_op jit(solution)/shard_map/ppermute | solution.py:937
  123.0 15.2 %collective-permute-start.20 = (bf16[128,384]{1,0:T(8,128)(2,1)S(1)}, bf16[128,384]{1,0:T(8,128)(2,1)S(1)}, u32[]{:S(2)}, u32[]{:S(2)}) collective-permute-start(bf16[128,384]{1,0:T(8,128)(2,1)S(1)} %get-tuple-element.106), channel_id=1, source_target_pairs={{0,1},{1,0},{2,3},{3,2},{4,5},{5,4},{6,7},{7,6},{8,9},{9,8},{10,11... | collective-permute-start | bytes 294920 | tf_op jit(solution)/shard_map/ppermute | solution.py:947
  123.3 14.9 %collective-permute-start.21 = (bf16[128,384]{1,0:T(8,128)(2,1)S(1)}, bf16[128,384]{1,0:T(8,128)(2,1)S(1)}, u32[]{:S(2)}, u32[]{:S(2)}) collective-permute-start(bf16[128,384]{1,0:T(8,128)(2,1)S(1)} %get-tuple-element.107), channel_id=1, source_target_pairs={{0,2},{1,3},{2,0},{3,1},{4,6},{5,7},{6,4},{7,5},{8,10},{9,11},{10,... | collective-permute-start | bytes 294920 | tf_op jit(solution)/shard_map/ppermute | solution.py:947
  124.8 13.5 %collective-permute-start.22 = (bf16[128,384]{1,0:T(8,128)(2,1)S(1)}, bf16[128,384]{1,0:T(8,128)(2,1)S(1)}, u32[]{:S(2)}, u32[]{:S(2)}) collective-permute-start(bf16[128,384]{1,0:T(8,128)(2,1)S(1)} %get-tuple-element.108), channel_id=1, source_target_pairs={{0,3},{1,2},{2,1},{3,0},{4,7},{5,6},{6,5},{7,4},{8,11},{9,10},{10,... | collective-permute-start | bytes 294920 | tf_op jit(solution)/shard_map/ppermute | solution.py:947
  128.1 10.2 %collective-permute-start.24 = (bf16[4,9,16,512]{3,2,1,0:T(8,128)(2,1)S(1)}, bf16[4,9,16,512]{3,2,1,0:T(8,128)(2,1)S(1)}, u32[]{:S(2)}, u32[]{:S(2)}) collective-permute-start(bf16[4,9,16,512]{3,2,1,0:T(8,128)(2,1)S(1)} %get-tuple-element.118.after), channel_id=1, source_target_pairs={{0,8},{4,20},{8,0},{12,28},{16,24},{20,4},{24,16},{28,12},{1,9},{5... | collective-permute-start | bytes 1769480 | tf_op jit(solution)/shard_map/ppermute | solution.py:944
  138.4 12.4 %collective-permute-start.25 = (bf16[4,9,16,512]{3,2,1,0:T(8,128)(2,1)S(1)}, bf16[4,9,16,512]{3,2,1,0:T(8,128)(2,1)S(1)}, u32[]{:S(2)}, u32[]{:S(2)}) collective-permute-start(bf16[4,9,16,512]{3,2,1,0:T(8,128)(2,1)S(1)} %mid_sum_b.1), channel_id=1, source_target_pairs={{0,16},{4,12},{8,24},{12,4},{16,0},{20,28},{24,8},{28,20},{1,17},{... | collective-permute-start | bytes 1769480 | tf_op jit(solution)/shard_map/ppermute | solution.py:944
  150.8 6.8 %copy-start.5 = (bf16[9,512,256]{2,1,0:T(8,128)(2,1)S(1)}, bf16[9,512,256]{2,1,0:T(8,128)(2,1)}, u32[]{:S(2)}) copy-start(bf16[9,512,256]{2,1,0:T(8,128)(2,1)} %copy-done.3) | copy-start | bytes 7077892
  156.7 6.3 %collective-permute-start.29 = (bf16[4,4,9,16,256]{4,3,2,1,0:T(8,128)(2,1)S(1)}, bf16[4,4,9,16,256]{4,3,2,1,0:T(8,128)(2,1)S(1)}, u32[]{:S(2)}, u32[]{:S(2)}) collective-permute-start(bf16[4,4,9,16,256]{4,3,2,1,0:T(8,128)(2,1)S(1)} %get-tuple-element.130), channel_id=1, source_target_pairs={{0,4},{4,0},{8,12},{12,8},{16,20},{20,16},{24,28},{28,24},{1,5},{5... | collective-permute-start | bytes 3538952 | tf_op jit(solution)/shard_map/ppermute | solution.py:937
  156.7 9.9 %collective-permute-start.31 = (bf16[4,9,16,512]{3,2,1,0:T(8,128)(2,1)S(1)}, bf16[4,9,16,512]{3,2,1,0:T(8,128)(2,1)S(1)}, u32[]{:S(2)}, u32[]{:S(2)}) collective-permute-start(bf16[4,9,16,512]{3,2,1,0:T(8,128)(2,1)S(1)} %release.9), channel_id=1, source_target_pairs={{0,8},{4,20},{8,0},{12,28},{16,24},{20,4},{24,16},{28,12},{1,9},{5... | collective-permute-start | bytes 1769480 | tf_op jit(solution)/shard_map/ppermute | solution.py:944
  163.3 12.4 %collective-permute-start.30 = (bf16[8,9,16,256]{3,2,1,0:T(8,128)(2,1)S(1)}, bf16[8,9,16,256]{3,2,1,0:T(8,128)(2,1)S(1)}, u32[]{:S(2)}, u32[]{:S(2)}) collective-permute-start(bf16[8,9,16,256]{3,2,1,0:T(8,128)(2,1)S(1)} %get-tuple-element.132), channel_id=1, source_target_pairs={{0,8},{4,20},{8,0},{12,28},{16,24},{20,4},{24,16},{28,12},{1,9},{5... | collective-permute-start | bytes 1769480 | tf_op jit(solution)/shard_map/ppermute | solution.py:944
  164.6 11.2 %collective-permute-start.27 = (bf16[64,1536]{1,0:T(8,128)(2,1)S(1)}, bf16[64,1536]{1,0:T(8,128)(2,1)S(1)}, u32[]{:S(2)}, u32[]{:S(2)}) collective-permute-start(bf16[64,1536]{1,0:T(8,128)(2,1)S(1)} %get-tuple-element.126), channel_id=1, source_target_pairs={{0,2},{1,3},{2,0},{3,1},{4,6},{5,7},{6,4},{7,5},{8,10},{9,11},{10,... | collective-permute-start | bytes 589832 | tf_op jit(solution)/shard_map/ppermute | solution.py:947
  166.9 12.7 %collective-permute-start.33 = (bf16[2,9,16,512]{3,2,1,0:T(8,128)(2,1)S(1)}, bf16[2,9,16,512]{3,2,1,0:T(8,128)(2,1)S(1)}, u32[]{:S(2)}, u32[]{:S(2)}) collective-permute-start(bf16[2,9,16,512]{3,2,1,0:T(8,128)(2,1)S(1)} %get-tuple-element.138), channel_id=1, source_target_pairs={{0,1},{1,0},{2,3},{3,2},{4,5},{5,4},{6,7},{7,6},{8,9},{9,8},{10,11... | collective-permute-start | bytes 884744 | tf_op jit(solution)/shard_map/ppermute | solution.py:947
  175.9 6.8 %collective-permute-start.32 = (bf16[4,9,16,256]{3,2,1,0:T(8,128)(2,1)S(1)}, bf16[4,9,16,256]{3,2,1,0:T(8,128)(2,1)S(1)}, u32[]{:S(2)}, u32[]{:S(2)}) collective-permute-start(bf16[4,9,16,256]{3,2,1,0:T(8,128)(2,1)S(1)} %get-tuple-element.137), channel_id=1, source_target_pairs={{0,16},{4,12},{8,24},{12,4},{16,0},{20,28},{24,8},{28,20},{1,17},{... | collective-permute-start | bytes 884744 | tf_op jit(solution)/shard_map/ppermute | solution.py:944
  176.8 8.6 %collective-permute-start.28 = (bf16[64,1536]{1,0:T(8,128)(2,1)S(1)}, bf16[64,1536]{1,0:T(8,128)(2,1)S(1)}, u32[]{:S(2)}, u32[]{:S(2)}) collective-permute-start(bf16[64,1536]{1,0:T(8,128)(2,1)S(1)} %get-tuple-element.127), channel_id=1, source_target_pairs={{0,3},{1,2},{2,1},{3,0},{4,7},{5,6},{6,5},{7,4},{8,11},{9,10},{10,... | collective-permute-start | bytes 589832 | tf_op jit(solution)/shard_map/ppermute | solution.py:947
  182.7 9.6 %collective-permute-start.34 = (bf16[2,9,16,256]{3,2,1,0:T(8,128)(2,1)S(1)}, bf16[2,9,16,256]{3,2,1,0:T(8,128)(2,1)S(1)}, u32[]{:S(2)}, u32[]{:S(2)}) collective-permute-start(bf16[2,9,16,256]{3,2,1,0:T(8,128)(2,1)S(1)} %get-tuple-element.142), channel_id=1, source_target_pairs={{0,1},{1,0},{2,3},{3,2},{4,5},{5,4},{6,7},{7,6},{8,9},{9,8},{10,11... | collective-permute-start | bytes 442376 | tf_op jit(solution)/shard_map/ppermute | solution.py:947
  182.8 9.6 %collective-permute-start.36 = (bf16[1,9,16,512]{3,2,1,0:T(8,128)(2,1)S(1)}, bf16[1,9,16,512]{3,2,1,0:T(8,128)(2,1)S(1)}, u32[]{:S(2)}, u32[]{:S(2)}) collective-permute-start(bf16[1,9,16,512]{3,2,1,0:T(8,128)(2,1)S(1)} %get-tuple-element.145), channel_id=1, source_target_pairs={{0,2},{1,3},{2,0},{3,1},{4,6},{5,7},{6,4},{7,5},{8,10},{9,11},{10,... | collective-permute-start | bytes 442376 | tf_op jit(solution)/shard_map/ppermute | solution.py:947
  185.4 13.5 %collective-permute-start.26 = (bf16[64,1536]{1,0:T(8,128)(2,1)S(1)}, bf16[64,1536]{1,0:T(8,128)(2,1)S(1)}, u32[]{:S(2)}, u32[]{:S(2)}) collective-permute-start(bf16[64,1536]{1,0:T(8,128)(2,1)S(1)} %get-tuple-element.125), channel_id=1, source_target_pairs={{0,1},{1,0},{2,3},{3,2},{4,5},{5,4},{6,7},{7,6},{8,9},{9,8},{10,11... | collective-permute-start | bytes 589832 | tf_op jit(solution)/shard_map/ppermute | solution.py:947
  192.4 5.7 %collective-permute-start.35 = (bf16[1,9,16,256]{3,2,1,0:T(8,128)(2,1)S(1)}, bf16[1,9,16,256]{3,2,1,0:T(8,128)(2,1)S(1)}, u32[]{:S(2)}, u32[]{:S(2)}) collective-permute-start(bf16[1,9,16,256]{3,2,1,0:T(8,128)(2,1)S(1)} %get-tuple-element.144), channel_id=1, source_target_pairs={{0,2},{1,3},{2,0},{3,1},{4,6},{5,7},{6,4},{7,5},{8,10},{9,11},{10,... | collective-permute-start | bytes 221192 | tf_op jit(solution)/shard_map/ppermute | solution.py:947
  192.5 7.7 %collective-permute-start.40 = (bf16[9,16,512]{2,1,0:T(8,128)(2,1)S(1)}, bf16[9,16,512]{2,1,0:T(8,128)(2,1)S(1)}, u32[]{:S(2)}, u32[]{:S(2)}) collective-permute-start(bf16[9,16,512]{2,1,0:T(8,128)(2,1)S(1)} %mid_sum_3.1.rest_0_.refs_0_), channel_id=1, source_target_pairs={{0,16},{4,12},{8,24},{12,4},{16,0},{20,28},{24,8},{28,20},{1,17},{... | collective-permute-start | bytes 442376 | tf_op jit(solution)/shard_map/ppermute | solution.py:968
  193.3 7.0 %collective-permute-start.41 = (bf16[9,16,512]{2,1,0:T(8,128)(2,1)S(1)}, bf16[9,16,512]{2,1,0:T(8,128)(2,1)S(1)}, u32[]{:S(2)}, u32[]{:S(2)}) collective-permute-start(bf16[9,16,512]{2,1,0:T(8,128)(2,1)S(1)} %mid_sum_3.1.rest_0_.refs_0_), channel_id=1, source_target_pairs={{0,8},{4,20},{8,0},{12,28},{16,24},{20,4},{24,16},{28,12},{1,9},{5... | collective-permute-start | bytes 442376 | tf_op jit(solution)/shard_map/ppermute | solution.py:968
  194.6 7.0 %collective-permute-start.42 = (bf16[9,16,512]{2,1,0:T(8,128)(2,1)S(1)}, bf16[9,16,512]{2,1,0:T(8,128)(2,1)S(1)}, u32[]{:S(2)}, u32[]{:S(2)}) collective-permute-start(bf16[9,16,512]{2,1,0:T(8,128)(2,1)S(1)} %mid_sum_3.1.rest_0_.refs_0_), channel_id=1, source_target_pairs={{0,24},{4,28},{8,16},{12,20},{16,8},{20,12},{24,0},{28,4},{1,25},{... | collective-permute-start | bytes 442376 | tf_op jit(solution)/shard_map/ppermute | solution.py:968
  198.1 4.4 %collective-permute-start.37 = (bf16[9,16,256]{2,1,0:T(8,128)(2,1)S(1)}, bf16[9,16,256]{2,1,0:T(8,128)(2,1)S(1)}, u32[]{:S(2)}, u32[]{:S(2)}) collective-permute-start(bf16[9,16,256]{2,1,0:T(8,128)(2,1)S(1)} %in_sum_3.1.refs_0_), channel_id=1, source_target_pairs={{0,16},{4,12},{8,24},{12,4},{16,0},{20,28},{24,8},{28,20},{1,17},{... | collective-permute-start | bytes 221192 | tf_op jit(solution)/shard_map/ppermute | solution.py:944
  198.9 4.4 %collective-permute-start.38 = (bf16[9,16,256]{2,1,0:T(8,128)(2,1)S(1)}, bf16[9,16,256]{2,1,0:T(8,128)(2,1)S(1)}, u32[]{:S(2)}, u32[]{:S(2)}) collective-permute-start(bf16[9,16,256]{2,1,0:T(8,128)(2,1)S(1)} %in_sum_3.1.refs_0_), channel_id=1, source_target_pairs={{0,8},{4,20},{8,0},{12,28},{16,24},{20,4},{24,16},{28,12},{1,9},{5... | collective-permute-start | bytes 221192 | tf_op jit(solution)/shard_map/ppermute | solution.py:944
  203.3 3.3 %collective-permute-start.43 = (bf16[4,9,16,512]{3,2,1,0:T(8,128)(2,1)S(1)}, bf16[4,9,16,512]{3,2,1,0:T(8,128)(2,1)S(1)}, u32[]{:S(2)}, u32[]{:S(2)}) collective-permute-start(bf16[4,9,16,512]{3,2,1,0:T(8,128)(2,1)S(1)} %mid_stack.1.mine), channel_id=1, source_target_pairs={{0,4},{4,0},{8,12},{12,8},{16,20},{20,16},{24,28},{28,24},{1,5},{5... | collective-permute-start | bytes 1769480 | tf_op jit(solution)/shard_map/ppermute | solution.py:937
  203.9 4.4 %collective-permute-start.39 = (bf16[9,16,256]{2,1,0:T(8,128)(2,1)S(1)}, bf16[9,16,256]{2,1,0:T(8,128)(2,1)S(1)}, u32[]{:S(2)}, u32[]{:S(2)}) collective-permute-start(bf16[9,16,256]{2,1,0:T(8,128)(2,1)S(1)} %collective-permute-done.37.refs_4_.refs_1_), channel_id=1, source_target_pairs={{0,8},{4,20},{8,0},{12,28},{16,24},{20,4},{24,16},{28,12},{1,9},{5... | collective-permute-start | bytes 221192 | tf_op jit(solution)/shard_map/ppermute | solution.py:944
  208.3 1.6 collective-permute-start.44
